TPU v7x, 32 devices: a whole 2x2x4 slice. The times are simulated.
32 devices in a mesh: gx: 4 (over x, core), gy: 2 (over y), gz: 4 (over z).
Axes of the slice: x: 2, y: 2, z: 4, core: 2. Of those that a mesh axis runs over, the one named last changes fastest.
Arguments:
- load: float32 [3, 128, 64, 512], P(None, 'gz', 'gy', 'gx'), may hold values from -6 to 6
- labels: int32 [128, 64, 512], P('gz', 'gy', 'gx'), may hold values from 0 to 15
- mask: int32 [128, 64, 512], P('gz', 'gy', 'gx'), may hold values 0 or 1
- table: float32 [16], replicated, may hold values from 0.25 to 2
Outputs:
- displacement: float32 [3, 128, 64, 512], P(None, 'gz', 'gy', 'gx')
- residual: float32 [3, 128, 64, 512], P(None, 'gz', 'gy', 'gx')
All inputs are finite; a program needn't handle non-finite values. No bound on the sum of `mask` on one device may be relied on, other than what follows from the above.
Results may differ from a plain program's by a relative error of at most 0.0003.
Values sent between devices are 32-bit elements; how exact they have to be, the bound alone decides.
No kernel may reach another device: no remote copies, remote signals or barrier semaphores. Data moves between devices by JAX's collectives and lax.ppermute only.
A program may use at most 128 MiB of HBM per device.

v0:
```python
import jax
import jax.numpy as jnp
from jax import lax
from jax.sharding import PartitionSpec as P

BRICK = 32
INTERSECTION = 4
SWEEPS = 2


LAMBDA_RATIO = 2.0
SIGMA_SHIFT = 0.1
REF_MODULUS = 1.5
VOID_MODULUS = 0.1
HIGHEST = lax.Precision.HIGHEST


def with_halo(cells, sides, width):
    for axis, dim in sides:
        count = lax.axis_size(axis)
        ends = count - 1
        head = lax.slice_in_dim(cells, 0, width, axis=dim)
        tail = lax.slice_in_dim(cells, cells.shape[dim] - width, cells.shape[dim], axis=dim)
        cells = jnp.concatenate(
            [
                lax.ppermute(tail, axis, [(i, (i + 1) % count) for i in range(ends)]),
                cells,
                lax.ppermute(head, axis, [((i + 1) % count, i) for i in range(ends)]),
            ],
            axis=dim,
        )
    return cells


def stiffness_ratio(component, direction):
    return LAMBDA_RATIO if component == direction else 1.0


def sine_table(length):
    grid = jnp.arange(1, length + 1, dtype=jnp.float32)
    return jnp.sqrt(2.0 / (length + 1)) * jnp.sin(
        jnp.pi * grid[:, None] * grid[None, :] / (length + 1)
    )


def eigen_values(length):
    grid = jnp.arange(1, length + 1, dtype=jnp.float32)
    return 2.0 - 2.0 * jnp.cos(jnp.pi * grid / (length + 1))


def ramp_weights(length, margin):
    position = jnp.arange(length, dtype=jnp.float32)
    rising = (position + 0.5) / (2 * margin)
    falling = (length - 0.5 - position) / (2 * margin)
    return jnp.minimum(jnp.minimum(rising, falling), 1.0)


def operator_core(padded_field, padded_modulus):
    centre_modulus = padded_modulus[1:-1, 1:-1, 1:-1]
    centre = padded_field[:, 1:-1, 1:-1, 1:-1]
    windows = []
    faces = []
    for direction in range(3):
        for offset in (0, 2):
            window = [slice(1, -1), slice(1, -1), slice(1, -1)]
            window[direction] = slice(offset, offset + centre_modulus.shape[direction])
            window = tuple(window)
            windows.append(window)
            faces.append(0.5 * (centre_modulus + padded_modulus[window]))
    results = []
    for component in range(3):
        total = SIGMA_SHIFT * centre_modulus * centre[component]
        for number in range(6):
            direction = number // 2
            total = total + stiffness_ratio(component, direction) * faces[number] * (
                centre[component] - padded_field[component][windows[number]]
            )
        results.append(total)
    return jnp.stack(results)


def transform_all(values, along_x, along_y, along_z):
    values = jnp.einsum("czyx,xk->czyk", values, along_x, precision=HIGHEST)
    values = jnp.einsum("czyx,yk->czkx", values, along_y, precision=HIGHEST)
    return jnp.einsum("czyx,zk->ckyx", values, along_z, precision=HIGHEST)


def fold_margin(values, dim, margin):
    extent = values.shape[dim]
    owned = extent - 4 * margin
    centre = lax.slice_in_dim(values, 2 * margin, 2 * margin + owned, axis=dim)
    lower = lax.slice_in_dim(values, 0, margin, axis=dim)
    upper = lax.slice_in_dim(values, extent - margin, extent, axis=dim)
    low_pad = [(0, 0)] * values.ndim
    low_pad[dim] = (0, owned - margin)
    high_pad = [(0, 0)] * values.ndim
    high_pad[dim] = (owned - margin, 0)
    return centre + jnp.pad(lower, low_pad) + jnp.pad(upper, high_pad)


def widen(residual):
    return with_halo(residual, (("gx", 3), ("gy", 2), ("gz", 1)), INTERSECTION)


def local(load, labels, mask, table):
    length = BRICK + 2 * INTERSECTION
    count_x = load.shape[3] // BRICK
    wide_x = count_x * BRICK + 2 * INTERSECTION
    sine = sine_table(length)
    eigen = eigen_values(length)
    eigen_wide = jnp.tile(eigen, count_x)
    denominators = jnp.stack(
        [
            REF_MODULUS
            * (
                stiffness_ratio(component, 0) * eigen[:, None, None]
                + stiffness_ratio(component, 1) * eigen[None, :, None]
                + stiffness_ratio(component, 2) * eigen_wide[None, None, :]
                + SIGMA_SHIFT
            )
            for component in range(3)
        ]
    )
    ramp = ramp_weights(length, INTERSECTION)
    ramped_sine = ramp[:, None] * sine
    position = jnp.arange(wide_x, dtype=jnp.int32)
    brick_start = jnp.arange(count_x, dtype=jnp.int32) * BRICK
    inner = jnp.arange(length, dtype=jnp.int32)
    picker = jnp.where(
        position[:, None, None] - brick_start[None, :, None] == inner[None, None, :], 1.0, 0.0
    )
    forward_x = jnp.einsum("xbi,ik->xbk", picker, ramped_sine, precision=HIGHEST).reshape(
        wide_x, count_x * length
    )
    backward_x = jnp.einsum("xbi,ki->bkx", picker, sine, precision=HIGHEST).reshape(
        count_x * length, wide_x
    )
    picks = jnp.arange(table.shape[0], dtype=jnp.int32)
    looked = jnp.sum(
        jnp.where(labels[None] == picks[:, None, None, None], table[:, None, None, None], 0.0),
        axis=0,
    )
    modulus = jnp.where(mask == 1, looked, VOID_MODULUS)
    solution = jnp.zeros_like(load)
    modulus_near = with_halo(modulus, (("gx", 2), ("gy", 1), ("gz", 0)), 1)
    residual = load
    for sweep in range(SWEEPS):
        spectrum = transform_all(widen(residual), forward_x, ramped_sine, ramped_sine)
        arrived = with_halo(
            transform_all(spectrum / denominators, backward_x, sine, sine),
            (("gx", 3), ("gy", 2), ("gz", 1)),
            INTERSECTION,
        )
        fold_arrived = arrived
        for dim in (1, 2, 3):
            fold_arrived = fold_margin(fold_arrived, dim, INTERSECTION)
        solution = solution + fold_arrived
        nearby = with_halo(fold_arrived, (("gx", 3), ("gy", 2), ("gz", 1)), 1)
        residual = residual - operator_core(nearby, modulus_near)
    return (solution, residual)


def solution(mesh):
    placed = (P(None, "gz", "gy", "gx"), P("gz", "gy", "gx"), P("gz", "gy", "gx"), P())
    return jax.shard_map(
        local,
        mesh=mesh,
        in_specs=placed,
        out_specs=(P(None, "gz", "gy", "gx"), P(None, "gz", "gy", "gx")),
        check_vma=False,
    )
```

profile of v0, /device:TPU:0, one launch (start us, length us, event | category | flops | bytes accessed | tf_op | source)
XLA Modules:
  0.0 407.0 jit_solution(5141565756267139515)
XLA Ops:
  25.8 7.0 %collective-permute-done.2 = f32[3,32,4,136]{3,1,2,0:T(8,128)S(1)} collective-permute-done((f32[3,32,4,136]{3,1,2,0:T(8,128)S(1)}, f32[3,32,4,136]{3,1,2,0:T(8,128)S(1)}, u32[]{:S(2)}, u32[]{:S(2)}) %collective-permute-start.2) | collective-permute-done | bytes 208928 | tf_op jit(solution)/shard_map/ppermute | solution.py:26
  33.1 4.6 %collective-permute-done.3 = f32[3,32,4,136]{3,1,2,0:T(8,128)S(1)} collective-permute-done((f32[3,32,4,136]{3,1,2,0:T(8,128)S(1)}, f32[3,32,4,136]{3,1,2,0:T(8,128)S(1)}, u32[]{:S(2)}, u32[]{:S(2)}) %collective-permute-start.3) | collective-permute-done | bytes 208928 | tf_op jit(solution)/shard_map/ppermute | solution.py:28
  43.9 9.1 %collective-permute-done.4 = f32[3,4,40,136]{3,2,1,0:T(8,128)S(1)} collective-permute-done((f32[3,4,40,136]{3,2,1,0:T(8,128)S(1)}, f32[3,4,40,136]{3,2,1,0:T(8,128)S(1)}, u32[]{:S(2)}, u32[]{:S(2)}) %collective-permute-start.4) | collective-permute-done | bytes 261152 | tf_op jit(solution)/shard_map/ppermute | solution.py:26
  57.2 5.0 %fusion = f32[3,40,40,160]{3,2,1,0:T(8,128)S(1)} fusion(f32[136,160,1,1]{0,1,3,2:T(8,128)S(1)} %bitcast.116, f32[3,4,40,136]{3,2,1,0:T(8,128)S(1)} %collective-permute-done.5, f32[3,32,4,136]{3,2,1,0:T(4,128)S(1)} %copy.92, f32[3,32,32,4]{3,2,1,0:T(8,128)S(1)} %copy-done.29, f32[3,32,32,128]{3,2,1,0:T(8,128)S(1)} %copy-done.4, ...), kind=kOutput, calls=%fused_computation.4 | convolution fusion | flops 1257292800 | bytes 5770240 | tf_op jit(solution)/shard_map/czyx,xk->czyk/dot_general | solution.py:83
  62.2 4.8 %convolution_bitcast_fusion.3 = f32[3,40,40,160]{3,2,1,0:T(8,128)S(1)} fusion(f32[3,40,40,160]{3,2,1,0:T(8,128)S(1)} %fusion, f32[40]{0:T(128)S(1)} %fusion.207, f32[40]{0:T(128)S(1)} %get-tuple-element.70, f32[40]{0:T(128)S(1)} %get-tuple-element.71), kind=kOutput, calls=%fused_computation.53 | convolution fusion | flops 368644800 | bytes 6144480 | tf_op jit(solution)/shard_map/czyx,yk->czkx/dot_general | solution.py:84
  67.1 7.0 %bitcast_divide_fusion.1 = f32[3,40,40,160]{3,1,2,0:T(8,128)S(1)} fusion(f32[1,40,40,160]{3,1,2,0:T(8,128)S(1)} %add_multiply_fusion, f32[1,40,40,160]{3,1,2,0:T(8,128)S(1)} %copy-done.39, f32[1,40,40,160]{3,1,2,0:T(8,128)S(1)} %copy-done.37, f32[3,40,40,160]{3,2,1,0:T(8,128)S(1)} %convolution_bitcast_fusion.3, f32[40]{0:T(128)S(1)} %fusion.207, ...), kind=kOutput, calls=%fused_computation.21 | convolution fusion | flops 370948800 | bytes 9216480 | tf_op jit(solution)/shard_map/czyx,zk->ckyx/dot_general | solution.py:85
  74.1 5.3 %fusion.24 = f32[3,40,40,136]{3,2,1,0:T(8,128)S(1)} fusion(f32[160,136,1,1]{1,0,3,2:T(8,128)S(1)} %bitcast.114, f32[3,40,40,160]{3,1,2,0:T(8,128)S(1)} %bitcast_divide_fusion.1), kind=kOutput, calls=%fused_computation.32 | convolution fusion | flops 1253376000 | bytes 5770240 | tf_op jit(solution)/shard_map/czyx,xk->czyk/dot_general | solution.py:83
  79.4 5.0 %convolution_bitcast_fusion.2 = f32[3,40,40,136]{3,2,1,0:T(8,128)S(1)} fusion(f32[3,40,40,136]{3,2,1,0:T(8,128)S(1)} %fusion.24, f32[40]{0:T(128)S(1)} %get-tuple-element.70, f32[40]{0:T(128)S(1)} %get-tuple-element.71), kind=kOutput, calls=%fused_computation.52 | convolution fusion | flops 313348800 | bytes 5222720 | tf_op jit(solution)/shard_map/czyx,yk->czkx/dot_general | solution.py:84
  84.5 6.4 %fusion.34 = f32[3,40,40,136]{3,1,2,0:T(8,128)S(1)} fusion(f32[3,40,40,136]{3,2,1,0:T(8,128)S(1)} %convolution_bitcast_fusion.2, f32[40]{0:T(128)S(1)} %get-tuple-element.70, f32[40]{0:T(128)S(1)} %get-tuple-element.71), kind=kOutput, calls=%fused_computation.48 | convolution fusion | flops 313348800 | bytes 5222720 | tf_op jit(solution)/shard_map/czyx,zk->ckyx/dot_general | solution.py:85
  114.4 6.5 %collective-permute-done.8 = f32[3,40,4,144]{3,1,2,0:T(8,128)S(1)} collective-permute-done((f32[3,40,4,144]{3,1,2,0:T(8,128)S(1)}, f32[3,40,4,144]{3,1,2,0:T(8,128)S(1)}, u32[]{:S(2)}, u32[]{:S(2)}) %collective-permute-start.8) | collective-permute-done | bytes 276512 | tf_op jit(solution)/shard_map/ppermute | solution.py:26
  121.0 4.7 %collective-permute-done.9 = f32[3,40,4,144]{3,1,2,0:T(8,128)S(1)} collective-permute-done((f32[3,40,4,144]{3,1,2,0:T(8,128)S(1)}, f32[3,40,4,144]{3,1,2,0:T(8,128)S(1)}, u32[]{:S(2)}, u32[]{:S(2)}) %collective-permute-start.9) | collective-permute-done | bytes 276512 | tf_op jit(solution)/shard_map/ppermute | solution.py:28
  132.0 4.5 %pad_maximum_fusion = f32[3,40,48,144]{3,1,2,0:T(8,128)S(1)} fusion(f32[3,40,4,144]{3,1,2,0:T(8,128)S(1)} %collective-permute-done.9, f32[3,40,40,4]{3,1,2,0:T(8,128)S(1)} %copy-done.11, f32[3,40,40,136]{3,1,2,0:T(8,128)S(1)} %bitcast.111, f32[3,40,40,4]{3,1,2,0:T(8,128)} %copy-done.9, f32[3,40,4,144]{3,1,2,0:T(8,128)S(1)} %collective-permute-done.8), kind=kLoop, calls=%fused_computation.2 | loop fusion | flops 3317760 | bytes 6635520 | tf_op jit(solution)/shard_map/concatenate | solution.py:24
  136.5 6.3 %collective-permute-done.10 = f32[3,4,48,144]{3,1,2,0:T(4,128)S(1)} collective-permute-done((f32[3,4,48,144]{3,1,2,0:T(4,128)S(1)}, f32[3,4,48,144]{3,1,2,0:T(4,128)S(1)}, u32[]{:S(2)}, u32[]{:S(2)}) %collective-permute-start.10) | collective-permute-done | bytes 331808 | tf_op jit(solution)/shard_map/ppermute | solution.py:26
  142.8 4.7 %collective-permute-done.11 = f32[3,4,48,144]{3,1,2,0:T(4,128)S(1)} collective-permute-done((f32[3,4,48,144]{3,1,2,0:T(4,128)S(1)}, f32[3,4,48,144]{3,1,2,0:T(4,128)S(1)}, u32[]{:S(2)}, u32[]{:S(2)}) %collective-permute-start.11) | collective-permute-done | bytes 331808 | tf_op jit(solution)/shard_map/ppermute | solution.py:28
  175.5 4.5 %collective-permute-start.14 = (f32[32,1,130]{2,0,1:T(8,128)S(1)}, f32[32,1,130]{2,0,1:T(8,128)S(1)}, u32[]{:S(2)}, u32[]{:S(2)}) collective-permute-start(f32[32,1,130]{2,0,1:T(8,128)S(1)} %get-tuple-element.58), channel_id=1, source_target_pairs={{0,4},{1,5},{2,6},{3,7},{8,12},{9,13},{10,14},{11,15},{16,20},{17,... | collective-permute-start | bytes 49928 | tf_op jit(solution)/shard_map/ppermute | solution.py:26
  187.3 4.5 %collective-permute-start.16 = (f32[1,34,130]{2,0,1:T(1,128)S(1)}, f32[1,34,130]{2,0,1:T(1,128)S(1)}, u32[]{:S(2)}, u32[]{:S(2)}) collective-permute-start(f32[1,34,130]{2,0,1:T(1,128)S(1)} %get-tuple-element.52), channel_id=1, source_target_pairs={{0,1},{1,2},{2,3},{4,5},{5,6},{6,7},{8,9},{9,10},{10,11},{12,13},{... | collective-permute-start | bytes 53048 | tf_op jit(solution)/shard_map/ppermute | solution.py:26
  225.8 4.7 %collective-permute-start.26 = (f32[3,32,4,136]{3,1,2,0:T(8,128)S(1)}, f32[3,32,4,136]{3,1,2,0:T(8,128)S(1)}, u32[]{:S(2)}, u32[]{:S(2)}) collective-permute-start(f32[3,32,4,136]{3,1,2,0:T(8,128)S(1)} %get-tuple-element.39), channel_id=1, source_target_pairs={{0,4},{1,5},{2,6},{3,7},{8,12},{9,13},{10,14},{11,15},{16,20},{17,... | collective-permute-start | bytes 626696 | tf_op jit(solution)/shard_map/ppermute | solution.py:26
  231.9 4.9 %collective-permute-done.26 = f32[3,32,4,136]{3,1,2,0:T(8,128)S(1)} collective-permute-done((f32[3,32,4,136]{3,1,2,0:T(8,128)S(1)}, f32[3,32,4,136]{3,1,2,0:T(8,128)S(1)}, u32[]{:S(2)}, u32[]{:S(2)}) %collective-permute-start.26) | collective-permute-done | bytes 208928 | tf_op jit(solution)/shard_map/ppermute | solution.py:26
  236.8 4.7 %collective-permute-done.27 = f32[3,32,4,136]{3,1,2,0:T(8,128)S(1)} collective-permute-done((f32[3,32,4,136]{3,1,2,0:T(8,128)S(1)}, f32[3,32,4,136]{3,1,2,0:T(8,128)S(1)}, u32[]{:S(2)}, u32[]{:S(2)}) %collective-permute-start.27) | collective-permute-done | bytes 208928 | tf_op jit(solution)/shard_map/ppermute | solution.py:28
  247.2 8.3 %collective-permute-done.28 = f32[3,4,40,136]{3,1,2,0:T(4,128)S(1)} collective-permute-done((f32[3,4,40,136]{3,1,2,0:T(4,128)S(1)}, f32[3,4,40,136]{3,1,2,0:T(4,128)S(1)}, u32[]{:S(2)}, u32[]{:S(2)}) %collective-permute-start.28) | collective-permute-done | bytes 261152 | tf_op jit(solution)/shard_map/ppermute | solution.py:26
  255.5 4.8 %collective-permute-done.29 = f32[3,4,40,136]{3,1,2,0:T(4,128)S(1)} collective-permute-done((f32[3,4,40,136]{3,1,2,0:T(4,128)S(1)}, f32[3,4,40,136]{3,1,2,0:T(4,128)S(1)}, u32[]{:S(2)}, u32[]{:S(2)}) %collective-permute-start.29) | collective-permute-done | bytes 261152 | tf_op jit(solution)/shard_map/ppermute | solution.py:28
  264.6 5.2 %fusion.20 = f32[3,40,40,160]{3,2,1,0:T(8,128)S(1)} fusion(f32[136,160,1,1]{0,1,3,2:T(8,128)S(1)} %bitcast.117, f32[3,40,40,136]{3,1,2,0:T(8,128)S(1)} %pad_maximum_fusion.3), kind=kOutput, calls=%fused_computation.28 | convolution fusion | flops 1253376000 | bytes 5770240 | tf_op jit(solution)/shard_map/czyx,xk->czyk/dot_general | solution.py:83
  269.9 4.9 %convolution_bitcast_fusion.1 = f32[3,40,40,160]{3,2,1,0:T(8,128)S(1)} fusion(f32[3,40,40,160]{3,2,1,0:T(8,128)S(1)} %fusion.20, f32[40]{0:T(128)S(1)} %fusion.207, f32[40]{0:T(128)S(1)} %get-tuple-element.70, f32[40]{0:T(128)S(1)} %get-tuple-element.71), kind=kOutput, calls=%fused_computation.51 | convolution fusion | flops 368644800 | bytes 6144480 | tf_op jit(solution)/shard_map/czyx,yk->czkx/dot_general | solution.py:84
  274.8 7.0 %bitcast_divide_fusion = f32[3,40,40,160]{3,1,2,0:T(8,128)S(1)} fusion(f32[1,40,40,160]{3,1,2,0:T(8,128)S(1)} %copy-done.42, f32[1,40,40,160]{3,1,2,0:T(8,128)S(1)} %copy-done.40, f32[1,40,40,160]{3,1,2,0:T(8,128)S(1)} %copy-done.38, f32[3,40,40,160]{3,2,1,0:T(8,128)S(1)} %convolution_bitcast_fusion.1, f32[40]{0:T(128)S(1)} %fusion.207, ...), kind=kOutput, calls=%fused_computation.20 | convolution fusion | flops 370948800 | bytes 9216480 | tf_op jit(solution)/shard_map/czyx,zk->ckyx/dot_general | solution.py:85
  281.8 5.3 %fusion.16 = f32[3,40,40,136]{3,2,1,0:T(8,128)S(1)} fusion(f32[160,136,1,1]{1,0,3,2:T(8,128)S(1)} %bitcast.115, f32[3,40,40,160]{3,1,2,0:T(8,128)S(1)} %bitcast_divide_fusion), kind=kOutput, calls=%fused_computation.24 | convolution fusion | flops 1253376000 | bytes 5770240 | tf_op jit(solution)/shard_map/czyx,xk->czyk/dot_general | solution.py:83
  287.1 5.0 %convolution_bitcast_fusion = f32[3,40,40,136]{3,2,1,0:T(8,128)S(1)} fusion(f32[3,40,40,136]{3,2,1,0:T(8,128)S(1)} %fusion.16, f32[40]{0:T(128)S(1)} %get-tuple-element.70, f32[40]{0:T(128)S(1)} %get-tuple-element.71), kind=kOutput, calls=%fused_computation.50 | convolution fusion | flops 313348800 | bytes 5222720 | tf_op jit(solution)/shard_map/czyx,yk->czkx/dot_general | solution.py:84
  292.1 6.4 %fusion.37 = f32[3,40,40,136]{3,1,2,0:T(8,128)S(1)} fusion(f32[3,40,40,136]{3,2,1,0:T(8,128)S(1)} %convolution_bitcast_fusion, f32[40]{0:T(128)S(1)} %get-tuple-element.70, f32[40]{0:T(128)S(1)} %get-tuple-element.71), kind=kOutput, calls=%fused_computation.49 | convolution fusion | flops 313348800 | bytes 5222720 | tf_op jit(solution)/shard_map/czyx,zk->ckyx/dot_general | solution.py:85
  324.4 6.2 %collective-permute-done.32 = f32[3,40,4,144]{3,1,2,0:T(8,128)S(1)} collective-permute-done((f32[3,40,4,144]{3,1,2,0:T(8,128)S(1)}, f32[3,40,4,144]{3,1,2,0:T(8,128)S(1)}, u32[]{:S(2)}, u32[]{:S(2)}) %collective-permute-start.32) | collective-permute-done | bytes 276512 | tf_op jit(solution)/shard_map/ppermute | solution.py:26
  330.6 4.7 %collective-permute-done.33 = f32[3,40,4,144]{3,1,2,0:T(8,128)S(1)} collective-permute-done((f32[3,40,4,144]{3,1,2,0:T(8,128)S(1)}, f32[3,40,4,144]{3,1,2,0:T(8,128)S(1)}, u32[]{:S(2)}, u32[]{:S(2)}) %collective-permute-start.33) | collective-permute-done | bytes 276512 | tf_op jit(solution)/shard_map/ppermute | solution.py:28
  342.8 6.9 %collective-permute-done.34 = f32[3,4,48,144]{3,1,2,0:T(4,128)S(1)} collective-permute-done((f32[3,4,48,144]{3,1,2,0:T(4,128)S(1)}, f32[3,4,48,144]{3,1,2,0:T(4,128)S(1)}, u32[]{:S(2)}, u32[]{:S(2)}) %collective-permute-start.34) | collective-permute-done | bytes 331808 | tf_op jit(solution)/shard_map/ppermute | solution.py:26
  349.7 4.7 %collective-permute-done.35 = f32[3,4,48,144]{3,1,2,0:T(4,128)S(1)} collective-permute-done((f32[3,4,48,144]{3,1,2,0:T(4,128)S(1)}, f32[3,4,48,144]{3,1,2,0:T(4,128)S(1)}, u32[]{:S(2)}, u32[]{:S(2)}) %collective-permute-start.35) | collective-permute-done | bytes 331808 | tf_op jit(solution)/shard_map/ppermute | solution.py:28
  380.4 4.7 %collective-permute-done.39 = f32[3,32,1,130]{3,1,2,0:T(8,128)S(1)} collective-permute-done((f32[3,32,1,130]{3,1,2,0:T(8,128)S(1)}, f32[3,32,1,130]{3,1,2,0:T(8,128)S(1)}, u32[]{:S(2)}, u32[]{:S(2)}) %collective-permute-start.39) | collective-permute-done | bytes 49952 | tf_op jit(solution)/shard_map/ppermute | solution.py:28
  (265 shorter events, 226.0 us)
Async XLA Ops:
  4.6 9.2 %collective-permute-start = (f32[3,32,32,4]{2,1,3,0:T(8,128)}, f32[3,32,32,4]{2,1,3,0:T(8,128)}, u32[]{:S(2)}, u32[]{:S(2)}) collective-permute-start(f32[3,32,32,4]{2,1,3,0:T(8,128)} %copy.142), channel_id=1, source_target_pairs={{0,8},{8,16},{16,24},{1,9},{9,17},{17,25},{2,10},{10,18},{18,26},{... | collective-permute-start | bytes 147464 | tf_op jit(solution)/shard_map/ppermute | solution.py:26
  20.1 12.7 %collective-permute-start.2 = (f32[3,32,4,136]{3,1,2,0:T(8,128)S(1)}, f32[3,32,4,136]{3,1,2,0:T(8,128)S(1)}, u32[]{:S(2)}, u32[]{:S(2)}) collective-permute-start(f32[3,32,4,136]{3,1,2,0:T(8,128)S(1)} %copy.89), channel_id=1, source_target_pairs={{0,4},{1,5},{2,6},{3,7},{8,12},{9,13},{10,14},{11,15},{16,20},{17,... | collective-permute-start | bytes 626696 | tf_op jit(solution)/shard_map/ppermute | solution.py:26
  24.5 13.1 %collective-permute-start.3 = (f32[3,32,4,136]{3,1,2,0:T(8,128)S(1)}, f32[3,32,4,136]{3,1,2,0:T(8,128)S(1)}, u32[]{:S(2)}, u32[]{:S(2)}) collective-permute-start(f32[3,32,4,136]{3,1,2,0:T(8,128)S(1)} %copy.90), channel_id=1, source_target_pairs={{4,0},{5,1},{6,2},{7,3},{12,8},{13,9},{14,10},{15,11},{20,16},{21,... | collective-permute-start | bytes 626696 | tf_op jit(solution)/shard_map/ppermute | solution.py:28
  38.4 14.7 %collective-permute-start.4 = (f32[3,4,40,136]{3,2,1,0:T(8,128)S(1)}, f32[3,4,40,136]{3,2,1,0:T(8,128)S(1)}, u32[]{:S(2)}, u32[]{:S(2)}) collective-permute-start(f32[3,4,40,136]{3,2,1,0:T(8,128)S(1)} %get-tuple-element.27), channel_id=1, source_target_pairs={{0,1},{1,2},{2,3},{4,5},{5,6},{6,7},{8,9},{9,10},{10,11},{12,13},{... | collective-permute-start | bytes 783368 | tf_op jit(solution)/shard_map/ppermute | solution.py:26
  41.9 15.3 %collective-permute-start.5 = (f32[3,4,40,136]{3,2,1,0:T(8,128)S(1)}, f32[3,4,40,136]{3,2,1,0:T(8,128)S(1)}, u32[]{:S(2)}, u32[]{:S(2)}) collective-permute-start(f32[3,4,40,136]{3,2,1,0:T(8,128)S(1)} %get-tuple-element.28), channel_id=1, source_target_pairs={{1,0},{2,1},{3,2},{5,4},{6,5},{7,6},{9,8},{10,9},{11,10},{13,12},{... | collective-permute-start | bytes 783368 | tf_op jit(solution)/shard_map/ppermute | solution.py:28
  109.5 11.5 %collective-permute-start.8 = (f32[3,40,4,144]{3,1,2,0:T(8,128)S(1)}, f32[3,40,4,144]{3,1,2,0:T(8,128)S(1)}, u32[]{:S(2)}, u32[]{:S(2)}) collective-permute-start(f32[3,40,4,144]{3,1,2,0:T(8,128)S(1)} %get-tuple-element.23), channel_id=1, source_target_pairs={{0,4},{1,5},{2,6},{3,7},{8,12},{9,13},{10,14},{11,15},{16,20},{17,... | collective-permute-start | bytes 829448 | tf_op jit(solution)/shard_map/ppermute | solution.py:26
  111.7 13.9 %collective-permute-start.9 = (f32[3,40,4,144]{3,1,2,0:T(8,128)S(1)}, f32[3,40,4,144]{3,1,2,0:T(8,128)S(1)}, u32[]{:S(2)}, u32[]{:S(2)}) collective-permute-start(f32[3,40,4,144]{3,1,2,0:T(8,128)S(1)} %get-tuple-element.24), channel_id=1, source_target_pairs={{4,0},{5,1},{6,2},{7,3},{12,8},{13,9},{14,10},{15,11},{20,16},{21,... | collective-permute-start | bytes 829448 | tf_op jit(solution)/shard_map/ppermute | solution.py:28
  126.6 16.3 %collective-permute-start.10 = (f32[3,4,48,144]{3,1,2,0:T(4,128)S(1)}, f32[3,4,48,144]{3,1,2,0:T(4,128)S(1)}, u32[]{:S(2)}, u32[]{:S(2)}) collective-permute-start(f32[3,4,48,144]{3,1,2,0:T(4,128)S(1)} %get-tuple-element.19), channel_id=1, source_target_pairs={{0,1},{1,2},{2,3},{4,5},{5,6},{6,7},{8,9},{9,10},{10,11},{12,13},{... | collective-permute-start | bytes 995336 | tf_op jit(solution)/shard_map/ppermute | solution.py:26
  130.1 17.5 %collective-permute-start.11 = (f32[3,4,48,144]{3,1,2,0:T(4,128)S(1)}, f32[3,4,48,144]{3,1,2,0:T(4,128)S(1)}, u32[]{:S(2)}, u32[]{:S(2)}) collective-permute-start(f32[3,4,48,144]{3,1,2,0:T(4,128)S(1)} %get-tuple-element.20), channel_id=1, source_target_pairs={{1,0},{2,1},{3,2},{5,4},{6,5},{7,6},{9,8},{10,9},{11,10},{13,12},{... | collective-permute-start | bytes 995336 | tf_op jit(solution)/shard_map/ppermute | solution.py:28
  155.4 11.3 %collective-permute-start.17 = (f32[3,32,32,1]{2,1,3,0:T(8,128)S(1)}, f32[3,32,32,1]{2,1,3,0:T(8,128)S(1)}, u32[]{:S(2)}, u32[]{:S(2)}) collective-permute-start(f32[3,32,32,1]{2,1,3,0:T(8,128)S(1)} %copy.105), channel_id=1, source_target_pairs={{0,8},{8,16},{16,24},{1,9},{9,17},{17,25},{2,10},{10,18},{18,26},{... | collective-permute-start | bytes 36872 | tf_op jit(solution)/shard_map/ppermute | solution.py:26
  159.9 9.2 %collective-permute-start.18 = (f32[3,32,32,1]{2,1,3,0:T(8,128)S(1)}, f32[3,32,32,1]{2,1,3,0:T(8,128)S(1)}, u32[]{:S(2)}, u32[]{:S(2)}) collective-permute-start(f32[3,32,32,1]{2,1,3,0:T(8,128)S(1)} %copy.106), channel_id=1, source_target_pairs={{8,0},{16,8},{24,16},{9,1},{17,9},{25,17},{10,2},{18,10},{26,18},{... | collective-permute-start | bytes 36872 | tf_op jit(solution)/shard_map/ppermute | solution.py:28
  162.3 13.0 %collective-permute-start.12 = (f32[32,32,1]{2,0,1:T(8,128)}, f32[32,32,1]{2,0,1:T(8,128)S(1)}, u32[]{:S(2)}, u32[]{:S(2)}) collective-permute-start(f32[32,32,1]{2,0,1:T(8,128)} %get-tuple-element.64), channel_id=1, source_target_pairs={{0,8},{8,16},{16,24},{1,9},{9,17},{17,25},{2,10},{10,18},{18,26},{... | collective-permute-start | bytes 12296 | tf_op jit(solution)/shard_map/ppermute | solution.py:26
  165.4 10.0 %collective-permute-start.13 = (f32[32,32,1]{2,0,1:T(8,128)}, f32[32,32,1]{2,0,1:T(8,128)S(1)}, u32[]{:S(2)}, u32[]{:S(2)}) collective-permute-start(f32[32,32,1]{2,0,1:T(8,128)} %get-tuple-element.63), channel_id=1, source_target_pairs={{8,0},{16,8},{24,16},{9,1},{17,9},{25,17},{10,2},{18,10},{26,18},{... | collective-permute-start | bytes 12296 | tf_op jit(solution)/shard_map/ppermute | solution.py:28
  172.6 8.9 %collective-permute-start.19 = (f32[3,32,1,130]{3,1,2,0:T(8,128)S(1)}, f32[3,32,1,130]{3,1,2,0:T(8,128)S(1)}, u32[]{:S(2)}, u32[]{:S(2)}) collective-permute-start(f32[3,32,1,130]{3,1,2,0:T(8,128)S(1)} %get-tuple-element.41), channel_id=1, source_target_pairs={{0,4},{1,5},{2,6},{3,7},{8,12},{9,13},{10,14},{11,15},{16,20},{17,... | collective-permute-start | bytes 149768 | tf_op jit(solution)/shard_map/ppermute | solution.py:26
  174.0 7.5 %collective-permute-start.20 = (f32[3,32,1,130]{3,1,2,0:T(8,128)S(1)}, f32[3,32,1,130]{3,1,2,0:T(8,128)S(1)}, u32[]{:S(2)}, u32[]{:S(2)}) collective-permute-start(f32[3,32,1,130]{3,1,2,0:T(8,128)S(1)} %get-tuple-element.42), channel_id=1, source_target_pairs={{4,0},{5,1},{6,2},{7,3},{12,8},{13,9},{14,10},{15,11},{20,16},{21,... | collective-permute-start | bytes 149768 | tf_op jit(solution)/shard_map/ppermute | solution.py:28
  175.5 11.5 %collective-permute-start.14 = (f32[32,1,130]{2,0,1:T(8,128)S(1)}, f32[32,1,130]{2,0,1:T(8,128)S(1)}, u32[]{:S(2)}, u32[]{:S(2)}) collective-permute-start(f32[32,1,130]{2,0,1:T(8,128)S(1)} %get-tuple-element.58), channel_id=1, source_target_pairs={{0,4},{1,5},{2,6},{3,7},{8,12},{9,13},{10,14},{11,15},{16,20},{17,... | collective-permute-start | bytes 49928 | tf_op jit(solution)/shard_map/ppermute | solution.py:26
  182.2 10.9 %collective-permute-start.21 = (f32[3,1,34,130]{3,1,2,0:T(1,128)S(1)}, f32[3,1,34,130]{3,1,2,0:T(1,128)S(1)}, u32[]{:S(2)}, u32[]{:S(2)}) collective-permute-start(f32[3,1,34,130]{3,1,2,0:T(1,128)S(1)} %get-tuple-element.33), channel_id=1, source_target_pairs={{0,1},{1,2},{2,3},{4,5},{5,6},{6,7},{8,9},{9,10},{10,11},{12,13},{... | collective-permute-start | bytes 159128 | tf_op jit(solution)/shard_map/ppermute | solution.py:26
  185.7 7.6 %collective-permute-start.22 = (f32[3,1,34,130]{3,1,2,0:T(1,128)S(1)}, f32[3,1,34,130]{3,1,2,0:T(1,128)S(1)}, u32[]{:S(2)}, u32[]{:S(2)}) collective-permute-start(f32[3,1,34,130]{3,1,2,0:T(1,128)S(1)} %get-tuple-element.34), channel_id=1, source_target_pairs={{1,0},{2,1},{3,2},{5,4},{6,5},{7,6},{9,8},{10,9},{11,10},{13,12},{... | collective-permute-start | bytes 159128 | tf_op jit(solution)/shard_map/ppermute | solution.py:28
  187.3 9.4 %collective-permute-start.16 = (f32[1,34,130]{2,0,1:T(1,128)S(1)}, f32[1,34,130]{2,0,1:T(1,128)S(1)}, u32[]{:S(2)}, u32[]{:S(2)}) collective-permute-start(f32[1,34,130]{2,0,1:T(1,128)S(1)} %get-tuple-element.52), channel_id=1, source_target_pairs={{0,1},{1,2},{2,3},{4,5},{5,6},{6,7},{8,9},{9,10},{10,11},{12,13},{... | collective-permute-start | bytes 53048 | tf_op jit(solution)/shard_map/ppermute | solution.py:26
  213.5 7.2 %collective-permute-start.25 = (f32[3,32,32,4]{2,1,3,0:T(8,128)S(1)}, f32[3,32,32,4]{2,1,3,0:T(8,128)}, u32[]{:S(2)}, u32[]{:S(2)}) collective-permute-start(f32[3,32,32,4]{2,1,3,0:T(8,128)S(1)} %copy.111), channel_id=1, source_target_pairs={{8,0},{16,8},{24,16},{9,1},{17,9},{25,17},{10,2},{18,10},{26,18},{... | collective-permute-start | bytes 147464 | tf_op jit(solution)/shard_map/ppermute | solution.py:28
  225.8 10.9 %collective-permute-start.26 = (f32[3,32,4,136]{3,1,2,0:T(8,128)S(1)}, f32[3,32,4,136]{3,1,2,0:T(8,128)S(1)}, u32[]{:S(2)}, u32[]{:S(2)}) collective-permute-start(f32[3,32,4,136]{3,1,2,0:T(8,128)S(1)} %get-tuple-element.39), channel_id=1, source_target_pairs={{0,4},{1,5},{2,6},{3,7},{8,12},{9,13},{10,14},{11,15},{16,20},{17,... | collective-permute-start | bytes 626696 | tf_op jit(solution)/shard_map/ppermute | solution.py:26
  230.6 10.9 %collective-permute-start.27 = (f32[3,32,4,136]{3,1,2,0:T(8,128)S(1)}, f32[3,32,4,136]{3,1,2,0:T(8,128)S(1)}, u32[]{:S(2)}, u32[]{:S(2)}) collective-permute-start(f32[3,32,4,136]{3,1,2,0:T(8,128)S(1)} %get-tuple-element.40), channel_id=1, source_target_pairs={{4,0},{5,1},{6,2},{7,3},{12,8},{13,9},{14,10},{15,11},{20,16},{21,... | collective-permute-start | bytes 626696 | tf_op jit(solution)/shard_map/ppermute | solution.py:28
  242.2 13.3 %collective-permute-start.28 = (f32[3,4,40,136]{3,1,2,0:T(4,128)S(1)}, f32[3,4,40,136]{3,1,2,0:T(4,128)S(1)}, u32[]{:S(2)}, u32[]{:S(2)}) collective-permute-start(f32[3,4,40,136]{3,1,2,0:T(4,128)S(1)} %get-tuple-element.25), channel_id=1, source_target_pairs={{0,1},{1,2},{2,3},{4,5},{5,6},{6,7},{8,9},{9,10},{10,11},{12,13},{... | collective-permute-start | bytes 783368 | tf_op jit(solution)/shard_map/ppermute | solution.py:26
  245.8 14.5 %collective-permute-start.29 = (f32[3,4,40,136]{3,1,2,0:T(4,128)S(1)}, f32[3,4,40,136]{3,1,2,0:T(4,128)S(1)}, u32[]{:S(2)}, u32[]{:S(2)}) collective-permute-start(f32[3,4,40,136]{3,1,2,0:T(4,128)S(1)} %get-tuple-element.26), channel_id=1, source_target_pairs={{1,0},{2,1},{3,2},{5,4},{6,5},{7,6},{9,8},{10,9},{11,10},{13,12},{... | collective-permute-start | bytes 783368 | tf_op jit(solution)/shard_map/ppermute | solution.py:28
  304.8 7.9 %collective-permute-start.30 = (f32[3,40,40,4]{2,1,3,0:T(8,128)S(1)}, f32[3,40,40,4]{2,1,3,0:T(8,128)S(1)}, u32[]{:S(2)}, u32[]{:S(2)}) collective-permute-start(f32[3,40,40,4]{2,1,3,0:T(8,128)S(1)} %copy.120), channel_id=1, source_target_pairs={{0,8},{8,16},{16,24},{1,9},{9,17},{17,25},{2,10},{10,18},{18,26},{... | collective-permute-start | bytes 230408 | tf_op jit(solution)/shard_map/ppermute | solution.py:26
  320.8 9.8 %collective-permute-start.32 = (f32[3,40,4,144]{3,1,2,0:T(8,128)S(1)}, f32[3,40,4,144]{3,1,2,0:T(8,128)S(1)}, u32[]{:S(2)}, u32[]{:S(2)}) collective-permute-start(f32[3,40,4,144]{3,1,2,0:T(8,128)S(1)} %get-tuple-element.21), channel_id=1, source_target_pairs={{0,4},{1,5},{2,6},{3,7},{8,12},{9,13},{10,14},{11,15},{16,20},{17,... | collective-permute-start | bytes 829448 | tf_op jit(solution)/shard_map/ppermute | solution.py:26
  322.7 12.6 %collective-permute-start.33 = (f32[3,40,4,144]{3,1,2,0:T(8,128)S(1)}, f32[3,40,4,144]{3,1,2,0:T(8,128)S(1)}, u32[]{:S(2)}, u32[]{:S(2)}) collective-permute-start(f32[3,40,4,144]{3,1,2,0:T(8,128)S(1)} %get-tuple-element.22), channel_id=1, source_target_pairs={{4,0},{5,1},{6,2},{7,3},{12,8},{13,9},{14,10},{15,11},{20,16},{21,... | collective-permute-start | bytes 829448 | tf_op jit(solution)/shard_map/ppermute | solution.py:28
  336.2 13.6 %collective-permute-start.34 = (f32[3,4,48,144]{3,1,2,0:T(4,128)S(1)}, f32[3,4,48,144]{3,1,2,0:T(4,128)S(1)}, u32[]{:S(2)}, u32[]{:S(2)}) collective-permute-start(f32[3,4,48,144]{3,1,2,0:T(4,128)S(1)} %get-tuple-element.17), channel_id=1, source_target_pairs={{0,1},{1,2},{2,3},{4,5},{5,6},{6,7},{8,9},{9,10},{10,11},{12,13},{... | collective-permute-start | bytes 995336 | tf_op jit(solution)/shard_map/ppermute | solution.py:26
  338.4 16.1 %collective-permute-start.35 = (f32[3,4,48,144]{3,1,2,0:T(4,128)S(1)}, f32[3,4,48,144]{3,1,2,0:T(4,128)S(1)}, u32[]{:S(2)}, u32[]{:S(2)}) collective-permute-start(f32[3,4,48,144]{3,1,2,0:T(4,128)S(1)} %get-tuple-element.18), channel_id=1, source_target_pairs={{1,0},{2,1},{3,2},{5,4},{6,5},{7,6},{9,8},{10,9},{11,10},{13,12},{... | collective-permute-start | bytes 995336 | tf_op jit(solution)/shard_map/ppermute | solution.py:28
  363.3 7.2 %collective-permute-start.36 = (f32[3,32,32,1]{2,1,3,0:T(8,128)S(1)}, f32[3,32,32,1]{2,1,3,0:T(8,128)S(1)}, u32[]{:S(2)}, u32[]{:S(2)}) collective-permute-start(f32[3,32,32,1]{2,1,3,0:T(8,128)S(1)} %copy.124), channel_id=1, source_target_pairs={{0,8},{8,16},{16,24},{1,9},{9,17},{17,25},{2,10},{10,18},{18,26},{... | collective-permute-start | bytes 36872 | tf_op jit(solution)/shard_map/ppermute | solution.py:26
  378.1 7.0 %collective-permute-start.39 = (f32[3,32,1,130]{3,1,2,0:T(8,128)S(1)}, f32[3,32,1,130]{3,1,2,0:T(8,128)S(1)}, u32[]{:S(2)}, u32[]{:S(2)}) collective-permute-start(f32[3,32,1,130]{3,1,2,0:T(8,128)S(1)} %get-tuple-element.38), channel_id=1, source_target_pairs={{4,0},{5,1},{6,2},{7,3},{12,8},{13,9},{14,10},{15,11},{20,16},{21,... | collective-permute-start | bytes 149768 | tf_op jit(solution)/shard_map/ppermute | solution.py:28
  387.5 7.0 %collective-permute-start.41 = (f32[3,1,34,130]{3,1,2,0:T(1,128)S(1)}, f32[3,1,34,130]{3,1,2,0:T(1,128)S(1)}, u32[]{:S(2)}, u32[]{:S(2)}) collective-permute-start(f32[3,1,34,130]{3,1,2,0:T(1,128)S(1)} %get-tuple-element.30), channel_id=1, source_target_pairs={{1,0},{2,1},{3,2},{5,4},{6,5},{7,6},{9,8},{10,9},{11,10},{13,12},{... | collective-permute-start | bytes 159128 | tf_op jit(solution)/shard_map/ppermute | solution.py:28
  (64 other events, 564.1 us)
where the time goes:
time: 413 us; the launch traced here: 407 us
  waiting for transfers between devices  107 us (26%)
  starting transfers between devices  90.9 us (22%)
  local copies, waits for them, and re-layouts  83.9 us (20%)
  matrix products  68.4 us (17%)
  other arithmetic  54.5 us (13%)
    ppermute x21, starting transfers between devices, with_halo(): lax.ppermute(tail, axis, [(i, (i + 1) % count) for i in range(ends)])  62 us
    ppermute x21, waiting for transfers between devices, with_halo(): lax.ppermute(tail, axis, [(i, (i + 1) % count) for i in range(ends)])  56.4 us
    ppermute x21, waiting for transfers between devices, with_halo(): lax.ppermute(head, axis, [((i + 1) % count, i) for i in range(ends)])  50.7 us
    ppermute x21, starting transfers between devices, with_halo(): lax.ppermute(head, axis, [((i + 1) % count, i) for i in range(ends)])  28.9 us
    slice x12, local copies, waits for them, and re-layouts, with_halo(): lax.slice_in_dim(cells, cells.shape[dim] - width, cells.shape[dim], axis=...  27.3 us
    dot_general x4, matrix products, transform_all(): return jnp.einsum('czyx,zk->ckyx', values, along_z, precision=HIGHEST)  26.9 us
    dot_general x4, matrix products, transform_all(): values = jnp.einsum('czyx,xk->czyk', values, along_x, precision=HIGHEST)  20.8 us
    dot_general x4, matrix products, transform_all(): values = jnp.einsum('czyx,yk->czkx', values, along_y, precision=HIGHEST)  19.8 us
  transfers between devices with their start and end apart: 42, of which 24 were waited for; matrix products, arithmetic and copies ran while one was open for 12% of the time, Pallas kernels for 0%

commit v1 on v0

v1 whole, which is shorter than its diff:
```python
import functools

import jax
import jax.numpy as jnp
import ml_dtypes
import numpy as np
from jax import lax
from jax.experimental import pallas as pl
from jax.experimental.pallas import tpu as pltpu
from jax.sharding import PartitionSpec as P

BRICK = 32
INTERSECTION = 4
LENGTH = BRICK + 2 * INTERSECTION
REACH = INTERSECTION + 1
WIDE = BRICK + 2 * REACH
LANES = 128
PAD = 8
FOLD = 2 * INTERSECTION + 1

LAMBDA_RATIO = 2.0
SIGMA_SHIFT = 0.1
REF_MODULUS = 1.5
VOID_MODULUS = 0.1

F32 = jnp.float32
BF16 = jnp.bfloat16
VMEM = pl.BlockSpec(memory_space=pltpu.VMEM)
SMEM = pl.BlockSpec(memory_space=pltpu.SMEM)


def halves(values):
    values = np.asarray(values, np.float32)
    high = values.astype(ml_dtypes.bfloat16)
    low = (values - high.astype(np.float32)).astype(ml_dtypes.bfloat16)
    return high, low


def right_table(values):
    high, low = halves(values)
    return np.block([[high, low], [high, np.zeros_like(low)]]).astype(ml_dtypes.bfloat16)


def left_table(values):
    high, low = halves(values)
    return np.concatenate([high, high, low], axis=1)


def tables(count_x):
    grid = np.arange(1, LENGTH + 1, dtype=np.float64)
    sine = np.sqrt(2.0 / (LENGTH + 1)) * np.sin(np.pi * np.outer(grid, grid) / (LENGTH + 1))
    eigen = 2.0 - 2.0 * np.cos(np.pi * grid / (LENGTH + 1))
    position = np.arange(LENGTH, dtype=np.float64)
    margin = 2 * INTERSECTION
    ramp = np.minimum(
        np.minimum((position + 0.5) / margin, (LENGTH - 0.5 - position) / margin), 1.0
    )
    rows = count_x * BRICK + 2 * PAD
    ramped = ramp[:, None] * sine
    along_y = np.zeros((LANES, LANES))
    back_y = np.zeros((LANES, LANES))
    for c in range(3):
        lane = c * WIDE + 1
        along_y[lane : lane + LENGTH, c * LENGTH : (c + 1) * LENGTH] = ramped
        back_y[c * LENGTH : (c + 1) * LENGTH, lane : lane + LENGTH] = sine
    along_x = np.zeros((count_x * LENGTH, rows))
    back_x = np.zeros((rows, count_x * LENGTH))
    for b in range(count_x):
        row = b * BRICK + PAD - INTERSECTION
        along_x[b * LENGTH : (b + 1) * LENGTH, row : row + LENGTH] = ramped.T
        back_x[row : row + LENGTH, b * LENGTH : (b + 1) * LENGTH] = sine
    half = LENGTH // 2
    eye = np.eye(8)
    even = left_table(np.kron(ramped[:half, 0::2].T, eye))
    odd = left_table(np.kron(ramped[:half, 1::2].T, eye))
    back_even = left_table(np.kron(sine[0::2, :half].T, eye))
    back_odd = left_table(np.kron(sine[1::2, :half].T, eye))
    ratio = lambda c, d: LAMBDA_RATIO if c == d else 1.0
    base = np.ones((count_x * LENGTH, LANES))
    steps = np.zeros((LENGTH, 8, LANES))
    order = np.concatenate([np.arange(0, LENGTH, 2), np.arange(1, LENGTH, 2)])
    for c in range(3):
        part = slice(c * LENGTH, (c + 1) * LENGTH)
        base[:, part] = REF_MODULUS * (
            ratio(c, 1) * eigen[None, :]
            + ratio(c, 2) * np.tile(eigen, count_x)[:, None]
            + SIGMA_SHIFT
        )
        steps[:, :, part] = REF_MODULUS * ratio(c, 0) * eigen[order][:, None, None]
    return [
        right_table(along_y),
        left_table(along_x),
        even,
        odd,
        back_even,
        back_odd,
        left_table(back_x),
        right_table(back_y),
        base.astype(np.float32),
        steps.astype(np.float32),
    ]


def phases(count):
    return 1 if count <= 2 else 2


def partners(count, phase):
    found = [i + 1 if (i + phase) % 2 == 0 else i - 1 for i in range(count)]
    return [j if 0 <= j < count else i for i, j in enumerate(found)]


def swap(value, axis, phase):
    target = partners(lax.axis_size(axis), phase)
    return lax.ppermute(value, axis, list(enumerate(target)))


def swap_both(value, first, phase_first, second, phase_second):
    rows = lax.axis_size(first)
    columns = lax.axis_size(second)
    one = partners(rows, phase_first)
    two = partners(columns, phase_second)
    pairs = []
    for i in range(rows):
        for j in range(columns):
            moved = one[i] != i and two[j] != j
            to = one[i] * columns + two[j] if moved else i * columns + j
            pairs.append((i * columns + j, to))
    return lax.ppermute(value, (first, second), pairs)


def spots(shape):
    lane = lax.broadcasted_iota(jnp.int32, shape, len(shape) - 1)
    region = jnp.where(lane >= 3 * WIDE, 3, jnp.where(lane >= 2 * WIDE, 2, jnp.where(lane >= WIDE, 1, 0)))
    spot = jnp.where(region == 3, 4 * LANES, lane - region * WIDE)
    return spot, region


def turn(values, shift):
    return pltpu.roll(values, lax.rem(shift + 2 * LANES, LANES), values.ndim - 1)


def pack(planes, width, start, spot, groups):
    total = jnp.zeros(spot.shape, F32)
    for g, plane in enumerate(planes):
        inside = (spot >= g * width) & (spot < (g + 1) * width)
        total = jnp.where(inside, turn(plane, g * width - start), total)
    return total


def unpack(packed, g, width, start, spot, use):
    inside = (spot >= start) & (spot < start + width) & use
    return jnp.where(inside, turn(packed, start - g * width), 0.0)


def side(pos_ref, dim, phase, count):
    place = pos_ref[dim]
    up = lax.rem(place + phase, 2) == 0
    use = jnp.where(up, place < count - 1, place > 0)
    return up, use


def pick(up, high, low):
    return jnp.where(up, high, low)


def two_terms(values):
    high = values.astype(BF16)
    low = (values - high.astype(F32)).astype(BF16)
    return high, low


def right_product(values, table):
    high, low = two_terms(values)
    product = jnp.dot(jnp.concatenate([high, low], axis=1), table, preferred_element_type=F32)
    return product[:, :LANES] + product[:, LANES:]


def left_product(table, values):
    high, low = two_terms(values)
    return jnp.dot(
        table, jnp.concatenate([high, low, high], axis=0), preferred_element_type=F32
    )


def solve(source, mid, target, consts):
    along_y, along_x, even, odd, back_even, back_odd, back_x, back_y, base, steps = consts
    rows = source.shape[1]
    half = LENGTH // 2

    def forward(t, _):
        both = jnp.concatenate([source[2 * t], source[2 * t + 1]], axis=0)
        turned = right_product(both, along_y[...])
        pair = jnp.concatenate([turned[:rows], turned[rows:]], axis=1)
        done = left_product(along_x[...], pair)
        mid[2 * t] = done[:, :LANES]
        mid[2 * t + 1] = done[:, LANES:]
        return 0

    lax.fori_loop(0, half, forward, 0)

    def across(g, _):
        start = pl.multiple_of(g * 16, 16)

        def plane(z):
            return jnp.concatenate(
                [mid[z, pl.ds(start, 8), :], mid[z, pl.ds(start + 8, 8), :]], axis=1
            )

        planes = [plane(z) for z in range(LENGTH)]
        sums = jnp.concatenate([planes[z] + planes[LENGTH - 1 - z] for z in range(half)], axis=0)
        gaps = jnp.concatenate([planes[z] - planes[LENGTH - 1 - z] for z in range(half)], axis=0)
        ground = jnp.concatenate(
            [base[pl.ds(start, 8), :], base[pl.ds(start + 8, 8), :]], axis=1
        )

        def divisors(first):
            return jnp.concatenate(
                [
                    ground + jnp.concatenate([steps[first + k], steps[first + k]], axis=1)
                    for k in range(half)
                ],
                axis=0,
            )

        near = left_product(back_even[...], left_product(even[...], sums) / divisors(0))
        far = left_product(back_odd[...], left_product(odd[...], gaps) / divisors(half))
        lower = near + far
        upper = near - far
        for z in range(half):
            for h in range(2):
                lanes = slice(h * LANES, (h + 1) * LANES)
                mid[z, pl.ds(start + 8 * h, 8), :] = lower[8 * z : 8 * z + 8, lanes]
                mid[LENGTH - 1 - z, pl.ds(start + 8 * h, 8), :] = upper[8 * z : 8 * z + 8, lanes]
        return 0

    lax.fori_loop(0, mid.shape[1] // 16, across, 0)

    def backward(t, _):
        pair = jnp.concatenate([mid[2 * t], mid[2 * t + 1]], axis=1)
        done = left_product(back_x[...], pair)
        both = jnp.concatenate([done[:, :LANES], done[:, LANES:]], axis=0)
        turned = right_product(both, back_y[...])
        target[2 * t] = turned[:rows]
        target[2 * t + 1] = turned[rows:]
        return 0

    lax.fori_loop(0, half, backward, 0)


def write_messages(pos_ref, solved, width, counts, outs_y, outs_z, outs_yz):
    rows = solved.shape[1]
    spot, _ = spots((rows, LANES))
    groups = WIDE // width
    _, count_y, count_z = counts
    for phase, out in enumerate(outs_z):
        up, _ = side(pos_ref, 0, phase, count_z)
        first = pick(up, LENGTH - width, 0)
        for i in range(width):
            out[i] = solved[first + i]
    for phase, out in enumerate(outs_y):
        up, _ = side(pos_ref, 1, phase, count_y)
        start = pick(up, WIDE - 1 - width, 1)
        many = LENGTH // groups

        def one(k, _, out=out, start=start, many=many):
            out[k] = pack(
                [solved[g * many + k] for g in range(groups)], width, start, spot, groups
            )
            return 0

        lax.fori_loop(0, many, one, 0)
    for number, out in enumerate(outs_yz):
        phase_y, phase_z = divmod(number, len(outs_z))
        up_y, _ = side(pos_ref, 1, phase_y, count_y)
        up_z, _ = side(pos_ref, 0, phase_z, count_z)
        start = pick(up_y, WIDE - 1 - width, 1)
        first = pick(up_z, LENGTH - width, 0)
        many = out.shape[0]
        for k in range(many):
            planes = [
                solved[first + g * many + k] for g in range(groups) if g * many + k < width
            ]
            out[k] = pack(planes, width, start, spot, groups)


def add_messages(pos_ref, solved, width, counts, ins_y, ins_z, ins_yz, field):
    rows = solved.shape[1]
    spot, _ = spots((rows, LANES))
    groups = WIDE // width
    _, count_y, count_z = counts
    first_y = [side(pos_ref, 1, phase, count_y) for phase in range(len(ins_y))]
    first_z = [side(pos_ref, 0, phase, count_z) for phase in range(len(ins_z))]
    many = LENGTH // groups

    def one(k, _):
        for g in range(groups):
            total = solved[g * many + k]
            for (up, use), ref in zip(first_y, ins_y):
                start = pick(up, WIDE - FOLD, FOLD - width)
                total = total + unpack(ref[k], g, width, start, spot, use)
            field[g * many + k + 1] = total
        return 0

    lax.fori_loop(0, many, one, 0)
    field[0] = jnp.zeros((rows, LANES), F32)
    field[WIDE - 1] = jnp.zeros((rows, LANES), F32)
    for phase_z, ((up_z, use_z), ref_z) in enumerate(zip(first_z, ins_z)):
        first = pick(up_z, WIDE - FOLD, FOLD - width)
        for i in range(width):
            total = ref_z[i]
            for phase_y, (up_y, use_y) in enumerate(first_y):
                ref = ins_yz[phase_y * len(ins_z) + phase_z]
                g, k = divmod(i, ref.shape[0])
                start = pick(up_y, WIDE - FOLD, FOLD - width)
                total = total + unpack(ref[k], g, width, start, spot, use_y)
            field[first + i] = field[first + i] + jnp.where(use_z, total, 0.0)


def grid_masks(pos_ref, rows, counts):
    count_x, count_y, count_z = counts
    spot, _ = spots((rows, LANES))
    row = lax.broadcasted_iota(jnp.int32, (rows, LANES), 0)
    low_y = pick(pos_ref[1] > 0, 0, REACH)
    high_y = pick(pos_ref[1] < count_y - 1, WIDE, REACH + BRICK)
    low_x = pick(pos_ref[2] > 0, 0, PAD)
    high_x = pick(pos_ref[2] < count_x - 1, rows, rows - PAD)
    inside = (spot >= low_y) & (spot < high_y) & (row >= low_x) & (row < high_x)
    low_z = pick(pos_ref[0] > 0, 0, REACH)
    high_z = pick(pos_ref[0] < count_z - 1, WIDE, REACH + BRICK)
    return inside, low_z, high_z


def complete(pos_ref, counts, partial, ins_x, field, first, last):
    rows = field.shape[1]
    inside, low_z, high_z = grid_masks(pos_ref, rows, counts)
    sides = [side(pos_ref, 2, phase, counts[0]) for phase in range(len(ins_x))]

    def one(z, _):
        on = inside & (z >= low_z) & (z < high_z)
        field[z] = partial[z]
        for (up, use), ref in zip(sides, ins_x):
            start = pl.multiple_of(pick(up, rows - 2 * PAD, 0), 2 * PAD)
            part = field[z, pl.ds(start, 2 * PAD), :]
            field[z, pl.ds(start, 2 * PAD), :] = part + jnp.where(use, ref[z], 0.0)
        field[z] = jnp.where(on, field[z], 0.0)
        return 0

    lax.fori_loop(first, last + 1, one, 0)


def stiffness(field, modulus, first, last, store):
    rows = field.shape[1]
    _, region = spots((rows, LANES))
    scale = [
        jnp.where(region == c, 0.5 * LAMBDA_RATIO, 0.5) for c in range(3)
    ]

    def rise(z):
        return (modulus[z] + modulus[z + 1]) * (field[z + 1] - field[z])

    def one(z, below):
        v = field[z]
        m = modulus[z]
        above = rise(z)
        gx = (m + pltpu.roll(m, rows - 1, 0)) * (pltpu.roll(v, rows - 1, 0) - v)
        gy = (m + pltpu.roll(m, LANES - 1, 1)) * (pltpu.roll(v, LANES - 1, 1) - v)
        total = SIGMA_SHIFT * m * v + scale[0] * (below - above)
        total = total + scale[1] * (pltpu.roll(gy, 1, 1) - gy)
        total = total + scale[2] * (pltpu.roll(gx, 1, 0) - gx)
        store(z, total)
        return above

    lax.fori_loop(first, last + 1, one, rise(first - 1))


def groups_of(refs, sizes):
    found = []
    at = 0
    for size in sizes:
        found.append(refs[at : at + size])
        at += size
    return found


def prepare_kernel(counts, sizes, pos_ref, table_ref, load, labels, mask, *refs):
    (load_out, modulus_out), outs_y, outs_z, outs_yz, (wide_load, wide_modulus) = groups_of(
        refs, (2,) + sizes[:3] + (2,)
    )
    columns = load.shape[3]
    wide_load[...] = jnp.zeros(wide_load.shape, F32)
    wide_modulus[...] = jnp.zeros(wide_modulus.shape, F32)

    def one(z, _):
        label = labels[z]
        looked = jnp.zeros(label.shape, F32)
        for k in range(table_ref.shape[0]):
            looked = jnp.where(label == k, table_ref[k], looked)
        value = jnp.where(mask[z] == 1, looked, VOID_MODULUS)
        for c in range(3):
            lane = c * WIDE + REACH
            wide_load[lane : lane + BRICK, :] = load[c, z]
            wide_modulus[lane : lane + BRICK, :] = value
        load_out[z] = wide_load[...].T
        modulus_out[z] = wide_modulus[...].T
        return 0

    lax.fori_loop(0, BRICK, one, 0)

    spot, region = spots((columns, LANES))
    _, count_y, count_z = counts
    groups = WIDE // REACH
    many = BRICK // groups
    for phase, out in enumerate(outs_z):
        up, _ = side(pos_ref, 0, phase, count_z)
        first = pick(up, BRICK - INTERSECTION, 0)
        for i in range(INTERSECTION):
            out[i] = load_out[first + i]
        first = pick(up, BRICK - REACH, 0)
        for k in range(2):
            total = modulus_out[first + k]
            for c in (1, 2):
                i = min(2 * c + k, REACH - 1)
                total = jnp.where(region == c, modulus_out[first + i], total)
            out[INTERSECTION + k] = total
    for phase, out in enumerate(outs_y):
        up, _ = side(pos_ref, 1, phase, count_y)
        start = pick(up, BRICK, REACH)
        for k in range(many):
            out[k] = pack(
                [load_out[g * many + k] for g in range(groups)], REACH, start, spot, groups
            )
        for k in range(2):
            total = jnp.zeros((columns, LANES), F32)
            for g in range(groups):
                turned = [
                    turn(modulus_out[(c * groups + g) * 2 + k], g * REACH - start)
                    for c in range(2)
                ]
                chosen = jnp.where(region == 0, turned[0], turned[1])
                inside = (spot >= g * REACH) & (spot < (g + 1) * REACH)
                total = jnp.where(inside, chosen, total)
            out[many + k] = total
    for number, out in enumerate(outs_yz):
        phase_y, phase_z = divmod(number, len(outs_z))
        up_y, _ = side(pos_ref, 1, phase_y, count_y)
        up_z, _ = side(pos_ref, 0, phase_z, count_z)
        start = pick(up_y, BRICK, REACH)
        first = pick(up_z, BRICK - INTERSECTION, 0)
        out[0] = pack(
            [load_out[first + i] for i in range(INTERSECTION)], REACH, start, spot, groups
        )
        first = pick(up_z, BRICK - REACH, 0)
        out[1] = pack([modulus_out[first + i] for i in range(REACH)], REACH, start, spot, groups)


def spread(values, region, source):
    total = jnp.zeros(values.shape, F32)
    for c in range(3):
        total = jnp.where(region == c, turn(values, (c - source) * WIDE), total)
    return total


def gather_kernel(counts, sizes, pos_ref, load, modulus, *refs):
    ins_y, ins_z, ins_yz, (load_out, modulus_out), outs_x = groups_of(
        refs, sizes[:3] + (2, sizes[3])
    )
    columns = load.shape[1]
    rows = columns + 2 * PAD
    core = slice(PAD, PAD + columns)
    spot, region = spots((columns, LANES))
    count_x, count_y, count_z = counts
    groups = WIDE // REACH
    many = BRICK // groups
    sides_y = [side(pos_ref, 1, phase, count_y) for phase in range(len(ins_y))]
    sides_z = [side(pos_ref, 0, phase, count_z) for phase in range(len(ins_z))]
    blank = jnp.zeros((PAD, LANES), F32)

    def store(out, z, value):
        out[z, :PAD, :] = blank
        out[z, core, :] = value
        out[z, rows - PAD :, :] = blank

    for z in range(BRICK):
        g, k = divmod(z, many)
        total = load[z]
        for (up, use), ref in zip(sides_y, ins_y):
            start = pick(up, REACH + BRICK, 0)
            total = total + unpack(ref[k], g, REACH, start, spot, use)
        store(load_out, z + INTERSECTION, total)
        c, rest = divmod(z, 2 * groups)
        g, k = divmod(rest, 2)
        total = modulus[z]
        for (up, use), ref in zip(sides_y, ins_y):
            start = pick(up, REACH + BRICK, 0)
            whole = spread(ref[many + k], region, c)
            total = total + unpack(whole, g, REACH, start, spot, use)
        store(modulus_out, z + REACH, total)
    zero = jnp.zeros((columns, LANES), F32)
    for i in range(INTERSECTION):
        store(load_out, i, zero)
        store(load_out, LENGTH - 1 - i, zero)
    for i in range(REACH):
        store(modulus_out, i, zero)
        store(modulus_out, WIDE - 1 - i, zero)
    for phase_z, ((up_z, use_z), ref_z) in enumerate(zip(sides_z, ins_z)):
        first = pick(up_z, INTERSECTION + BRICK, 0)
        for i in range(INTERSECTION):
            total = ref_z[i]
            for phase_y, (up_y, use_y) in enumerate(sides_y):
                ref = ins_yz[phase_y * len(ins_z) + phase_z]
                start = pick(up_y, REACH + BRICK, 0)
                total = total + unpack(ref[0], i, REACH, start, spot, use_y)
            load_out[first + i, core, :] = load_out[first + i, core, :] + jnp.where(
                use_z, total, 0.0
            )
        first = pick(up_z, REACH + BRICK, 0)
        for i in range(REACH):
            c, k = divmod(i, 2)
            total = spread(ref_z[INTERSECTION + k], region, c)
            for phase_y, (up_y, use_y) in enumerate(sides_y):
                ref = ins_yz[phase_y * len(ins_z) + phase_z]
                start = pick(up_y, REACH + BRICK, 0)
                total = total + unpack(ref[1], i, REACH, start, spot, use_y)
            modulus_out[first + i, core, :] = modulus_out[first + i, core, :] + jnp.where(
                use_z, total, 0.0
            )
    _, edge_region = spots((PAD, LANES))
    third = WIDE // 3
    for phase, out in enumerate(outs_x):
        up, _ = side(pos_ref, 2, phase, count_x)
        start = pl.multiple_of(pick(up, rows - 2 * PAD, PAD), PAD)
        for z in range(LENGTH):
            out[z] = load_out[z, pl.ds(start, PAD), :]
        for k in range(third):
            total = modulus_out[k, pl.ds(start, PAD), :]
            for c in (1, 2):
                part = modulus_out[k + c * third, pl.ds(start, PAD), :]
                total = jnp.where(edge_region == c, part, total)
            out[LENGTH + k] = total


def first_kernel(counts, sizes, pos_ref, load, modulus, *refs):
    ins_x, consts, (field_out, modulus_out, solved), outs_y, outs_z, outs_yz, (mid,) = groups_of(
        refs, (sizes[3], 10, 3) + sizes[:3] + (1,)
    )
    rows = load.shape[1]
    _, region = spots((PAD, LANES))
    sides = [side(pos_ref, 2, phase, counts[0]) for phase in range(len(ins_x))]
    third = WIDE // 3

    def copy(z, _):
        field_out[z] = load[z]
        modulus_out[z] = modulus[z]
        return 0

    lax.fori_loop(0, LENGTH, copy, 0)
    for z in range(LENGTH, WIDE):
        modulus_out[z] = modulus[z]
    for (up, use), ref in zip(sides, ins_x):
        start = pl.multiple_of(pick(up, rows - PAD, 0), PAD)
        for z in range(LENGTH):
            part = field_out[z, pl.ds(start, PAD), :]
            field_out[z, pl.ds(start, PAD), :] = part + jnp.where(use, ref[z], 0.0)
        for z in range(WIDE):
            c, k = divmod(z, third)
            part = modulus_out[z, pl.ds(start, PAD), :]
            modulus_out[z, pl.ds(start, PAD), :] = part + jnp.where(
                use, spread(ref[LENGTH + k], region, c), 0.0
            )
    solve(field_out, mid, solved, consts)
    write_messages(pos_ref, solved, FOLD, counts, outs_y, outs_z, outs_yz)


def fold_kernel(width, counts, sizes, pos_ref, solved, *refs):
    ins_y, ins_z, ins_yz, (field,), outs_x = groups_of(refs, sizes[:3] + (1, sizes[3]))
    rows = solved.shape[1]
    add_messages(pos_ref, solved, width, counts, ins_y, ins_z, ins_yz, field)
    for phase, out in enumerate(outs_x):
        up, _ = side(pos_ref, 2, phase, counts[0])
        start = pl.multiple_of(pick(up, rows - 2 * PAD, 0), 2 * PAD)
        for z in range(WIDE):
            out[z] = field[z, pl.ds(start, 2 * PAD), :]


def second_kernel(counts, sizes, pos_ref, partial, residual, modulus, *refs):
    (
        ins_x,
        consts,
        (solved, moved, left),
        outs_y,
        outs_z,
        outs_yz,
        (mid, field, renewed),
    ) = groups_of(refs, (sizes[3], 10, 3) + sizes[:3] + (3,))
    rows = partial.shape[1]
    complete(pos_ref, counts, partial, ins_x, field, 0, WIDE - 1)
    inside, low_z, high_z = grid_masks(pos_ref, rows, counts)

    def store(z, product):
        on = inside & (z >= low_z) & (z < high_z)
        renewed[z - 1] = jnp.where(on, residual[z - 1] - product, 0.0)

    stiffness(field, modulus, 1, WIDE - 2, store)

    def keep(z, _):
        moved[z] = field[z + REACH, PAD : rows - PAD, :]
        left[z] = renewed[z + INTERSECTION, PAD : rows - PAD, :]
        return 0

    lax.fori_loop(0, BRICK, keep, 0)
    solve(renewed, mid, solved, consts)
    write_messages(pos_ref, solved, REACH, counts, outs_y, outs_z, outs_yz)


def last_kernel(counts, sizes, pos_ref, partial, modulus, moved, left, *refs):
    ins_x, (displacement, residual), (field, turned_one, turned_two) = groups_of(
        refs, (sizes[3], 2, 3)
    )
    rows = partial.shape[1]
    complete(pos_ref, counts, partial, ins_x, field, INTERSECTION, REACH + BRICK)
    core = slice(PAD, rows - PAD)

    def store(z, product):
        at = z - REACH
        turned_one[...] = (moved[at] + field[z, core, :]).T
        turned_two[...] = (left[at] - product[core]).T
        for c in range(3):
            lane = c * WIDE + REACH
            displacement[c, at] = turned_one[lane : lane + BRICK, :]
            residual[c, at] = turned_two[lane : lane + BRICK, :]

    stiffness(field, modulus, REACH, REACH + BRICK - 1, store)


def call(kernel, inputs, outs, scratch=(), smem=1):
    return pl.pallas_call(
        kernel,
        out_shape=[jax.ShapeDtypeStruct(shape, F32) for shape in outs],
        in_specs=[SMEM] * smem + [VMEM] * (len(inputs) - smem),
        out_specs=[VMEM] * len(outs),
        scratch_shapes=[pltpu.VMEM(shape, F32) for shape in scratch],
        compiler_params=pltpu.CompilerParams(vmem_limit_bytes=48 * 1024 * 1024),
    )(*inputs)


def local(load, labels, mask, table):
    columns = load.shape[3]
    rows = columns + 2 * PAD
    counts = tuple(lax.axis_size(axis) for axis in ("gx", "gy", "gz"))
    ways = tuple(phases(count) for count in counts)
    sizes = (ways[1], ways[2], ways[1] * ways[2], ways[0])
    pos = jnp.stack([lax.axis_index(axis) for axis in ("gz", "gy", "gx")]).astype(jnp.int32)
    consts = [jnp.asarray(value) for value in tables(columns // BRICK)]
    spectral = (LENGTH, columns // BRICK * LENGTH, LANES)

    def exchange_yz(values):
        y, z, yz = groups_of(values, sizes[:3])
        z = [swap(value, "gz", phase) for phase, value in enumerate(z)]
        y = [swap(value, "gy", phase) for phase, value in enumerate(y)]
        yz = [
            swap_both(value, "gy", number // ways[2], "gz", number % ways[2])
            for number, value in enumerate(yz)
        ]
        return [*y, *z, *yz]

    def exchange_x(values):
        return [swap(value, "gx", phase) for phase, value in enumerate(values)]

    def message_shapes(width, height):
        groups = WIDE // width
        return (
            [(LENGTH // groups, height, LANES)] * sizes[0]
            + [(width, height, LANES)] * sizes[1]
            + [(-(-width // groups), height, LANES)] * sizes[2]
        )

    bind = lambda kernel, *first: functools.partial(kernel, *first, counts, sizes)
    core = (BRICK, columns, LANES)
    tall = (LENGTH, rows, LANES)
    wide = (WIDE, rows, LANES)
    many = BRICK // (WIDE // REACH)

    load_core, modulus_core, *out = call(
        bind(prepare_kernel),
        [pos, table, load, labels, mask],
        [core, core]
        + [(many + 2, columns, LANES)] * sizes[0]
        + [(INTERSECTION + 2, columns, LANES)] * sizes[1]
        + [(2, columns, LANES)] * sizes[2],
        [(LANES, columns)] * 2,
        smem=2,
    )
    residual, modulus, *out = call(
        bind(gather_kernel),
        [pos, load_core, modulus_core, *exchange_yz(out)],
        [tall, wide] + [(LENGTH + WIDE // 3, PAD, LANES)] * sizes[3],
    )
    residual, modulus, solved, *out = call(
        bind(first_kernel),
        [pos, residual, modulus, *exchange_x(out), *consts],
        [tall, wide, tall] + message_shapes(FOLD, rows),
        [spectral],
    )
    partial, *out = call(
        bind(fold_kernel, FOLD),
        [pos, solved, *exchange_yz(out)],
        [wide] + [(WIDE, 2 * PAD, LANES)] * sizes[3],
    )
    solved, moved, left, *out = call(
        bind(second_kernel),
        [pos, partial, residual, modulus, *exchange_x(out), *consts],
        [tall, core, core] + message_shapes(REACH, rows),
        [spectral, wide, tall],
    )
    partial, *out = call(
        bind(fold_kernel, REACH),
        [pos, solved, *exchange_yz(out)],
        [wide] + [(WIDE, 2 * PAD, LANES)] * sizes[3],
    )
    displacement, residual = call(
        bind(last_kernel),
        [pos, partial, modulus, moved, left, *exchange_x(out)],
        [load.shape, load.shape],
        [wide] + [(LANES, columns)] * 2,
    )
    return displacement, residual


def solution(mesh):
    placed = (P(None, "gz", "gy", "gx"), P("gz", "gy", "gx"), P("gz", "gy", "gx"), P())
    return jax.shard_map(
        local,
        mesh=mesh,
        in_specs=placed,
        out_specs=(P(None, "gz", "gy", "gx"), P(None, "gz", "gy", "gx")),
        check_vma=False,
    )
```

time: 413 us -> 195 us (0.47)
  the two profiles are of different devices: /device:TPU:0 before, /device:TPU:9 now
where the time goes in v1:
time: 195 us; the launch traced here: 194 us
  Pallas kernels  107 us (55%)
  waiting for transfers between devices  41.1 us (21%)
  starting transfers between devices  35.9 us (18%)
  local copies, waits for them, and re-layouts  9.45 us (5%)
    pallas_call x7, Pallas kernels, call(): pl.pallas_call(kernel, out_shape=[jax.ShapeDtypeStruct(shape, F32) for sh...  107 us
    ppermute x15, starting transfers between devices, swap(): return lax.ppermute(value, axis, list(enumerate(target)))  27.7 us
    ppermute x6, waiting for transfers between devices, swap_both(): return lax.ppermute(value, (first, second), pairs)  23.9 us
    ppermute x15, waiting for transfers between devices, swap(): return lax.ppermute(value, axis, list(enumerate(target)))  17.2 us
    unnamed x36, local copies, waits for them, and re-layouts  9.45 us
    ppermute x6, starting transfers between devices, swap_both(): return lax.ppermute(value, (first, second), pairs)  8.19 us
  transfers between devices with their start and end apart: 21, of which 10 were waited for; matrix products, arithmetic and copies ran while one was open for 0% of the time, Pallas kernels for 0%

profile of v1, /device:TPU:9, one launch (start us, length us, event | category | flops | bytes accessed | tf_op | source)
XLA Modules:
  0.0 194.1 jit_solution(11513382538116123953)
XLA Ops:
  0.7 1.4 copy-done.4
  4.9 7.5 %shard_map.149 = (f32[32,128,128]{2,1,0:T(8,128)S(1)}, f32[32,128,128]{2,1,0:T(8,128)}, f32[6,128,128]{2,1,0:T(8,128)S(1)}, f32[6,128,128]{2,1,0:T(8,128)S(1)}, ...) custom-call(s32[3]{0:T(128)S(1)} %pad_add_fusion.pos_ref, f32[16]{0:T(128)S(1)} %copy-done.17, ...), custom_call_target="tpu_custom_call" | custom-call | tf_op jit(solution)/shard_map/pallas_call | solution.py:637
  12.5 1.2 collective-permute-start
  13.9 4.3 %collective-permute-start.2 = (f32[6,128,128]{2,1,0:T(8,128)S(1)}, f32[6,128,128]{2,1,0:T(8,128)S(1)}, u32[]{:S(2)}, u32[]{:S(2)}) collective-permute-start(f32[6,128,128]{2,1,0:T(8,128)S(1)} %get-tuple-element.39), channel_id=1, source_target_pairs={{0,0},{1,2},{2,1},{3,3},{4,4},{5,6},{6,5},{7,7},{8,8},{9,10},{10,9... | collective-permute-start | bytes 1179656 | tf_op jit(solution)/shard_map/ppermute | solution.py:115
  18.3 1.9 collective-permute-start.4
  20.2 5.6 %collective-permute-done.3.refs_3_ = f32[2,128,128]{2,1,0:T(8,128)S(1)} collective-permute-done((f32[2,128,128]{2,1,0:T(8,128)S(1)}, f32[2,128,128]{2,1,0:T(8,128)S(1)}, u32[]{:S(2)}, u32[]{:S(2)}) %collective-permute-start.3) | collective-permute-done | bytes 131104 | tf_op jit(solution)/shard_map/ppermute | solution.py:129
  25.8 3.0 %collective-permute-done.4.refs_4_ = f32[2,128,128]{2,1,0:T(8,128)S(1)} collective-permute-done((f32[2,128,128]{2,1,0:T(8,128)S(1)}, f32[2,128,128]{2,1,0:T(8,128)S(1)}, u32[]{:S(2)}, u32[]{:S(2)}) %collective-permute-start.4) | collective-permute-done | bytes 131104 | tf_op jit(solution)/shard_map/ppermute | solution.py:129
  28.9 1.6 copy-done.2
  30.5 7.6 %shard_map.150 = (f32[40,144,128]{2,1,0:T(8,128)}, f32[42,144,128]{2,1,0:T(8,128)}, f32[54,8,128]{2,1,0:T(8,128)S(1)}, f32[54,8,128]{2,1,0:T(8,128)S(1)}) custom-call(s32[3]{0:T(128)S(1)} %pad_add_fusion.pos_ref, f32[32,128,128]{2,1,0:T(8,128)S(1)} %get-tuple-element.35.load, f32[32,128,128]{2,1,0:T(8,128)S(1)} %copy-done.2, ...), custom_call_target="tpu_custom_call" | custom-call | tf_op jit(solution)/shard_map/pallas_call | solution.py:637
  38.0 2.2 %collective-permute-start.5 = (f32[54,8,128]{2,1,0:T(8,128)S(1)}, f32[54,8,128]{2,1,0:T(8,128)S(1)}, u32[]{:S(2)}, u32[]{:S(2)}) collective-permute-start(f32[54,8,128]{2,1,0:T(8,128)S(1)} %get-tuple-element.44), channel_id=1, source_target_pairs={{0,8},{8,0},{16,24},{24,16},{1,9},{9,1},{17,25},{25,17},{2,10},{10... | collective-permute-start | bytes 663560 | tf_op jit(solution)/shard_map/ppermute | solution.py:115
  40.2 3.0 %collective-permute-start.6 = (f32[54,8,128]{2,1,0:T(8,128)S(1)}, f32[54,8,128]{2,1,0:T(8,128)S(1)}, u32[]{:S(2)}, u32[]{:S(2)}) collective-permute-start(f32[54,8,128]{2,1,0:T(8,128)S(1)} %get-tuple-element.45), channel_id=1, source_target_pairs={{0,0},{8,16},{16,8},{24,24},{1,1},{9,17},{17,9},{25,25},{2,2},{10,... | collective-permute-start | bytes 663560 | tf_op jit(solution)/shard_map/ppermute | solution.py:115
  43.2 4.2 %collective-permute-done.6.refs_1_ = f32[54,8,128]{2,1,0:T(8,128)S(1)} collective-permute-done((f32[54,8,128]{2,1,0:T(8,128)S(1)}, f32[54,8,128]{2,1,0:T(8,128)S(1)}, u32[]{:S(2)}, u32[]{:S(2)}) %collective-permute-start.6) | collective-permute-done | bytes 221216 | tf_op jit(solution)/shard_map/ppermute | solution.py:115
  47.5 30.7 %shard_map.151 = (f32[40,144,128]{2,1,0:T(8,128)}, f32[42,144,128]{2,1,0:T(8,128)}, f32[40,144,128]{2,1,0:T(8,128)}, f32[10,144,128]{2,1,0:T(8,128)S(1)}, f32[9,...) custom-call(s32[3]{0:T(128)S(1)} %pad_add_fusion.pos_ref, ...), custom_call_target="tpu_custom_call" | custom-call | tf_op jit(solution)/shard_map/pallas_call | solution.py:637
  79.5 3.4 %collective-permute-start.9 = (f32[9,144,128]{2,1,0:T(8,128)S(1)}, f32[9,144,128]{2,1,0:T(8,128)S(1)}, u32[]{:S(2)}, u32[]{:S(2)}) collective-permute-start(f32[9,144,128]{2,1,0:T(8,128)S(1)} %get-tuple-element.49), channel_id=1, source_target_pairs={{0,0},{1,2},{2,1},{3,3},{4,4},{5,6},{6,5},{7,7},{8,8},{9,10},{10,9... | collective-permute-start | bytes 1990664 | tf_op jit(solution)/shard_map/ppermute | solution.py:115
  83.0 3.0 %collective-permute-start.11 = (f32[3,144,128]{2,1,0:T(8,128)S(1)}, f32[3,144,128]{2,1,0:T(8,128)S(1)}, u32[]{:S(2)}, u32[]{:S(2)}) collective-permute-start(f32[3,144,128]{2,1,0:T(8,128)S(1)} %get-tuple-element.51), channel_id=1, source_target_pairs={{0,0},{1,6},{2,5},{3,3},{4,4},{5,2},{6,1},{7,7},{8,8},{9,14},{10,1... | collective-permute-start | bytes 663560 | tf_op jit(solution)/shard_map/ppermute | solution.py:129
  86.0 10.4 %collective-permute-done.10.refs_3_ = f32[3,144,128]{2,1,0:T(8,128)S(1)} collective-permute-done((f32[3,144,128]{2,1,0:T(8,128)S(1)}, f32[3,144,128]{2,1,0:T(8,128)S(1)}, u32[]{:S(2)}, u32[]{:S(2)}) %collective-permute-start.10) | collective-permute-done | bytes 221216 | tf_op jit(solution)/shard_map/ppermute | solution.py:129
  96.4 1.8 collective-permute-done.11.refs_4_
  98.3 2.4 %collective-permute-done.7.refs_0_ = f32[10,144,128]{2,1,0:T(8,128)S(1)} collective-permute-done((f32[10,144,128]{2,1,0:T(8,128)S(1)}, f32[10,144,128]{2,1,0:T(8,128)S(1)}, u32[]{:S(2)}, u32[]{:S(2)}) %collective-permute-start.7) | collective-permute-done | bytes 737312 | tf_op jit(solution)/shard_map/ppermute | solution.py:115
  100.7 1.8 copy-done.1
  102.5 4.2 %shard_map.152 = (f32[42,144,128]{2,1,0:T(8,128)}, f32[42,16,128]{2,1,0:T(8,128)S(1)}, f32[42,16,128]{2,1,0:T(8,128)S(1)}) custom-call(s32[3]{0:T(128)S(1)} %pad_add_fusion.pos_ref, f32[40,144,128]{2,1,0:T(8,128)S(1)} %copy-done.1, f32[10,144,128]{2,1,0:T(8,128)S(1)} %collective-permute-done.7.refs_0_, f32[9,144,128]{2,1,0:T(8,128)S(1)} %collective-permute-done.8.refs_1_, ...), custom_call_target="tpu_custom_call" | custom-call | tf_op jit(solution)/shard_map/pallas_call | solution.py:637
  106.7 2.9 %collective-permute-start.13 = (f32[42,16,128]{2,1,0:T(8,128)S(1)}, f32[42,16,128]{2,1,0:T(8,128)S(1)}, u32[]{:S(2)}, u32[]{:S(2)}) collective-permute-start(f32[42,16,128]{2,1,0:T(8,128)S(1)} %get-tuple-element.56), channel_id=1, source_target_pairs={{0,0},{8,16},{16,8},{24,24},{1,1},{9,17},{17,9},{25,25},{2,2},{10,... | collective-permute-start | bytes 1032200 | tf_op jit(solution)/shard_map/ppermute | solution.py:115
  109.6 5.7 %collective-permute-done.13.refs_1_ = f32[42,16,128]{2,1,0:T(8,128)S(1)} collective-permute-done((f32[42,16,128]{2,1,0:T(8,128)S(1)}, f32[42,16,128]{2,1,0:T(8,128)S(1)}, u32[]{:S(2)}, u32[]{:S(2)}) %collective-permute-start.13) | collective-permute-done | bytes 344096 | tf_op jit(solution)/shard_map/ppermute | solution.py:115
  115.2 38.7 %shard_map.153 = (f32[40,144,128]{2,1,0:T(8,128)}, f32[32,128,128]{2,1,0:T(8,128)S(1)}, f32[32,128,128]{2,1,0:T(8,128)}, f32[5,144,128]{2,1,0:T(8,128)S(1)}, f32...) custom-call(s32[3]{0:T(128)S(1)} %pad_add_fusion.pos_ref, ...), custom_call_target="tpu_custom_call" | custom-call | tf_op jit(solution)/shard_map/pallas_call | solution.py:637
  154.0 1.2 collective-permute-start.14
  155.2 3.3 %collective-permute-start.16 = (f32[5,144,128]{2,1,0:T(8,128)S(1)}, f32[5,144,128]{2,1,0:T(8,128)S(1)}, u32[]{:S(2)}, u32[]{:S(2)}) collective-permute-start(f32[5,144,128]{2,1,0:T(8,128)S(1)} %get-tuple-element.60), channel_id=1, source_target_pairs={{0,0},{1,2},{2,1},{3,3},{4,4},{5,6},{6,5},{7,7},{8,8},{9,10},{10,9... | collective-permute-start | bytes 1105928 | tf_op jit(solution)/shard_map/ppermute | solution.py:115
  158.6 3.0 %collective-permute-start.18 = (f32[1,144,128]{2,1,0:T(8,128)S(1)}, f32[1,144,128]{2,1,0:T(8,128)S(1)}, u32[]{:S(2)}, u32[]{:S(2)}) collective-permute-start(f32[1,144,128]{2,1,0:T(8,128)S(1)} %get-tuple-element.62), channel_id=1, source_target_pairs={{0,0},{1,6},{2,5},{3,3},{4,4},{5,2},{6,1},{7,7},{8,8},{9,14},{10,1... | collective-permute-start | bytes 221192 | tf_op jit(solution)/shard_map/ppermute | solution.py:129
  162.7 1.9 collective-permute-done.18.refs_4_
  164.6 1.8 copy-done
  166.5 3.7 %shard_map.154 = (f32[42,144,128]{2,1,0:T(8,128)}, f32[42,16,128]{2,1,0:T(8,128)S(1)}, f32[42,16,128]{2,1,0:T(8,128)S(1)}) custom-call(s32[3]{0:T(128)S(1)} %pad_add_fusion.pos_ref, f32[40,144,128]{2,1,0:T(8,128)S(1)} %copy-done, f32[5,144,128]{2,1,0:T(8,128)S(1)} %collective-permute-done.14.refs_0_, f32[5,144,128]{2,1,0:T(8,128)S(1)} %collective-permute-done.15.refs_1_, ...), custom_call_target="tpu_custom_call" | custom-call | tf_op jit(solution)/shard_map/pallas_call | solution.py:637
  170.1 4.8 %collective-permute-start.20 = (f32[42,16,128]{2,1,0:T(8,128)S(1)}, f32[42,16,128]{2,1,0:T(8,128)S(1)}, u32[]{:S(2)}, u32[]{:S(2)}) collective-permute-start(f32[42,16,128]{2,1,0:T(8,128)S(1)} %get-tuple-element.67), channel_id=1, source_target_pairs={{0,0},{8,16},{16,8},{24,24},{1,1},{9,17},{17,9},{25,25},{2,2},{10,... | collective-permute-start | bytes 1032200 | tf_op jit(solution)/shard_map/ppermute | solution.py:115
  175.0 4.9 %collective-permute-done.20.refs_1_ = f32[42,16,128]{2,1,0:T(8,128)S(1)} collective-permute-done((f32[42,16,128]{2,1,0:T(8,128)S(1)}, f32[42,16,128]{2,1,0:T(8,128)S(1)}, u32[]{:S(2)}, u32[]{:S(2)}) %collective-permute-start.20) | collective-permute-done | bytes 344096 | tf_op jit(solution)/shard_map/ppermute | solution.py:115
  179.9 14.2 %shard_map.155 = (f32[3,32,32,128]{3,2,1,0:T(8,128)}, f32[3,32,32,128]{3,2,1,0:T(8,128)}) custom-call(s32[3]{0:T(128)S(1)} %pad_add_fusion.pos_ref, f32[42,144,128]{2,1,0:T(8,128)} %get-tuple-element.63.partial, f32[42,144,128]{2,1,0:T(8,128)} %get-tuple-element.54.modulus, f32[32,128,128]{2,1,0:T(8,128)S(1)} %get-tuple-element.64.moved, ...), custom_call_target="tpu_custom_call" | custom-call | tf_op jit(solution)/shard_map/pallas_call | solution.py:637
  (54 shorter events, 5.6 us)
Async XLA Ops:
  4.9 42.6 %copy-start.5 = (f32[40,8,128]{2,1,0:T(8,128)S(1)}, f32[40,8,128]{2,1,0:T(8,128)}, u32[]{:S(2)}) copy-start(f32[40,8,128]{2,1,0:T(8,128)} %constant.41.clone.refs_11_) | copy-start | bytes 491524
  4.9 42.6 %copy-start.6 = (bf16[160,480]{1,0:T(8,128)(2,1)S(1)}, bf16[160,480]{1,0:T(8,128)(2,1)}, u32[]{:S(2)}) copy-start(bf16[160,480]{1,0:T(8,128)(2,1)} %constant.37.clone.refs_7_) | copy-start | bytes 460804
  4.9 42.6 %copy-start.7 = (bf16[160,480]{1,0:T(8,128)(2,1)S(1)}, bf16[160,480]{1,0:T(8,128)(2,1)}, u32[]{:S(2)}) copy-start(bf16[160,480]{1,0:T(8,128)(2,1)} %constant.36.clone.refs_6_) | copy-start | bytes 460804
  4.9 42.6 %copy-start.8 = (bf16[160,480]{1,0:T(8,128)(2,1)S(1)}, bf16[160,480]{1,0:T(8,128)(2,1)}, u32[]{:S(2)}) copy-start(bf16[160,480]{1,0:T(8,128)(2,1)} %constant.35.clone.refs_5_) | copy-start | bytes 460804
  4.9 42.6 %copy-start.9 = (bf16[160,480]{1,0:T(8,128)(2,1)S(1)}, bf16[160,480]{1,0:T(8,128)(2,1)}, u32[]{:S(2)}) copy-start(bf16[160,480]{1,0:T(8,128)(2,1)} %constant.34.clone.refs_4_) | copy-start | bytes 460804
  4.9 42.6 %copy-start.10 = (bf16[160,432]{1,0:T(8,128)(2,1)S(1)}, bf16[160,432]{1,0:T(8,128)(2,1)}, u32[]{:S(2)}) copy-start(bf16[160,432]{1,0:T(8,128)(2,1)} %constant.33.clone.refs_3_) | copy-start | bytes 414724
  4.9 42.6 %copy-start.11 = (bf16[144,480]{1,0:T(8,128)(2,1)S(1)}, bf16[144,480]{1,0:T(8,128)(2,1)}, u32[]{:S(2)}) copy-start(bf16[144,480]{1,0:T(8,128)(2,1)} %constant.38.clone.refs_8_) | copy-start | bytes 414724
  4.9 42.6 %copy-start.12 = (bf16[256,256]{1,0:T(8,128)(2,1)S(1)}, bf16[256,256]{1,0:T(8,128)(2,1)}, u32[]{:S(2)}) copy-start(bf16[256,256]{1,0:T(8,128)(2,1)} %constant.39.clone.refs_9_) | copy-start | bytes 393220
  4.9 42.6 %copy-start.13 = (bf16[256,256]{1,0:T(8,128)(2,1)S(1)}, bf16[256,256]{1,0:T(8,128)(2,1)}, u32[]{:S(2)}) copy-start(bf16[256,256]{1,0:T(8,128)(2,1)} %constant.32.clone.refs_2_) | copy-start | bytes 393220
  4.9 42.6 %copy-start.16 = (f32[160,128]{1,0:T(8,128)S(1)}, f32[160,128]{1,0:T(8,128)}, u32[]{:S(2)}) copy-start(f32[160,128]{1,0:T(8,128)} %constant.40.clone.refs_10_) | copy-start | bytes 245764
  12.5 16.4 %collective-permute-start = (f32[6,128,128]{2,1,0:T(8,128)S(1)}, f32[6,128,128]{2,1,0:T(8,128)S(1)}, u32[]{:S(2)}, u32[]{:S(2)}) collective-permute-start(f32[6,128,128]{2,1,0:T(8,128)S(1)} %get-tuple-element.37), channel_id=1, source_target_pairs={{0,4},{4,0},{1,5},{5,1},{2,6},{6,2},{3,7},{7,3},{8,12},{12,8},{9,1... | collective-permute-start | bytes 1179656 | tf_op jit(solution)/shard_map/ppermute | solution.py:115
  13.7 15.1 %collective-permute-start.1 = (f32[6,128,128]{2,1,0:T(8,128)S(1)}, f32[6,128,128]{2,1,0:T(8,128)S(1)}, u32[]{:S(2)}, u32[]{:S(2)}) collective-permute-start(f32[6,128,128]{2,1,0:T(8,128)S(1)} %get-tuple-element.38), channel_id=1, source_target_pairs={{0,1},{1,0},{2,3},{3,2},{4,5},{5,4},{6,7},{7,6},{8,9},{9,8},{10,11... | collective-permute-start | bytes 1179656 | tf_op jit(solution)/shard_map/ppermute | solution.py:115
  13.9 15.0 %collective-permute-start.2 = (f32[6,128,128]{2,1,0:T(8,128)S(1)}, f32[6,128,128]{2,1,0:T(8,128)S(1)}, u32[]{:S(2)}, u32[]{:S(2)}) collective-permute-start(f32[6,128,128]{2,1,0:T(8,128)S(1)} %get-tuple-element.39), channel_id=1, source_target_pairs={{0,0},{1,2},{2,1},{3,3},{4,4},{5,6},{6,5},{7,7},{8,8},{9,10},{10,9... | collective-permute-start | bytes 1179656 | tf_op jit(solution)/shard_map/ppermute | solution.py:115
  18.2 7.6 %collective-permute-start.3 = (f32[2,128,128]{2,1,0:T(8,128)S(1)}, f32[2,128,128]{2,1,0:T(8,128)S(1)}, u32[]{:S(2)}, u32[]{:S(2)}) collective-permute-start(f32[2,128,128]{2,1,0:T(8,128)S(1)} %get-tuple-element.40), channel_id=1, source_target_pairs={{0,5},{1,4},{2,7},{3,6},{4,1},{5,0},{6,3},{7,2},{8,13},{9,12},{10,... | collective-permute-start | bytes 393224 | tf_op jit(solution)/shard_map/ppermute | solution.py:129
  18.3 10.6 %collective-permute-start.4 = (f32[2,128,128]{2,1,0:T(8,128)S(1)}, f32[2,128,128]{2,1,0:T(8,128)S(1)}, u32[]{:S(2)}, u32[]{:S(2)}) collective-permute-start(f32[2,128,128]{2,1,0:T(8,128)S(1)} %get-tuple-element.41), channel_id=1, source_target_pairs={{0,0},{1,6},{2,5},{3,3},{4,4},{5,2},{6,1},{7,7},{8,8},{9,14},{10,1... | collective-permute-start | bytes 393224 | tf_op jit(solution)/shard_map/ppermute | solution.py:129
  38.0 5.2 %collective-permute-start.5 = (f32[54,8,128]{2,1,0:T(8,128)S(1)}, f32[54,8,128]{2,1,0:T(8,128)S(1)}, u32[]{:S(2)}, u32[]{:S(2)}) collective-permute-start(f32[54,8,128]{2,1,0:T(8,128)S(1)} %get-tuple-element.44), channel_id=1, source_target_pairs={{0,8},{8,0},{16,24},{24,16},{1,9},{9,1},{17,25},{25,17},{2,10},{10... | collective-permute-start | bytes 663560 | tf_op jit(solution)/shard_map/ppermute | solution.py:115
  40.2 7.2 %collective-permute-start.6 = (f32[54,8,128]{2,1,0:T(8,128)S(1)}, f32[54,8,128]{2,1,0:T(8,128)S(1)}, u32[]{:S(2)}, u32[]{:S(2)}) collective-permute-start(f32[54,8,128]{2,1,0:T(8,128)S(1)} %get-tuple-element.45), channel_id=1, source_target_pairs={{0,0},{8,16},{16,8},{24,24},{1,1},{9,17},{17,9},{25,25},{2,2},{10,... | collective-permute-start | bytes 663560 | tf_op jit(solution)/shard_map/ppermute | solution.py:115
  78.3 22.4 %collective-permute-start.7 = (f32[10,144,128]{2,1,0:T(8,128)S(1)}, f32[10,144,128]{2,1,0:T(8,128)S(1)}, u32[]{:S(2)}, u32[]{:S(2)}) collective-permute-start(f32[10,144,128]{2,1,0:T(8,128)S(1)} %get-tuple-element.47), channel_id=1, source_target_pairs={{0,4},{4,0},{1,5},{5,1},{2,6},{6,2},{3,7},{7,3},{8,12},{12,8},{9,1... | collective-permute-start | bytes 2211848 | tf_op jit(solution)/shard_map/ppermute | solution.py:115
  79.5 18.8 %collective-permute-start.8 = (f32[9,144,128]{2,1,0:T(8,128)S(1)}, f32[9,144,128]{2,1,0:T(8,128)S(1)}, u32[]{:S(2)}, u32[]{:S(2)}) collective-permute-start(f32[9,144,128]{2,1,0:T(8,128)S(1)} %get-tuple-element.48), channel_id=1, source_target_pairs={{0,1},{1,0},{2,3},{3,2},{4,5},{5,4},{6,7},{7,6},{8,9},{9,8},{10,11... | collective-permute-start | bytes 1990664 | tf_op jit(solution)/shard_map/ppermute | solution.py:115
  79.5 18.8 %collective-permute-start.9 = (f32[9,144,128]{2,1,0:T(8,128)S(1)}, f32[9,144,128]{2,1,0:T(8,128)S(1)}, u32[]{:S(2)}, u32[]{:S(2)}) collective-permute-start(f32[9,144,128]{2,1,0:T(8,128)S(1)} %get-tuple-element.49), channel_id=1, source_target_pairs={{0,0},{1,2},{2,1},{3,3},{4,4},{5,6},{6,5},{7,7},{8,8},{9,10},{10,9... | collective-permute-start | bytes 1990664 | tf_op jit(solution)/shard_map/ppermute | solution.py:115
  82.9 13.6 %collective-permute-start.10 = (f32[3,144,128]{2,1,0:T(8,128)S(1)}, f32[3,144,128]{2,1,0:T(8,128)S(1)}, u32[]{:S(2)}, u32[]{:S(2)}) collective-permute-start(f32[3,144,128]{2,1,0:T(8,128)S(1)} %get-tuple-element.50), channel_id=1, source_target_pairs={{0,5},{1,4},{2,7},{3,6},{4,1},{5,0},{6,3},{7,2},{8,13},{9,12},{10,... | collective-permute-start | bytes 663560 | tf_op jit(solution)/shard_map/ppermute | solution.py:129
  83.0 15.3 %collective-permute-start.11 = (f32[3,144,128]{2,1,0:T(8,128)S(1)}, f32[3,144,128]{2,1,0:T(8,128)S(1)}, u32[]{:S(2)}, u32[]{:S(2)}) collective-permute-start(f32[3,144,128]{2,1,0:T(8,128)S(1)} %get-tuple-element.51), channel_id=1, source_target_pairs={{0,0},{1,6},{2,5},{3,3},{4,4},{5,2},{6,1},{7,7},{8,8},{9,14},{10,1... | collective-permute-start | bytes 663560 | tf_op jit(solution)/shard_map/ppermute | solution.py:129
  106.7 2.9 %collective-permute-start.12 = (f32[42,16,128]{2,1,0:T(8,128)S(1)}, f32[42,16,128]{2,1,0:T(8,128)S(1)}, u32[]{:S(2)}, u32[]{:S(2)}) collective-permute-start(f32[42,16,128]{2,1,0:T(8,128)S(1)} %get-tuple-element.55), channel_id=1, source_target_pairs={{0,8},{8,0},{16,24},{24,16},{1,9},{9,1},{17,25},{25,17},{2,10},{10... | collective-permute-start | bytes 1032200 | tf_op jit(solution)/shard_map/ppermute | solution.py:115
  106.7 8.6 %collective-permute-start.13 = (f32[42,16,128]{2,1,0:T(8,128)S(1)}, f32[42,16,128]{2,1,0:T(8,128)S(1)}, u32[]{:S(2)}, u32[]{:S(2)}) collective-permute-start(f32[42,16,128]{2,1,0:T(8,128)S(1)} %get-tuple-element.56), channel_id=1, source_target_pairs={{0,0},{8,16},{16,8},{24,24},{1,1},{9,17},{17,9},{25,25},{2,2},{10,... | collective-permute-start | bytes 1032200 | tf_op jit(solution)/shard_map/ppermute | solution.py:115
  154.0 10.7 %collective-permute-start.14 = (f32[5,144,128]{2,1,0:T(8,128)S(1)}, f32[5,144,128]{2,1,0:T(8,128)S(1)}, u32[]{:S(2)}, u32[]{:S(2)}) collective-permute-start(f32[5,144,128]{2,1,0:T(8,128)S(1)} %get-tuple-element.58), channel_id=1, source_target_pairs={{0,4},{4,0},{1,5},{5,1},{2,6},{6,2},{3,7},{7,3},{8,12},{12,8},{9,1... | collective-permute-start | bytes 1105928 | tf_op jit(solution)/shard_map/ppermute | solution.py:115
  155.2 9.4 %collective-permute-start.15 = (f32[5,144,128]{2,1,0:T(8,128)S(1)}, f32[5,144,128]{2,1,0:T(8,128)S(1)}, u32[]{:S(2)}, u32[]{:S(2)}) collective-permute-start(f32[5,144,128]{2,1,0:T(8,128)S(1)} %get-tuple-element.59), channel_id=1, source_target_pairs={{0,1},{1,0},{2,3},{3,2},{4,5},{5,4},{6,7},{7,6},{8,9},{9,8},{10,11... | collective-permute-start | bytes 1105928 | tf_op jit(solution)/shard_map/ppermute | solution.py:115
  155.2 9.4 %collective-permute-start.16 = (f32[5,144,128]{2,1,0:T(8,128)S(1)}, f32[5,144,128]{2,1,0:T(8,128)S(1)}, u32[]{:S(2)}, u32[]{:S(2)}) collective-permute-start(f32[5,144,128]{2,1,0:T(8,128)S(1)} %get-tuple-element.60), channel_id=1, source_target_pairs={{0,0},{1,2},{2,1},{3,3},{4,4},{5,6},{6,5},{7,7},{8,8},{9,10},{10,9... | collective-permute-start | bytes 1105928 | tf_op jit(solution)/shard_map/ppermute | solution.py:115
  158.5 4.2 %collective-permute-start.17 = (f32[1,144,128]{2,1,0:T(8,128)S(1)}, f32[1,144,128]{2,1,0:T(8,128)S(1)}, u32[]{:S(2)}, u32[]{:S(2)}) collective-permute-start(f32[1,144,128]{2,1,0:T(8,128)S(1)} %get-tuple-element.61), channel_id=1, source_target_pairs={{0,5},{1,4},{2,7},{3,6},{4,1},{5,0},{6,3},{7,2},{8,13},{9,12},{10,... | collective-permute-start | bytes 221192 | tf_op jit(solution)/shard_map/ppermute | solution.py:129
  158.6 6.0 %collective-permute-start.18 = (f32[1,144,128]{2,1,0:T(8,128)S(1)}, f32[1,144,128]{2,1,0:T(8,128)S(1)}, u32[]{:S(2)}, u32[]{:S(2)}) collective-permute-start(f32[1,144,128]{2,1,0:T(8,128)S(1)} %get-tuple-element.62), channel_id=1, source_target_pairs={{0,0},{1,6},{2,5},{3,3},{4,4},{5,2},{6,1},{7,7},{8,8},{9,14},{10,1... | collective-permute-start | bytes 221192 | tf_op jit(solution)/shard_map/ppermute | solution.py:129
  166.5 13.4 %copy-start.3 = (f32[32,128,128]{2,1,0:T(8,128)S(1)}, f32[32,128,128]{2,1,0:T(8,128)}, u32[]{:S(2)}) copy-start(f32[32,128,128]{2,1,0:T(8,128)} %get-tuple-element.65.left) | copy-start | bytes 6291460
  170.1 4.8 %collective-permute-start.19 = (f32[42,16,128]{2,1,0:T(8,128)S(1)}, f32[42,16,128]{2,1,0:T(8,128)S(1)}, u32[]{:S(2)}, u32[]{:S(2)}) collective-permute-start(f32[42,16,128]{2,1,0:T(8,128)S(1)} %get-tuple-element.66), channel_id=1, source_target_pairs={{0,8},{8,0},{16,24},{24,16},{1,9},{9,1},{17,25},{25,17},{2,10},{10... | collective-permute-start | bytes 1032200 | tf_op jit(solution)/shard_map/ppermute | solution.py:115
  170.1 9.7 %collective-permute-start.20 = (f32[42,16,128]{2,1,0:T(8,128)S(1)}, f32[42,16,128]{2,1,0:T(8,128)S(1)}, u32[]{:S(2)}, u32[]{:S(2)}) collective-permute-start(f32[42,16,128]{2,1,0:T(8,128)S(1)} %get-tuple-element.67), channel_id=1, source_target_pairs={{0,0},{8,16},{16,8},{24,24},{1,1},{9,17},{17,9},{25,25},{2,2},{10,... | collective-permute-start | bytes 1032200 | tf_op jit(solution)/shard_map/ppermute | solution.py:115
  (7 other events, 9.4 us)

commit v2 on v1

--- a/solution.py
+++ b/solution.py
@@ -197,7 +197,7 @@
         mid[2 * t + 1] = done[:, LANES:]
         return 0
 
-    lax.fori_loop(0, half, forward, 0)
+    lax.fori_loop(0, half, forward, 0, unroll=10)
 
     def across(g, _):
         start = pl.multiple_of(g * 16, 16)
@@ -234,7 +234,7 @@
                 mid[LENGTH - 1 - z, pl.ds(start + 8 * h, 8), :] = upper[8 * z : 8 * z + 8, lanes]
         return 0
 
-    lax.fori_loop(0, mid.shape[1] // 16, across, 0)
+    lax.fori_loop(0, mid.shape[1] // 16, across, 0, unroll=5)
 
     def backward(t, _):
         pair = jnp.concatenate([mid[2 * t], mid[2 * t + 1]], axis=1)
@@ -245,7 +245,7 @@
         target[2 * t + 1] = turned[rows:]
         return 0
 
-    lax.fori_loop(0, half, backward, 0)
+    lax.fori_loop(0, half, backward, 0, unroll=10)
 
 
 def write_messages(pos_ref, solved, width, counts, outs_y, outs_z, outs_yz):
@@ -269,7 +269,7 @@
             )
             return 0
 
-        lax.fori_loop(0, many, one, 0)
+        lax.fori_loop(0, many, one, 0, unroll=5)
     for number, out in enumerate(outs_yz):
         phase_y, phase_z = divmod(number, len(outs_z))
         up_y, _ = side(pos_ref, 1, phase_y, count_y)
@@ -302,7 +302,7 @@
             field[g * many + k + 1] = total
         return 0
 
-    lax.fori_loop(0, many, one, 0)
+    lax.fori_loop(0, many, one, 0, unroll=5)
     field[0] = jnp.zeros((rows, LANES), F32)
     field[WIDE - 1] = jnp.zeros((rows, LANES), F32)
     for phase_z, ((up_z, use_z), ref_z) in enumerate(zip(first_z, ins_z)):
@@ -346,7 +346,7 @@
         field[z] = jnp.where(on, field[z], 0.0)
         return 0
 
-    lax.fori_loop(first, last + 1, one, 0)
+    lax.fori_loop(first, last + 1, one, 0, unroll=2)
 
 
 def stiffness(field, modulus, first, last, store):
@@ -371,7 +371,7 @@
         store(z, total)
         return above
 
-    lax.fori_loop(first, last + 1, one, rise(first - 1))
+    lax.fori_loop(first, last + 1, one, rise(first - 1), unroll=4)
 
 
 def groups_of(refs, sizes):
@@ -405,7 +405,7 @@
         modulus_out[z] = wide_modulus[...].T
         return 0
 
-    lax.fori_loop(0, BRICK, one, 0)
+    lax.fori_loop(0, BRICK, one, 0, unroll=4)
 
     spot, region = spots((columns, LANES))
     _, count_y, count_z = counts
@@ -554,7 +554,7 @@
         modulus_out[z] = modulus[z]
         return 0
 
-    lax.fori_loop(0, LENGTH, copy, 0)
+    lax.fori_loop(0, LENGTH, copy, 0, unroll=4)
     for z in range(LENGTH, WIDE):
         modulus_out[z] = modulus[z]
     for (up, use), ref in zip(sides, ins_x):
@@ -608,7 +608,7 @@
         left[z] = renewed[z + INTERSECTION, PAD : rows - PAD, :]
         return 0
 
-    lax.fori_loop(0, BRICK, keep, 0)
+    lax.fori_loop(0, BRICK, keep, 0, unroll=4)
     solve(renewed, mid, solved, consts)
     write_messages(pos_ref, solved, REACH, counts, outs_y, outs_z, outs_yz)
 

time: 195 us -> 154 us (0.79)
  Pallas kernels: 107 us -> 66 us
    pallas_call x7, Pallas kernels: 107 us -> 66 us  [call(): pl.pallas_call(kernel, out_shape=[jax.ShapeDtypeStruct(shape, F32) for sh...]
where the time goes in v2:
time: 154 us; the launch traced here: 153 us
  Pallas kernels  66 us (43%)
  waiting for transfers between devices  40.9 us (27%)
  starting transfers between devices  35.9 us (23%)
  local copies, waits for them, and re-layouts  9.45 us (6%)
    pallas_call x7, Pallas kernels, call(): pl.pallas_call(kernel, out_shape=[jax.ShapeDtypeStruct(shape, F32) for sh...  66 us
    ppermute x15, starting transfers between devices, swap(): return lax.ppermute(value, axis, list(enumerate(target)))  27.8 us
    ppermute x6, waiting for transfers between devices, swap_both(): return lax.ppermute(value, (first, second), pairs)  23.9 us
    ppermute x15, waiting for transfers between devices, swap(): return lax.ppermute(value, axis, list(enumerate(target)))  17 us
    unnamed x36, local copies, waits for them, and re-layouts  9.45 us
    ppermute x6, starting transfers between devices, swap_both(): return lax.ppermute(value, (first, second), pairs)  8.19 us
  transfers between devices with their start and end apart: 21, of which 10 were waited for; matrix products, arithmetic and copies ran while one was open for 0% of the time, Pallas kernels for 0%

profile of v2, /device:TPU:9, one launch (start us, length us, event | category | flops | bytes accessed | tf_op | source)
XLA Modules:
  0.0 153.3 jit_solution(7971751727925860740)
XLA Ops:
  0.7 1.4 copy-done.4
  4.9 5.3 %shard_map.149 = (f32[32,128,128]{2,1,0:T(8,128)S(1)}, f32[32,128,128]{2,1,0:T(8,128)}, f32[6,128,128]{2,1,0:T(8,128)S(1)}, f32[6,128,128]{2,1,0:T(8,128)S(1)}, ...) custom-call(s32[3]{0:T(128)S(1)} %pad_add_fusion.pos_ref, f32[16]{0:T(128)S(1)} %copy-done.17, ...), custom_call_target="tpu_custom_call" | custom-call | tf_op jit(solution)/shard_map/pallas_call | solution.py:637
  10.3 1.2 collective-permute-start
  11.7 4.3 %collective-permute-start.2 = (f32[6,128,128]{2,1,0:T(8,128)S(1)}, f32[6,128,128]{2,1,0:T(8,128)S(1)}, u32[]{:S(2)}, u32[]{:S(2)}) collective-permute-start(f32[6,128,128]{2,1,0:T(8,128)S(1)} %get-tuple-element.39), channel_id=1, source_target_pairs={{0,0},{1,2},{2,1},{3,3},{4,4},{5,6},{6,5},{7,7},{8,8},{9,10},{10,9... | collective-permute-start | bytes 1179656 | tf_op jit(solution)/shard_map/ppermute | solution.py:115
  16.1 1.9 %collective-permute-start.4 = (f32[2,128,128]{2,1,0:T(8,128)S(1)}, f32[2,128,128]{2,1,0:T(8,128)S(1)}, u32[]{:S(2)}, u32[]{:S(2)}) collective-permute-start(f32[2,128,128]{2,1,0:T(8,128)S(1)} %get-tuple-element.41), channel_id=1, source_target_pairs={{0,0},{1,6},{2,5},{3,3},{4,4},{5,2},{6,1},{7,7},{8,8},{9,14},{10,1... | collective-permute-start | bytes 393224 | tf_op jit(solution)/shard_map/ppermute | solution.py:129
  18.0 5.6 %collective-permute-done.3.refs_3_ = f32[2,128,128]{2,1,0:T(8,128)S(1)} collective-permute-done((f32[2,128,128]{2,1,0:T(8,128)S(1)}, f32[2,128,128]{2,1,0:T(8,128)S(1)}, u32[]{:S(2)}, u32[]{:S(2)}) %collective-permute-start.3) | collective-permute-done | bytes 131104 | tf_op jit(solution)/shard_map/ppermute | solution.py:129
  23.6 3.0 %collective-permute-done.4.refs_4_ = f32[2,128,128]{2,1,0:T(8,128)S(1)} collective-permute-done((f32[2,128,128]{2,1,0:T(8,128)S(1)}, f32[2,128,128]{2,1,0:T(8,128)S(1)}, u32[]{:S(2)}, u32[]{:S(2)}) %collective-permute-start.4) | collective-permute-done | bytes 131104 | tf_op jit(solution)/shard_map/ppermute | solution.py:129
  26.7 1.6 %copy-done.2 = f32[32,128,128]{2,1,0:T(8,128)S(1)} copy-done((f32[32,128,128]{2,1,0:T(8,128)S(1)}, f32[32,128,128]{2,1,0:T(8,128)}, u32[]{:S(2)}) %copy-start.2) | copy-done | bytes 2097176
  28.3 7.6 %shard_map.150 = (f32[40,144,128]{2,1,0:T(8,128)}, f32[42,144,128]{2,1,0:T(8,128)}, f32[54,8,128]{2,1,0:T(8,128)S(1)}, f32[54,8,128]{2,1,0:T(8,128)S(1)}) custom-call(s32[3]{0:T(128)S(1)} %pad_add_fusion.pos_ref, f32[32,128,128]{2,1,0:T(8,128)S(1)} %get-tuple-element.35.load, f32[32,128,128]{2,1,0:T(8,128)S(1)} %copy-done.2, ...), custom_call_target="tpu_custom_call" | custom-call | tf_op jit(solution)/shard_map/pallas_call | solution.py:637
  35.8 2.2 %collective-permute-start.5 = (f32[54,8,128]{2,1,0:T(8,128)S(1)}, f32[54,8,128]{2,1,0:T(8,128)S(1)}, u32[]{:S(2)}, u32[]{:S(2)}) collective-permute-start(f32[54,8,128]{2,1,0:T(8,128)S(1)} %get-tuple-element.44), channel_id=1, source_target_pairs={{0,8},{8,0},{16,24},{24,16},{1,9},{9,1},{17,25},{25,17},{2,10},{10... | collective-permute-start | bytes 663560 | tf_op jit(solution)/shard_map/ppermute | solution.py:115
  38.0 3.0 %collective-permute-start.6 = (f32[54,8,128]{2,1,0:T(8,128)S(1)}, f32[54,8,128]{2,1,0:T(8,128)S(1)}, u32[]{:S(2)}, u32[]{:S(2)}) collective-permute-start(f32[54,8,128]{2,1,0:T(8,128)S(1)} %get-tuple-element.45), channel_id=1, source_target_pairs={{0,0},{8,16},{16,8},{24,24},{1,1},{9,17},{17,9},{25,25},{2,2},{10,... | collective-permute-start | bytes 663560 | tf_op jit(solution)/shard_map/ppermute | solution.py:115
  41.0 4.2 %collective-permute-done.6.refs_1_ = f32[54,8,128]{2,1,0:T(8,128)S(1)} collective-permute-done((f32[54,8,128]{2,1,0:T(8,128)S(1)}, f32[54,8,128]{2,1,0:T(8,128)S(1)}, u32[]{:S(2)}, u32[]{:S(2)}) %collective-permute-start.6) | collective-permute-done | bytes 221216 | tf_op jit(solution)/shard_map/ppermute | solution.py:115
  45.3 15.0 %shard_map.151 = (f32[40,144,128]{2,1,0:T(8,128)}, f32[42,144,128]{2,1,0:T(8,128)}, f32[40,144,128]{2,1,0:T(8,128)}, f32[10,144,128]{2,1,0:T(8,128)S(1)}, f32[9,...) custom-call(s32[3]{0:T(128)S(1)} %pad_add_fusion.pos_ref, ...), custom_call_target="tpu_custom_call" | custom-call | tf_op jit(solution)/shard_map/pallas_call | solution.py:637
  61.6 3.4 %collective-permute-start.9 = (f32[9,144,128]{2,1,0:T(8,128)S(1)}, f32[9,144,128]{2,1,0:T(8,128)S(1)}, u32[]{:S(2)}, u32[]{:S(2)}) collective-permute-start(f32[9,144,128]{2,1,0:T(8,128)S(1)} %get-tuple-element.49), channel_id=1, source_target_pairs={{0,0},{1,2},{2,1},{3,3},{4,4},{5,6},{6,5},{7,7},{8,8},{9,10},{10,9... | collective-permute-start | bytes 1990664 | tf_op jit(solution)/shard_map/ppermute | solution.py:115
  65.0 3.0 %collective-permute-start.11 = (f32[3,144,128]{2,1,0:T(8,128)S(1)}, f32[3,144,128]{2,1,0:T(8,128)S(1)}, u32[]{:S(2)}, u32[]{:S(2)}) collective-permute-start(f32[3,144,128]{2,1,0:T(8,128)S(1)} %get-tuple-element.51), channel_id=1, source_target_pairs={{0,0},{1,6},{2,5},{3,3},{4,4},{5,2},{6,1},{7,7},{8,8},{9,14},{10,1... | collective-permute-start | bytes 663560 | tf_op jit(solution)/shard_map/ppermute | solution.py:129
  68.1 10.4 %collective-permute-done.10.refs_3_ = f32[3,144,128]{2,1,0:T(8,128)S(1)} collective-permute-done((f32[3,144,128]{2,1,0:T(8,128)S(1)}, f32[3,144,128]{2,1,0:T(8,128)S(1)}, u32[]{:S(2)}, u32[]{:S(2)}) %collective-permute-start.10) | collective-permute-done | bytes 221216 | tf_op jit(solution)/shard_map/ppermute | solution.py:129
  78.5 1.8 %collective-permute-done.11.refs_4_ = f32[3,144,128]{2,1,0:T(8,128)S(1)} collective-permute-done((f32[3,144,128]{2,1,0:T(8,128)S(1)}, f32[3,144,128]{2,1,0:T(8,128)S(1)}, u32[]{:S(2)}, u32[]{:S(2)}) %collective-permute-start.11) | collective-permute-done | bytes 221216 | tf_op jit(solution)/shard_map/ppermute | solution.py:129
  80.3 2.4 %collective-permute-done.7.refs_0_ = f32[10,144,128]{2,1,0:T(8,128)S(1)} collective-permute-done((f32[10,144,128]{2,1,0:T(8,128)S(1)}, f32[10,144,128]{2,1,0:T(8,128)S(1)}, u32[]{:S(2)}, u32[]{:S(2)}) %collective-permute-start.7) | collective-permute-done | bytes 737312 | tf_op jit(solution)/shard_map/ppermute | solution.py:115
  82.7 1.8 %copy-done.1 = f32[40,144,128]{2,1,0:T(8,128)S(1)} copy-done((f32[40,144,128]{2,1,0:T(8,128)S(1)}, f32[40,144,128]{2,1,0:T(8,128)}, u32[]{:S(2)}) %copy-start.1) | copy-done | bytes 2949144
  84.6 3.6 %shard_map.152 = (f32[42,144,128]{2,1,0:T(8,128)}, f32[42,16,128]{2,1,0:T(8,128)S(1)}, f32[42,16,128]{2,1,0:T(8,128)S(1)}) custom-call(s32[3]{0:T(128)S(1)} %pad_add_fusion.pos_ref, f32[40,144,128]{2,1,0:T(8,128)S(1)} %copy-done.1, f32[10,144,128]{2,1,0:T(8,128)S(1)} %collective-permute-done.7.refs_0_, f32[9,144,128]{2,1,0:T(8,128)S(1)} %collective-permute-done.8.refs_1_, ...), custom_call_target="tpu_custom_call" | custom-call | tf_op jit(solution)/shard_map/pallas_call | solution.py:637
  88.2 3.0 %collective-permute-start.13 = (f32[42,16,128]{2,1,0:T(8,128)S(1)}, f32[42,16,128]{2,1,0:T(8,128)S(1)}, u32[]{:S(2)}, u32[]{:S(2)}) collective-permute-start(f32[42,16,128]{2,1,0:T(8,128)S(1)} %get-tuple-element.56), channel_id=1, source_target_pairs={{0,0},{8,16},{16,8},{24,24},{1,1},{9,17},{17,9},{25,25},{2,2},{10,... | collective-permute-start | bytes 1032200 | tf_op jit(solution)/shard_map/ppermute | solution.py:115
  91.2 5.5 %collective-permute-done.13.refs_1_ = f32[42,16,128]{2,1,0:T(8,128)S(1)} collective-permute-done((f32[42,16,128]{2,1,0:T(8,128)S(1)}, f32[42,16,128]{2,1,0:T(8,128)S(1)}, u32[]{:S(2)}, u32[]{:S(2)}) %collective-permute-start.13) | collective-permute-done | bytes 344096 | tf_op jit(solution)/shard_map/ppermute | solution.py:115
  96.7 19.7 %shard_map.153 = (f32[40,144,128]{2,1,0:T(8,128)}, f32[32,128,128]{2,1,0:T(8,128)S(1)}, f32[32,128,128]{2,1,0:T(8,128)}, f32[5,144,128]{2,1,0:T(8,128)S(1)}, f32...) custom-call(s32[3]{0:T(128)S(1)} %pad_add_fusion.pos_ref, ...), custom_call_target="tpu_custom_call" | custom-call | tf_op jit(solution)/shard_map/pallas_call | solution.py:637
  116.5 1.2 collective-permute-start.14
  117.7 3.3 %collective-permute-start.16 = (f32[5,144,128]{2,1,0:T(8,128)S(1)}, f32[5,144,128]{2,1,0:T(8,128)S(1)}, u32[]{:S(2)}, u32[]{:S(2)}) collective-permute-start(f32[5,144,128]{2,1,0:T(8,128)S(1)} %get-tuple-element.60), channel_id=1, source_target_pairs={{0,0},{1,2},{2,1},{3,3},{4,4},{5,6},{6,5},{7,7},{8,8},{9,10},{10,9... | collective-permute-start | bytes 1105928 | tf_op jit(solution)/shard_map/ppermute | solution.py:115
  121.1 3.0 %collective-permute-start.18 = (f32[1,144,128]{2,1,0:T(8,128)S(1)}, f32[1,144,128]{2,1,0:T(8,128)S(1)}, u32[]{:S(2)}, u32[]{:S(2)}) collective-permute-start(f32[1,144,128]{2,1,0:T(8,128)S(1)} %get-tuple-element.62), channel_id=1, source_target_pairs={{0,0},{1,6},{2,5},{3,3},{4,4},{5,2},{6,1},{7,7},{8,8},{9,14},{10,1... | collective-permute-start | bytes 221192 | tf_op jit(solution)/shard_map/ppermute | solution.py:129
  125.2 1.9 %collective-permute-done.18.refs_4_ = f32[1,144,128]{2,1,0:T(8,128)S(1)} collective-permute-done((f32[1,144,128]{2,1,0:T(8,128)S(1)}, f32[1,144,128]{2,1,0:T(8,128)S(1)}, u32[]{:S(2)}, u32[]{:S(2)}) %collective-permute-start.18) | collective-permute-done | bytes 73760 | tf_op jit(solution)/shard_map/ppermute | solution.py:129
  127.1 1.8 %copy-done = f32[40,144,128]{2,1,0:T(8,128)S(1)} copy-done((f32[40,144,128]{2,1,0:T(8,128)S(1)}, f32[40,144,128]{2,1,0:T(8,128)}, u32[]{:S(2)}) %copy-start) | copy-done | bytes 2949144
  129.0 3.3 %shard_map.154 = (f32[42,144,128]{2,1,0:T(8,128)}, f32[42,16,128]{2,1,0:T(8,128)S(1)}, f32[42,16,128]{2,1,0:T(8,128)S(1)}) custom-call(s32[3]{0:T(128)S(1)} %pad_add_fusion.pos_ref, f32[40,144,128]{2,1,0:T(8,128)S(1)} %copy-done, f32[5,144,128]{2,1,0:T(8,128)S(1)} %collective-permute-done.14.refs_0_, f32[5,144,128]{2,1,0:T(8,128)S(1)} %collective-permute-done.15.refs_1_, ...), custom_call_target="tpu_custom_call" | custom-call | tf_op jit(solution)/shard_map/pallas_call | solution.py:637
  132.3 4.7 %collective-permute-start.20 = (f32[42,16,128]{2,1,0:T(8,128)S(1)}, f32[42,16,128]{2,1,0:T(8,128)S(1)}, u32[]{:S(2)}, u32[]{:S(2)}) collective-permute-start(f32[42,16,128]{2,1,0:T(8,128)S(1)} %get-tuple-element.67), channel_id=1, source_target_pairs={{0,0},{8,16},{16,8},{24,24},{1,1},{9,17},{17,9},{25,25},{2,2},{10,... | collective-permute-start | bytes 1032200 | tf_op jit(solution)/shard_map/ppermute | solution.py:115
  136.9 4.9 %collective-permute-done.20.refs_1_ = f32[42,16,128]{2,1,0:T(8,128)S(1)} collective-permute-done((f32[42,16,128]{2,1,0:T(8,128)S(1)}, f32[42,16,128]{2,1,0:T(8,128)S(1)}, u32[]{:S(2)}, u32[]{:S(2)}) %collective-permute-start.20) | collective-permute-done | bytes 344096 | tf_op jit(solution)/shard_map/ppermute | solution.py:115
  141.9 11.5 %shard_map.155 = (f32[3,32,32,128]{3,2,1,0:T(8,128)}, f32[3,32,32,128]{3,2,1,0:T(8,128)}) custom-call(s32[3]{0:T(128)S(1)} %pad_add_fusion.pos_ref, f32[42,144,128]{2,1,0:T(8,128)} %get-tuple-element.63.partial, f32[42,144,128]{2,1,0:T(8,128)} %get-tuple-element.54.modulus, f32[32,128,128]{2,1,0:T(8,128)S(1)} %get-tuple-element.64.moved, ...), custom_call_target="tpu_custom_call" | custom-call | tf_op jit(solution)/shard_map/pallas_call | solution.py:637
  (54 shorter events, 5.6 us)
Async XLA Ops:
  4.9 40.4 %copy-start.5 = (f32[40,8,128]{2,1,0:T(8,128)S(1)}, f32[40,8,128]{2,1,0:T(8,128)}, u32[]{:S(2)}) copy-start(f32[40,8,128]{2,1,0:T(8,128)} %constant.41.clone.refs_11_) | copy-start | bytes 491524
  4.9 40.4 %copy-start.6 = (bf16[160,480]{1,0:T(8,128)(2,1)S(1)}, bf16[160,480]{1,0:T(8,128)(2,1)}, u32[]{:S(2)}) copy-start(bf16[160,480]{1,0:T(8,128)(2,1)} %constant.37.clone.refs_7_) | copy-start | bytes 460804
  4.9 40.4 %copy-start.7 = (bf16[160,480]{1,0:T(8,128)(2,1)S(1)}, bf16[160,480]{1,0:T(8,128)(2,1)}, u32[]{:S(2)}) copy-start(bf16[160,480]{1,0:T(8,128)(2,1)} %constant.36.clone.refs_6_) | copy-start | bytes 460804
  4.9 40.4 %copy-start.8 = (bf16[160,480]{1,0:T(8,128)(2,1)S(1)}, bf16[160,480]{1,0:T(8,128)(2,1)}, u32[]{:S(2)}) copy-start(bf16[160,480]{1,0:T(8,128)(2,1)} %constant.35.clone.refs_5_) | copy-start | bytes 460804
  4.9 40.4 %copy-start.9 = (bf16[160,480]{1,0:T(8,128)(2,1)S(1)}, bf16[160,480]{1,0:T(8,128)(2,1)}, u32[]{:S(2)}) copy-start(bf16[160,480]{1,0:T(8,128)(2,1)} %constant.34.clone.refs_4_) | copy-start | bytes 460804
  4.9 40.4 %copy-start.10 = (bf16[160,432]{1,0:T(8,128)(2,1)S(1)}, bf16[160,432]{1,0:T(8,128)(2,1)}, u32[]{:S(2)}) copy-start(bf16[160,432]{1,0:T(8,128)(2,1)} %constant.33.clone.refs_3_) | copy-start | bytes 414724
  4.9 40.4 %copy-start.11 = (bf16[144,480]{1,0:T(8,128)(2,1)S(1)}, bf16[144,480]{1,0:T(8,128)(2,1)}, u32[]{:S(2)}) copy-start(bf16[144,480]{1,0:T(8,128)(2,1)} %constant.38.clone.refs_8_) | copy-start | bytes 414724
  4.9 40.4 %copy-start.12 = (bf16[256,256]{1,0:T(8,128)(2,1)S(1)}, bf16[256,256]{1,0:T(8,128)(2,1)}, u32[]{:S(2)}) copy-start(bf16[256,256]{1,0:T(8,128)(2,1)} %constant.39.clone.refs_9_) | copy-start | bytes 393220
  4.9 40.4 %copy-start.13 = (bf16[256,256]{1,0:T(8,128)(2,1)S(1)}, bf16[256,256]{1,0:T(8,128)(2,1)}, u32[]{:S(2)}) copy-start(bf16[256,256]{1,0:T(8,128)(2,1)} %constant.32.clone.refs_2_) | copy-start | bytes 393220
  4.9 40.4 %copy-start.16 = (f32[160,128]{1,0:T(8,128)S(1)}, f32[160,128]{1,0:T(8,128)}, u32[]{:S(2)}) copy-start(f32[160,128]{1,0:T(8,128)} %constant.40.clone.refs_10_) | copy-start | bytes 245764
  10.3 16.4 %collective-permute-start = (f32[6,128,128]{2,1,0:T(8,128)S(1)}, f32[6,128,128]{2,1,0:T(8,128)S(1)}, u32[]{:S(2)}, u32[]{:S(2)}) collective-permute-start(f32[6,128,128]{2,1,0:T(8,128)S(1)} %get-tuple-element.37), channel_id=1, source_target_pairs={{0,4},{4,0},{1,5},{5,1},{2,6},{6,2},{3,7},{7,3},{8,12},{12,8},{9,1... | collective-permute-start | bytes 1179656 | tf_op jit(solution)/shard_map/ppermute | solution.py:115
  11.5 15.1 %collective-permute-start.1 = (f32[6,128,128]{2,1,0:T(8,128)S(1)}, f32[6,128,128]{2,1,0:T(8,128)S(1)}, u32[]{:S(2)}, u32[]{:S(2)}) collective-permute-start(f32[6,128,128]{2,1,0:T(8,128)S(1)} %get-tuple-element.38), channel_id=1, source_target_pairs={{0,1},{1,0},{2,3},{3,2},{4,5},{5,4},{6,7},{7,6},{8,9},{9,8},{10,11... | collective-permute-start | bytes 1179656 | tf_op jit(solution)/shard_map/ppermute | solution.py:115
  11.7 15.0 %collective-permute-start.2 = (f32[6,128,128]{2,1,0:T(8,128)S(1)}, f32[6,128,128]{2,1,0:T(8,128)S(1)}, u32[]{:S(2)}, u32[]{:S(2)}) collective-permute-start(f32[6,128,128]{2,1,0:T(8,128)S(1)} %get-tuple-element.39), channel_id=1, source_target_pairs={{0,0},{1,2},{2,1},{3,3},{4,4},{5,6},{6,5},{7,7},{8,8},{9,10},{10,9... | collective-permute-start | bytes 1179656 | tf_op jit(solution)/shard_map/ppermute | solution.py:115
  16.0 7.6 %collective-permute-start.3 = (f32[2,128,128]{2,1,0:T(8,128)S(1)}, f32[2,128,128]{2,1,0:T(8,128)S(1)}, u32[]{:S(2)}, u32[]{:S(2)}) collective-permute-start(f32[2,128,128]{2,1,0:T(8,128)S(1)} %get-tuple-element.40), channel_id=1, source_target_pairs={{0,5},{1,4},{2,7},{3,6},{4,1},{5,0},{6,3},{7,2},{8,13},{9,12},{10,... | collective-permute-start | bytes 393224 | tf_op jit(solution)/shard_map/ppermute | solution.py:129
  16.1 10.6 %collective-permute-start.4 = (f32[2,128,128]{2,1,0:T(8,128)S(1)}, f32[2,128,128]{2,1,0:T(8,128)S(1)}, u32[]{:S(2)}, u32[]{:S(2)}) collective-permute-start(f32[2,128,128]{2,1,0:T(8,128)S(1)} %get-tuple-element.41), channel_id=1, source_target_pairs={{0,0},{1,6},{2,5},{3,3},{4,4},{5,2},{6,1},{7,7},{8,8},{9,14},{10,1... | collective-permute-start | bytes 393224 | tf_op jit(solution)/shard_map/ppermute | solution.py:129
  35.8 5.2 %collective-permute-start.5 = (f32[54,8,128]{2,1,0:T(8,128)S(1)}, f32[54,8,128]{2,1,0:T(8,128)S(1)}, u32[]{:S(2)}, u32[]{:S(2)}) collective-permute-start(f32[54,8,128]{2,1,0:T(8,128)S(1)} %get-tuple-element.44), channel_id=1, source_target_pairs={{0,8},{8,0},{16,24},{24,16},{1,9},{9,1},{17,25},{25,17},{2,10},{10... | collective-permute-start | bytes 663560 | tf_op jit(solution)/shard_map/ppermute | solution.py:115
  38.0 7.2 %collective-permute-start.6 = (f32[54,8,128]{2,1,0:T(8,128)S(1)}, f32[54,8,128]{2,1,0:T(8,128)S(1)}, u32[]{:S(2)}, u32[]{:S(2)}) collective-permute-start(f32[54,8,128]{2,1,0:T(8,128)S(1)} %get-tuple-element.45), channel_id=1, source_target_pairs={{0,0},{8,16},{16,8},{24,24},{1,1},{9,17},{17,9},{25,25},{2,2},{10,... | collective-permute-start | bytes 663560 | tf_op jit(solution)/shard_map/ppermute | solution.py:115
  60.3 22.4 %collective-permute-start.7 = (f32[10,144,128]{2,1,0:T(8,128)S(1)}, f32[10,144,128]{2,1,0:T(8,128)S(1)}, u32[]{:S(2)}, u32[]{:S(2)}) collective-permute-start(f32[10,144,128]{2,1,0:T(8,128)S(1)} %get-tuple-element.47), channel_id=1, source_target_pairs={{0,4},{4,0},{1,5},{5,1},{2,6},{6,2},{3,7},{7,3},{8,12},{12,8},{9,1... | collective-permute-start | bytes 2211848 | tf_op jit(solution)/shard_map/ppermute | solution.py:115
  61.6 18.8 %collective-permute-start.8 = (f32[9,144,128]{2,1,0:T(8,128)S(1)}, f32[9,144,128]{2,1,0:T(8,128)S(1)}, u32[]{:S(2)}, u32[]{:S(2)}) collective-permute-start(f32[9,144,128]{2,1,0:T(8,128)S(1)} %get-tuple-element.48), channel_id=1, source_target_pairs={{0,1},{1,0},{2,3},{3,2},{4,5},{5,4},{6,7},{7,6},{8,9},{9,8},{10,11... | collective-permute-start | bytes 1990664 | tf_op jit(solution)/shard_map/ppermute | solution.py:115
  61.6 18.8 %collective-permute-start.9 = (f32[9,144,128]{2,1,0:T(8,128)S(1)}, f32[9,144,128]{2,1,0:T(8,128)S(1)}, u32[]{:S(2)}, u32[]{:S(2)}) collective-permute-start(f32[9,144,128]{2,1,0:T(8,128)S(1)} %get-tuple-element.49), channel_id=1, source_target_pairs={{0,0},{1,2},{2,1},{3,3},{4,4},{5,6},{6,5},{7,7},{8,8},{9,10},{10,9... | collective-permute-start | bytes 1990664 | tf_op jit(solution)/shard_map/ppermute | solution.py:115
  64.9 13.6 %collective-permute-start.10 = (f32[3,144,128]{2,1,0:T(8,128)S(1)}, f32[3,144,128]{2,1,0:T(8,128)S(1)}, u32[]{:S(2)}, u32[]{:S(2)}) collective-permute-start(f32[3,144,128]{2,1,0:T(8,128)S(1)} %get-tuple-element.50), channel_id=1, source_target_pairs={{0,5},{1,4},{2,7},{3,6},{4,1},{5,0},{6,3},{7,2},{8,13},{9,12},{10,... | collective-permute-start | bytes 663560 | tf_op jit(solution)/shard_map/ppermute | solution.py:129
  65.0 15.3 %collective-permute-start.11 = (f32[3,144,128]{2,1,0:T(8,128)S(1)}, f32[3,144,128]{2,1,0:T(8,128)S(1)}, u32[]{:S(2)}, u32[]{:S(2)}) collective-permute-start(f32[3,144,128]{2,1,0:T(8,128)S(1)} %get-tuple-element.51), channel_id=1, source_target_pairs={{0,0},{1,6},{2,5},{3,3},{4,4},{5,2},{6,1},{7,7},{8,8},{9,14},{10,1... | collective-permute-start | bytes 663560 | tf_op jit(solution)/shard_map/ppermute | solution.py:129
  88.2 3.0 %collective-permute-start.12 = (f32[42,16,128]{2,1,0:T(8,128)S(1)}, f32[42,16,128]{2,1,0:T(8,128)S(1)}, u32[]{:S(2)}, u32[]{:S(2)}) collective-permute-start(f32[42,16,128]{2,1,0:T(8,128)S(1)} %get-tuple-element.55), channel_id=1, source_target_pairs={{0,8},{8,0},{16,24},{24,16},{1,9},{9,1},{17,25},{25,17},{2,10},{10... | collective-permute-start | bytes 1032200 | tf_op jit(solution)/shard_map/ppermute | solution.py:115
  88.2 8.6 %collective-permute-start.13 = (f32[42,16,128]{2,1,0:T(8,128)S(1)}, f32[42,16,128]{2,1,0:T(8,128)S(1)}, u32[]{:S(2)}, u32[]{:S(2)}) collective-permute-start(f32[42,16,128]{2,1,0:T(8,128)S(1)} %get-tuple-element.56), channel_id=1, source_target_pairs={{0,0},{8,16},{16,8},{24,24},{1,1},{9,17},{17,9},{25,25},{2,2},{10,... | collective-permute-start | bytes 1032200 | tf_op jit(solution)/shard_map/ppermute | solution.py:115
  116.5 10.6 %collective-permute-start.14 = (f32[5,144,128]{2,1,0:T(8,128)S(1)}, f32[5,144,128]{2,1,0:T(8,128)S(1)}, u32[]{:S(2)}, u32[]{:S(2)}) collective-permute-start(f32[5,144,128]{2,1,0:T(8,128)S(1)} %get-tuple-element.58), channel_id=1, source_target_pairs={{0,4},{4,0},{1,5},{5,1},{2,6},{6,2},{3,7},{7,3},{8,12},{12,8},{9,1... | collective-permute-start | bytes 1105928 | tf_op jit(solution)/shard_map/ppermute | solution.py:115
  117.7 9.4 %collective-permute-start.15 = (f32[5,144,128]{2,1,0:T(8,128)S(1)}, f32[5,144,128]{2,1,0:T(8,128)S(1)}, u32[]{:S(2)}, u32[]{:S(2)}) collective-permute-start(f32[5,144,128]{2,1,0:T(8,128)S(1)} %get-tuple-element.59), channel_id=1, source_target_pairs={{0,1},{1,0},{2,3},{3,2},{4,5},{5,4},{6,7},{7,6},{8,9},{9,8},{10,11... | collective-permute-start | bytes 1105928 | tf_op jit(solution)/shard_map/ppermute | solution.py:115
  117.7 9.4 %collective-permute-start.16 = (f32[5,144,128]{2,1,0:T(8,128)S(1)}, f32[5,144,128]{2,1,0:T(8,128)S(1)}, u32[]{:S(2)}, u32[]{:S(2)}) collective-permute-start(f32[5,144,128]{2,1,0:T(8,128)S(1)} %get-tuple-element.60), channel_id=1, source_target_pairs={{0,0},{1,2},{2,1},{3,3},{4,4},{5,6},{6,5},{7,7},{8,8},{9,10},{10,9... | collective-permute-start | bytes 1105928 | tf_op jit(solution)/shard_map/ppermute | solution.py:115
  121.0 4.2 %collective-permute-start.17 = (f32[1,144,128]{2,1,0:T(8,128)S(1)}, f32[1,144,128]{2,1,0:T(8,128)S(1)}, u32[]{:S(2)}, u32[]{:S(2)}) collective-permute-start(f32[1,144,128]{2,1,0:T(8,128)S(1)} %get-tuple-element.61), channel_id=1, source_target_pairs={{0,5},{1,4},{2,7},{3,6},{4,1},{5,0},{6,3},{7,2},{8,13},{9,12},{10,... | collective-permute-start | bytes 221192 | tf_op jit(solution)/shard_map/ppermute | solution.py:129
  121.1 6.0 %collective-permute-start.18 = (f32[1,144,128]{2,1,0:T(8,128)S(1)}, f32[1,144,128]{2,1,0:T(8,128)S(1)}, u32[]{:S(2)}, u32[]{:S(2)}) collective-permute-start(f32[1,144,128]{2,1,0:T(8,128)S(1)} %get-tuple-element.62), channel_id=1, source_target_pairs={{0,0},{1,6},{2,5},{3,3},{4,4},{5,2},{6,1},{7,7},{8,8},{9,14},{10,1... | collective-permute-start | bytes 221192 | tf_op jit(solution)/shard_map/ppermute | solution.py:129
  129.0 12.9 %copy-start.3 = (f32[32,128,128]{2,1,0:T(8,128)S(1)}, f32[32,128,128]{2,1,0:T(8,128)}, u32[]{:S(2)}) copy-start(f32[32,128,128]{2,1,0:T(8,128)} %get-tuple-element.65.left) | copy-start | bytes 6291460
  132.3 4.7 %collective-permute-start.19 = (f32[42,16,128]{2,1,0:T(8,128)S(1)}, f32[42,16,128]{2,1,0:T(8,128)S(1)}, u32[]{:S(2)}, u32[]{:S(2)}) collective-permute-start(f32[42,16,128]{2,1,0:T(8,128)S(1)} %get-tuple-element.66), channel_id=1, source_target_pairs={{0,8},{8,0},{16,24},{24,16},{1,9},{9,1},{17,25},{25,17},{2,10},{10... | collective-permute-start | bytes 1032200 | tf_op jit(solution)/shard_map/ppermute | solution.py:115
  132.3 9.6 %collective-permute-start.20 = (f32[42,16,128]{2,1,0:T(8,128)S(1)}, f32[42,16,128]{2,1,0:T(8,128)S(1)}, u32[]{:S(2)}, u32[]{:S(2)}) collective-permute-start(f32[42,16,128]{2,1,0:T(8,128)S(1)} %get-tuple-element.67), channel_id=1, source_target_pairs={{0,0},{8,16},{16,8},{24,24},{1,1},{9,17},{17,9},{25,25},{2,2},{10,... | collective-permute-start | bytes 1032200 | tf_op jit(solution)/shard_map/ppermute | solution.py:115
  (7 other events, 9.4 us)

commit v3 on v2

v3 whole, which is shorter than its diff:
```python
import functools

import jax
import jax.numpy as jnp
import ml_dtypes
import numpy as np
from jax import lax
from jax.experimental import pallas as pl
from jax.experimental.pallas import tpu as pltpu
from jax.sharding import PartitionSpec as P

BRICK = 32
INTERSECTION = 4
LENGTH = BRICK + 2 * INTERSECTION
REACH = INTERSECTION + 1
WIDE = BRICK + 2 * REACH
LANES = 128
PAD = 8
FOLD = 2 * INTERSECTION + 1

LAMBDA_RATIO = 2.0
SIGMA_SHIFT = 0.1
REF_MODULUS = 1.5
VOID_MODULUS = 0.1

F32 = jnp.float32
BF16 = jnp.bfloat16
VMEM = pl.BlockSpec(memory_space=pltpu.VMEM)
SMEM = pl.BlockSpec(memory_space=pltpu.SMEM)


def halves(values):
    values = np.asarray(values, np.float32)
    high = values.astype(ml_dtypes.bfloat16)
    low = (values - high.astype(np.float32)).astype(ml_dtypes.bfloat16)
    return high, low


def right_table(values):
    high, low = halves(values)
    return np.block([[high, low], [high, np.zeros_like(low)]]).astype(ml_dtypes.bfloat16)


def left_table(values):
    high, low = halves(values)
    return np.concatenate([high, high, low], axis=1)


def tables(count_x):
    grid = np.arange(1, LENGTH + 1, dtype=np.float64)
    sine = np.sqrt(2.0 / (LENGTH + 1)) * np.sin(np.pi * np.outer(grid, grid) / (LENGTH + 1))
    eigen = 2.0 - 2.0 * np.cos(np.pi * grid / (LENGTH + 1))
    position = np.arange(LENGTH, dtype=np.float64)
    margin = 2 * INTERSECTION
    ramp = np.minimum(
        np.minimum((position + 0.5) / margin, (LENGTH - 0.5 - position) / margin), 1.0
    )
    rows = count_x * BRICK + 2 * PAD
    ramped = ramp[:, None] * sine
    along_y = np.zeros((LANES, LANES))
    back_y = np.zeros((LANES, LANES))
    for c in range(3):
        lane = c * WIDE + 1
        along_y[lane : lane + LENGTH, c * LENGTH : (c + 1) * LENGTH] = ramped
        back_y[c * LENGTH : (c + 1) * LENGTH, lane : lane + LENGTH] = sine
    along_x = np.zeros((count_x * LENGTH, rows))
    back_x = np.zeros((rows - 2 * INTERSECTION, count_x * LENGTH))
    for b in range(count_x):
        row = b * BRICK + PAD - INTERSECTION
        along_x[b * LENGTH : (b + 1) * LENGTH, row : row + LENGTH] = ramped.T
        back_x[b * BRICK : b * BRICK + LENGTH, b * LENGTH : (b + 1) * LENGTH] = sine
    half = LENGTH // 2
    eye = np.eye(8)
    even = left_table(np.kron(ramped[:half, 0::2].T, eye))
    odd = left_table(np.kron(ramped[:half, 1::2].T, eye))
    back_even = left_table(np.kron(sine[0::2, :half].T, eye))
    back_odd = left_table(np.kron(sine[1::2, :half].T, eye))
    ratio = lambda c, d: LAMBDA_RATIO if c == d else 1.0
    base = np.ones((count_x * LENGTH, LANES))
    steps = np.zeros((LENGTH, 8, LANES))
    order = np.concatenate([np.arange(0, LENGTH, 2), np.arange(1, LENGTH, 2)])
    for c in range(3):
        part = slice(c * LENGTH, (c + 1) * LENGTH)
        base[:, part] = REF_MODULUS * (
            ratio(c, 1) * eigen[None, :]
            + ratio(c, 2) * np.tile(eigen, count_x)[:, None]
            + SIGMA_SHIFT
        )
        steps[:, :, part] = REF_MODULUS * ratio(c, 0) * eigen[order][:, None, None]
    return [
        right_table(along_y),
        left_table(along_x),
        even,
        odd,
        back_even,
        back_odd,
        left_table(back_x),
        right_table(back_y),
        base.astype(np.float32),
        steps.astype(np.float32),
    ]


def phases(count):
    return 1 if count <= 2 else 2


def partners(count, phase):
    found = [i + 1 if (i + phase) % 2 == 0 else i - 1 for i in range(count)]
    return [j if 0 <= j < count else i for i, j in enumerate(found)]


def swap(value, axis, phase):
    target = partners(lax.axis_size(axis), phase)
    return lax.ppermute(value, axis, list(enumerate(target)))


def swap_both(value, first, phase_first, second, phase_second):
    rows = lax.axis_size(first)
    columns = lax.axis_size(second)
    one = partners(rows, phase_first)
    two = partners(columns, phase_second)
    pairs = []
    for i in range(rows):
        for j in range(columns):
            moved = one[i] != i and two[j] != j
            to = one[i] * columns + two[j] if moved else i * columns + j
            pairs.append((i * columns + j, to))
    return lax.ppermute(value, (first, second), pairs)


def spots(shape):
    lane = lax.broadcasted_iota(jnp.int32, shape, len(shape) - 1)
    region = jnp.where(lane >= 3 * WIDE, 3, jnp.where(lane >= 2 * WIDE, 2, jnp.where(lane >= WIDE, 1, 0)))
    spot = jnp.where(region == 3, 4 * LANES, lane - region * WIDE)
    return spot, region


def turn(values, shift):
    return pltpu.roll(values, lax.rem(shift + 2 * LANES, LANES), values.ndim - 1)


def pack(planes, width, start, spot, groups):
    total = jnp.zeros(spot.shape, F32)
    for g, plane in enumerate(planes):
        inside = (spot >= g * width) & (spot < (g + 1) * width)
        total = jnp.where(inside, turn(plane, g * width - start), total)
    return total


def unpack(packed, g, width, start, spot, use):
    inside = (spot >= start) & (spot < start + width) & use
    return jnp.where(inside, turn(packed, start - g * width), 0.0)


def side(pos_ref, dim, phase, count):
    place = pos_ref[dim]
    up = lax.rem(place + phase, 2) == 0
    use = jnp.where(up, place < count - 1, place > 0)
    return up, use


def pick(up, high, low):
    return jnp.where(up, high, low)


def two_terms(values):
    high = values.astype(BF16)
    low = (values - high.astype(F32)).astype(BF16)
    return high, low


def right_product(values, table):
    high, low = two_terms(values)
    product = jnp.dot(jnp.concatenate([high, low], axis=1), table, preferred_element_type=F32)
    return product[:, :LANES] + product[:, LANES:]


def left_product(table, values):
    high, low = two_terms(values)
    return jnp.dot(
        table, jnp.concatenate([high, low, high], axis=0), preferred_element_type=F32
    )


def along(columns):
    return columns + 2 * INTERSECTION


def solve(source, mid, target, consts):
    along_y, along_x, even, odd, back_even, back_odd, back_x, back_y, base, steps = consts
    rows = target.shape[1]
    half = LENGTH // 2

    def forward(t, _):
        both = jnp.concatenate([source(2 * t), source(2 * t + 1)], axis=0)
        turned = right_product(both, along_y[...])
        height = both.shape[0] // 2
        pair = jnp.concatenate([turned[:height], turned[height:]], axis=1)
        done = left_product(along_x[...], pair)
        mid[2 * t] = done[:, :LANES]
        mid[2 * t + 1] = done[:, LANES:]
        return 0

    lax.fori_loop(0, half, forward, 0, unroll=10)

    def across(g, _):
        start = pl.multiple_of(g * 16, 16)

        def plane(z):
            return jnp.concatenate(
                [mid[z, pl.ds(start, 8), :], mid[z, pl.ds(start + 8, 8), :]], axis=1
            )

        planes = [plane(z) for z in range(LENGTH)]
        sums = jnp.concatenate([planes[z] + planes[LENGTH - 1 - z] for z in range(half)], axis=0)
        gaps = jnp.concatenate([planes[z] - planes[LENGTH - 1 - z] for z in range(half)], axis=0)
        ground = jnp.concatenate(
            [base[pl.ds(start, 8), :], base[pl.ds(start + 8, 8), :]], axis=1
        )

        def divisors(first):
            return jnp.concatenate(
                [
                    ground + jnp.concatenate([steps[first + k], steps[first + k]], axis=1)
                    for k in range(half)
                ],
                axis=0,
            )

        near = left_product(back_even[...], left_product(even[...], sums) / divisors(0))
        far = left_product(back_odd[...], left_product(odd[...], gaps) / divisors(half))
        lower = near + far
        upper = near - far
        for z in range(half):
            for h in range(2):
                lanes = slice(h * LANES, (h + 1) * LANES)
                mid[z, pl.ds(start + 8 * h, 8), :] = lower[8 * z : 8 * z + 8, lanes]
                mid[LENGTH - 1 - z, pl.ds(start + 8 * h, 8), :] = upper[8 * z : 8 * z + 8, lanes]
        return 0

    lax.fori_loop(0, mid.shape[1] // 16, across, 0, unroll=5)

    def backward(t, _):
        pair = jnp.concatenate([mid[2 * t], mid[2 * t + 1]], axis=1)
        done = left_product(back_x[...], pair)
        both = jnp.concatenate([done[:, :LANES], done[:, LANES:]], axis=0)
        turned = right_product(both, back_y[...])
        target[2 * t] = turned[:rows]
        target[2 * t + 1] = turned[rows:]
        return 0

    lax.fori_loop(0, half, backward, 0, unroll=10)


def write_messages(pos_ref, solved, width, counts, outs_y, outs_z, outs_yz):
    rows = solved.shape[1]
    spot, _ = spots((rows, LANES))
    groups = WIDE // width
    _, count_y, count_z = counts
    for phase, out in enumerate(outs_z):
        up, _ = side(pos_ref, 0, phase, count_z)
        first = pick(up, LENGTH - width, 0)
        for i in range(width):
            out[i] = solved[first + i]
    for phase, out in enumerate(outs_y):
        up, _ = side(pos_ref, 1, phase, count_y)
        start = pick(up, WIDE - 1 - width, 1)
        many = LENGTH // groups

        def one(k, _, out=out, start=start, many=many):
            out[k] = pack(
                [solved[g * many + k] for g in range(groups)], width, start, spot, groups
            )
            return 0

        lax.fori_loop(0, many, one, 0, unroll=5)
    for number, out in enumerate(outs_yz):
        phase_y, phase_z = divmod(number, len(outs_z))
        up_y, _ = side(pos_ref, 1, phase_y, count_y)
        up_z, _ = side(pos_ref, 0, phase_z, count_z)
        start = pick(up_y, WIDE - 1 - width, 1)
        first = pick(up_z, LENGTH - width, 0)
        many = out.shape[0]
        for k in range(many):
            planes = [
                solved[first + g * many + k] for g in range(groups) if g * many + k < width
            ]
            out[k] = pack(planes, width, start, spot, groups)


def planes_of(width):
    return range(FOLD - width, WIDE - FOLD + width)


def add_messages(pos_ref, solved, width, counts, ins_y, ins_z, ins_yz, window, put, get):
    height = solved.shape[1] if window is None else window.size
    rows = slice(None) if window is None else window
    spot, _ = spots((height, LANES))
    groups = WIDE // width
    _, count_y, count_z = counts
    sides_y = [side(pos_ref, 1, phase, count_y) for phase in range(len(ins_y))]
    sides_z = [side(pos_ref, 0, phase, count_z) for phase in range(len(ins_z))]
    many = LENGTH // groups
    wanted = planes_of(width)
    for z in range(LENGTH):
        if z + 1 not in wanted:
            continue
        g, k = divmod(z, many)
        total = solved[z, rows, :]
        for (up, use), ref in zip(sides_y, ins_y):
            start = pick(up, WIDE - FOLD, FOLD - width)
            total = total + unpack(ref[k, rows, :], g, width, start, spot, use)
        put(z + 1 - wanted[0], total)
    for plane in (0, WIDE - 1):
        if plane in wanted:
            put(plane - wanted[0], jnp.zeros((height, LANES), F32))
    for phase_z, ((up_z, use_z), ref_z) in enumerate(zip(sides_z, ins_z)):
        first = pick(up_z, WIDE - FOLD - wanted[0], 0)
        for i in range(width):
            total = ref_z[i, rows, :]
            for phase_y, (up_y, use_y) in enumerate(sides_y):
                ref = ins_yz[phase_y * len(ins_z) + phase_z]
                g, k = divmod(i, ref.shape[0])
                start = pick(up_y, WIDE - FOLD, FOLD - width)
                total = total + unpack(ref[k, rows, :], g, width, start, spot, use_y)
            put(first + i, get(first + i) + jnp.where(use_z, total, 0.0))


def grid_masks(pos_ref, rows, counts):
    count_x, count_y, count_z = counts
    spot, _ = spots((rows, LANES))
    row = lax.broadcasted_iota(jnp.int32, (rows, LANES), 0)
    low_y = pick(pos_ref[1] > 0, 0, REACH)
    high_y = pick(pos_ref[1] < count_y - 1, WIDE, REACH + BRICK)
    low_x = pick(pos_ref[2] > 0, 0, PAD)
    high_x = pick(pos_ref[2] < count_x - 1, rows, rows - PAD)
    inside = (spot >= low_y) & (spot < high_y) & (row >= low_x) & (row < high_x)
    low_z = pick(pos_ref[0] > 0, 0, REACH)
    high_z = pick(pos_ref[0] < count_z - 1, WIDE, REACH + BRICK)
    return inside, low_z, high_z


def from_sides(sides, refs, index):
    low = high = None
    for (up, use), ref in zip(sides, refs):
        value = index(ref)
        one = jnp.where(use & jnp.logical_not(up), value, 0.0)
        two = jnp.where(use & up, value, 0.0)
        low = one if low is None else low + one
        high = two if high is None else high + two
    return low, high


def complete(pos_ref, counts, partial, ins_x, height, field, first):
    rows = field.shape[1]
    inside, low_z, high_z = grid_masks(pos_ref, rows, counts)
    sides = [side(pos_ref, 2, phase, counts[0]) for phase in range(len(ins_x))]
    row = lax.broadcasted_iota(jnp.int32, (16, LANES), 0)
    blank = jnp.zeros((8, LANES), F32)

    def one(z, _):
        low, high = from_sides(sides, ins_x, lambda ref: ref[z])
        if height == 16:
            low = jnp.where(row < 12, pltpu.roll(low, 12, 0), 0.0)
            high = jnp.where(row < 4, 0.0, pltpu.roll(high, 4, 0))
        else:
            low = pltpu.roll(jnp.concatenate([low, blank], axis=0), 4, 0)
            high = pltpu.roll(jnp.concatenate([high, blank], axis=0), 4, 0)
        on = inside & (z + first >= low_z) & (z + first < high_z)
        whole = jnp.concatenate(
            [
                partial[z, :16, :] + low,
                partial[z, 16 : rows - 16, :],
                partial[z, rows - 16 :, :] + high,
            ],
            axis=0,
        )
        field[z] = jnp.where(on, whole, 0.0)
        return 0

    lax.fori_loop(0, field.shape[0], one, 0, unroll=2)


def widened(pos_ref, counts, modulus, ins_x):
    rows = modulus.shape[1]
    sides = [side(pos_ref, 2, phase, counts[0]) for phase in range(len(ins_x))]
    _, region = spots((PAD, LANES))
    third = WIDE // 3

    def plane(z):
        c = z // third
        k = z - c * third
        row = pl.multiple_of(k % 2 * PAD, PAD)
        low, high = from_sides(sides, ins_x, lambda ref: ref[WIDE + k // 2, pl.ds(row, PAD), :])
        edges = []
        for value in (low, high):
            total = turn(value, (2 * WIDE - c * WIDE))
            for target in (0, 1):
                total = jnp.where(region == target, turn(value, (target - c) * WIDE), total)
            edges.append(total)
        return jnp.concatenate([edges[0], modulus[z, PAD : rows - PAD, :], edges[1]], axis=0)

    return plane


def stiffness(field, modulus, first, last, shift, store):
    rows = field.shape[1]
    _, region = spots((rows, LANES))
    scale = [
        jnp.where(region == c, 0.5 * LAMBDA_RATIO, 0.5) for c in range(3)
    ]

    def one(z, carry):
        below, m = carry
        v = field[z - shift]
        next_m = modulus(z + 1)
        above = (m + next_m) * (field[z + 1 - shift] - v)
        gx = (m + pltpu.roll(m, rows - 1, 0)) * (pltpu.roll(v, rows - 1, 0) - v)
        gy = (m + pltpu.roll(m, LANES - 1, 1)) * (pltpu.roll(v, LANES - 1, 1) - v)
        total = SIGMA_SHIFT * m * v + scale[0] * (below - above)
        total = total + scale[1] * (pltpu.roll(gy, 1, 1) - gy)
        total = total + scale[2] * (pltpu.roll(gx, 1, 0) - gx)
        store(z, total)
        return above, next_m

    m = modulus(first)
    below = (modulus(first - 1) + m) * (field[first - shift] - field[first - 1 - shift])
    lax.fori_loop(first, last + 1, one, (below, m), unroll=4)


def groups_of(refs, sizes):
    found = []
    at = 0
    for size in sizes:
        found.append(refs[at : at + size])
        at += size
    return found


def prepare_kernel(counts, sizes, pos_ref, table_ref, load, labels, mask, *refs):
    (modulus_out,), outs_y, outs_z, outs_yz = groups_of(refs, (1,) + sizes[:3])
    _, count_y, count_z = counts

    def one(z, _):
        label = labels[z]
        looked = jnp.zeros(label.shape, F32)
        for k in range(table_ref.shape[0]):
            looked = jnp.where(label == k, table_ref[k], looked)
        modulus_out[z] = jnp.where(mask[z] == 1, looked, VOID_MODULUS)
        return 0

    lax.fori_loop(0, BRICK, one, 0, unroll=4)
    thin = INTERSECTION
    pairs = BRICK // 2

    def ends(plane, up, count):
        return jnp.where(up, plane[BRICK - count :, :], plane[:count, :])

    for phase, out in enumerate(outs_z):
        up, _ = side(pos_ref, 0, phase, count_z)
        first = pick(up, BRICK - thin, 0)
        for c in range(3):
            for i in range(thin):
                out[c * thin + i] = load[c, first + i]
        first = pick(up, BRICK - REACH, 0)
        for i in range(REACH):
            out[3 * thin + i] = modulus_out[first + i]
    for phase, out in enumerate(outs_y):
        up, _ = side(pos_ref, 1, phase, count_y)
        for c in range(4):
            for z in range(BRICK):
                plane = load[c, z] if c < 3 else modulus_out[z]
                row = z % 2 * thin
                out[c * pairs + z // 2, row : row + thin, :] = ends(plane, up, thin)
        for z in range(BRICK):
            plane = modulus_out[z]
            fifth = jnp.where(
                up, plane[BRICK - REACH : BRICK - thin, :], plane[thin:REACH, :]
            )
            out[4 * pairs + z // 8, z % 8 : z % 8 + 1, :] = fifth
    for number, out in enumerate(outs_yz):
        phase_y, phase_z = divmod(number, len(outs_z))
        up_y, _ = side(pos_ref, 1, phase_y, count_y)
        up_z, _ = side(pos_ref, 0, phase_z, count_z)
        first = pick(up_z, BRICK - thin, 0)
        for c in range(3):
            for i in range(thin):
                row = i % 2 * thin
                out[c * 2 + i // 2, row : row + thin, :] = ends(load[c, first + i], up_y, thin)
        first = pick(up_z, BRICK - REACH, 0)
        for i in range(REACH):
            out[6 + i] = ends(modulus_out[first + i], up_y, 8)


def gather_kernel(counts, sizes, pos_ref, load, *refs):
    ins_y, ins_z, ins_yz, (load_out,), outs_x, (wide,) = groups_of(
        refs, sizes[:3] + (1, sizes[3], 1)
    )
    columns = load.shape[3]
    rows = columns + 2 * PAD
    count_x, count_y, count_z = counts
    thin = INTERSECTION
    pairs = BRICK // 2
    sides_y = [side(pos_ref, 1, phase, count_y) for phase in range(len(ins_y))]
    sides_z = [side(pos_ref, 0, phase, count_z) for phase in range(len(ins_z))]
    blank = jnp.zeros((PAD, LANES), F32)

    def place(slot, c, centre, low, high):
        lane = c * WIDE + REACH
        wide[slot, lane : lane + BRICK, :] = centre
        wide[slot, lane - thin : lane, :] = low
        wide[slot, lane + BRICK : lane + BRICK + thin, :] = high

    def finish(z):
        load_out[z, :PAD, :] = blank
        load_out[z, PAD : PAD + columns, :] = wide[z].T
        load_out[z, rows - PAD :, :] = blank

    def clear(z, _):
        wide[z] = jnp.zeros((LANES, columns), F32)
        return 0

    lax.fori_loop(0, LENGTH, clear, 0, unroll=4)

    def pair(t, _):
        for h in range(2):
            z = 2 * t + h
            for c in range(3):
                low, high = from_sides(
                    sides_y, ins_y, lambda ref: ref[c * pairs + t, h * thin : (h + 1) * thin, :]
                )
                place(z + thin, c, load[c, z], low, high)
        for h in range(2):
            finish(2 * t + h + thin)
        return 0

    lax.fori_loop(0, pairs, pair, 0, unroll=2)
    for i in range(thin):
        row = i % 2 * thin
        for c in range(3):
            centre = from_sides(sides_z, ins_z, lambda ref: ref[c * thin + i])
            corner = [[], []]
            for phase_y in range(len(ins_y)):
                refs_z = ins_yz[phase_y * len(ins_z) : (phase_y + 1) * len(ins_z)]
                found = from_sides(
                    sides_z, refs_z, lambda ref: ref[c * 2 + i // 2, row : row + thin, :]
                )
                corner[0].append(found[0])
                corner[1].append(found[1])
            for which, slot in ((0, i), (1, thin + BRICK + i)):
                low, high = from_sides(sides_y, corner[which], lambda value: value)
                place(slot, c, centre[which], low, high)
        finish(i)
        finish(thin + BRICK + i)
    for phase, out in enumerate(outs_x):
        up, _ = side(pos_ref, 2, phase, count_x)
        start = pl.multiple_of(pick(up, rows - 2 * PAD, PAD), PAD)
        for z in range(LENGTH):
            out[z] = load_out[z, pl.ds(start, PAD), :]


def modulus_kernel(counts, sizes, pos_ref, modulus, *refs):
    ins_y, ins_z, ins_yz, (modulus_out,), (wide,) = groups_of(refs, sizes[:3] + (1, 1))
    columns = modulus.shape[2]
    rows = columns + 2 * PAD
    count_x, count_y, count_z = counts
    thin = INTERSECTION
    pairs = BRICK // 2
    sides_y = [side(pos_ref, 1, phase, count_y) for phase in range(len(ins_y))]
    sides_z = [side(pos_ref, 0, phase, count_z) for phase in range(len(ins_z))]
    blank = jnp.zeros((PAD, LANES), F32)

    def finish(z, centre, low, high, low_end, high_end):
        for c in range(3):
            lane = c * WIDE + REACH
            wide[z, lane : lane + BRICK, :] = centre
            wide[z, lane - thin : lane, :] = low
            wide[z, lane + BRICK : lane + BRICK + thin, :] = high
            wide[z, lane - REACH : lane - thin, :] = low_end
            wide[z, lane + BRICK + thin : lane + BRICK + REACH, :] = high_end
        wide[z, 3 * WIDE :, :] = jnp.zeros((LANES - 3 * WIDE, columns), F32)
        modulus_out[z, :PAD, :] = blank
        modulus_out[z, PAD : PAD + columns, :] = wide[z].T
        modulus_out[z, rows - PAD :, :] = blank

    for z in range(BRICK):
        row = z % 2 * thin
        low, high = from_sides(
            sides_y, ins_y, lambda ref: ref[3 * pairs + z // 2, row : row + thin, :]
        )
        low_end, high_end = from_sides(
            sides_y, ins_y, lambda ref: ref[4 * pairs + z // 8, z % 8 : z % 8 + 1, :]
        )
        finish(z + REACH, modulus[z], low, high, low_end, high_end)
    for i in range(REACH):
        centre = from_sides(sides_z, ins_z, lambda ref: ref[3 * thin + i])
        corner = [[], []]
        for phase_y in range(len(ins_y)):
            refs_z = ins_yz[phase_y * len(ins_z) : (phase_y + 1) * len(ins_z)]
            found = from_sides(sides_z, refs_z, lambda ref: ref[6 + i])
            corner[0].append(found[0])
            corner[1].append(found[1])
        for which, slot in ((0, i), (1, REACH + BRICK + i)):
            low, high = from_sides(sides_y, corner[which], lambda value: value)
            finish(
                slot,
                centre[which],
                low[8 - thin :, :],
                high[:thin, :],
                low[8 - REACH : 8 - thin, :],
                high[thin:REACH, :],
            )


def patched(pos_ref, counts, residual, ins_x):
    rows = residual.shape[1]
    sides = [side(pos_ref, 2, phase, counts[0]) for phase in range(len(ins_x))]

    def plane(z):
        low, high = from_sides(sides, ins_x, lambda ref: ref[z])
        return jnp.concatenate([low, residual[z, PAD : rows - PAD, :], high], axis=0)

    return plane


def first_kernel(counts, sizes, pos_ref, residual, *refs):
    ins_x, consts, (solved,), outs_y, outs_z, outs_yz, (mid,) = groups_of(
        refs, (sizes[3], 10, 1) + sizes[:3] + (1,)
    )
    solve(patched(pos_ref, counts, residual, ins_x), mid, solved, consts)
    write_messages(pos_ref, solved, FOLD, counts, outs_y, outs_z, outs_yz)


def edge_kernel(width, height, counts, sizes, pos_ref, solved, *refs):
    extra = 1 if width == FOLD else 0
    ins_y, ins_z, ins_yz, modulus, outs_x = groups_of(refs, sizes[:3] + (extra, sizes[3]))
    rows = solved.shape[1]
    _, region = spots((PAD, LANES))
    third = WIDE // 3
    for phase, out in enumerate(outs_x):
        up, _ = side(pos_ref, 2, phase, counts[0])
        window = pl.ds(pl.multiple_of(pick(up, rows - height, 0), 8), height)

        def put(plane, value, out=out):
            out[plane] = value

        def get(plane, out=out):
            return out[plane]

        add_messages(pos_ref, solved, width, counts, ins_y, ins_z, ins_yz, window, put, get)
        for ref in modulus:
            place = pl.ds(pl.multiple_of(pick(up, ref.shape[1] - 2 * PAD, PAD), PAD), PAD)
            for k in range(third):
                total = ref[k, place, :]
                for c in (1, 2):
                    total = jnp.where(region == c, ref[k + c * third, place, :], total)
                row = k % 2 * PAD
                out[WIDE + k // 2, row : row + PAD, :] = total


def fold_kernel(width, counts, sizes, pos_ref, solved, *refs):
    ins_y, ins_z, ins_yz, (field,) = groups_of(refs, sizes[:3] + (1,))
    rows = solved.shape[1]
    thin = INTERSECTION
    core = slice(thin, thin + rows)
    blank = jnp.zeros((thin, LANES), F32)

    def put(plane, value):
        field[plane, core, :] = value

    def get(plane):
        return field[plane, core, :]

    for z in range(field.shape[0]):
        field[z, :thin, :] = blank
        field[z, thin + rows :, :] = blank
    add_messages(pos_ref, solved, width, counts, ins_y, ins_z, ins_yz, None, put, get)


def second_kernel(counts, sizes, pos_ref, partial, residual, modulus, *refs):
    (
        ins_load,
        ins_x,
        consts,
        (solved, field, renewed),
        outs_y,
        outs_z,
        outs_yz,
        (mid,),
    ) = groups_of(refs, (sizes[3], sizes[3], 10, 3) + sizes[:3] + (1,))
    rows = partial.shape[1]
    complete(pos_ref, counts, partial, ins_x, 16, field, 0)
    inside, low_z, high_z = grid_masks(pos_ref, rows, counts)
    before = patched(pos_ref, counts, residual, ins_load)

    def store(z, product):
        on = inside & (z >= low_z) & (z < high_z)
        renewed[z - 1] = jnp.where(on, before(z - 1) - product, 0.0)

    stiffness(field, widened(pos_ref, counts, modulus, ins_x), 1, WIDE - 2, 0, store)
    solve(lambda z: renewed[z], mid, solved, consts)
    write_messages(pos_ref, solved, REACH, counts, outs_y, outs_z, outs_yz)


def last_kernel(counts, sizes, pos_ref, partial, modulus, moved, left, *refs):
    ins_x, ins_modulus, (displacement, residual), (field,) = groups_of(
        refs, (sizes[3], sizes[3], 2, 1)
    )
    rows = partial.shape[1]
    first = planes_of(REACH)[0]
    complete(pos_ref, counts, partial, ins_x, 8, field, first)
    core = slice(PAD, rows - PAD)

    def store(z, product):
        at = z - REACH
        one = (moved[z, core, :] + field[z - first, core, :]).T
        two = (left[z - 1, core, :] - product[core]).T
        for c in range(3):
            lane = c * WIDE + REACH
            displacement[c, at] = one[lane : lane + BRICK, :]
            residual[c, at] = two[lane : lane + BRICK, :]

    stiffness(
        field,
        widened(pos_ref, counts, modulus, ins_modulus),
        REACH,
        REACH + BRICK - 1,
        first,
        store,
    )


def call(kernel, inputs, outs, scratch=(), smem=1, limit=24, work=0):
    return pl.pallas_call(
        kernel,
        out_shape=[jax.ShapeDtypeStruct(shape, F32) for shape in outs],
        in_specs=[SMEM] * smem + [VMEM] * (len(inputs) - smem),
        out_specs=[VMEM] * len(outs),
        scratch_shapes=[pltpu.VMEM(shape, F32) for shape in scratch],
        compiler_params=pltpu.CompilerParams(vmem_limit_bytes=limit * 1024 * 1024),
        cost_estimate=pl.CostEstimate(flops=work, bytes_accessed=work, transcendentals=0),
    )(*inputs)


def local(load, labels, mask, table):
    columns = load.shape[3]
    rows = columns + 2 * PAD
    counts = tuple(lax.axis_size(axis) for axis in ("gx", "gy", "gz"))
    ways = tuple(phases(count) for count in counts)
    sizes = (ways[1], ways[2], ways[1] * ways[2], ways[0])
    pos = jnp.stack([lax.axis_index(axis) for axis in ("gz", "gy", "gx")]).astype(jnp.int32)
    consts = [jnp.asarray(value) for value in tables(columns // BRICK)]
    spectral = (LENGTH, columns // BRICK * LENGTH, LANES)

    def exchange_yz(values):
        y, z, yz = groups_of(values, sizes[:3])
        z = [swap(value, "gz", phase) for phase, value in enumerate(z)]
        y = [swap(value, "gy", phase) for phase, value in enumerate(y)]
        yz = [
            swap_both(value, "gy", number // ways[2], "gz", number % ways[2])
            for number, value in enumerate(yz)
        ]
        return [*y, *z, *yz]

    def exchange_x(values):
        return [swap(value, "gx", phase) for phase, value in enumerate(values)]

    def message_shapes(width, height):
        groups = WIDE // width
        return (
            [(LENGTH // groups, height, LANES)] * sizes[0]
            + [(width, height, LANES)] * sizes[1]
            + [(-(-width // groups), height, LANES)] * sizes[2]
        )

    bind = lambda kernel, *first: functools.partial(kernel, *first, counts, sizes)
    thick = along(columns)
    thin = (LENGTH, thick, LANES)
    tall = (LENGTH, rows, LANES)
    wide = (WIDE, rows, LANES)
    near = len(planes_of(REACH))

    modulus_core, *out = call(
        bind(prepare_kernel),
        [pos, table, load, labels, mask],
        [(BRICK, BRICK, columns)]
        + [(2 * BRICK + BRICK // 8, 8, columns)] * sizes[0]
        + [(3 * INTERSECTION + REACH, BRICK, columns)] * sizes[1]
        + [(6 + REACH, 8, columns)] * sizes[2],
        smem=2,
    )
    margins = exchange_yz(out)
    residual, *out = call(
        bind(gather_kernel),
        [pos, load, *margins],
        [tall] + [(LENGTH, PAD, LANES)] * sizes[3],
        [(LENGTH, LANES, columns)],
    )
    from_x = exchange_x(out)
    (modulus,) = call(
        bind(modulus_kernel),
        [pos, modulus_core, *margins],
        [wide],
        [(WIDE, LANES, columns)],
        work=8000000,
    )
    solved, *out = call(
        bind(first_kernel),
        [pos, residual, *from_x, *consts],
        [thin] + message_shapes(FOLD, thick),
        [spectral],
    )
    margins = exchange_yz(out)
    first_edges = exchange_x(
        call(
            bind(edge_kernel, FOLD, 16),
            [pos, solved, *margins, modulus],
            [(WIDE + WIDE // 6, 16, LANES)] * sizes[3],
        )
    )
    (partial,) = call(
        bind(fold_kernel, FOLD), [pos, solved, *margins], [wide], work=8000000
    )
    solved, moved, left, *out = call(
        bind(second_kernel),
        [pos, partial, residual, modulus, *from_x, *first_edges, *consts],
        [thin, wide, tall] + message_shapes(REACH, thick),
        [spectral],
        limit=32,
    )
    margins = exchange_yz(out)
    edges = exchange_x(
        call(
            bind(edge_kernel, REACH, 8), [pos, solved, *margins], [(near, 8, LANES)] * sizes[3]
        )
    )
    (partial,) = call(
        bind(fold_kernel, REACH), [pos, solved, *margins], [(near, rows, LANES)], work=8000000
    )
    displacement, residual = call(
        bind(last_kernel),
        [pos, partial, modulus, moved, left, *edges, *first_edges],
        [load.shape, load.shape],
        [(near, rows, LANES)],
        limit=32,
    )
    return displacement, residual


def solution(mesh):
    placed = (P(None, "gz", "gy", "gx"), P("gz", "gy", "gx"), P("gz", "gy", "gx"), P())
    return jax.shard_map(
        local,
        mesh=mesh,
        in_specs=placed,
        out_specs=(P(None, "gz", "gy", "gx"), P(None, "gz", "gy", "gx")),
        check_vma=False,
    )
```

time: 154 us -> 119 us (0.77)
  Pallas kernels: 66 us -> 48 us
  waiting for transfers between devices: 40.9 us -> 28.9 us
  local copies, waits for them, and re-layouts: 9.45 us -> 4.21 us
    pallas_call x7 -> x10, Pallas kernels: 66 us -> 48 us  [call(): pl.pallas_call(kernel, out_shape=[jax.ShapeDtypeStruct(shape, F32) for sh...]
    ppermute x6, waiting for transfers between devices: 23.9 us -> 17.5 us  [swap_both(): return lax.ppermute(value, (first, second), pairs)]
    ppermute x15, waiting for transfers between devices: 17 us -> 11.5 us  [swap(): return lax.ppermute(value, axis, list(enumerate(target)))]
    unnamed x36 -> x30, local copies, waits for them, and re-layouts: 9.45 us -> 4.21 us
  transfers between devices with their start and end apart: 21 -> 21, of which waited for: 10 -> 10; matrix products, arithmetic and copies ran while one was open for 0% -> 0% of each run, Pallas kernels for 0% -> 4%
where the time goes in v3:
time: 119 us; the launch traced here: 118 us
  Pallas kernels  48 us (40%)
  starting transfers between devices  36.3 us (31%)
  waiting for transfers between devices  28.9 us (24%)
  local copies, waits for them, and re-layouts  4.21 us (4%)
    pallas_call x10, Pallas kernels, call(): pl.pallas_call(kernel, out_shape=[jax.ShapeDtypeStruct(shape, F32) for sh...  48 us
    ppermute x15, starting transfers between devices, swap(): return lax.ppermute(value, axis, list(enumerate(target)))  28.1 us
    ppermute x6, waiting for transfers between devices, swap_both(): return lax.ppermute(value, (first, second), pairs)  17.5 us
    ppermute x15, waiting for transfers between devices, swap(): return lax.ppermute(value, axis, list(enumerate(target)))  11.5 us
    ppermute x6, starting transfers between devices, swap_both(): return lax.ppermute(value, (first, second), pairs)  8.19 us
    unnamed x30, local copies, waits for them, and re-layouts  4.21 us
  transfers between devices with their start and end apart: 21, of which 10 were waited for; matrix products, arithmetic and copies ran while one was open for 0% of the time, Pallas kernels for 4%

profile of v3, /device:TPU:9, one launch (start us, length us, event | category | flops | bytes accessed | tf_op | source)
XLA Modules:
  0.0 118.5 jit_solution(3447727140291089716)
XLA Ops:
  0.7 1.4 %copy-done = f32[3,32,32,128]{3,2,1,0:T(8,128)S(1)} copy-done((f32[3,32,32,128]{3,2,1,0:T(8,128)S(1)}, f32[3,32,32,128]{3,2,1,0:T(8,128)}, u32[]{:S(2)}) %copy-start) | copy-done | bytes 1572888
  2.1 1.0 copy-done.11
  5.0 1.3 %shard_map.149 = (f32[32,32,128]{2,1,0:T(8,128)S(1)}, f32[68,8,128]{2,1,0:T(8,128)S(1)}, f32[17,32,128]{2,1,0:T(8,128)S(1)}, f32[17,32,128]{2,1,0:T(8,128)S(1)},...) custom-call(s32[3]{0:T(128)S(1)} %pad_add_fusion.pos_ref, f32[16]{0:T(128)S(1)} %copy-done.14, ...), custom_call_target="tpu_custom_call" | custom-call | tf_op jit(solution)/shard_map/pallas_call | solution.py:735
  6.3 1.3 %collective-permute-start = (f32[68,8,128]{2,1,0:T(8,128)S(1)}, f32[68,8,128]{2,1,0:T(8,128)S(1)}, u32[]{:S(2)}, u32[]{:S(2)}) collective-permute-start(f32[68,8,128]{2,1,0:T(8,128)S(1)} %get-tuple-element.29), channel_id=1, source_target_pairs={{0,4},{4,0},{1,5},{5,1},{2,6},{6,2},{3,7},{7,3},{8,12},{12,8},{9,1... | collective-permute-start | bytes 835592 | tf_op jit(solution)/shard_map/ppermute | solution.py:115
  7.8 4.3 %collective-permute-start.2 = (f32[17,32,128]{2,1,0:T(8,128)S(1)}, f32[17,32,128]{2,1,0:T(8,128)S(1)}, u32[]{:S(2)}, u32[]{:S(2)}) collective-permute-start(f32[17,32,128]{2,1,0:T(8,128)S(1)} %get-tuple-element.31), channel_id=1, source_target_pairs={{0,0},{1,2},{2,1},{3,3},{4,4},{5,6},{6,5},{7,7},{8,8},{9,10},{10,9... | collective-permute-start | bytes 835592 | tf_op jit(solution)/shard_map/ppermute | solution.py:115
  12.2 1.9 %collective-permute-start.4 = (f32[11,8,128]{2,1,0:T(8,128)S(1)}, f32[11,8,128]{2,1,0:T(8,128)S(1)}, u32[]{:S(2)}, u32[]{:S(2)}) collective-permute-start(f32[11,8,128]{2,1,0:T(8,128)S(1)} %get-tuple-element.33), channel_id=1, source_target_pairs={{0,0},{1,6},{2,5},{3,3},{4,4},{5,2},{6,1},{7,7},{8,8},{9,14},{10,1... | collective-permute-start | bytes 135176 | tf_op jit(solution)/shard_map/ppermute | solution.py:129
  14.1 2.3 %collective-permute-done.3.refs_3_ = f32[11,8,128]{2,1,0:T(8,128)S(1)} collective-permute-done((f32[11,8,128]{2,1,0:T(8,128)S(1)}, f32[11,8,128]{2,1,0:T(8,128)S(1)}, u32[]{:S(2)}, u32[]{:S(2)}) %collective-permute-start.3) | collective-permute-done | bytes 45088 | tf_op jit(solution)/shard_map/ppermute | solution.py:129
  16.4 2.0 %collective-permute-done.4.refs_4_ = f32[11,8,128]{2,1,0:T(8,128)S(1)} collective-permute-done((f32[11,8,128]{2,1,0:T(8,128)S(1)}, f32[11,8,128]{2,1,0:T(8,128)S(1)}, u32[]{:S(2)}, u32[]{:S(2)}) %collective-permute-start.4) | collective-permute-done | bytes 45088 | tf_op jit(solution)/shard_map/ppermute | solution.py:129
  18.5 2.1 %shard_map.150 = (f32[40,144,128]{2,1,0:T(8,128)S(1)}, f32[40,8,128]{2,1,0:T(8,128)S(1)}, f32[40,8,128]{2,1,0:T(8,128)S(1)}) custom-call(s32[3]{0:T(128)S(1)} %pad_add_fusion.pos_ref, f32[3,32,32,128]{3,2,1,0:T(8,128)S(1)} %copy-done.1, f32[68,8,128]{2,1,0:T(8,128)S(1)} %collective-permute-done.refs_0_, f32[17,32,128]{2,1,0:T(8,128)S(1)} %collective-permute-done.1.refs_1_, ...), custom_call_target="tpu_custom_call" | custom-call | tf_op jit(solution)/shard_map/pallas_call | solution.py:735
  20.6 2.2 %collective-permute-start.5 = (f32[40,8,128]{2,1,0:T(8,128)S(1)}, f32[40,8,128]{2,1,0:T(8,128)S(1)}, u32[]{:S(2)}, u32[]{:S(2)}) collective-permute-start(f32[40,8,128]{2,1,0:T(8,128)S(1)} %get-tuple-element.35), channel_id=1, source_target_pairs={{0,8},{8,0},{16,24},{24,16},{1,9},{9,1},{17,25},{25,17},{2,10},{10... | collective-permute-start | bytes 491528 | tf_op jit(solution)/shard_map/ppermute | solution.py:115
  22.8 3.0 %collective-permute-start.6 = (f32[40,8,128]{2,1,0:T(8,128)S(1)}, f32[40,8,128]{2,1,0:T(8,128)S(1)}, u32[]{:S(2)}, u32[]{:S(2)}) collective-permute-start(f32[40,8,128]{2,1,0:T(8,128)S(1)} %get-tuple-element.36), channel_id=1, source_target_pairs={{0,0},{8,16},{16,8},{24,24},{1,1},{9,17},{17,9},{25,25},{2,2},{10,... | collective-permute-start | bytes 491528 | tf_op jit(solution)/shard_map/ppermute | solution.py:115
  25.9 3.6 %collective-permute-done.6.refs_1_ = f32[40,8,128]{2,1,0:T(8,128)S(1)} collective-permute-done((f32[40,8,128]{2,1,0:T(8,128)S(1)}, f32[40,8,128]{2,1,0:T(8,128)S(1)}, u32[]{:S(2)}, u32[]{:S(2)}) %collective-permute-start.6) | collective-permute-done | bytes 163872 | tf_op jit(solution)/shard_map/ppermute | solution.py:115
  29.5 11.8 %shard_map.151 = (f32[40,136,128]{2,1,0:T(8,128)S(1)}, f32[10,136,128]{2,1,0:T(8,128)S(1)}, f32[9,136,128]{2,1,0:T(8,128)S(1)}, f32[9,136,128]{2,1,0:T(8,128)S(1...) custom-call(s32[3]{0:T(128)S(1)} %pad_add_fusion.pos_ref, f32[40,144,128]{2,1,0:T(8,128)S(1)} %get-tuple-element.34.residual, ...), custom_call_target="tpu_custom_call" | custom-call | tf_op jit(solution)/shard_map/pallas_call | solution.py:735
  41.3 1.3 %collective-permute-start.7 = (f32[10,136,128]{2,1,0:T(8,128)S(1)}, f32[10,136,128]{2,1,0:T(8,128)S(1)}, u32[]{:S(2)}, u32[]{:S(2)}) collective-permute-start(f32[10,136,128]{2,1,0:T(8,128)S(1)} %get-tuple-element.38), channel_id=1, source_target_pairs={{0,4},{4,0},{1,5},{5,1},{2,6},{6,2},{3,7},{7,3},{8,12},{12,8},{9,1... | collective-permute-start | bytes 2088968 | tf_op jit(solution)/shard_map/ppermute | solution.py:115
  42.6 3.4 %collective-permute-start.9 = (f32[9,136,128]{2,1,0:T(8,128)S(1)}, f32[9,136,128]{2,1,0:T(8,128)S(1)}, u32[]{:S(2)}, u32[]{:S(2)}) collective-permute-start(f32[9,136,128]{2,1,0:T(8,128)S(1)} %get-tuple-element.40), channel_id=1, source_target_pairs={{0,0},{1,2},{2,1},{3,3},{4,4},{5,6},{6,5},{7,7},{8,8},{9,10},{10,9... | collective-permute-start | bytes 1880072 | tf_op jit(solution)/shard_map/ppermute | solution.py:115
  46.1 3.0 %collective-permute-start.11 = (f32[3,136,128]{2,1,0:T(8,128)S(1)}, f32[3,136,128]{2,1,0:T(8,128)S(1)}, u32[]{:S(2)}, u32[]{:S(2)}) collective-permute-start(f32[3,136,128]{2,1,0:T(8,128)S(1)} %get-tuple-element.42), channel_id=1, source_target_pairs={{0,0},{1,6},{2,5},{3,3},{4,4},{5,2},{6,1},{7,7},{8,8},{9,14},{10,1... | collective-permute-start | bytes 626696 | tf_op jit(solution)/shard_map/ppermute | solution.py:129
  49.1 1.4 %shard_map.153.refs_5_.modulus = f32[42,144,128]{2,1,0:T(8,128)S(1)} custom-call(s32[3]{0:T(128)S(1)} %pad_add_fusion.pos_ref, f32[32,32,128]{2,1,0:T(8,128)S(1)} %get-tuple-element.43.modulus, f32[68,8,128]{2,1,0:T(8,128)S(1)} %collective-permute-done.refs_0_, f32[17,32,128]{2,1,0:T(8,128)S(1)} %collective-permute-done.1.refs_1_, ...), custom_call_target="tpu_custom_call" | custom-call | flops 8000000 | bytes 8000000 | tf_op jit(solution)/shard_map/pallas_call | solution.py:735
  50.5 8.3 %collective-permute-done.10.refs_3_ = f32[3,136,128]{2,1,0:T(8,128)S(1)} collective-permute-done((f32[3,136,128]{2,1,0:T(8,128)S(1)}, f32[3,136,128]{2,1,0:T(8,128)S(1)}, u32[]{:S(2)}, u32[]{:S(2)}) %collective-permute-start.10) | collective-permute-done | bytes 208928 | tf_op jit(solution)/shard_map/ppermute | solution.py:129
  58.8 1.9 %collective-permute-done.11.refs_4_ = f32[3,136,128]{2,1,0:T(8,128)S(1)} collective-permute-done((f32[3,136,128]{2,1,0:T(8,128)S(1)}, f32[3,136,128]{2,1,0:T(8,128)S(1)}, u32[]{:S(2)}, u32[]{:S(2)}) %collective-permute-start.11) | collective-permute-done | bytes 208928 | tf_op jit(solution)/shard_map/ppermute | solution.py:129
  60.7 2.2 %collective-permute-done.7.refs_0_ = f32[10,136,128]{2,1,0:T(8,128)S(1)} collective-permute-done((f32[10,136,128]{2,1,0:T(8,128)S(1)}, f32[10,136,128]{2,1,0:T(8,128)S(1)}, u32[]{:S(2)}, u32[]{:S(2)}) %collective-permute-start.7) | collective-permute-done | bytes 696352 | tf_op jit(solution)/shard_map/ppermute | solution.py:115
  63.9 3.0 %collective-permute-start.13 = (f32[49,16,128]{2,1,0:T(8,128)S(1)}, f32[49,16,128]{2,1,0:T(8,128)S(1)}, u32[]{:S(2)}, u32[]{:S(2)}) collective-permute-start(f32[49,16,128]{2,1,0:T(8,128)S(1)} %get-tuple-element.45), channel_id=1, source_target_pairs={{0,0},{8,16},{16,8},{24,24},{1,1},{9,17},{17,9},{25,25},{2,2},{10,... | collective-permute-start | bytes 1204232 | tf_op jit(solution)/shard_map/ppermute | solution.py:115
  66.9 1.7 %shard_map.152.partial = f32[42,144,128]{2,1,0:T(8,128)S(1)} custom-call(s32[3]{0:T(128)S(1)} %pad_add_fusion.pos_ref, f32[40,136,128]{2,1,0:T(8,128)S(1)} %get-tuple-element.37.solved, f32[10,136,128]{2,1,0:T(8,128)S(1)} %collective-permute-done.7.refs_0_, f32[9,136,128]{2,1,0:T(8,128)S(1)} %collective-permute-done.8.refs_1_, ...), custom_call_target="tpu_custom_call" | custom-call | flops 8000000 | bytes 8000000 | tf_op jit(solution)/shard_map/pallas_call | solution.py:735
  68.6 4.4 %collective-permute-done.13.refs_3_ = f32[49,16,128]{2,1,0:T(8,128)S(1)} collective-permute-done((f32[49,16,128]{2,1,0:T(8,128)S(1)}, f32[49,16,128]{2,1,0:T(8,128)S(1)}, u32[]{:S(2)}, u32[]{:S(2)}) %collective-permute-start.13) | collective-permute-done | bytes 401440 | tf_op jit(solution)/shard_map/ppermute | solution.py:115
  73.1 17.6 %shard_map.155 = (f32[40,136,128]{2,1,0:T(8,128)S(1)}, f32[42,144,128]{2,1,0:T(8,128)S(1)}, f32[40,144,128]{2,1,0:T(8,128)S(1)}, f32[5,136,128]{2,1,0:T(8,128)S(...) custom-call(s32[3]{0:T(128)S(1)} %pad_add_fusion.pos_ref, ...), custom_call_target="tpu_custom_call" | custom-call | tf_op jit(solution)/shard_map/pallas_call | solution.py:735
  90.7 1.3 %collective-permute-start.14 = (f32[5,136,128]{2,1,0:T(8,128)S(1)}, f32[5,136,128]{2,1,0:T(8,128)S(1)}, u32[]{:S(2)}, u32[]{:S(2)}) collective-permute-start(f32[5,136,128]{2,1,0:T(8,128)S(1)} %get-tuple-element.47), channel_id=1, source_target_pairs={{0,4},{4,0},{1,5},{5,1},{2,6},{6,2},{3,7},{7,3},{8,12},{12,8},{9,1... | collective-permute-start | bytes 1044488 | tf_op jit(solution)/shard_map/ppermute | solution.py:115
  92.0 3.3 %collective-permute-start.16 = (f32[5,136,128]{2,1,0:T(8,128)S(1)}, f32[5,136,128]{2,1,0:T(8,128)S(1)}, u32[]{:S(2)}, u32[]{:S(2)}) collective-permute-start(f32[5,136,128]{2,1,0:T(8,128)S(1)} %get-tuple-element.49), channel_id=1, source_target_pairs={{0,0},{1,2},{2,1},{3,3},{4,4},{5,6},{6,5},{7,7},{8,8},{9,10},{10,9... | collective-permute-start | bytes 1044488 | tf_op jit(solution)/shard_map/ppermute | solution.py:115
  95.4 3.0 %collective-permute-start.18 = (f32[1,136,128]{2,1,0:T(8,128)S(1)}, f32[1,136,128]{2,1,0:T(8,128)S(1)}, u32[]{:S(2)}, u32[]{:S(2)}) collective-permute-start(f32[1,136,128]{2,1,0:T(8,128)S(1)} %get-tuple-element.51), channel_id=1, source_target_pairs={{0,0},{1,6},{2,5},{3,3},{4,4},{5,2},{6,1},{7,7},{8,8},{9,14},{10,1... | collective-permute-start | bytes 208904 | tf_op jit(solution)/shard_map/ppermute | solution.py:129
  99.5 1.9 %collective-permute-done.18.refs_4_ = f32[1,136,128]{2,1,0:T(8,128)S(1)} collective-permute-done((f32[1,136,128]{2,1,0:T(8,128)S(1)}, f32[1,136,128]{2,1,0:T(8,128)S(1)}, u32[]{:S(2)}, u32[]{:S(2)}) %collective-permute-start.18) | collective-permute-done | bytes 69664 | tf_op jit(solution)/shard_map/ppermute | solution.py:129
  102.2 4.6 %collective-permute-start.20 = (f32[34,8,128]{2,1,0:T(8,128)S(1)}, f32[34,8,128]{2,1,0:T(8,128)S(1)}, u32[]{:S(2)}, u32[]{:S(2)}) collective-permute-start(f32[34,8,128]{2,1,0:T(8,128)S(1)} %get-tuple-element.55), channel_id=1, source_target_pairs={{0,0},{8,16},{16,8},{24,24},{1,1},{9,17},{17,9},{25,25},{2,2},{10,... | collective-permute-start | bytes 417800 | tf_op jit(solution)/shard_map/ppermute | solution.py:115
  106.8 1.5 %shard_map.156.partial = f32[34,144,128]{2,1,0:T(8,128)S(1)} custom-call(s32[3]{0:T(128)S(1)} %pad_add_fusion.pos_ref, f32[40,136,128]{2,1,0:T(8,128)S(1)} %get-tuple-element.46.solved, f32[5,136,128]{2,1,0:T(8,128)S(1)} %collective-permute-done.14.refs_0_, f32[5,136,128]{2,1,0:T(8,128)S(1)} %collective-permute-done.15.refs_1_, ...), custom_call_target="tpu_custom_call" | custom-call | flops 8000000 | bytes 8000000 | tf_op jit(solution)/shard_map/pallas_call | solution.py:735
  108.3 1.2 %collective-permute-done.20.refs_1_ = f32[34,8,128]{2,1,0:T(8,128)S(1)} collective-permute-done((f32[34,8,128]{2,1,0:T(8,128)S(1)}, f32[34,8,128]{2,1,0:T(8,128)S(1)}, u32[]{:S(2)}, u32[]{:S(2)}) %collective-permute-start.20) | collective-permute-done | bytes 139296 | tf_op jit(solution)/shard_map/ppermute | solution.py:115
  109.5 8.9 %shard_map.158 = (f32[3,32,32,128]{3,2,1,0:T(8,128)}, f32[3,32,32,128]{3,2,1,0:T(8,128)}) custom-call(s32[3]{0:T(128)S(1)} %pad_add_fusion.pos_ref, f32[34,144,128]{2,1,0:T(8,128)S(1)} %shard_map.156.partial, f32[42,144,128]{2,1,0:T(8,128)S(1)} %shard_map.153.refs_5_.modulus, f32[42,144,128]{2,1,0:T(8,128)S(1)} %get-tuple-element.52.moved, ...), custom_call_target="tpu_custom_call" | custom-call | tf_op jit(solution)/shard_map/pallas_call | solution.py:735
  (51 shorter events, 5.0 us)
Async XLA Ops:
  4.9 13.6 %copy-start.1 = (f32[3,32,32,128]{3,2,1,0:T(8,128)S(1)}, f32[3,32,32,128]{3,2,1,0:T(8,128)}, u32[]{:S(2)}) copy-start(f32[3,32,32,128]{3,2,1,0:T(8,128)} %load.3) | copy-start | bytes 4718596
  4.9 24.6 %copy-start.2 = (f32[40,8,128]{2,1,0:T(8,128)S(1)}, f32[40,8,128]{2,1,0:T(8,128)}, u32[]{:S(2)}) copy-start(f32[40,8,128]{2,1,0:T(8,128)} %constant.41.clone.refs_11_.refs_13_) | copy-start | bytes 491524
  4.9 24.6 %copy-start.3 = (bf16[160,480]{1,0:T(8,128)(2,1)S(1)}, bf16[160,480]{1,0:T(8,128)(2,1)}, u32[]{:S(2)}) copy-start(bf16[160,480]{1,0:T(8,128)(2,1)} %constant.37.clone.refs_7_.refs_9_) | copy-start | bytes 460804
  4.9 24.6 %copy-start.4 = (bf16[160,480]{1,0:T(8,128)(2,1)S(1)}, bf16[160,480]{1,0:T(8,128)(2,1)}, u32[]{:S(2)}) copy-start(bf16[160,480]{1,0:T(8,128)(2,1)} %constant.36.clone.refs_6_.refs_8_) | copy-start | bytes 460804
  4.9 24.6 %copy-start.5 = (bf16[160,480]{1,0:T(8,128)(2,1)S(1)}, bf16[160,480]{1,0:T(8,128)(2,1)}, u32[]{:S(2)}) copy-start(bf16[160,480]{1,0:T(8,128)(2,1)} %constant.35.clone.refs_5_.refs_7_) | copy-start | bytes 460804
  4.9 24.6 %copy-start.6 = (bf16[160,480]{1,0:T(8,128)(2,1)S(1)}, bf16[160,480]{1,0:T(8,128)(2,1)}, u32[]{:S(2)}) copy-start(bf16[160,480]{1,0:T(8,128)(2,1)} %constant.34.clone.refs_4_.refs_6_) | copy-start | bytes 460804
  4.9 24.6 %copy-start.7 = (bf16[160,432]{1,0:T(8,128)(2,1)S(1)}, bf16[160,432]{1,0:T(8,128)(2,1)}, u32[]{:S(2)}) copy-start(bf16[160,432]{1,0:T(8,128)(2,1)} %constant.33.clone.refs_3_.refs_5_) | copy-start | bytes 414724
  4.9 24.6 %copy-start.8 = (bf16[136,480]{1,0:T(8,128)(2,1)S(1)}, bf16[136,480]{1,0:T(8,128)(2,1)}, u32[]{:S(2)}) copy-start(bf16[136,480]{1,0:T(8,128)(2,1)} %constant.38.clone.refs_8_.refs_10_) | copy-start | bytes 391684
  4.9 24.6 %copy-start.9 = (bf16[256,256]{1,0:T(8,128)(2,1)S(1)}, bf16[256,256]{1,0:T(8,128)(2,1)}, u32[]{:S(2)}) copy-start(bf16[256,256]{1,0:T(8,128)(2,1)} %constant.39.clone.refs_9_.refs_11_) | copy-start | bytes 393220
  4.9 24.6 %copy-start.10 = (bf16[256,256]{1,0:T(8,128)(2,1)S(1)}, bf16[256,256]{1,0:T(8,128)(2,1)}, u32[]{:S(2)}) copy-start(bf16[256,256]{1,0:T(8,128)(2,1)} %constant.32.clone.refs_2_.refs_4_) | copy-start | bytes 393220
  4.9 24.6 %copy-start.13 = (f32[160,128]{1,0:T(8,128)S(1)}, f32[160,128]{1,0:T(8,128)}, u32[]{:S(2)}) copy-start(f32[160,128]{1,0:T(8,128)} %constant.40.clone.refs_10_.refs_12_) | copy-start | bytes 245764
  6.3 12.2 %collective-permute-start = (f32[68,8,128]{2,1,0:T(8,128)S(1)}, f32[68,8,128]{2,1,0:T(8,128)S(1)}, u32[]{:S(2)}, u32[]{:S(2)}) collective-permute-start(f32[68,8,128]{2,1,0:T(8,128)S(1)} %get-tuple-element.29), channel_id=1, source_target_pairs={{0,4},{4,0},{1,5},{5,1},{2,6},{6,2},{3,7},{7,3},{8,12},{12,8},{9,1... | collective-permute-start | bytes 835592 | tf_op jit(solution)/shard_map/ppermute | solution.py:115
  7.6 10.8 %collective-permute-start.1 = (f32[17,32,128]{2,1,0:T(8,128)S(1)}, f32[17,32,128]{2,1,0:T(8,128)S(1)}, u32[]{:S(2)}, u32[]{:S(2)}) collective-permute-start(f32[17,32,128]{2,1,0:T(8,128)S(1)} %get-tuple-element.30), channel_id=1, source_target_pairs={{0,1},{1,0},{2,3},{3,2},{4,5},{5,4},{6,7},{7,6},{8,9},{9,8},{10,11... | collective-permute-start | bytes 835592 | tf_op jit(solution)/shard_map/ppermute | solution.py:115
  7.8 10.7 %collective-permute-start.2 = (f32[17,32,128]{2,1,0:T(8,128)S(1)}, f32[17,32,128]{2,1,0:T(8,128)S(1)}, u32[]{:S(2)}, u32[]{:S(2)}) collective-permute-start(f32[17,32,128]{2,1,0:T(8,128)S(1)} %get-tuple-element.31), channel_id=1, source_target_pairs={{0,0},{1,2},{2,1},{3,3},{4,4},{5,6},{6,5},{7,7},{8,8},{9,10},{10,9... | collective-permute-start | bytes 835592 | tf_op jit(solution)/shard_map/ppermute | solution.py:115
  12.1 4.3 %collective-permute-start.3 = (f32[11,8,128]{2,1,0:T(8,128)S(1)}, f32[11,8,128]{2,1,0:T(8,128)S(1)}, u32[]{:S(2)}, u32[]{:S(2)}) collective-permute-start(f32[11,8,128]{2,1,0:T(8,128)S(1)} %get-tuple-element.32), channel_id=1, source_target_pairs={{0,5},{1,4},{2,7},{3,6},{4,1},{5,0},{6,3},{7,2},{8,13},{9,12},{10,... | collective-permute-start | bytes 135176 | tf_op jit(solution)/shard_map/ppermute | solution.py:129
  12.2 6.3 %collective-permute-start.4 = (f32[11,8,128]{2,1,0:T(8,128)S(1)}, f32[11,8,128]{2,1,0:T(8,128)S(1)}, u32[]{:S(2)}, u32[]{:S(2)}) collective-permute-start(f32[11,8,128]{2,1,0:T(8,128)S(1)} %get-tuple-element.33), channel_id=1, source_target_pairs={{0,0},{1,6},{2,5},{3,3},{4,4},{5,2},{6,1},{7,7},{8,8},{9,14},{10,1... | collective-permute-start | bytes 135176 | tf_op jit(solution)/shard_map/ppermute | solution.py:129
  20.6 5.3 %collective-permute-start.5 = (f32[40,8,128]{2,1,0:T(8,128)S(1)}, f32[40,8,128]{2,1,0:T(8,128)S(1)}, u32[]{:S(2)}, u32[]{:S(2)}) collective-permute-start(f32[40,8,128]{2,1,0:T(8,128)S(1)} %get-tuple-element.35), channel_id=1, source_target_pairs={{0,8},{8,0},{16,24},{24,16},{1,9},{9,1},{17,25},{25,17},{2,10},{10... | collective-permute-start | bytes 491528 | tf_op jit(solution)/shard_map/ppermute | solution.py:115
  22.8 6.6 %collective-permute-start.6 = (f32[40,8,128]{2,1,0:T(8,128)S(1)}, f32[40,8,128]{2,1,0:T(8,128)S(1)}, u32[]{:S(2)}, u32[]{:S(2)}) collective-permute-start(f32[40,8,128]{2,1,0:T(8,128)S(1)} %get-tuple-element.36), channel_id=1, source_target_pairs={{0,0},{8,16},{16,8},{24,24},{1,1},{9,17},{17,9},{25,25},{2,2},{10,... | collective-permute-start | bytes 491528 | tf_op jit(solution)/shard_map/ppermute | solution.py:115
  41.3 21.6 %collective-permute-start.7 = (f32[10,136,128]{2,1,0:T(8,128)S(1)}, f32[10,136,128]{2,1,0:T(8,128)S(1)}, u32[]{:S(2)}, u32[]{:S(2)}) collective-permute-start(f32[10,136,128]{2,1,0:T(8,128)S(1)} %get-tuple-element.38), channel_id=1, source_target_pairs={{0,4},{4,0},{1,5},{5,1},{2,6},{6,2},{3,7},{7,3},{8,12},{12,8},{9,1... | collective-permute-start | bytes 2088968 | tf_op jit(solution)/shard_map/ppermute | solution.py:115
  42.6 18.1 %collective-permute-start.8 = (f32[9,136,128]{2,1,0:T(8,128)S(1)}, f32[9,136,128]{2,1,0:T(8,128)S(1)}, u32[]{:S(2)}, u32[]{:S(2)}) collective-permute-start(f32[9,136,128]{2,1,0:T(8,128)S(1)} %get-tuple-element.39), channel_id=1, source_target_pairs={{0,1},{1,0},{2,3},{3,2},{4,5},{5,4},{6,7},{7,6},{8,9},{9,8},{10,11... | collective-permute-start | bytes 1880072 | tf_op jit(solution)/shard_map/ppermute | solution.py:115
  42.6 18.1 %collective-permute-start.9 = (f32[9,136,128]{2,1,0:T(8,128)S(1)}, f32[9,136,128]{2,1,0:T(8,128)S(1)}, u32[]{:S(2)}, u32[]{:S(2)}) collective-permute-start(f32[9,136,128]{2,1,0:T(8,128)S(1)} %get-tuple-element.40), channel_id=1, source_target_pairs={{0,0},{1,2},{2,1},{3,3},{4,4},{5,6},{6,5},{7,7},{8,8},{9,10},{10,9... | collective-permute-start | bytes 1880072 | tf_op jit(solution)/shard_map/ppermute | solution.py:115
  46.0 12.8 %collective-permute-start.10 = (f32[3,136,128]{2,1,0:T(8,128)S(1)}, f32[3,136,128]{2,1,0:T(8,128)S(1)}, u32[]{:S(2)}, u32[]{:S(2)}) collective-permute-start(f32[3,136,128]{2,1,0:T(8,128)S(1)} %get-tuple-element.41), channel_id=1, source_target_pairs={{0,5},{1,4},{2,7},{3,6},{4,1},{5,0},{6,3},{7,2},{8,13},{9,12},{10,... | collective-permute-start | bytes 626696 | tf_op jit(solution)/shard_map/ppermute | solution.py:129
  46.1 14.6 %collective-permute-start.11 = (f32[3,136,128]{2,1,0:T(8,128)S(1)}, f32[3,136,128]{2,1,0:T(8,128)S(1)}, u32[]{:S(2)}, u32[]{:S(2)}) collective-permute-start(f32[3,136,128]{2,1,0:T(8,128)S(1)} %get-tuple-element.42), channel_id=1, source_target_pairs={{0,0},{1,6},{2,5},{3,3},{4,4},{5,2},{6,1},{7,7},{8,8},{9,14},{10,1... | collective-permute-start | bytes 626696 | tf_op jit(solution)/shard_map/ppermute | solution.py:129
  63.8 4.8 %collective-permute-start.12 = (f32[49,16,128]{2,1,0:T(8,128)S(1)}, f32[49,16,128]{2,1,0:T(8,128)S(1)}, u32[]{:S(2)}, u32[]{:S(2)}) collective-permute-start(f32[49,16,128]{2,1,0:T(8,128)S(1)} %get-tuple-element.44), channel_id=1, source_target_pairs={{0,8},{8,0},{16,24},{24,16},{1,9},{9,1},{17,25},{25,17},{2,10},{10... | collective-permute-start | bytes 1204232 | tf_op jit(solution)/shard_map/ppermute | solution.py:115
  63.9 9.2 %collective-permute-start.13 = (f32[49,16,128]{2,1,0:T(8,128)S(1)}, f32[49,16,128]{2,1,0:T(8,128)S(1)}, u32[]{:S(2)}, u32[]{:S(2)}) collective-permute-start(f32[49,16,128]{2,1,0:T(8,128)S(1)} %get-tuple-element.45), channel_id=1, source_target_pairs={{0,0},{8,16},{16,8},{24,24},{1,1},{9,17},{17,9},{25,25},{2,2},{10,... | collective-permute-start | bytes 1204232 | tf_op jit(solution)/shard_map/ppermute | solution.py:115
  90.7 10.7 %collective-permute-start.14 = (f32[5,136,128]{2,1,0:T(8,128)S(1)}, f32[5,136,128]{2,1,0:T(8,128)S(1)}, u32[]{:S(2)}, u32[]{:S(2)}) collective-permute-start(f32[5,136,128]{2,1,0:T(8,128)S(1)} %get-tuple-element.47), channel_id=1, source_target_pairs={{0,4},{4,0},{1,5},{5,1},{2,6},{6,2},{3,7},{7,3},{8,12},{12,8},{9,1... | collective-permute-start | bytes 1044488 | tf_op jit(solution)/shard_map/ppermute | solution.py:115
  92.0 9.4 %collective-permute-start.15 = (f32[5,136,128]{2,1,0:T(8,128)S(1)}, f32[5,136,128]{2,1,0:T(8,128)S(1)}, u32[]{:S(2)}, u32[]{:S(2)}) collective-permute-start(f32[5,136,128]{2,1,0:T(8,128)S(1)} %get-tuple-element.48), channel_id=1, source_target_pairs={{0,1},{1,0},{2,3},{3,2},{4,5},{5,4},{6,7},{7,6},{8,9},{9,8},{10,11... | collective-permute-start | bytes 1044488 | tf_op jit(solution)/shard_map/ppermute | solution.py:115
  92.0 9.4 %collective-permute-start.16 = (f32[5,136,128]{2,1,0:T(8,128)S(1)}, f32[5,136,128]{2,1,0:T(8,128)S(1)}, u32[]{:S(2)}, u32[]{:S(2)}) collective-permute-start(f32[5,136,128]{2,1,0:T(8,128)S(1)} %get-tuple-element.49), channel_id=1, source_target_pairs={{0,0},{1,2},{2,1},{3,3},{4,4},{5,6},{6,5},{7,7},{8,8},{9,10},{10,9... | collective-permute-start | bytes 1044488 | tf_op jit(solution)/shard_map/ppermute | solution.py:115
  95.4 4.1 %collective-permute-start.17 = (f32[1,136,128]{2,1,0:T(8,128)S(1)}, f32[1,136,128]{2,1,0:T(8,128)S(1)}, u32[]{:S(2)}, u32[]{:S(2)}) collective-permute-start(f32[1,136,128]{2,1,0:T(8,128)S(1)} %get-tuple-element.50), channel_id=1, source_target_pairs={{0,5},{1,4},{2,7},{3,6},{4,1},{5,0},{6,3},{7,2},{8,13},{9,12},{10,... | collective-permute-start | bytes 208904 | tf_op jit(solution)/shard_map/ppermute | solution.py:129
  95.4 6.0 %collective-permute-start.18 = (f32[1,136,128]{2,1,0:T(8,128)S(1)}, f32[1,136,128]{2,1,0:T(8,128)S(1)}, u32[]{:S(2)}, u32[]{:S(2)}) collective-permute-start(f32[1,136,128]{2,1,0:T(8,128)S(1)} %get-tuple-element.51), channel_id=1, source_target_pairs={{0,0},{1,6},{2,5},{3,3},{4,4},{5,2},{6,1},{7,7},{8,8},{9,14},{10,1... | collective-permute-start | bytes 208904 | tf_op jit(solution)/shard_map/ppermute | solution.py:129
  102.1 6.1 %collective-permute-start.19 = (f32[34,8,128]{2,1,0:T(8,128)S(1)}, f32[34,8,128]{2,1,0:T(8,128)S(1)}, u32[]{:S(2)}, u32[]{:S(2)}) collective-permute-start(f32[34,8,128]{2,1,0:T(8,128)S(1)} %get-tuple-element.54), channel_id=1, source_target_pairs={{0,8},{8,0},{16,24},{24,16},{1,9},{9,1},{17,25},{25,17},{2,10},{10... | collective-permute-start | bytes 417800 | tf_op jit(solution)/shard_map/ppermute | solution.py:115
  102.2 7.3 %collective-permute-start.20 = (f32[34,8,128]{2,1,0:T(8,128)S(1)}, f32[34,8,128]{2,1,0:T(8,128)S(1)}, u32[]{:S(2)}, u32[]{:S(2)}) collective-permute-start(f32[34,8,128]{2,1,0:T(8,128)S(1)} %get-tuple-element.55), channel_id=1, source_target_pairs={{0,0},{8,16},{16,8},{24,24},{1,1},{9,17},{17,9},{25,25},{2,2},{10,... | collective-permute-start | bytes 417800 | tf_op jit(solution)/shard_map/ppermute | solution.py:115
  (4 other events, 4.1 us)

commit v4 on v3

--- a/solution.py
+++ b/solution.py
@@ -27,6 +27,7 @@
 BF16 = jnp.bfloat16
 VMEM = pl.BlockSpec(memory_space=pltpu.VMEM)
 SMEM = pl.BlockSpec(memory_space=pltpu.SMEM)
+HBM = pl.BlockSpec(memory_space=pltpu.HBM)
 
 
 def halves(values):
@@ -110,23 +111,25 @@
     return [j if 0 <= j < count else i for i, j in enumerate(found)]
 
 
-def swap(value, axis, phase):
-    target = partners(lax.axis_size(axis), phase)
-    return lax.ppermute(value, axis, list(enumerate(target)))
-
-
-def swap_both(value, first, phase_first, second, phase_second):
-    rows = lax.axis_size(first)
-    columns = lax.axis_size(second)
-    one = partners(rows, phase_first)
-    two = partners(columns, phase_second)
+def swap(value, mesh, moves, filler):
+    names = mesh.axis_names
+    shape = [mesh.shape[name] for name in names]
+    found = {name: partners(mesh.shape[name], phase) for name, phase in moves.items()}
+    spare = None if filler is None else partners(mesh.shape[filler], 0)
     pairs = []
-    for i in range(rows):
-        for j in range(columns):
-            moved = one[i] != i and two[j] != j
-            to = one[i] * columns + two[j] if moved else i * columns + j
-            pairs.append((i * columns + j, to))
-    return lax.ppermute(value, (first, second), pairs)
+    for place in np.ndindex(*shape):
+        target = list(place)
+        for name, other in found.items():
+            target[names.index(name)] = other[place[names.index(name)]]
+        if any(target[names.index(name)] == place[names.index(name)] for name in found):
+            target = list(place)
+            if filler is not None:
+                target[names.index(filler)] = spare[place[names.index(filler)]]
+        pairs.append(tuple(int(np.ravel_multi_index(at, shape)) for at in (place, target)))
+    if filler is None and len(found) == 1:
+        ((name, other),) = found.items()
+        return lax.ppermute(value, name, list(enumerate(other)))
+    return lax.ppermute(value, names, pairs)
 
 
 def spots(shape):
@@ -256,6 +259,7 @@
 def write_messages(pos_ref, solved, width, counts, outs_y, outs_z, outs_yz):
     rows = solved.shape[1]
     spot, _ = spots((rows, LANES))
+    lane = lax.broadcasted_iota(jnp.int32, (rows, LANES), 1)
     groups = WIDE // width
     _, count_y, count_z = counts
     for phase, out in enumerate(outs_z):
@@ -281,12 +285,16 @@
         up_z, _ = side(pos_ref, 0, phase_z, count_z)
         start = pick(up_y, WIDE - 1 - width, 1)
         first = pick(up_z, LENGTH - width, 0)
-        many = out.shape[0]
-        for k in range(many):
-            planes = [
-                solved[first + g * many + k] for g in range(groups) if g * many + k < width
-            ]
-            out[k] = pack(planes, width, start, spot, groups)
+        slots = LANES // width
+        for k in range(out.shape[0]):
+            total = jnp.zeros((rows, LANES), F32)
+            for j in range(slots):
+                i, c = divmod(k * slots + j, 3)
+                if i < width:
+                    inside = (lane >= j * width) & (lane < (j + 1) * width)
+                    moved = turn(solved[first + i], j * width - c * WIDE - start)
+                    total = jnp.where(inside, moved, total)
+            out[k] = total
 
 
 def planes_of(width):
@@ -296,7 +304,7 @@
 def add_messages(pos_ref, solved, width, counts, ins_y, ins_z, ins_yz, window, put, get):
     height = solved.shape[1] if window is None else window.size
     rows = slice(None) if window is None else window
-    spot, _ = spots((height, LANES))
+    spot, region = spots((height, LANES))
     groups = WIDE // width
     _, count_y, count_z = counts
     sides_y = [side(pos_ref, 1, phase, count_y) for phase in range(len(ins_y))]
@@ -321,9 +329,14 @@
             total = ref_z[i, rows, :]
             for phase_y, (up_y, use_y) in enumerate(sides_y):
                 ref = ins_yz[phase_y * len(ins_z) + phase_z]
-                g, k = divmod(i, ref.shape[0])
                 start = pick(up_y, WIDE - FOLD, FOLD - width)
-                total = total + unpack(ref[k, rows, :], g, width, start, spot, use_y)
+                part = jnp.zeros((height, LANES), F32)
+                for c in range(3):
+                    k, j = divmod(3 * i + c, LANES // width)
+                    moved = turn(ref[k, rows, :], start + c * WIDE - j * width)
+                    part = jnp.where(region == c, moved, part)
+                inside = (spot >= start) & (spot < start + width) & use_y
+                total = total + jnp.where(inside, part, 0.0)
             put(first + i, get(first + i) + jnp.where(use_z, total, 0.0))
 
 
@@ -352,7 +365,7 @@
     return low, high
 
 
-def complete(pos_ref, counts, partial, ins_x, height, field, first):
+def complete(pos_ref, counts, partial, ins_x, ninth, field, first):
     rows = field.shape[1]
     inside, low_z, high_z = grid_masks(pos_ref, rows, counts)
     sides = [side(pos_ref, 2, phase, counts[0]) for phase in range(len(ins_x))]
@@ -361,12 +374,15 @@
 
     def one(z, _):
         low, high = from_sides(sides, ins_x, lambda ref: ref[z])
-        if height == 16:
-            low = jnp.where(row < 12, pltpu.roll(low, 12, 0), 0.0)
-            high = jnp.where(row < 4, 0.0, pltpu.roll(high, 4, 0))
-        else:
-            low = pltpu.roll(jnp.concatenate([low, blank], axis=0), 4, 0)
-            high = pltpu.roll(jnp.concatenate([high, blank], axis=0), 4, 0)
+        low = pltpu.roll(jnp.concatenate([low, blank], axis=0), 4, 0)
+        high = pltpu.roll(jnp.concatenate([high, blank], axis=0), 4, 0)
+        if ninth:
+            at = z % 8
+            under, over = from_sides(
+                sides, ins_x, lambda ref: ref[NINTH + z // 8, at : at + 1, :]
+            )
+            low = jnp.where(row == 3, under, low)
+            high = jnp.where(row == 12, over, high)
         on = inside & (z + first >= low_z) & (z + first < high_z)
         whole = jnp.concatenate(
             [
@@ -379,7 +395,11 @@
         field[z] = jnp.where(on, whole, 0.0)
         return 0
 
-    lax.fori_loop(0, field.shape[0], one, 0, unroll=2)
+    if ninth:
+        for z in range(field.shape[0]):
+            one(z, 0)
+    else:
+        lax.fori_loop(0, field.shape[0], one, 0, unroll=2)
 
 
 def widened(pos_ref, counts, modulus, ins_x):
@@ -390,9 +410,7 @@
 
     def plane(z):
         c = z // third
-        k = z - c * third
-        row = pl.multiple_of(k % 2 * PAD, PAD)
-        low, high = from_sides(sides, ins_x, lambda ref: ref[WIDE + k // 2, pl.ds(row, PAD), :])
+        low, high = from_sides(sides, ins_x, lambda ref: ref[THIRD + z - c * third])
         edges = []
         for value in (low, high):
             total = turn(value, (2 * WIDE - c * WIDE))
@@ -438,9 +456,20 @@
     return found
 
 
-def prepare_kernel(counts, sizes, pos_ref, table_ref, load, labels, mask, *refs):
-    (modulus_out,), outs_y, outs_z, outs_yz = groups_of(refs, (1,) + sizes[:3])
+def prepare_kernel(counts, sizes, pos_ref, table_in, load_in, labels_in, mask_in, *refs):
+    (modulus_out,), outs_y, outs_z, outs_yz, fetched = groups_of(refs, (1,) + sizes[:3] + (5,))
+    table_ref, labels, mask, load, arrived = fetched
     _, count_y, count_z = counts
+    copies = [
+        pltpu.make_async_copy(source, target, arrived.at[number])
+        for number, (source, target) in enumerate(
+            [(table_in, table_ref), (labels_in, labels), (mask_in, mask), (load_in, load)]
+        )
+    ]
+    for copy in copies:
+        copy.start()
+    for copy in copies[:3]:
+        copy.wait()
 
     def one(z, _):
         label = labels[z]
@@ -451,6 +480,7 @@
         return 0
 
     lax.fori_loop(0, BRICK, one, 0, unroll=4)
+    copies[3].wait()
     thin = INTERSECTION
     pairs = BRICK // 2
 
@@ -632,31 +662,45 @@
     write_messages(pos_ref, solved, FOLD, counts, outs_y, outs_z, outs_yz)
 
 
-def edge_kernel(width, height, counts, sizes, pos_ref, solved, *refs):
+NINTH = WIDE
+THIRD = NINTH + -(-WIDE // 8)
+
+
+def edge_kernel(width, counts, sizes, pos_ref, solved, *refs):
     extra = 1 if width == FOLD else 0
-    ins_y, ins_z, ins_yz, modulus, outs_x = groups_of(refs, sizes[:3] + (extra, sizes[3]))
+    ins_y, ins_z, ins_yz, modulus, outs_x, scratch = groups_of(
+        refs, sizes[:3] + (extra, sizes[3], extra)
+    )
     rows = solved.shape[1]
+    height = 16 if extra else 8
     _, region = spots((PAD, LANES))
     third = WIDE // 3
     for phase, out in enumerate(outs_x):
         up, _ = side(pos_ref, 2, phase, counts[0])
         window = pl.ds(pl.multiple_of(pick(up, rows - height, 0), 8), height)
 
-        def put(plane, value, out=out):
-            out[plane] = value
-
-        def get(plane, out=out):
-            return out[plane]
+        found = scratch[0] if extra else out
+
+        def put(plane, value, found=found):
+            found[plane] = value
+
+        def get(plane, found=found):
+            return found[plane]
 
         add_messages(pos_ref, solved, width, counts, ins_y, ins_z, ins_yz, window, put, get)
+        if extra:
+            for z in range(WIDE):
+                outer = found[z]
+                out[z] = jnp.where(up, outer[8:], outer[:8])
+                ninth = jnp.where(up, outer[7:8], outer[8:9])
+                out[NINTH + z // 8, z % 8 : z % 8 + 1, :] = ninth
         for ref in modulus:
             place = pl.ds(pl.multiple_of(pick(up, ref.shape[1] - 2 * PAD, PAD), PAD), PAD)
             for k in range(third):
                 total = ref[k, place, :]
                 for c in (1, 2):
                     total = jnp.where(region == c, ref[k + c * third, place, :], total)
-                row = k % 2 * PAD
-                out[WIDE + k // 2, row : row + PAD, :] = total
+                out[THIRD + k] = total
 
 
 def fold_kernel(width, counts, sizes, pos_ref, solved, *refs):
@@ -690,7 +734,7 @@
         (mid,),
     ) = groups_of(refs, (sizes[3], sizes[3], 10, 3) + sizes[:3] + (1,))
     rows = partial.shape[1]
-    complete(pos_ref, counts, partial, ins_x, 16, field, 0)
+    complete(pos_ref, counts, partial, ins_x, True, field, 0)
     inside, low_z, high_z = grid_masks(pos_ref, rows, counts)
     before = patched(pos_ref, counts, residual, ins_load)
 
@@ -709,7 +753,7 @@
     )
     rows = partial.shape[1]
     first = planes_of(REACH)[0]
-    complete(pos_ref, counts, partial, ins_x, 8, field, first)
+    complete(pos_ref, counts, partial, ins_x, False, field, first)
     core = slice(PAD, rows - PAD)
 
     def store(z, product):
@@ -731,19 +775,21 @@
     )
 
 
-def call(kernel, inputs, outs, scratch=(), smem=1, limit=24, work=0):
+def call(kernel, inputs, outs, scratch=(), distant=0, limit=24, work=0):
     return pl.pallas_call(
         kernel,
         out_shape=[jax.ShapeDtypeStruct(shape, F32) for shape in outs],
-        in_specs=[SMEM] * smem + [VMEM] * (len(inputs) - smem),
+        in_specs=[SMEM] + [HBM] * distant + [VMEM] * (len(inputs) - 1 - distant),
         out_specs=[VMEM] * len(outs),
-        scratch_shapes=[pltpu.VMEM(shape, F32) for shape in scratch],
+        scratch_shapes=[
+            pltpu.VMEM(shape, F32) if isinstance(shape, tuple) else shape for shape in scratch
+        ],
         compiler_params=pltpu.CompilerParams(vmem_limit_bytes=limit * 1024 * 1024),
         cost_estimate=pl.CostEstimate(flops=work, bytes_accessed=work, transcendentals=0),
     )(*inputs)
 
 
-def local(load, labels, mask, table):
+def local(mesh, load, labels, mask, table):
     columns = load.shape[3]
     rows = columns + 2 * PAD
     counts = tuple(lax.axis_size(axis) for axis in ("gx", "gy", "gz"))
@@ -755,23 +801,23 @@
 
     def exchange_yz(values):
         y, z, yz = groups_of(values, sizes[:3])
-        z = [swap(value, "gz", phase) for phase, value in enumerate(z)]
-        y = [swap(value, "gy", phase) for phase, value in enumerate(y)]
+        z = [swap(value, mesh, {"gz": phase}, None) for phase, value in enumerate(z)]
+        y = [swap(value, mesh, {"gy": phase}, None) for phase, value in enumerate(y)]
         yz = [
-            swap_both(value, "gy", number // ways[2], "gz", number % ways[2])
+            swap(value, mesh, {"gy": number // ways[2], "gz": number % ways[2]}, None)
             for number, value in enumerate(yz)
         ]
         return [*y, *z, *yz]
 
     def exchange_x(values):
-        return [swap(value, "gx", phase) for phase, value in enumerate(values)]
+        return [swap(value, mesh, {"gx": phase}, None) for phase, value in enumerate(values)]
 
     def message_shapes(width, height):
         groups = WIDE // width
         return (
             [(LENGTH // groups, height, LANES)] * sizes[0]
             + [(width, height, LANES)] * sizes[1]
-            + [(-(-width // groups), height, LANES)] * sizes[2]
+            + [(-(-3 * width // (LANES // width)), height, LANES)] * sizes[2]
         )
 
     bind = lambda kernel, *first: functools.partial(kernel, *first, counts, sizes)
@@ -788,7 +834,15 @@
         + [(2 * BRICK + BRICK // 8, 8, columns)] * sizes[0]
         + [(3 * INTERSECTION + REACH, BRICK, columns)] * sizes[1]
         + [(6 + REACH, 8, columns)] * sizes[2],
-        smem=2,
+        [
+            pltpu.SMEM(table.shape, F32),
+            pltpu.VMEM(labels.shape, jnp.int32),
+            pltpu.VMEM(mask.shape, jnp.int32),
+            pltpu.VMEM(load.shape, F32),
+            pltpu.SemaphoreType.DMA((4,)),
+        ],
+        distant=4,
+        limit=61,
     )
     margins = exchange_yz(out)
     residual, *out = call(
@@ -814,9 +868,10 @@
     margins = exchange_yz(out)
     first_edges = exchange_x(
         call(
-            bind(edge_kernel, FOLD, 16),
+            bind(edge_kernel, FOLD),
             [pos, solved, *margins, modulus],
-            [(WIDE + WIDE // 6, 16, LANES)] * sizes[3],
+            [(THIRD + WIDE // 3, 8, LANES)] * sizes[3],
+            [(WIDE, 16, LANES)],
         )
     )
     (partial,) = call(
@@ -832,7 +887,7 @@
     margins = exchange_yz(out)
     edges = exchange_x(
         call(
-            bind(edge_kernel, REACH, 8), [pos, solved, *margins], [(near, 8, LANES)] * sizes[3]
+            bind(edge_kernel, REACH), [pos, solved, *margins], [(near, 8, LANES)] * sizes[3]
         )
     )
     (partial,) = call(
@@ -851,7 +906,7 @@
 def solution(mesh):
     placed = (P(None, "gz", "gy", "gx"), P("gz", "gy", "gx"), P("gz", "gy", "gx"), P())
     return jax.shard_map(
-        local,
+        functools.partial(local, mesh),
         mesh=mesh,
         in_specs=placed,
         out_specs=(P(None, "gz", "gy", "gx"), P(None, "gz", "gy", "gx")),

time: 119 us -> 115 us (0.966)
  waiting for transfers between devices: 28.9 us -> 23.5 us
  Pallas kernels: 48 us -> 52.2 us
  local copies, waits for them, and re-layouts: 4.21 us -> 0.69 us
    ppermute x21, waiting for transfers between devices: 28.9 us -> 23.5 us  [the longest x6 15.8 us: swap(): return lax.ppermute(value, names, pairs)]
    pallas_call x10, Pallas kernels: 48 us -> 52.2 us  [call(): pl.pallas_call(kernel, out_shape=[jax.ShapeDtypeStruct(shape, F32) for sh...]
    unnamed x30 -> x28, local copies, waits for them, and re-layouts: 4.21 us -> 0.69 us
  transfers between devices with their start and end apart: 21 -> 21, of which waited for: 10 -> 10; matrix products, arithmetic and copies ran while one was open for 0% -> 0% of each run, Pallas kernels for 4% -> 5%
where the time goes in v4:
time: 115 us; the launch traced here: 114 us
  Pallas kernels  52.2 us (45%)
  starting transfers between devices  36.5 us (32%)
  waiting for transfers between devices  23.5 us (20%)
    pallas_call x10, Pallas kernels, call(): pl.pallas_call(kernel, out_shape=[jax.ShapeDtypeStruct(shape, F32) for sh...  52.2 us
    ppermute x15, starting transfers between devices, swap(): return lax.ppermute(value, name, list(enumerate(other)))  27.6 us
    ppermute x6, waiting for transfers between devices, swap(): return lax.ppermute(value, names, pairs)  15.8 us
    ppermute x6, starting transfers between devices, swap(): return lax.ppermute(value, names, pairs)  8.85 us
    ppermute x15, waiting for transfers between devices, swap(): return lax.ppermute(value, name, list(enumerate(other)))  7.67 us
  transfers between devices with their start and end apart: 21, of which 10 were waited for; matrix products, arithmetic and copies ran while one was open for 0% of the time, Pallas kernels for 5%

profile of v4, /device:TPU:9, one launch (start us, length us, event | category | flops | bytes accessed | tf_op | source)
XLA Modules:
  0.0 114.5 jit_solution(1761725062329627026)
XLA Ops:
  1.4 3.8 %shard_map.149 = (f32[32,32,128]{2,1,0:T(8,128)}, f32[68,8,128]{2,1,0:T(8,128)}, f32[17,32,128]{2,1,0:T(8,128)}, f32[17,32,128]{2,1,0:T(8,128)}, f32[11,8,128]{2,1,0:T(8,128)}, /*index=5*/f32[11,8,128]{2,1,0:T(8,128)}) custom-call(s32[3]{0:T(128)} %pad_add_fusion.pos_ref, f32[16]{0:T(128)} %table_in.1, f32[3,32,32,128]{3,2,1,0:T(8,128)} %load.1, ...), custom_call_target="tpu_custom_call" | custom-call | tf_op jit(solution)/shard_map/pallas_call | solution.py:779
  5.2 1.3 %collective-permute-start = (f32[68,8,128]{2,1,0:T(8,128)}, f32[68,8,128]{2,1,0:T(8,128)S(1)}, u32[]{:S(2)}, u32[]{:S(2)}) collective-permute-start(f32[68,8,128]{2,1,0:T(8,128)} %get-tuple-element.29), channel_id=1, source_target_pairs={{0,4},{4,0},{1,5},{5,1},{2,6},{6,2},{3,7},{7,3},{8,12},{12,8},{9,1... | collective-permute-start | bytes 835592 | tf_op jit(solution)/shard_map/ppermute | solution.py:131
  6.6 4.3 %collective-permute-start.2 = (f32[17,32,128]{2,1,0:T(8,128)}, f32[17,32,128]{2,1,0:T(8,128)S(1)}, u32[]{:S(2)}, u32[]{:S(2)}) collective-permute-start(f32[17,32,128]{2,1,0:T(8,128)} %get-tuple-element.31), channel_id=1, source_target_pairs={{0,0},{1,2},{2,1},{3,3},{4,4},{5,6},{6,5},{7,7},{8,8},{9,10},{10,9... | collective-permute-start | bytes 835592 | tf_op jit(solution)/shard_map/ppermute | solution.py:131
  11.0 2.6 %collective-permute-start.4 = (f32[11,8,128]{2,1,0:T(8,128)}, f32[11,8,128]{2,1,0:T(8,128)S(1)}, u32[]{:S(2)}, u32[]{:S(2)}) collective-permute-start(f32[11,8,128]{2,1,0:T(8,128)} %get-tuple-element.33), channel_id=1, source_target_pairs={{0,0},{1,6},{2,5},{3,3},{4,4},{5,2},{6,1},{7,7},{8,8},{9,14},{10,1... | collective-permute-start | bytes 135176 | tf_op jit(solution)/shard_map/ppermute | solution.py:132
  13.6 1.9 %collective-permute-done.3.refs_3_ = f32[11,8,128]{2,1,0:T(8,128)S(1)} collective-permute-done((f32[11,8,128]{2,1,0:T(8,128)}, f32[11,8,128]{2,1,0:T(8,128)S(1)}, u32[]{:S(2)}, u32[]{:S(2)}) %collective-permute-start.3) | collective-permute-done | bytes 45088 | tf_op jit(solution)/shard_map/ppermute | solution.py:132
  15.5 2.0 %collective-permute-done.4.refs_4_ = f32[11,8,128]{2,1,0:T(8,128)S(1)} collective-permute-done((f32[11,8,128]{2,1,0:T(8,128)}, f32[11,8,128]{2,1,0:T(8,128)S(1)}, u32[]{:S(2)}, u32[]{:S(2)}) %collective-permute-start.4) | collective-permute-done | bytes 45088 | tf_op jit(solution)/shard_map/ppermute | solution.py:132
  18.1 2.1 %shard_map.150 = (f32[40,144,128]{2,1,0:T(8,128)S(1)}, f32[40,8,128]{2,1,0:T(8,128)S(1)}, f32[40,8,128]{2,1,0:T(8,128)S(1)}) custom-call(s32[3]{0:T(128)S(1)} %copy-done.12, f32[3,32,32,128]{3,2,1,0:T(8,128)S(1)} %copy-done, f32[68,8,128]{2,1,0:T(8,128)S(1)} %collective-permute-done.refs_0_, f32[17,32,128]{2,1,0:T(8,128)S(1)} %collective-permute-done.1.refs_1_, ...), custom_call_target="tpu_custom_call" | custom-call | tf_op jit(solution)/shard_map/pallas_call | solution.py:779
  20.3 2.2 %collective-permute-start.5 = (f32[40,8,128]{2,1,0:T(8,128)S(1)}, f32[40,8,128]{2,1,0:T(8,128)S(1)}, u32[]{:S(2)}, u32[]{:S(2)}) collective-permute-start(f32[40,8,128]{2,1,0:T(8,128)S(1)} %get-tuple-element.35), channel_id=1, source_target_pairs={{0,8},{8,0},{16,24},{24,16},{1,9},{9,1},{17,25},{25,17},{2,10},{10... | collective-permute-start | bytes 491528 | tf_op jit(solution)/shard_map/ppermute | solution.py:131
  22.5 3.1 %collective-permute-start.6 = (f32[40,8,128]{2,1,0:T(8,128)S(1)}, f32[40,8,128]{2,1,0:T(8,128)S(1)}, u32[]{:S(2)}, u32[]{:S(2)}) collective-permute-start(f32[40,8,128]{2,1,0:T(8,128)S(1)} %get-tuple-element.36), channel_id=1, source_target_pairs={{0,0},{8,16},{16,8},{24,24},{1,1},{9,17},{17,9},{25,25},{2,2},{10,... | collective-permute-start | bytes 491528 | tf_op jit(solution)/shard_map/ppermute | solution.py:131
  25.7 3.5 %collective-permute-done.6.refs_1_ = f32[40,8,128]{2,1,0:T(8,128)S(1)} collective-permute-done((f32[40,8,128]{2,1,0:T(8,128)S(1)}, f32[40,8,128]{2,1,0:T(8,128)S(1)}, u32[]{:S(2)}, u32[]{:S(2)}) %collective-permute-start.6) | collective-permute-done | bytes 163872 | tf_op jit(solution)/shard_map/ppermute | solution.py:131
  29.2 12.4 %shard_map.151 = (f32[40,136,128]{2,1,0:T(8,128)S(1)}, f32[10,136,128]{2,1,0:T(8,128)S(1)}, f32[9,136,128]{2,1,0:T(8,128)S(1)}, f32[9,136,128]{2,1,0:T(8,128)S(1...) custom-call(s32[3]{0:T(128)S(1)} %copy-done.12, f32[40,144,128]{2,1,0:T(8,128)S(1)} %get-tuple-element.34.residual, ...), custom_call_target="tpu_custom_call" | custom-call | tf_op jit(solution)/shard_map/pallas_call | solution.py:779
  41.7 1.3 %collective-permute-start.7 = (f32[10,136,128]{2,1,0:T(8,128)S(1)}, f32[10,136,128]{2,1,0:T(8,128)S(1)}, u32[]{:S(2)}, u32[]{:S(2)}) collective-permute-start(f32[10,136,128]{2,1,0:T(8,128)S(1)} %get-tuple-element.38), channel_id=1, source_target_pairs={{0,4},{4,0},{1,5},{5,1},{2,6},{6,2},{3,7},{7,3},{8,12},{12,8},{9,1... | collective-permute-start | bytes 2088968 | tf_op jit(solution)/shard_map/ppermute | solution.py:131
  43.0 3.4 %collective-permute-start.9 = (f32[9,136,128]{2,1,0:T(8,128)S(1)}, f32[9,136,128]{2,1,0:T(8,128)S(1)}, u32[]{:S(2)}, u32[]{:S(2)}) collective-permute-start(f32[9,136,128]{2,1,0:T(8,128)S(1)} %get-tuple-element.40), channel_id=1, source_target_pairs={{0,0},{1,2},{2,1},{3,3},{4,4},{5,6},{6,5},{7,7},{8,8},{9,10},{10,9... | collective-permute-start | bytes 1880072 | tf_op jit(solution)/shard_map/ppermute | solution.py:131
  46.4 3.0 %collective-permute-start.11 = (f32[2,136,128]{2,1,0:T(8,128)S(1)}, f32[2,136,128]{2,1,0:T(8,128)S(1)}, u32[]{:S(2)}, u32[]{:S(2)}) collective-permute-start(f32[2,136,128]{2,1,0:T(8,128)S(1)} %get-tuple-element.42), channel_id=1, source_target_pairs={{0,0},{1,6},{2,5},{3,3},{4,4},{5,2},{6,1},{7,7},{8,8},{9,14},{10,1... | collective-permute-start | bytes 417800 | tf_op jit(solution)/shard_map/ppermute | solution.py:132
  49.5 1.4 %shard_map.153.refs_5_.modulus = f32[42,144,128]{2,1,0:T(8,128)S(1)} custom-call(s32[3]{0:T(128)S(1)} %copy-done.13, f32[32,32,128]{2,1,0:T(8,128)S(1)} %copy-done.10, f32[68,8,128]{2,1,0:T(8,128)S(1)} %collective-permute-done.refs_0_, f32[17,32,128]{2,1,0:T(8,128)S(1)} %collective-permute-done.1.refs_1_, f32[17,32,128]{2,1,0:T(8,128)S(1)} %collective-permute-done.2.refs_2_, ...), custom_call_target="tpu_custom_call" | custom-call | flops 8000000 | bytes 8000000 | tf_op jit(solution)/shard_map/pallas_call | solution.py:779
  50.9 6.5 %collective-permute-done.10.refs_3_ = f32[2,136,128]{2,1,0:T(8,128)S(1)} collective-permute-done((f32[2,136,128]{2,1,0:T(8,128)S(1)}, f32[2,136,128]{2,1,0:T(8,128)S(1)}, u32[]{:S(2)}, u32[]{:S(2)}) %collective-permute-start.10) | collective-permute-done | bytes 139296 | tf_op jit(solution)/shard_map/ppermute | solution.py:132
  57.4 1.8 %collective-permute-done.11.refs_4_ = f32[2,136,128]{2,1,0:T(8,128)S(1)} collective-permute-done((f32[2,136,128]{2,1,0:T(8,128)S(1)}, f32[2,136,128]{2,1,0:T(8,128)S(1)}, u32[]{:S(2)}, u32[]{:S(2)}) %collective-permute-start.11) | collective-permute-done | bytes 139296 | tf_op jit(solution)/shard_map/ppermute | solution.py:132
  59.2 1.1 collective-permute-done.7.refs_0_
  60.3 1.1 shard_map.154
  61.4 3.0 %collective-permute-start.13 = (f32[62,8,128]{2,1,0:T(8,128)S(1)}, f32[62,8,128]{2,1,0:T(8,128)S(1)}, u32[]{:S(2)}, u32[]{:S(2)}) collective-permute-start(f32[62,8,128]{2,1,0:T(8,128)S(1)} %get-tuple-element.45), channel_id=1, source_target_pairs={{0,0},{8,16},{16,8},{24,24},{1,1},{9,17},{17,9},{25,25},{2,2},{10,... | collective-permute-start | bytes 761864 | tf_op jit(solution)/shard_map/ppermute | solution.py:131
  64.5 2.3 %shard_map.152.partial = f32[42,144,128]{2,1,0:T(8,128)S(1)} custom-call(s32[3]{0:T(128)S(1)} %copy-done.13, f32[40,136,128]{2,1,0:T(8,128)S(1)} %get-tuple-element.37.solved, f32[10,136,128]{2,1,0:T(8,128)S(1)} %collective-permute-done.7.refs_0_, f32[9,136,128]{2,1,0:T(8,128)S(1)} %collective-permute-done.8.refs_1_, ...), custom_call_target="tpu_custom_call" | custom-call | flops 8000000 | bytes 8000000 | tf_op jit(solution)/shard_map/pallas_call | solution.py:779
  66.8 2.2 %collective-permute-done.13.refs_3_ = f32[62,8,128]{2,1,0:T(8,128)S(1)} collective-permute-done((f32[62,8,128]{2,1,0:T(8,128)S(1)}, f32[62,8,128]{2,1,0:T(8,128)S(1)}, u32[]{:S(2)}, u32[]{:S(2)}) %collective-permute-start.13) | collective-permute-done | bytes 253984 | tf_op jit(solution)/shard_map/ppermute | solution.py:131
  69.0 17.6 %shard_map.155 = (f32[40,136,128]{2,1,0:T(8,128)S(1)}, f32[42,144,128]{2,1,0:T(8,128)S(1)}, f32[40,144,128]{2,1,0:T(8,128)S(1)}, f32[5,136,128]{2,1,0:T(8,128)S(...) custom-call(s32[3]{0:T(128)S(1)} %copy-done.13, ...), custom_call_target="tpu_custom_call" | custom-call | tf_op jit(solution)/shard_map/pallas_call | solution.py:779
  86.7 1.3 %collective-permute-start.14 = (f32[5,136,128]{2,1,0:T(8,128)S(1)}, f32[5,136,128]{2,1,0:T(8,128)S(1)}, u32[]{:S(2)}, u32[]{:S(2)}) collective-permute-start(f32[5,136,128]{2,1,0:T(8,128)S(1)} %get-tuple-element.47), channel_id=1, source_target_pairs={{0,4},{4,0},{1,5},{5,1},{2,6},{6,2},{3,7},{7,3},{8,12},{12,8},{9,1... | collective-permute-start | bytes 1044488 | tf_op jit(solution)/shard_map/ppermute | solution.py:131
  88.0 3.4 %collective-permute-start.16 = (f32[5,136,128]{2,1,0:T(8,128)S(1)}, f32[5,136,128]{2,1,0:T(8,128)S(1)}, u32[]{:S(2)}, u32[]{:S(2)}) collective-permute-start(f32[5,136,128]{2,1,0:T(8,128)S(1)} %get-tuple-element.49), channel_id=1, source_target_pairs={{0,0},{1,2},{2,1},{3,3},{4,4},{5,6},{6,5},{7,7},{8,8},{9,10},{10,9... | collective-permute-start | bytes 1044488 | tf_op jit(solution)/shard_map/ppermute | solution.py:131
  91.4 3.0 %collective-permute-start.18 = (f32[1,136,128]{2,1,0:T(8,128)S(1)}, f32[1,136,128]{2,1,0:T(8,128)S(1)}, u32[]{:S(2)}, u32[]{:S(2)}) collective-permute-start(f32[1,136,128]{2,1,0:T(8,128)S(1)} %get-tuple-element.51), channel_id=1, source_target_pairs={{0,0},{1,6},{2,5},{3,3},{4,4},{5,2},{6,1},{7,7},{8,8},{9,14},{10,1... | collective-permute-start | bytes 208904 | tf_op jit(solution)/shard_map/ppermute | solution.py:132
  94.4 1.7 %collective-permute-done.17.refs_3_ = f32[1,136,128]{2,1,0:T(8,128)S(1)} collective-permute-done((f32[1,136,128]{2,1,0:T(8,128)S(1)}, f32[1,136,128]{2,1,0:T(8,128)S(1)}, u32[]{:S(2)}, u32[]{:S(2)}) %collective-permute-start.17) | collective-permute-done | bytes 69664 | tf_op jit(solution)/shard_map/ppermute | solution.py:132
  96.1 1.9 %collective-permute-done.18.refs_4_ = f32[1,136,128]{2,1,0:T(8,128)S(1)} collective-permute-done((f32[1,136,128]{2,1,0:T(8,128)S(1)}, f32[1,136,128]{2,1,0:T(8,128)S(1)}, u32[]{:S(2)}, u32[]{:S(2)}) %collective-permute-start.18) | collective-permute-done | bytes 69664 | tf_op jit(solution)/shard_map/ppermute | solution.py:132
  98.9 3.9 %collective-permute-start.20 = (f32[34,8,128]{2,1,0:T(8,128)S(1)}, f32[34,8,128]{2,1,0:T(8,128)S(1)}, u32[]{:S(2)}, u32[]{:S(2)}) collective-permute-start(f32[34,8,128]{2,1,0:T(8,128)S(1)} %get-tuple-element.55), channel_id=1, source_target_pairs={{0,0},{8,16},{16,8},{24,24},{1,1},{9,17},{17,9},{25,25},{2,2},{10,... | collective-permute-start | bytes 417800 | tf_op jit(solution)/shard_map/ppermute | solution.py:131
  102.8 1.8 %shard_map.156.partial = f32[34,144,128]{2,1,0:T(8,128)S(1)} custom-call(s32[3]{0:T(128)S(1)} %copy-done.13, f32[40,136,128]{2,1,0:T(8,128)S(1)} %get-tuple-element.46.solved, f32[5,136,128]{2,1,0:T(8,128)S(1)} %collective-permute-done.14.refs_0_, f32[5,136,128]{2,1,0:T(8,128)S(1)} %collective-permute-done.15.refs_1_, ...), custom_call_target="tpu_custom_call" | custom-call | flops 8000000 | bytes 8000000 | tf_op jit(solution)/shard_map/pallas_call | solution.py:779
  104.6 0.9 collective-permute-done.20.refs_1_
  105.5 8.9 %shard_map.158 = (f32[3,32,32,128]{3,2,1,0:T(8,128)}, f32[3,32,32,128]{3,2,1,0:T(8,128)}) custom-call(s32[3]{0:T(128)S(1)} %copy-done.13, f32[34,144,128]{2,1,0:T(8,128)S(1)} %shard_map.156.partial, f32[42,144,128]{2,1,0:T(8,128)S(1)} %shard_map.153.refs_5_.modulus, f32[42,144,128]{2,1,0:T(8,128)S(1)} %get-tuple-element.52.moved, ...), custom_call_target="tpu_custom_call" | custom-call | tf_op jit(solution)/shard_map/pallas_call | solution.py:779
  (49 shorter events, 2.6 us)
Async XLA Ops:
  0.6 28.5 %copy-start.1 = (f32[40,8,128]{2,1,0:T(8,128)S(1)}, f32[40,8,128]{2,1,0:T(8,128)}, u32[]{:S(2)}) copy-start(f32[40,8,128]{2,1,0:T(8,128)} %constant.41.clone.refs_11_.refs_13_) | copy-start | bytes 491524
  0.6 28.5 %copy-start.11 = (f32[160,128]{1,0:T(8,128)S(1)}, f32[160,128]{1,0:T(8,128)}, u32[]{:S(2)}) copy-start(f32[160,128]{1,0:T(8,128)} %constant.40.clone.refs_10_.refs_12_) | copy-start | bytes 245764
  0.7 28.5 %copy-start.2 = (bf16[160,480]{1,0:T(8,128)(2,1)S(1)}, bf16[160,480]{1,0:T(8,128)(2,1)}, u32[]{:S(2)}) copy-start(bf16[160,480]{1,0:T(8,128)(2,1)} %constant.37.clone.refs_7_.refs_9_) | copy-start | bytes 460804
  0.7 28.5 %copy-start.3 = (bf16[160,480]{1,0:T(8,128)(2,1)S(1)}, bf16[160,480]{1,0:T(8,128)(2,1)}, u32[]{:S(2)}) copy-start(bf16[160,480]{1,0:T(8,128)(2,1)} %constant.36.clone.refs_6_.refs_8_) | copy-start | bytes 460804
  0.7 28.5 %copy-start.4 = (bf16[160,480]{1,0:T(8,128)(2,1)S(1)}, bf16[160,480]{1,0:T(8,128)(2,1)}, u32[]{:S(2)}) copy-start(bf16[160,480]{1,0:T(8,128)(2,1)} %constant.35.clone.refs_5_.refs_7_) | copy-start | bytes 460804
  0.7 28.5 %copy-start.5 = (bf16[160,480]{1,0:T(8,128)(2,1)S(1)}, bf16[160,480]{1,0:T(8,128)(2,1)}, u32[]{:S(2)}) copy-start(bf16[160,480]{1,0:T(8,128)(2,1)} %constant.34.clone.refs_4_.refs_6_) | copy-start | bytes 460804
  0.7 28.5 %copy-start.6 = (bf16[160,432]{1,0:T(8,128)(2,1)S(1)}, bf16[160,432]{1,0:T(8,128)(2,1)}, u32[]{:S(2)}) copy-start(bf16[160,432]{1,0:T(8,128)(2,1)} %constant.33.clone.refs_3_.refs_5_) | copy-start | bytes 414724
  0.7 28.5 %copy-start.7 = (bf16[136,480]{1,0:T(8,128)(2,1)S(1)}, bf16[136,480]{1,0:T(8,128)(2,1)}, u32[]{:S(2)}) copy-start(bf16[136,480]{1,0:T(8,128)(2,1)} %constant.38.clone.refs_8_.refs_10_) | copy-start | bytes 391684
  0.7 28.5 %copy-start.8 = (bf16[256,256]{1,0:T(8,128)(2,1)S(1)}, bf16[256,256]{1,0:T(8,128)(2,1)}, u32[]{:S(2)}) copy-start(bf16[256,256]{1,0:T(8,128)(2,1)} %constant.39.clone.refs_9_.refs_11_) | copy-start | bytes 393220
  5.2 12.4 %collective-permute-start = (f32[68,8,128]{2,1,0:T(8,128)}, f32[68,8,128]{2,1,0:T(8,128)S(1)}, u32[]{:S(2)}, u32[]{:S(2)}) collective-permute-start(f32[68,8,128]{2,1,0:T(8,128)} %get-tuple-element.29), channel_id=1, source_target_pairs={{0,4},{4,0},{1,5},{5,1},{2,6},{6,2},{3,7},{7,3},{8,12},{12,8},{9,1... | collective-permute-start | bytes 835592 | tf_op jit(solution)/shard_map/ppermute | solution.py:131
  6.5 11.1 %collective-permute-start.1 = (f32[17,32,128]{2,1,0:T(8,128)}, f32[17,32,128]{2,1,0:T(8,128)S(1)}, u32[]{:S(2)}, u32[]{:S(2)}) collective-permute-start(f32[17,32,128]{2,1,0:T(8,128)} %get-tuple-element.30), channel_id=1, source_target_pairs={{0,1},{1,0},{2,3},{3,2},{4,5},{5,4},{6,7},{7,6},{8,9},{9,8},{10,11... | collective-permute-start | bytes 835592 | tf_op jit(solution)/shard_map/ppermute | solution.py:131
  6.6 10.9 %collective-permute-start.2 = (f32[17,32,128]{2,1,0:T(8,128)}, f32[17,32,128]{2,1,0:T(8,128)S(1)}, u32[]{:S(2)}, u32[]{:S(2)}) collective-permute-start(f32[17,32,128]{2,1,0:T(8,128)} %get-tuple-element.31), channel_id=1, source_target_pairs={{0,0},{1,2},{2,1},{3,3},{4,4},{5,6},{6,5},{7,7},{8,8},{9,10},{10,9... | collective-permute-start | bytes 835592 | tf_op jit(solution)/shard_map/ppermute | solution.py:131
  11.0 4.5 %collective-permute-start.3 = (f32[11,8,128]{2,1,0:T(8,128)}, f32[11,8,128]{2,1,0:T(8,128)S(1)}, u32[]{:S(2)}, u32[]{:S(2)}) collective-permute-start(f32[11,8,128]{2,1,0:T(8,128)} %get-tuple-element.32), channel_id=1, source_target_pairs={{0,5},{1,4},{2,7},{3,6},{4,1},{5,0},{6,3},{7,2},{8,13},{9,12},{10,... | collective-permute-start | bytes 135176 | tf_op jit(solution)/shard_map/ppermute | solution.py:132
  11.0 6.5 %collective-permute-start.4 = (f32[11,8,128]{2,1,0:T(8,128)}, f32[11,8,128]{2,1,0:T(8,128)S(1)}, u32[]{:S(2)}, u32[]{:S(2)}) collective-permute-start(f32[11,8,128]{2,1,0:T(8,128)} %get-tuple-element.33), channel_id=1, source_target_pairs={{0,0},{1,6},{2,5},{3,3},{4,4},{5,2},{6,1},{7,7},{8,8},{9,14},{10,1... | collective-permute-start | bytes 135176 | tf_op jit(solution)/shard_map/ppermute | solution.py:132
  20.3 29.2 %copy-start.10 = (f32[32,32,128]{2,1,0:T(8,128)S(1)}, f32[32,32,128]{2,1,0:T(8,128)}, u32[]{:S(2)}) copy-start(f32[32,32,128]{2,1,0:T(8,128)} %get-tuple-element.43.modulus) | copy-start | bytes 1572868
  20.3 29.2 %copy-start.13 = (s32[3]{0:T(128)S(1)}, s32[3]{0:T(128)}, u32[]{:S(2)}) copy-start(s32[3]{0:T(128)} %pad_add_fusion.pos_ref) | copy-start | bytes 40
  20.3 5.4 %collective-permute-start.5 = (f32[40,8,128]{2,1,0:T(8,128)S(1)}, f32[40,8,128]{2,1,0:T(8,128)S(1)}, u32[]{:S(2)}, u32[]{:S(2)}) collective-permute-start(f32[40,8,128]{2,1,0:T(8,128)S(1)} %get-tuple-element.35), channel_id=1, source_target_pairs={{0,8},{8,0},{16,24},{24,16},{1,9},{9,1},{17,25},{25,17},{2,10},{10... | collective-permute-start | bytes 491528 | tf_op jit(solution)/shard_map/ppermute | solution.py:131
  22.5 6.6 %collective-permute-start.6 = (f32[40,8,128]{2,1,0:T(8,128)S(1)}, f32[40,8,128]{2,1,0:T(8,128)S(1)}, u32[]{:S(2)}, u32[]{:S(2)}) collective-permute-start(f32[40,8,128]{2,1,0:T(8,128)S(1)} %get-tuple-element.36), channel_id=1, source_target_pairs={{0,0},{8,16},{16,8},{24,24},{1,1},{9,17},{17,9},{25,25},{2,2},{10,... | collective-permute-start | bytes 491528 | tf_op jit(solution)/shard_map/ppermute | solution.py:131
  41.7 18.6 %collective-permute-start.7 = (f32[10,136,128]{2,1,0:T(8,128)S(1)}, f32[10,136,128]{2,1,0:T(8,128)S(1)}, u32[]{:S(2)}, u32[]{:S(2)}) collective-permute-start(f32[10,136,128]{2,1,0:T(8,128)S(1)} %get-tuple-element.38), channel_id=1, source_target_pairs={{0,4},{4,0},{1,5},{5,1},{2,6},{6,2},{3,7},{7,3},{8,12},{12,8},{9,1... | collective-permute-start | bytes 2088968 | tf_op jit(solution)/shard_map/ppermute | solution.py:131
  43.0 16.2 %collective-permute-start.8 = (f32[9,136,128]{2,1,0:T(8,128)S(1)}, f32[9,136,128]{2,1,0:T(8,128)S(1)}, u32[]{:S(2)}, u32[]{:S(2)}) collective-permute-start(f32[9,136,128]{2,1,0:T(8,128)S(1)} %get-tuple-element.39), channel_id=1, source_target_pairs={{0,1},{1,0},{2,3},{3,2},{4,5},{5,4},{6,7},{7,6},{8,9},{9,8},{10,11... | collective-permute-start | bytes 1880072 | tf_op jit(solution)/shard_map/ppermute | solution.py:131
  43.0 16.2 %collective-permute-start.9 = (f32[9,136,128]{2,1,0:T(8,128)S(1)}, f32[9,136,128]{2,1,0:T(8,128)S(1)}, u32[]{:S(2)}, u32[]{:S(2)}) collective-permute-start(f32[9,136,128]{2,1,0:T(8,128)S(1)} %get-tuple-element.40), channel_id=1, source_target_pairs={{0,0},{1,2},{2,1},{3,3},{4,4},{5,6},{6,5},{7,7},{8,8},{9,10},{10,9... | collective-permute-start | bytes 1880072 | tf_op jit(solution)/shard_map/ppermute | solution.py:131
  46.3 11.0 %collective-permute-start.10 = (f32[2,136,128]{2,1,0:T(8,128)S(1)}, f32[2,136,128]{2,1,0:T(8,128)S(1)}, u32[]{:S(2)}, u32[]{:S(2)}) collective-permute-start(f32[2,136,128]{2,1,0:T(8,128)S(1)} %get-tuple-element.41), channel_id=1, source_target_pairs={{0,5},{1,4},{2,7},{3,6},{4,1},{5,0},{6,3},{7,2},{8,13},{9,12},{10,... | collective-permute-start | bytes 417800 | tf_op jit(solution)/shard_map/ppermute | solution.py:132
  46.4 12.8 %collective-permute-start.11 = (f32[2,136,128]{2,1,0:T(8,128)S(1)}, f32[2,136,128]{2,1,0:T(8,128)S(1)}, u32[]{:S(2)}, u32[]{:S(2)}) collective-permute-start(f32[2,136,128]{2,1,0:T(8,128)S(1)} %get-tuple-element.42), channel_id=1, source_target_pairs={{0,0},{1,6},{2,5},{3,3},{4,4},{5,2},{6,1},{7,7},{8,8},{9,14},{10,1... | collective-permute-start | bytes 417800 | tf_op jit(solution)/shard_map/ppermute | solution.py:132
  61.4 5.5 %collective-permute-start.12 = (f32[62,8,128]{2,1,0:T(8,128)S(1)}, f32[62,8,128]{2,1,0:T(8,128)S(1)}, u32[]{:S(2)}, u32[]{:S(2)}) collective-permute-start(f32[62,8,128]{2,1,0:T(8,128)S(1)} %get-tuple-element.44), channel_id=1, source_target_pairs={{0,8},{8,0},{16,24},{24,16},{1,9},{9,1},{17,25},{25,17},{2,10},{10... | collective-permute-start | bytes 761864 | tf_op jit(solution)/shard_map/ppermute | solution.py:131
  61.4 7.6 %collective-permute-start.13 = (f32[62,8,128]{2,1,0:T(8,128)S(1)}, f32[62,8,128]{2,1,0:T(8,128)S(1)}, u32[]{:S(2)}, u32[]{:S(2)}) collective-permute-start(f32[62,8,128]{2,1,0:T(8,128)S(1)} %get-tuple-element.45), channel_id=1, source_target_pairs={{0,0},{8,16},{16,8},{24,24},{1,1},{9,17},{17,9},{25,25},{2,2},{10,... | collective-permute-start | bytes 761864 | tf_op jit(solution)/shard_map/ppermute | solution.py:131
  86.7 11.4 %collective-permute-start.14 = (f32[5,136,128]{2,1,0:T(8,128)S(1)}, f32[5,136,128]{2,1,0:T(8,128)S(1)}, u32[]{:S(2)}, u32[]{:S(2)}) collective-permute-start(f32[5,136,128]{2,1,0:T(8,128)S(1)} %get-tuple-element.47), channel_id=1, source_target_pairs={{0,4},{4,0},{1,5},{5,1},{2,6},{6,2},{3,7},{7,3},{8,12},{12,8},{9,1... | collective-permute-start | bytes 1044488 | tf_op jit(solution)/shard_map/ppermute | solution.py:131
  88.0 10.1 %collective-permute-start.15 = (f32[5,136,128]{2,1,0:T(8,128)S(1)}, f32[5,136,128]{2,1,0:T(8,128)S(1)}, u32[]{:S(2)}, u32[]{:S(2)}) collective-permute-start(f32[5,136,128]{2,1,0:T(8,128)S(1)} %get-tuple-element.48), channel_id=1, source_target_pairs={{0,1},{1,0},{2,3},{3,2},{4,5},{5,4},{6,7},{7,6},{8,9},{9,8},{10,11... | collective-permute-start | bytes 1044488 | tf_op jit(solution)/shard_map/ppermute | solution.py:131
  88.0 10.1 %collective-permute-start.16 = (f32[5,136,128]{2,1,0:T(8,128)S(1)}, f32[5,136,128]{2,1,0:T(8,128)S(1)}, u32[]{:S(2)}, u32[]{:S(2)}) collective-permute-start(f32[5,136,128]{2,1,0:T(8,128)S(1)} %get-tuple-element.49), channel_id=1, source_target_pairs={{0,0},{1,2},{2,1},{3,3},{4,4},{5,6},{6,5},{7,7},{8,8},{9,10},{10,9... | collective-permute-start | bytes 1044488 | tf_op jit(solution)/shard_map/ppermute | solution.py:131
  91.3 4.8 %collective-permute-start.17 = (f32[1,136,128]{2,1,0:T(8,128)S(1)}, f32[1,136,128]{2,1,0:T(8,128)S(1)}, u32[]{:S(2)}, u32[]{:S(2)}) collective-permute-start(f32[1,136,128]{2,1,0:T(8,128)S(1)} %get-tuple-element.50), channel_id=1, source_target_pairs={{0,5},{1,4},{2,7},{3,6},{4,1},{5,0},{6,3},{7,2},{8,13},{9,12},{10,... | collective-permute-start | bytes 208904 | tf_op jit(solution)/shard_map/ppermute | solution.py:132
  91.4 6.6 %collective-permute-start.18 = (f32[1,136,128]{2,1,0:T(8,128)S(1)}, f32[1,136,128]{2,1,0:T(8,128)S(1)}, u32[]{:S(2)}, u32[]{:S(2)}) collective-permute-start(f32[1,136,128]{2,1,0:T(8,128)S(1)} %get-tuple-element.51), channel_id=1, source_target_pairs={{0,0},{1,6},{2,5},{3,3},{4,4},{5,2},{6,1},{7,7},{8,8},{9,14},{10,1... | collective-permute-start | bytes 208904 | tf_op jit(solution)/shard_map/ppermute | solution.py:132
  98.8 5.8 %collective-permute-start.19 = (f32[34,8,128]{2,1,0:T(8,128)S(1)}, f32[34,8,128]{2,1,0:T(8,128)S(1)}, u32[]{:S(2)}, u32[]{:S(2)}) collective-permute-start(f32[34,8,128]{2,1,0:T(8,128)S(1)} %get-tuple-element.54), channel_id=1, source_target_pairs={{0,8},{8,0},{16,24},{24,16},{1,9},{9,1},{17,25},{25,17},{2,10},{10... | collective-permute-start | bytes 417800 | tf_op jit(solution)/shard_map/ppermute | solution.py:131
  98.9 6.6 %collective-permute-start.20 = (f32[34,8,128]{2,1,0:T(8,128)S(1)}, f32[34,8,128]{2,1,0:T(8,128)S(1)}, u32[]{:S(2)}, u32[]{:S(2)}) collective-permute-start(f32[34,8,128]{2,1,0:T(8,128)S(1)} %get-tuple-element.55), channel_id=1, source_target_pairs={{0,0},{8,16},{16,8},{24,24},{1,1},{9,17},{17,9},{25,25},{2,2},{10,... | collective-permute-start | bytes 417800 | tf_op jit(solution)/shard_map/ppermute | solution.py:131
  (3 other events, 45.9 us)

commit v5 on v4

--- a/solution.py
+++ b/solution.py
@@ -799,18 +799,18 @@
     consts = [jnp.asarray(value) for value in tables(columns // BRICK)]
     spectral = (LENGTH, columns // BRICK * LENGTH, LANES)
 
-    def exchange_yz(values):
+    def exchange_yz(values, filler=None):
         y, z, yz = groups_of(values, sizes[:3])
-        z = [swap(value, mesh, {"gz": phase}, None) for phase, value in enumerate(z)]
+        z = [swap(value, mesh, {"gz": phase}, filler) for phase, value in enumerate(z)]
         y = [swap(value, mesh, {"gy": phase}, None) for phase, value in enumerate(y)]
         yz = [
-            swap(value, mesh, {"gy": number // ways[2], "gz": number % ways[2]}, None)
+            swap(value, mesh, {"gy": number // ways[2], "gz": number % ways[2]}, filler)
             for number, value in enumerate(yz)
         ]
         return [*y, *z, *yz]
 
-    def exchange_x(values):
-        return [swap(value, mesh, {"gx": phase}, None) for phase, value in enumerate(values)]
+    def exchange_x(values, filler=None):
+        return [swap(value, mesh, {"gx": phase}, filler) for phase, value in enumerate(values)]
 
     def message_shapes(width, height):
         groups = WIDE // width
@@ -844,7 +844,7 @@
         distant=4,
         limit=61,
     )
-    margins = exchange_yz(out)
+    margins = exchange_yz(out, "gx")
     residual, *out = call(
         bind(gather_kernel),
         [pos, load, *margins],
@@ -888,7 +888,8 @@
     edges = exchange_x(
         call(
             bind(edge_kernel, REACH), [pos, solved, *margins], [(near, 8, LANES)] * sizes[3]
-        )
+        ),
+        "gy",
     )
     (partial,) = call(
         bind(fold_kernel, REACH), [pos, solved, *margins], [(near, rows, LANES)], work=8000000

time: 115 us -> 111 us (0.965)
  starting transfers between devices: 36.5 us -> 32.1 us
    ppermute x15 -> x11, starting transfers between devices: 27.6 us -> 18.8 us  [swap(): return lax.ppermute(value, name, list(enumerate(other)))]
    ppermute x6 -> x10, starting transfers between devices: 8.85 us -> 13.2 us  [swap(): return lax.ppermute(value, names, pairs)]
    ppermute x6 -> x10, waiting for transfers between devices: 15.8 us -> 17.7 us  [swap(): return lax.ppermute(value, names, pairs)]
    ppermute x15 -> x11, waiting for transfers between devices: 7.67 us -> 6.74 us  [swap(): return lax.ppermute(value, name, list(enumerate(other)))]
where the time goes in v5:
time: 111 us
  Pallas kernels  52.2 us (47%)
  starting transfers between devices  32.1 us (29%)
  waiting for transfers between devices  24.4 us (22%)
    pallas_call x10, Pallas kernels, call(): pl.pallas_call(kernel, out_shape=[jax.ShapeDtypeStruct(shape, F32) for sh...  52.2 us
    ppermute x11, starting transfers between devices, swap(): return lax.ppermute(value, name, list(enumerate(other)))  18.8 us
    ppermute x10, waiting for transfers between devices, swap(): return lax.ppermute(value, names, pairs)  17.7 us
    ppermute x10, starting transfers between devices, swap(): return lax.ppermute(value, names, pairs)  13.2 us
    ppermute x11, waiting for transfers between devices, swap(): return lax.ppermute(value, name, list(enumerate(other)))  6.74 us
  transfers between devices with their start and end apart: 21, of which 10 were waited for; matrix products, arithmetic and copies ran while one was open for 0% of the time, Pallas kernels for 5%

profile of v5, /device:TPU:9, one launch (start us, length us, event | category | flops | bytes accessed | tf_op | source)
XLA Modules:
  0.0 111.0 jit_solution(18053463408684575851)
XLA Ops:
  1.4 3.8 %shard_map.149 = (f32[32,32,128]{2,1,0:T(8,128)}, f32[68,8,128]{2,1,0:T(8,128)}, f32[17,32,128]{2,1,0:T(8,128)}, f32[17,32,128]{2,1,0:T(8,128)}, f32[11,8,128]{2,1,0:T(8,128)}, /*index=5*/f32[11,8,128]{2,1,0:T(8,128)}) custom-call(s32[3]{0:T(128)} %pad_add_fusion.pos_ref, f32[16]{0:T(128)} %table_in.1, f32[3,32,32,128]{3,2,1,0:T(8,128)} %load.1, ...), custom_call_target="tpu_custom_call" | custom-call | tf_op jit(solution)/shard_map/pallas_call | solution.py:779
  5.2 1.3 %collective-permute-start = (f32[68,8,128]{2,1,0:T(8,128)}, f32[68,8,128]{2,1,0:T(8,128)S(1)}, u32[]{:S(2)}, u32[]{:S(2)}) collective-permute-start(f32[68,8,128]{2,1,0:T(8,128)} %get-tuple-element.29), channel_id=1, source_target_pairs={{0,4},{4,0},{1,5},{5,1},{2,6},{6,2},{3,7},{7,3},{8,12},{12,8},{9,1... | collective-permute-start | bytes 835592 | tf_op jit(solution)/shard_map/ppermute | solution.py:131
  6.6 2.4 %collective-permute-start.2 = (f32[17,32,128]{2,1,0:T(8,128)}, f32[17,32,128]{2,1,0:T(8,128)S(1)}, u32[]{:S(2)}, u32[]{:S(2)}) collective-permute-start(f32[17,32,128]{2,1,0:T(8,128)} %get-tuple-element.31), channel_id=1, source_target_pairs={{0,8},{1,2},{2,1},{3,11},{4,12},{5,6},{6,5},{7,15},{8,0},{9,10},{1... | collective-permute-start | bytes 835592 | tf_op jit(solution)/shard_map/ppermute | solution.py:132
  9.1 2.3 %collective-permute-start.4 = (f32[11,8,128]{2,1,0:T(8,128)}, f32[11,8,128]{2,1,0:T(8,128)S(1)}, u32[]{:S(2)}, u32[]{:S(2)}) collective-permute-start(f32[11,8,128]{2,1,0:T(8,128)} %get-tuple-element.33), channel_id=1, source_target_pairs={{0,8},{1,6},{2,5},{3,11},{4,12},{5,2},{6,1},{7,15},{8,0},{9,14},{1... | collective-permute-start | bytes 135176 | tf_op jit(solution)/shard_map/ppermute | solution.py:132
  11.4 3.1 %collective-permute-done.3.refs_3_ = f32[11,8,128]{2,1,0:T(8,128)S(1)} collective-permute-done((f32[11,8,128]{2,1,0:T(8,128)}, f32[11,8,128]{2,1,0:T(8,128)S(1)}, u32[]{:S(2)}, u32[]{:S(2)}) %collective-permute-start.3) | collective-permute-done | bytes 45088 | tf_op jit(solution)/shard_map/ppermute | solution.py:132
  14.5 1.4 %collective-permute-done.4.refs_4_ = f32[11,8,128]{2,1,0:T(8,128)S(1)} collective-permute-done((f32[11,8,128]{2,1,0:T(8,128)}, f32[11,8,128]{2,1,0:T(8,128)S(1)}, u32[]{:S(2)}, u32[]{:S(2)}) %collective-permute-start.4) | collective-permute-done | bytes 45088 | tf_op jit(solution)/shard_map/ppermute | solution.py:132
  16.5 2.1 %shard_map.150 = (f32[40,144,128]{2,1,0:T(8,128)S(1)}, f32[40,8,128]{2,1,0:T(8,128)S(1)}, f32[40,8,128]{2,1,0:T(8,128)S(1)}) custom-call(s32[3]{0:T(128)S(1)} %copy-done.12, f32[3,32,32,128]{3,2,1,0:T(8,128)S(1)} %copy-done, f32[68,8,128]{2,1,0:T(8,128)S(1)} %collective-permute-done.refs_0_, f32[17,32,128]{2,1,0:T(8,128)S(1)} %collective-permute-done.1.refs_1_, ...), custom_call_target="tpu_custom_call" | custom-call | tf_op jit(solution)/shard_map/pallas_call | solution.py:779
  18.7 1.9 %collective-permute-start.5 = (f32[40,8,128]{2,1,0:T(8,128)S(1)}, f32[40,8,128]{2,1,0:T(8,128)S(1)}, u32[]{:S(2)}, u32[]{:S(2)}) collective-permute-start(f32[40,8,128]{2,1,0:T(8,128)S(1)} %get-tuple-element.35), channel_id=1, source_target_pairs={{0,8},{8,0},{16,24},{24,16},{1,9},{9,1},{17,25},{25,17},{2,10},{10... | collective-permute-start | bytes 491528 | tf_op jit(solution)/shard_map/ppermute | solution.py:131
  20.6 3.1 %collective-permute-start.6 = (f32[40,8,128]{2,1,0:T(8,128)S(1)}, f32[40,8,128]{2,1,0:T(8,128)S(1)}, u32[]{:S(2)}, u32[]{:S(2)}) collective-permute-start(f32[40,8,128]{2,1,0:T(8,128)S(1)} %get-tuple-element.36), channel_id=1, source_target_pairs={{0,0},{8,16},{16,8},{24,24},{1,1},{9,17},{17,9},{25,25},{2,2},{10,... | collective-permute-start | bytes 491528 | tf_op jit(solution)/shard_map/ppermute | solution.py:131
  23.8 3.5 %collective-permute-done.6.refs_1_ = f32[40,8,128]{2,1,0:T(8,128)S(1)} collective-permute-done((f32[40,8,128]{2,1,0:T(8,128)S(1)}, f32[40,8,128]{2,1,0:T(8,128)S(1)}, u32[]{:S(2)}, u32[]{:S(2)}) %collective-permute-start.6) | collective-permute-done | bytes 163872 | tf_op jit(solution)/shard_map/ppermute | solution.py:131
  27.3 12.4 %shard_map.151 = (f32[40,136,128]{2,1,0:T(8,128)S(1)}, f32[10,136,128]{2,1,0:T(8,128)S(1)}, f32[9,136,128]{2,1,0:T(8,128)S(1)}, f32[9,136,128]{2,1,0:T(8,128)S(1...) custom-call(s32[3]{0:T(128)S(1)} %copy-done.12, f32[40,144,128]{2,1,0:T(8,128)S(1)} %get-tuple-element.34.residual, ...), custom_call_target="tpu_custom_call" | custom-call | tf_op jit(solution)/shard_map/pallas_call | solution.py:779
  39.8 1.3 %collective-permute-start.7 = (f32[10,136,128]{2,1,0:T(8,128)S(1)}, f32[10,136,128]{2,1,0:T(8,128)S(1)}, u32[]{:S(2)}, u32[]{:S(2)}) collective-permute-start(f32[10,136,128]{2,1,0:T(8,128)S(1)} %get-tuple-element.38), channel_id=1, source_target_pairs={{0,4},{4,0},{1,5},{5,1},{2,6},{6,2},{3,7},{7,3},{8,12},{12,8},{9,1... | collective-permute-start | bytes 2088968 | tf_op jit(solution)/shard_map/ppermute | solution.py:131
  41.1 3.4 %collective-permute-start.9 = (f32[9,136,128]{2,1,0:T(8,128)S(1)}, f32[9,136,128]{2,1,0:T(8,128)S(1)}, u32[]{:S(2)}, u32[]{:S(2)}) collective-permute-start(f32[9,136,128]{2,1,0:T(8,128)S(1)} %get-tuple-element.40), channel_id=1, source_target_pairs={{0,0},{1,2},{2,1},{3,3},{4,4},{5,6},{6,5},{7,7},{8,8},{9,10},{10,9... | collective-permute-start | bytes 1880072 | tf_op jit(solution)/shard_map/ppermute | solution.py:131
  44.5 3.0 %collective-permute-start.11 = (f32[2,136,128]{2,1,0:T(8,128)S(1)}, f32[2,136,128]{2,1,0:T(8,128)S(1)}, u32[]{:S(2)}, u32[]{:S(2)}) collective-permute-start(f32[2,136,128]{2,1,0:T(8,128)S(1)} %get-tuple-element.42), channel_id=1, source_target_pairs={{0,0},{1,6},{2,5},{3,3},{4,4},{5,2},{6,1},{7,7},{8,8},{9,14},{10,1... | collective-permute-start | bytes 417800 | tf_op jit(solution)/shard_map/ppermute | solution.py:132
  47.6 1.4 %shard_map.153.refs_5_.modulus = f32[42,144,128]{2,1,0:T(8,128)S(1)} custom-call(s32[3]{0:T(128)S(1)} %copy-done.13, f32[32,32,128]{2,1,0:T(8,128)S(1)} %copy-done.10, f32[68,8,128]{2,1,0:T(8,128)S(1)} %collective-permute-done.refs_0_, f32[17,32,128]{2,1,0:T(8,128)S(1)} %collective-permute-done.1.refs_1_, f32[17,32,128]{2,1,0:T(8,128)S(1)} %collective-permute-done.2.refs_2_, ...), custom_call_target="tpu_custom_call" | custom-call | flops 8000000 | bytes 8000000 | tf_op jit(solution)/shard_map/pallas_call | solution.py:779
  49.0 6.5 %collective-permute-done.10.refs_3_ = f32[2,136,128]{2,1,0:T(8,128)S(1)} collective-permute-done((f32[2,136,128]{2,1,0:T(8,128)S(1)}, f32[2,136,128]{2,1,0:T(8,128)S(1)}, u32[]{:S(2)}, u32[]{:S(2)}) %collective-permute-start.10) | collective-permute-done | bytes 139296 | tf_op jit(solution)/shard_map/ppermute | solution.py:132
  55.5 1.8 %collective-permute-done.11.refs_4_ = f32[2,136,128]{2,1,0:T(8,128)S(1)} collective-permute-done((f32[2,136,128]{2,1,0:T(8,128)S(1)}, f32[2,136,128]{2,1,0:T(8,128)S(1)}, u32[]{:S(2)}, u32[]{:S(2)}) %collective-permute-start.11) | collective-permute-done | bytes 139296 | tf_op jit(solution)/shard_map/ppermute | solution.py:132
  57.3 1.1 collective-permute-done.7.refs_0_
  58.4 1.1 shard_map.154
  59.5 3.0 %collective-permute-start.13 = (f32[62,8,128]{2,1,0:T(8,128)S(1)}, f32[62,8,128]{2,1,0:T(8,128)S(1)}, u32[]{:S(2)}, u32[]{:S(2)}) collective-permute-start(f32[62,8,128]{2,1,0:T(8,128)S(1)} %get-tuple-element.45), channel_id=1, source_target_pairs={{0,0},{8,16},{16,8},{24,24},{1,1},{9,17},{17,9},{25,25},{2,2},{10,... | collective-permute-start | bytes 761864 | tf_op jit(solution)/shard_map/ppermute | solution.py:131
  62.6 2.3 %shard_map.152.partial = f32[42,144,128]{2,1,0:T(8,128)S(1)} custom-call(s32[3]{0:T(128)S(1)} %copy-done.13, f32[40,136,128]{2,1,0:T(8,128)S(1)} %get-tuple-element.37.solved, f32[10,136,128]{2,1,0:T(8,128)S(1)} %collective-permute-done.7.refs_0_, f32[9,136,128]{2,1,0:T(8,128)S(1)} %collective-permute-done.8.refs_1_, ...), custom_call_target="tpu_custom_call" | custom-call | flops 8000000 | bytes 8000000 | tf_op jit(solution)/shard_map/pallas_call | solution.py:779
  64.9 2.2 %collective-permute-done.13.refs_3_ = f32[62,8,128]{2,1,0:T(8,128)S(1)} collective-permute-done((f32[62,8,128]{2,1,0:T(8,128)S(1)}, f32[62,8,128]{2,1,0:T(8,128)S(1)}, u32[]{:S(2)}, u32[]{:S(2)}) %collective-permute-start.13) | collective-permute-done | bytes 253984 | tf_op jit(solution)/shard_map/ppermute | solution.py:131
  67.1 17.6 %shard_map.155 = (f32[40,136,128]{2,1,0:T(8,128)S(1)}, f32[42,144,128]{2,1,0:T(8,128)S(1)}, f32[40,144,128]{2,1,0:T(8,128)S(1)}, f32[5,136,128]{2,1,0:T(8,128)S(...) custom-call(s32[3]{0:T(128)S(1)} %copy-done.13, ...), custom_call_target="tpu_custom_call" | custom-call | tf_op jit(solution)/shard_map/pallas_call | solution.py:779
  84.8 1.3 %collective-permute-start.14 = (f32[5,136,128]{2,1,0:T(8,128)S(1)}, f32[5,136,128]{2,1,0:T(8,128)S(1)}, u32[]{:S(2)}, u32[]{:S(2)}) collective-permute-start(f32[5,136,128]{2,1,0:T(8,128)S(1)} %get-tuple-element.47), channel_id=1, source_target_pairs={{0,4},{4,0},{1,5},{5,1},{2,6},{6,2},{3,7},{7,3},{8,12},{12,8},{9,1... | collective-permute-start | bytes 1044488 | tf_op jit(solution)/shard_map/ppermute | solution.py:131
  86.1 3.4 %collective-permute-start.16 = (f32[5,136,128]{2,1,0:T(8,128)S(1)}, f32[5,136,128]{2,1,0:T(8,128)S(1)}, u32[]{:S(2)}, u32[]{:S(2)}) collective-permute-start(f32[5,136,128]{2,1,0:T(8,128)S(1)} %get-tuple-element.49), channel_id=1, source_target_pairs={{0,0},{1,2},{2,1},{3,3},{4,4},{5,6},{6,5},{7,7},{8,8},{9,10},{10,9... | collective-permute-start | bytes 1044488 | tf_op jit(solution)/shard_map/ppermute | solution.py:131
  89.5 3.0 %collective-permute-start.18 = (f32[1,136,128]{2,1,0:T(8,128)S(1)}, f32[1,136,128]{2,1,0:T(8,128)S(1)}, u32[]{:S(2)}, u32[]{:S(2)}) collective-permute-start(f32[1,136,128]{2,1,0:T(8,128)S(1)} %get-tuple-element.51), channel_id=1, source_target_pairs={{0,0},{1,6},{2,5},{3,3},{4,4},{5,2},{6,1},{7,7},{8,8},{9,14},{10,1... | collective-permute-start | bytes 208904 | tf_op jit(solution)/shard_map/ppermute | solution.py:132
  92.6 1.7 %collective-permute-done.17.refs_3_ = f32[1,136,128]{2,1,0:T(8,128)S(1)} collective-permute-done((f32[1,136,128]{2,1,0:T(8,128)S(1)}, f32[1,136,128]{2,1,0:T(8,128)S(1)}, u32[]{:S(2)}, u32[]{:S(2)}) %collective-permute-start.17) | collective-permute-done | bytes 69664 | tf_op jit(solution)/shard_map/ppermute | solution.py:132
  94.3 1.9 %collective-permute-done.18.refs_4_ = f32[1,136,128]{2,1,0:T(8,128)S(1)} collective-permute-done((f32[1,136,128]{2,1,0:T(8,128)S(1)}, f32[1,136,128]{2,1,0:T(8,128)S(1)}, u32[]{:S(2)}, u32[]{:S(2)}) %collective-permute-start.18) | collective-permute-done | bytes 69664 | tf_op jit(solution)/shard_map/ppermute | solution.py:132
  97.0 2.1 %collective-permute-start.20 = (f32[34,8,128]{2,1,0:T(8,128)S(1)}, f32[34,8,128]{2,1,0:T(8,128)S(1)}, u32[]{:S(2)}, u32[]{:S(2)}) collective-permute-start(f32[34,8,128]{2,1,0:T(8,128)S(1)} %get-tuple-element.55), channel_id=1, source_target_pairs={{0,4},{1,5},{2,6},{3,7},{4,0},{5,1},{6,2},{7,3},{8,16},{9,17},{10,... | collective-permute-start | bytes 417800 | tf_op jit(solution)/shard_map/ppermute | solution.py:132
  99.1 1.8 %shard_map.156.partial = f32[34,144,128]{2,1,0:T(8,128)S(1)} custom-call(s32[3]{0:T(128)S(1)} %copy-done.13, f32[40,136,128]{2,1,0:T(8,128)S(1)} %get-tuple-element.46.solved, f32[5,136,128]{2,1,0:T(8,128)S(1)} %collective-permute-done.14.refs_0_, f32[5,136,128]{2,1,0:T(8,128)S(1)} %collective-permute-done.15.refs_1_, ...), custom_call_target="tpu_custom_call" | custom-call | flops 8000000 | bytes 8000000 | tf_op jit(solution)/shard_map/pallas_call | solution.py:779
  100.9 1.2 %collective-permute-done.20.refs_1_ = f32[34,8,128]{2,1,0:T(8,128)S(1)} collective-permute-done((f32[34,8,128]{2,1,0:T(8,128)S(1)}, f32[34,8,128]{2,1,0:T(8,128)S(1)}, u32[]{:S(2)}, u32[]{:S(2)}) %collective-permute-start.20) | collective-permute-done | bytes 139296 | tf_op jit(solution)/shard_map/ppermute | solution.py:132
  102.1 8.9 %shard_map.158 = (f32[3,32,32,128]{3,2,1,0:T(8,128)}, f32[3,32,32,128]{3,2,1,0:T(8,128)}) custom-call(s32[3]{0:T(128)S(1)} %copy-done.13, f32[34,144,128]{2,1,0:T(8,128)S(1)} %shard_map.156.partial, f32[42,144,128]{2,1,0:T(8,128)S(1)} %shard_map.153.refs_5_.modulus, f32[42,144,128]{2,1,0:T(8,128)S(1)} %get-tuple-element.52.moved, ...), custom_call_target="tpu_custom_call" | custom-call | tf_op jit(solution)/shard_map/pallas_call | solution.py:779
  (49 shorter events, 2.6 us)
Async XLA Ops:
  0.6 26.6 %copy-start.1 = (f32[40,8,128]{2,1,0:T(8,128)S(1)}, f32[40,8,128]{2,1,0:T(8,128)}, u32[]{:S(2)}) copy-start(f32[40,8,128]{2,1,0:T(8,128)} %constant.41.clone.refs_11_.refs_13_) | copy-start | bytes 491524
  0.6 26.6 %copy-start.11 = (f32[160,128]{1,0:T(8,128)S(1)}, f32[160,128]{1,0:T(8,128)}, u32[]{:S(2)}) copy-start(f32[160,128]{1,0:T(8,128)} %constant.40.clone.refs_10_.refs_12_) | copy-start | bytes 245764
  0.7 26.6 %copy-start.2 = (bf16[160,480]{1,0:T(8,128)(2,1)S(1)}, bf16[160,480]{1,0:T(8,128)(2,1)}, u32[]{:S(2)}) copy-start(bf16[160,480]{1,0:T(8,128)(2,1)} %constant.37.clone.refs_7_.refs_9_) | copy-start | bytes 460804
  0.7 26.6 %copy-start.3 = (bf16[160,480]{1,0:T(8,128)(2,1)S(1)}, bf16[160,480]{1,0:T(8,128)(2,1)}, u32[]{:S(2)}) copy-start(bf16[160,480]{1,0:T(8,128)(2,1)} %constant.36.clone.refs_6_.refs_8_) | copy-start | bytes 460804
  0.7 26.6 %copy-start.4 = (bf16[160,480]{1,0:T(8,128)(2,1)S(1)}, bf16[160,480]{1,0:T(8,128)(2,1)}, u32[]{:S(2)}) copy-start(bf16[160,480]{1,0:T(8,128)(2,1)} %constant.35.clone.refs_5_.refs_7_) | copy-start | bytes 460804
  0.7 26.6 %copy-start.5 = (bf16[160,480]{1,0:T(8,128)(2,1)S(1)}, bf16[160,480]{1,0:T(8,128)(2,1)}, u32[]{:S(2)}) copy-start(bf16[160,480]{1,0:T(8,128)(2,1)} %constant.34.clone.refs_4_.refs_6_) | copy-start | bytes 460804
  0.7 26.6 %copy-start.6 = (bf16[160,432]{1,0:T(8,128)(2,1)S(1)}, bf16[160,432]{1,0:T(8,128)(2,1)}, u32[]{:S(2)}) copy-start(bf16[160,432]{1,0:T(8,128)(2,1)} %constant.33.clone.refs_3_.refs_5_) | copy-start | bytes 414724
  0.7 26.6 %copy-start.7 = (bf16[136,480]{1,0:T(8,128)(2,1)S(1)}, bf16[136,480]{1,0:T(8,128)(2,1)}, u32[]{:S(2)}) copy-start(bf16[136,480]{1,0:T(8,128)(2,1)} %constant.38.clone.refs_8_.refs_10_) | copy-start | bytes 391684
  0.7 26.6 %copy-start.8 = (bf16[256,256]{1,0:T(8,128)(2,1)S(1)}, bf16[256,256]{1,0:T(8,128)(2,1)}, u32[]{:S(2)}) copy-start(bf16[256,256]{1,0:T(8,128)(2,1)} %constant.39.clone.refs_9_.refs_11_) | copy-start | bytes 393220
  5.2 10.8 %collective-permute-start = (f32[68,8,128]{2,1,0:T(8,128)}, f32[68,8,128]{2,1,0:T(8,128)S(1)}, u32[]{:S(2)}, u32[]{:S(2)}) collective-permute-start(f32[68,8,128]{2,1,0:T(8,128)} %get-tuple-element.29), channel_id=1, source_target_pairs={{0,4},{4,0},{1,5},{5,1},{2,6},{6,2},{3,7},{7,3},{8,12},{12,8},{9,1... | collective-permute-start | bytes 835592 | tf_op jit(solution)/shard_map/ppermute | solution.py:131
  6.5 9.5 %collective-permute-start.1 = (f32[17,32,128]{2,1,0:T(8,128)}, f32[17,32,128]{2,1,0:T(8,128)S(1)}, u32[]{:S(2)}, u32[]{:S(2)}) collective-permute-start(f32[17,32,128]{2,1,0:T(8,128)} %get-tuple-element.30), channel_id=1, source_target_pairs={{0,1},{1,0},{2,3},{3,2},{4,5},{5,4},{6,7},{7,6},{8,9},{9,8},{10,11... | collective-permute-start | bytes 835592 | tf_op jit(solution)/shard_map/ppermute | solution.py:132
  6.6 9.3 %collective-permute-start.2 = (f32[17,32,128]{2,1,0:T(8,128)}, f32[17,32,128]{2,1,0:T(8,128)S(1)}, u32[]{:S(2)}, u32[]{:S(2)}) collective-permute-start(f32[17,32,128]{2,1,0:T(8,128)} %get-tuple-element.31), channel_id=1, source_target_pairs={{0,8},{1,2},{2,1},{3,11},{4,12},{5,6},{6,5},{7,15},{8,0},{9,10},{1... | collective-permute-start | bytes 835592 | tf_op jit(solution)/shard_map/ppermute | solution.py:132
  9.1 5.4 %collective-permute-start.3 = (f32[11,8,128]{2,1,0:T(8,128)}, f32[11,8,128]{2,1,0:T(8,128)S(1)}, u32[]{:S(2)}, u32[]{:S(2)}) collective-permute-start(f32[11,8,128]{2,1,0:T(8,128)} %get-tuple-element.32), channel_id=1, source_target_pairs={{0,5},{1,4},{2,7},{3,6},{4,1},{5,0},{6,3},{7,2},{8,13},{9,12},{10,... | collective-permute-start | bytes 135176 | tf_op jit(solution)/shard_map/ppermute | solution.py:132
  9.1 6.8 %collective-permute-start.4 = (f32[11,8,128]{2,1,0:T(8,128)}, f32[11,8,128]{2,1,0:T(8,128)S(1)}, u32[]{:S(2)}, u32[]{:S(2)}) collective-permute-start(f32[11,8,128]{2,1,0:T(8,128)} %get-tuple-element.33), channel_id=1, source_target_pairs={{0,8},{1,6},{2,5},{3,11},{4,12},{5,2},{6,1},{7,15},{8,0},{9,14},{1... | collective-permute-start | bytes 135176 | tf_op jit(solution)/shard_map/ppermute | solution.py:132
  18.7 28.9 %copy-start.10 = (f32[32,32,128]{2,1,0:T(8,128)S(1)}, f32[32,32,128]{2,1,0:T(8,128)}, u32[]{:S(2)}) copy-start(f32[32,32,128]{2,1,0:T(8,128)} %get-tuple-element.43.modulus) | copy-start | bytes 1572868
  18.7 28.9 %copy-start.13 = (s32[3]{0:T(128)S(1)}, s32[3]{0:T(128)}, u32[]{:S(2)}) copy-start(s32[3]{0:T(128)} %pad_add_fusion.pos_ref) | copy-start | bytes 40
  18.7 5.1 %collective-permute-start.5 = (f32[40,8,128]{2,1,0:T(8,128)S(1)}, f32[40,8,128]{2,1,0:T(8,128)S(1)}, u32[]{:S(2)}, u32[]{:S(2)}) collective-permute-start(f32[40,8,128]{2,1,0:T(8,128)S(1)} %get-tuple-element.35), channel_id=1, source_target_pairs={{0,8},{8,0},{16,24},{24,16},{1,9},{9,1},{17,25},{25,17},{2,10},{10... | collective-permute-start | bytes 491528 | tf_op jit(solution)/shard_map/ppermute | solution.py:131
  20.6 6.6 %collective-permute-start.6 = (f32[40,8,128]{2,1,0:T(8,128)S(1)}, f32[40,8,128]{2,1,0:T(8,128)S(1)}, u32[]{:S(2)}, u32[]{:S(2)}) collective-permute-start(f32[40,8,128]{2,1,0:T(8,128)S(1)} %get-tuple-element.36), channel_id=1, source_target_pairs={{0,0},{8,16},{16,8},{24,24},{1,1},{9,17},{17,9},{25,25},{2,2},{10,... | collective-permute-start | bytes 491528 | tf_op jit(solution)/shard_map/ppermute | solution.py:131
  39.8 18.6 %collective-permute-start.7 = (f32[10,136,128]{2,1,0:T(8,128)S(1)}, f32[10,136,128]{2,1,0:T(8,128)S(1)}, u32[]{:S(2)}, u32[]{:S(2)}) collective-permute-start(f32[10,136,128]{2,1,0:T(8,128)S(1)} %get-tuple-element.38), channel_id=1, source_target_pairs={{0,4},{4,0},{1,5},{5,1},{2,6},{6,2},{3,7},{7,3},{8,12},{12,8},{9,1... | collective-permute-start | bytes 2088968 | tf_op jit(solution)/shard_map/ppermute | solution.py:131
  41.1 16.2 %collective-permute-start.8 = (f32[9,136,128]{2,1,0:T(8,128)S(1)}, f32[9,136,128]{2,1,0:T(8,128)S(1)}, u32[]{:S(2)}, u32[]{:S(2)}) collective-permute-start(f32[9,136,128]{2,1,0:T(8,128)S(1)} %get-tuple-element.39), channel_id=1, source_target_pairs={{0,1},{1,0},{2,3},{3,2},{4,5},{5,4},{6,7},{7,6},{8,9},{9,8},{10,11... | collective-permute-start | bytes 1880072 | tf_op jit(solution)/shard_map/ppermute | solution.py:131
  41.1 16.2 %collective-permute-start.9 = (f32[9,136,128]{2,1,0:T(8,128)S(1)}, f32[9,136,128]{2,1,0:T(8,128)S(1)}, u32[]{:S(2)}, u32[]{:S(2)}) collective-permute-start(f32[9,136,128]{2,1,0:T(8,128)S(1)} %get-tuple-element.40), channel_id=1, source_target_pairs={{0,0},{1,2},{2,1},{3,3},{4,4},{5,6},{6,5},{7,7},{8,8},{9,10},{10,9... | collective-permute-start | bytes 1880072 | tf_op jit(solution)/shard_map/ppermute | solution.py:131
  44.5 11.0 %collective-permute-start.10 = (f32[2,136,128]{2,1,0:T(8,128)S(1)}, f32[2,136,128]{2,1,0:T(8,128)S(1)}, u32[]{:S(2)}, u32[]{:S(2)}) collective-permute-start(f32[2,136,128]{2,1,0:T(8,128)S(1)} %get-tuple-element.41), channel_id=1, source_target_pairs={{0,5},{1,4},{2,7},{3,6},{4,1},{5,0},{6,3},{7,2},{8,13},{9,12},{10,... | collective-permute-start | bytes 417800 | tf_op jit(solution)/shard_map/ppermute | solution.py:132
  44.5 12.8 %collective-permute-start.11 = (f32[2,136,128]{2,1,0:T(8,128)S(1)}, f32[2,136,128]{2,1,0:T(8,128)S(1)}, u32[]{:S(2)}, u32[]{:S(2)}) collective-permute-start(f32[2,136,128]{2,1,0:T(8,128)S(1)} %get-tuple-element.42), channel_id=1, source_target_pairs={{0,0},{1,6},{2,5},{3,3},{4,4},{5,2},{6,1},{7,7},{8,8},{9,14},{10,1... | collective-permute-start | bytes 417800 | tf_op jit(solution)/shard_map/ppermute | solution.py:132
  59.5 5.5 %collective-permute-start.12 = (f32[62,8,128]{2,1,0:T(8,128)S(1)}, f32[62,8,128]{2,1,0:T(8,128)S(1)}, u32[]{:S(2)}, u32[]{:S(2)}) collective-permute-start(f32[62,8,128]{2,1,0:T(8,128)S(1)} %get-tuple-element.44), channel_id=1, source_target_pairs={{0,8},{8,0},{16,24},{24,16},{1,9},{9,1},{17,25},{25,17},{2,10},{10... | collective-permute-start | bytes 761864 | tf_op jit(solution)/shard_map/ppermute | solution.py:131
  59.5 7.6 %collective-permute-start.13 = (f32[62,8,128]{2,1,0:T(8,128)S(1)}, f32[62,8,128]{2,1,0:T(8,128)S(1)}, u32[]{:S(2)}, u32[]{:S(2)}) collective-permute-start(f32[62,8,128]{2,1,0:T(8,128)S(1)} %get-tuple-element.45), channel_id=1, source_target_pairs={{0,0},{8,16},{16,8},{24,24},{1,1},{9,17},{17,9},{25,25},{2,2},{10,... | collective-permute-start | bytes 761864 | tf_op jit(solution)/shard_map/ppermute | solution.py:131
  84.8 11.4 %collective-permute-start.14 = (f32[5,136,128]{2,1,0:T(8,128)S(1)}, f32[5,136,128]{2,1,0:T(8,128)S(1)}, u32[]{:S(2)}, u32[]{:S(2)}) collective-permute-start(f32[5,136,128]{2,1,0:T(8,128)S(1)} %get-tuple-element.47), channel_id=1, source_target_pairs={{0,4},{4,0},{1,5},{5,1},{2,6},{6,2},{3,7},{7,3},{8,12},{12,8},{9,1... | collective-permute-start | bytes 1044488 | tf_op jit(solution)/shard_map/ppermute | solution.py:131
  86.1 10.1 %collective-permute-start.15 = (f32[5,136,128]{2,1,0:T(8,128)S(1)}, f32[5,136,128]{2,1,0:T(8,128)S(1)}, u32[]{:S(2)}, u32[]{:S(2)}) collective-permute-start(f32[5,136,128]{2,1,0:T(8,128)S(1)} %get-tuple-element.48), channel_id=1, source_target_pairs={{0,1},{1,0},{2,3},{3,2},{4,5},{5,4},{6,7},{7,6},{8,9},{9,8},{10,11... | collective-permute-start | bytes 1044488 | tf_op jit(solution)/shard_map/ppermute | solution.py:131
  86.1 10.1 %collective-permute-start.16 = (f32[5,136,128]{2,1,0:T(8,128)S(1)}, f32[5,136,128]{2,1,0:T(8,128)S(1)}, u32[]{:S(2)}, u32[]{:S(2)}) collective-permute-start(f32[5,136,128]{2,1,0:T(8,128)S(1)} %get-tuple-element.49), channel_id=1, source_target_pairs={{0,0},{1,2},{2,1},{3,3},{4,4},{5,6},{6,5},{7,7},{8,8},{9,10},{10,9... | collective-permute-start | bytes 1044488 | tf_op jit(solution)/shard_map/ppermute | solution.py:131
  89.5 4.8 %collective-permute-start.17 = (f32[1,136,128]{2,1,0:T(8,128)S(1)}, f32[1,136,128]{2,1,0:T(8,128)S(1)}, u32[]{:S(2)}, u32[]{:S(2)}) collective-permute-start(f32[1,136,128]{2,1,0:T(8,128)S(1)} %get-tuple-element.50), channel_id=1, source_target_pairs={{0,5},{1,4},{2,7},{3,6},{4,1},{5,0},{6,3},{7,2},{8,13},{9,12},{10,... | collective-permute-start | bytes 208904 | tf_op jit(solution)/shard_map/ppermute | solution.py:132
  89.5 6.6 %collective-permute-start.18 = (f32[1,136,128]{2,1,0:T(8,128)S(1)}, f32[1,136,128]{2,1,0:T(8,128)S(1)}, u32[]{:S(2)}, u32[]{:S(2)}) collective-permute-start(f32[1,136,128]{2,1,0:T(8,128)S(1)} %get-tuple-element.51), channel_id=1, source_target_pairs={{0,0},{1,6},{2,5},{3,3},{4,4},{5,2},{6,1},{7,7},{8,8},{9,14},{10,1... | collective-permute-start | bytes 208904 | tf_op jit(solution)/shard_map/ppermute | solution.py:132
  96.9 4.0 %collective-permute-start.19 = (f32[34,8,128]{2,1,0:T(8,128)S(1)}, f32[34,8,128]{2,1,0:T(8,128)S(1)}, u32[]{:S(2)}, u32[]{:S(2)}) collective-permute-start(f32[34,8,128]{2,1,0:T(8,128)S(1)} %get-tuple-element.54), channel_id=1, source_target_pairs={{0,8},{1,9},{2,10},{3,11},{4,12},{5,13},{6,14},{7,15},{8,0},{9,1},... | collective-permute-start | bytes 417800 | tf_op jit(solution)/shard_map/ppermute | solution.py:132
  97.0 5.1 %collective-permute-start.20 = (f32[34,8,128]{2,1,0:T(8,128)S(1)}, f32[34,8,128]{2,1,0:T(8,128)S(1)}, u32[]{:S(2)}, u32[]{:S(2)}) collective-permute-start(f32[34,8,128]{2,1,0:T(8,128)S(1)} %get-tuple-element.55), channel_id=1, source_target_pairs={{0,4},{1,5},{2,6},{3,7},{4,0},{5,1},{6,2},{7,3},{8,16},{9,17},{10,... | collective-permute-start | bytes 417800 | tf_op jit(solution)/shard_map/ppermute | solution.py:132
  (3 other events, 42.4 us)

commit v6 on v5

--- a/solution.py
+++ b/solution.py
@@ -191,8 +191,12 @@
 
 
 def solve(source, mid, target, consts):
+    spectrum(source, mid, consts)
+    recover(mid, target, consts[6:8], lambda t: t)
+
+
+def spectrum(source, mid, consts):
     along_y, along_x, even, odd, back_even, back_odd, back_x, back_y, base, steps = consts
-    rows = target.shape[1]
     half = LENGTH // 2
 
     def forward(t, _):
@@ -244,8 +248,14 @@
 
     lax.fori_loop(0, mid.shape[1] // 16, across, 0, unroll=5)
 
+
+def recover(mid, target, consts, where):
+    back_x, back_y = consts
+    rows = target.shape[1]
+
     def backward(t, _):
-        pair = jnp.concatenate([mid[2 * t], mid[2 * t + 1]], axis=1)
+        at = where(t)
+        pair = jnp.concatenate([mid[2 * at], mid[2 * at + 1]], axis=1)
         done = left_product(back_x[...], pair)
         both = jnp.concatenate([done[:, :LANES], done[:, LANES:]], axis=0)
         turned = right_product(both, back_y[...])
@@ -253,24 +263,24 @@
         target[2 * t + 1] = turned[rows:]
         return 0
 
-    lax.fori_loop(0, half, backward, 0, unroll=10)
+    lax.fori_loop(0, target.shape[0] // 2, backward, 0, unroll=10)
 
 
 def write_messages(pos_ref, solved, width, counts, outs_y, outs_z, outs_yz):
-    rows = solved.shape[1]
+    count, rows, _ = solved.shape
     spot, _ = spots((rows, LANES))
     lane = lax.broadcasted_iota(jnp.int32, (rows, LANES), 1)
     groups = WIDE // width
     _, count_y, count_z = counts
     for phase, out in enumerate(outs_z):
         up, _ = side(pos_ref, 0, phase, count_z)
-        first = pick(up, LENGTH - width, 0)
+        first = pick(up, count - width, 0)
         for i in range(width):
             out[i] = solved[first + i]
     for phase, out in enumerate(outs_y):
         up, _ = side(pos_ref, 1, phase, count_y)
         start = pick(up, WIDE - 1 - width, 1)
-        many = LENGTH // groups
+        many = count // groups
 
         def one(k, _, out=out, start=start, many=many):
             out[k] = pack(
@@ -284,7 +294,7 @@
         up_y, _ = side(pos_ref, 1, phase_y, count_y)
         up_z, _ = side(pos_ref, 0, phase_z, count_z)
         start = pick(up_y, WIDE - 1 - width, 1)
-        first = pick(up_z, LENGTH - width, 0)
+        first = pick(up_z, count - width, 0)
         slots = LANES // width
         for k in range(out.shape[0]):
             total = jnp.zeros((rows, LANES), F32)
@@ -297,16 +307,28 @@
             out[k] = total
 
 
+QUARTER = LENGTH // 4
+
+
+def place_of(z, parts):
+    if parts == 1:
+        return 0, z
+    if QUARTER <= z < LENGTH - QUARTER:
+        return 1, z - QUARTER
+    return 0, z if z < QUARTER else z - 2 * QUARTER
+
+
 def planes_of(width):
     return range(FOLD - width, WIDE - FOLD + width)
 
 
 def add_messages(pos_ref, solved, width, counts, ins_y, ins_z, ins_yz, window, put, get):
-    height = solved.shape[1] if window is None else window.size
+    height = solved[0].shape[1] if window is None else window.size
     rows = slice(None) if window is None else window
     spot, region = spots((height, LANES))
     groups = WIDE // width
     _, count_y, count_z = counts
+    parts = len(solved)
     sides_y = [side(pos_ref, 1, phase, count_y) for phase in range(len(ins_y))]
     sides_z = [side(pos_ref, 0, phase, count_z) for phase in range(len(ins_z))]
     many = LENGTH // groups
@@ -314,8 +336,9 @@
     for z in range(LENGTH):
         if z + 1 not in wanted:
             continue
+        part, at = place_of(z, parts)
         g, k = divmod(z, many)
-        total = solved[z, rows, :]
+        total = solved[part][at, rows, :]
         for (up, use), ref in zip(sides_y, ins_y):
             start = pick(up, WIDE - FOLD, FOLD - width)
             total = total + unpack(ref[k, rows, :], g, width, start, spot, use)
@@ -655,23 +678,40 @@
 
 
 def first_kernel(counts, sizes, pos_ref, residual, *refs):
-    ins_x, consts, (solved,), outs_y, outs_z, outs_yz, (mid,) = groups_of(
-        refs, (sizes[3], 10, 1) + sizes[:3] + (1,)
-    )
-    solve(patched(pos_ref, counts, residual, ins_x), mid, solved, consts)
-    write_messages(pos_ref, solved, FOLD, counts, outs_y, outs_z, outs_yz)
+    ins_x, consts, (outer, mid), outs_z, outs_yz = groups_of(
+        refs, (sizes[3], 10, 2) + sizes[1:3]
+    )
+    spectrum(patched(pos_ref, counts, residual, ins_x), mid, consts)
+    quarter = QUARTER // 2
+    recover(mid, outer, consts[6:8], lambda t: jnp.where(t < quarter, t, t + 2 * quarter))
+    write_messages(pos_ref, outer, FOLD, counts, [], outs_z, outs_yz)
+
+
+def inner_kernel(counts, sizes, pos_ref, outer, mid, back_x, back_y, inner, *outs_y):
+    recover(mid, inner, (back_x, back_y), lambda t: t + QUARTER // 2)
+    spot, _ = spots(outer.shape[1:])
+    groups = WIDE // FOLD
+    many = LENGTH // groups
+    for phase, out in enumerate(outs_y):
+        up, _ = side(pos_ref, 1, phase, counts[1])
+        start = pick(up, WIDE - 1 - FOLD, 1)
+        for k in range(many):
+            places = [place_of(g * many + k, 2) for g in range(groups)]
+            planes = [(outer, inner)[part][at] for part, at in places]
+            out[k] = pack(planes, FOLD, start, spot, groups)
 
 
 NINTH = WIDE
 THIRD = NINTH + -(-WIDE // 8)
 
 
-def edge_kernel(width, counts, sizes, pos_ref, solved, *refs):
+def edge_kernel(width, counts, sizes, pos_ref, *refs):
     extra = 1 if width == FOLD else 0
-    ins_y, ins_z, ins_yz, modulus, outs_x, scratch = groups_of(
-        refs, sizes[:3] + (extra, sizes[3], extra)
-    )
-    rows = solved.shape[1]
+    parts = 1 + extra
+    solved, ins_y, ins_z, ins_yz, modulus, outs_x, scratch = groups_of(
+        refs, (parts,) + sizes[:3] + (extra, sizes[3], extra)
+    )
+    rows = solved[0].shape[1]
     height = 16 if extra else 8
     _, region = spots((PAD, LANES))
     third = WIDE // 3
@@ -703,9 +743,12 @@
                 out[THIRD + k] = total
 
 
-def fold_kernel(width, counts, sizes, pos_ref, solved, *refs):
-    ins_y, ins_z, ins_yz, (field,) = groups_of(refs, sizes[:3] + (1,))
-    rows = solved.shape[1]
+def fold_kernel(width, counts, sizes, pos_ref, *refs):
+    parts = 2 if width == FOLD else 1
+    solved, ins_y, ins_z, ins_yz, (field,) = groups_of(
+        refs, (parts,) + sizes[:3] + (1,)
+    )
+    rows = solved[0].shape[1]
     thin = INTERSECTION
     core = slice(thin, thin + rows)
     blank = jnp.zeros((thin, LANES), F32)
@@ -800,9 +843,9 @@
     spectral = (LENGTH, columns // BRICK * LENGTH, LANES)
 
     def exchange_yz(values, filler=None):
-        y, z, yz = groups_of(values, sizes[:3])
+        y, z, yz = groups_of(values, (len(values) - sizes[1] - sizes[2],) + sizes[1:3])
         z = [swap(value, mesh, {"gz": phase}, filler) for phase, value in enumerate(z)]
-        y = [swap(value, mesh, {"gy": phase}, None) for phase, value in enumerate(y)]
+        y = [swap(value, mesh, {"gy": n % ways[1]}, None) for n, value in enumerate(y)]
         yz = [
             swap(value, mesh, {"gy": number // ways[2], "gz": number % ways[2]}, filler)
             for number, value in enumerate(yz)
@@ -812,10 +855,10 @@
     def exchange_x(values, filler=None):
         return [swap(value, mesh, {"gx": phase}, filler) for phase, value in enumerate(values)]
 
-    def message_shapes(width, height):
+    def message_shapes(width, height, count=LENGTH):
         groups = WIDE // width
         return (
-            [(LENGTH // groups, height, LANES)] * sizes[0]
+            [(count // groups, height, LANES)] * sizes[0]
             + [(width, height, LANES)] * sizes[1]
             + [(-(-3 * width // (LANES // width)), height, LANES)] * sizes[2]
         )
@@ -859,23 +902,29 @@
         [(WIDE, LANES, columns)],
         work=8000000,
     )
-    solved, *out = call(
-        bind(first_kernel),
-        [pos, residual, *from_x, *consts],
-        [thin] + message_shapes(FOLD, thick),
-        [spectral],
-    )
-    margins = exchange_yz(out)
+    part = (LENGTH // 2, thick, LANES)
+    first_shapes = message_shapes(FOLD, thick)
+    outer, mid, *out = call(
+        bind(first_kernel), [pos, residual, *from_x, *consts], [part, spectral] + first_shapes[sizes[0] :]
+    )
+    inner, *late = call(
+        bind(inner_kernel),
+        [pos, outer, mid, *consts[6:8]],
+        [part] + first_shapes[: sizes[0]],
+        work=8000000,
+    )
+    solved = [outer, inner]
+    margins = exchange_yz([*late, *out])
     first_edges = exchange_x(
         call(
             bind(edge_kernel, FOLD),
-            [pos, solved, *margins, modulus],
+            [pos, *solved, *margins, modulus],
             [(THIRD + WIDE // 3, 8, LANES)] * sizes[3],
             [(WIDE, 16, LANES)],
         )
     )
     (partial,) = call(
-        bind(fold_kernel, FOLD), [pos, solved, *margins], [wide], work=8000000
+        bind(fold_kernel, FOLD), [pos, *solved, *margins], [wide], work=8000000
     )
     solved, moved, left, *out = call(
         bind(second_kernel),

time: 111 us -> 111 us (level)
    pallas_call x10 -> x11, Pallas kernels: 52.2 us -> 51.3 us  [call(): pl.pallas_call(kernel, out_shape=[jax.ShapeDtypeStruct(shape, F32) for sh...]
where the time goes in v6:
time: 111 us; the launch traced here: 110 us
  Pallas kernels  51.3 us (46%)
  starting transfers between devices  32 us (29%)
  waiting for transfers between devices  24.6 us (22%)
    pallas_call x11, Pallas kernels, call(): pl.pallas_call(kernel, out_shape=[jax.ShapeDtypeStruct(shape, F32) for sh...  51.3 us
    ppermute x11, starting transfers between devices, swap(): return lax.ppermute(value, name, list(enumerate(other)))  18.7 us
    ppermute x10, waiting for transfers between devices, swap(): return lax.ppermute(value, names, pairs)  17.7 us
    ppermute x10, starting transfers between devices, swap(): return lax.ppermute(value, names, pairs)  13.2 us
    ppermute x11, waiting for transfers between devices, swap(): return lax.ppermute(value, name, list(enumerate(other)))  6.86 us
  transfers between devices with their start and end apart: 21, of which 10 were waited for; matrix products, arithmetic and copies ran while one was open for 0% of the time, Pallas kernels for 5%

profile of v6, /device:TPU:9, one launch (start us, length us, event | category | flops | bytes accessed | tf_op | source)
XLA Modules:
  0.0 110.2 jit_solution(559379461140829647)
XLA Ops:
  1.4 3.8 %shard_map.149 = (f32[32,32,128]{2,1,0:T(8,128)}, f32[68,8,128]{2,1,0:T(8,128)}, f32[17,32,128]{2,1,0:T(8,128)}, f32[17,32,128]{2,1,0:T(8,128)}, f32[11,8,128]{2,1,0:T(8,128)}, /*index=5*/f32[11,8,128]{2,1,0:T(8,128)}) custom-call(s32[3]{0:T(128)} %pad_add_fusion.pos_ref, f32[16]{0:T(128)} %table_in.1, f32[3,32,32,128]{3,2,1,0:T(8,128)} %load.1, ...), custom_call_target="tpu_custom_call" | custom-call | tf_op jit(solution)/shard_map/pallas_call | solution.py:822
  5.2 1.3 %collective-permute-start = (f32[68,8,128]{2,1,0:T(8,128)}, f32[68,8,128]{2,1,0:T(8,128)S(1)}, u32[]{:S(2)}, u32[]{:S(2)}) collective-permute-start(f32[68,8,128]{2,1,0:T(8,128)} %get-tuple-element.31), channel_id=1, source_target_pairs={{0,4},{4,0},{1,5},{5,1},{2,6},{6,2},{3,7},{7,3},{8,12},{12,8},{9,1... | collective-permute-start | bytes 835592 | tf_op jit(solution)/shard_map/ppermute | solution.py:131
  6.7 2.4 %collective-permute-start.2 = (f32[17,32,128]{2,1,0:T(8,128)}, f32[17,32,128]{2,1,0:T(8,128)S(1)}, u32[]{:S(2)}, u32[]{:S(2)}) collective-permute-start(f32[17,32,128]{2,1,0:T(8,128)} %get-tuple-element.33), channel_id=1, source_target_pairs={{0,8},{1,2},{2,1},{3,11},{4,12},{5,6},{6,5},{7,15},{8,0},{9,10},{1... | collective-permute-start | bytes 835592 | tf_op jit(solution)/shard_map/ppermute | solution.py:132
  9.1 2.3 %collective-permute-start.4 = (f32[11,8,128]{2,1,0:T(8,128)}, f32[11,8,128]{2,1,0:T(8,128)S(1)}, u32[]{:S(2)}, u32[]{:S(2)}) collective-permute-start(f32[11,8,128]{2,1,0:T(8,128)} %get-tuple-element.35), channel_id=1, source_target_pairs={{0,8},{1,6},{2,5},{3,11},{4,12},{5,2},{6,1},{7,15},{8,0},{9,14},{1... | collective-permute-start | bytes 135176 | tf_op jit(solution)/shard_map/ppermute | solution.py:132
  11.4 3.1 %collective-permute-done.3.refs_3_ = f32[11,8,128]{2,1,0:T(8,128)S(1)} collective-permute-done((f32[11,8,128]{2,1,0:T(8,128)}, f32[11,8,128]{2,1,0:T(8,128)S(1)}, u32[]{:S(2)}, u32[]{:S(2)}) %collective-permute-start.3) | collective-permute-done | bytes 45088 | tf_op jit(solution)/shard_map/ppermute | solution.py:132
  14.5 1.4 %collective-permute-done.4.refs_4_ = f32[11,8,128]{2,1,0:T(8,128)S(1)} collective-permute-done((f32[11,8,128]{2,1,0:T(8,128)}, f32[11,8,128]{2,1,0:T(8,128)S(1)}, u32[]{:S(2)}, u32[]{:S(2)}) %collective-permute-start.4) | collective-permute-done | bytes 45088 | tf_op jit(solution)/shard_map/ppermute | solution.py:132
  16.6 2.1 %shard_map.150 = (f32[40,144,128]{2,1,0:T(8,128)S(1)}, f32[40,8,128]{2,1,0:T(8,128)S(1)}, f32[40,8,128]{2,1,0:T(8,128)S(1)}) custom-call(s32[3]{0:T(128)S(1)} %copy-done.12, f32[3,32,32,128]{3,2,1,0:T(8,128)S(1)} %copy-done, f32[68,8,128]{2,1,0:T(8,128)S(1)} %collective-permute-done.refs_0_, f32[17,32,128]{2,1,0:T(8,128)S(1)} %collective-permute-done.1.refs_1_, ...), custom_call_target="tpu_custom_call" | custom-call | tf_op jit(solution)/shard_map/pallas_call | solution.py:822
  18.8 1.9 %collective-permute-start.5 = (f32[40,8,128]{2,1,0:T(8,128)S(1)}, f32[40,8,128]{2,1,0:T(8,128)S(1)}, u32[]{:S(2)}, u32[]{:S(2)}) collective-permute-start(f32[40,8,128]{2,1,0:T(8,128)S(1)} %get-tuple-element.37), channel_id=1, source_target_pairs={{0,8},{8,0},{16,24},{24,16},{1,9},{9,1},{17,25},{25,17},{2,10},{10... | collective-permute-start | bytes 491528 | tf_op jit(solution)/shard_map/ppermute | solution.py:131
  20.7 3.0 %collective-permute-start.6 = (f32[40,8,128]{2,1,0:T(8,128)S(1)}, f32[40,8,128]{2,1,0:T(8,128)S(1)}, u32[]{:S(2)}, u32[]{:S(2)}) collective-permute-start(f32[40,8,128]{2,1,0:T(8,128)S(1)} %get-tuple-element.38), channel_id=1, source_target_pairs={{0,0},{8,16},{16,8},{24,24},{1,1},{9,17},{17,9},{25,25},{2,2},{10,... | collective-permute-start | bytes 491528 | tf_op jit(solution)/shard_map/ppermute | solution.py:131
  23.7 3.6 %collective-permute-done.6.refs_1_ = f32[40,8,128]{2,1,0:T(8,128)S(1)} collective-permute-done((f32[40,8,128]{2,1,0:T(8,128)S(1)}, f32[40,8,128]{2,1,0:T(8,128)S(1)}, u32[]{:S(2)}, u32[]{:S(2)}) %collective-permute-start.6) | collective-permute-done | bytes 163872 | tf_op jit(solution)/shard_map/ppermute | solution.py:131
  27.4 8.5 %shard_map.151 = (f32[20,136,128]{2,1,0:T(8,128)S(1)}, f32[40,160,128]{2,1,0:T(8,128)S(1)}, f32[9,136,128]{2,1,0:T(8,128)S(1)}, f32[9,136,128]{2,1,0:T(8,128)S(1...) custom-call(s32[3]{0:T(128)S(1)} %copy-done.12, f32[40,144,128]{2,1,0:T(8,128)S(1)} %get-tuple-element.36.residual, ...), custom_call_target="tpu_custom_call" | custom-call | tf_op jit(solution)/shard_map/pallas_call | solution.py:822
  35.9 3.1 %shard_map.152 = (f32[20,136,128]{2,1,0:T(8,128)S(1)}, f32[10,136,128]{2,1,0:T(8,128)S(1)}) custom-call(s32[3]{0:T(128)S(1)} %copy-done.12, f32[20,136,128]{2,1,0:T(8,128)S(1)} %get-tuple-element.39.outer.refs_0_, f32[40,160,128]{2,1,0:T(8,128)S(1)} %get-tuple-element.40.mid, bf16[136,480]{1,0:T(8,128)(2,1)S(1)} %copy-done.1, bf16[256,256]{1,0:T(8,128)(2,1)S(1)} %copy-done.2), custom_call_target="tpu_custom_call" | custom-call | flops 8000000 | bytes 8000000 | tf_op jit(solution)/shard_map/pallas_call | solution.py:822
  39.0 1.3 %collective-permute-start.7 = (f32[10,136,128]{2,1,0:T(8,128)S(1)}, f32[10,136,128]{2,1,0:T(8,128)S(1)}, u32[]{:S(2)}, u32[]{:S(2)}) collective-permute-start(f32[10,136,128]{2,1,0:T(8,128)S(1)} %get-tuple-element.42), channel_id=1, source_target_pairs={{0,4},{4,0},{1,5},{5,1},{2,6},{6,2},{3,7},{7,3},{8,12},{12,8},{9,1... | collective-permute-start | bytes 2088968 | tf_op jit(solution)/shard_map/ppermute | solution.py:131
  40.3 3.4 %collective-permute-start.9 = (f32[9,136,128]{2,1,0:T(8,128)S(1)}, f32[9,136,128]{2,1,0:T(8,128)S(1)}, u32[]{:S(2)}, u32[]{:S(2)}) collective-permute-start(f32[9,136,128]{2,1,0:T(8,128)S(1)} %get-tuple-element.44), channel_id=1, source_target_pairs={{0,0},{1,2},{2,1},{3,3},{4,4},{5,6},{6,5},{7,7},{8,8},{9,10},{10,9... | collective-permute-start | bytes 1880072 | tf_op jit(solution)/shard_map/ppermute | solution.py:131
  43.8 3.0 %collective-permute-start.11 = (f32[2,136,128]{2,1,0:T(8,128)S(1)}, f32[2,136,128]{2,1,0:T(8,128)S(1)}, u32[]{:S(2)}, u32[]{:S(2)}) collective-permute-start(f32[2,136,128]{2,1,0:T(8,128)S(1)} %get-tuple-element.46), channel_id=1, source_target_pairs={{0,0},{1,6},{2,5},{3,3},{4,4},{5,2},{6,1},{7,7},{8,8},{9,14},{10,1... | collective-permute-start | bytes 417800 | tf_op jit(solution)/shard_map/ppermute | solution.py:132
  46.9 1.4 %shard_map.154.refs_7_.modulus = f32[42,144,128]{2,1,0:T(8,128)S(1)} custom-call(s32[3]{0:T(128)S(1)} %copy-done.13, f32[32,32,128]{2,1,0:T(8,128)S(1)} %copy-done.10, f32[68,8,128]{2,1,0:T(8,128)S(1)} %collective-permute-done.refs_0_, f32[17,32,128]{2,1,0:T(8,128)S(1)} %collective-permute-done.1.refs_1_, f32[17,32,128]{2,1,0:T(8,128)S(1)} %collective-permute-done.2.refs_2_, ...), custom_call_target="tpu_custom_call" | custom-call | flops 8000000 | bytes 8000000 | tf_op jit(solution)/shard_map/pallas_call | solution.py:822
  48.2 6.5 %collective-permute-done.10.refs_5_ = f32[2,136,128]{2,1,0:T(8,128)S(1)} collective-permute-done((f32[2,136,128]{2,1,0:T(8,128)S(1)}, f32[2,136,128]{2,1,0:T(8,128)S(1)}, u32[]{:S(2)}, u32[]{:S(2)}) %collective-permute-start.10) | collective-permute-done | bytes 139296 | tf_op jit(solution)/shard_map/ppermute | solution.py:132
  54.7 1.8 %collective-permute-done.11.refs_6_ = f32[2,136,128]{2,1,0:T(8,128)S(1)} collective-permute-done((f32[2,136,128]{2,1,0:T(8,128)S(1)}, f32[2,136,128]{2,1,0:T(8,128)S(1)}, u32[]{:S(2)}, u32[]{:S(2)}) %collective-permute-start.11) | collective-permute-done | bytes 139296 | tf_op jit(solution)/shard_map/ppermute | solution.py:132
  57.6 1.1 shard_map.155
  58.8 3.0 %collective-permute-start.13 = (f32[62,8,128]{2,1,0:T(8,128)S(1)}, f32[62,8,128]{2,1,0:T(8,128)S(1)}, u32[]{:S(2)}, u32[]{:S(2)}) collective-permute-start(f32[62,8,128]{2,1,0:T(8,128)S(1)} %get-tuple-element.49), channel_id=1, source_target_pairs={{0,0},{8,16},{16,8},{24,24},{1,1},{9,17},{17,9},{25,25},{2,2},{10,... | collective-permute-start | bytes 761864 | tf_op jit(solution)/shard_map/ppermute | solution.py:131
  61.9 2.3 %shard_map.153.partial = f32[42,144,128]{2,1,0:T(8,128)S(1)} custom-call(s32[3]{0:T(128)S(1)} %copy-done.13, f32[20,136,128]{2,1,0:T(8,128)S(1)} %get-tuple-element.39.outer.refs_0_, f32[20,136,128]{2,1,0:T(8,128)S(1)} %get-tuple-element.41.refs_1_, f32[10,136,128]{2,1,0:T(8,128)S(1)} %collective-permute-done.7.refs_2_, ...), custom_call_target="tpu_custom_call" | custom-call | flops 8000000 | bytes 8000000 | tf_op jit(solution)/shard_map/pallas_call | solution.py:822
  64.2 2.2 %collective-permute-done.13.refs_3_ = f32[62,8,128]{2,1,0:T(8,128)S(1)} collective-permute-done((f32[62,8,128]{2,1,0:T(8,128)S(1)}, f32[62,8,128]{2,1,0:T(8,128)S(1)}, u32[]{:S(2)}, u32[]{:S(2)}) %collective-permute-start.13) | collective-permute-done | bytes 253984 | tf_op jit(solution)/shard_map/ppermute | solution.py:131
  66.4 17.5 %shard_map.156 = (f32[40,136,128]{2,1,0:T(8,128)S(1)}, f32[42,144,128]{2,1,0:T(8,128)S(1)}, f32[40,144,128]{2,1,0:T(8,128)S(1)}, f32[5,136,128]{2,1,0:T(8,128)S(...) custom-call(s32[3]{0:T(128)S(1)} %copy-done.13, ...), custom_call_target="tpu_custom_call" | custom-call | tf_op jit(solution)/shard_map/pallas_call | solution.py:822
  84.0 1.3 %collective-permute-start.14 = (f32[5,136,128]{2,1,0:T(8,128)S(1)}, f32[5,136,128]{2,1,0:T(8,128)S(1)}, u32[]{:S(2)}, u32[]{:S(2)}) collective-permute-start(f32[5,136,128]{2,1,0:T(8,128)S(1)} %get-tuple-element.51), channel_id=1, source_target_pairs={{0,4},{4,0},{1,5},{5,1},{2,6},{6,2},{3,7},{7,3},{8,12},{12,8},{9,1... | collective-permute-start | bytes 1044488 | tf_op jit(solution)/shard_map/ppermute | solution.py:131
  85.3 3.4 %collective-permute-start.16 = (f32[5,136,128]{2,1,0:T(8,128)S(1)}, f32[5,136,128]{2,1,0:T(8,128)S(1)}, u32[]{:S(2)}, u32[]{:S(2)}) collective-permute-start(f32[5,136,128]{2,1,0:T(8,128)S(1)} %get-tuple-element.53), channel_id=1, source_target_pairs={{0,0},{1,2},{2,1},{3,3},{4,4},{5,6},{6,5},{7,7},{8,8},{9,10},{10,9... | collective-permute-start | bytes 1044488 | tf_op jit(solution)/shard_map/ppermute | solution.py:131
  88.7 3.0 %collective-permute-start.18 = (f32[1,136,128]{2,1,0:T(8,128)S(1)}, f32[1,136,128]{2,1,0:T(8,128)S(1)}, u32[]{:S(2)}, u32[]{:S(2)}) collective-permute-start(f32[1,136,128]{2,1,0:T(8,128)S(1)} %get-tuple-element.55), channel_id=1, source_target_pairs={{0,0},{1,6},{2,5},{3,3},{4,4},{5,2},{6,1},{7,7},{8,8},{9,14},{10,1... | collective-permute-start | bytes 208904 | tf_op jit(solution)/shard_map/ppermute | solution.py:132
  91.8 1.7 %collective-permute-done.17.refs_4_ = f32[1,136,128]{2,1,0:T(8,128)S(1)} collective-permute-done((f32[1,136,128]{2,1,0:T(8,128)S(1)}, f32[1,136,128]{2,1,0:T(8,128)S(1)}, u32[]{:S(2)}, u32[]{:S(2)}) %collective-permute-start.17) | collective-permute-done | bytes 69664 | tf_op jit(solution)/shard_map/ppermute | solution.py:132
  93.5 1.9 %collective-permute-done.18.refs_5_ = f32[1,136,128]{2,1,0:T(8,128)S(1)} collective-permute-done((f32[1,136,128]{2,1,0:T(8,128)S(1)}, f32[1,136,128]{2,1,0:T(8,128)S(1)}, u32[]{:S(2)}, u32[]{:S(2)}) %collective-permute-start.18) | collective-permute-done | bytes 69664 | tf_op jit(solution)/shard_map/ppermute | solution.py:132
  96.2 2.1 %collective-permute-start.20 = (f32[34,8,128]{2,1,0:T(8,128)S(1)}, f32[34,8,128]{2,1,0:T(8,128)S(1)}, u32[]{:S(2)}, u32[]{:S(2)}) collective-permute-start(f32[34,8,128]{2,1,0:T(8,128)S(1)} %get-tuple-element.59), channel_id=1, source_target_pairs={{0,4},{1,5},{2,6},{3,7},{4,0},{5,1},{6,2},{7,3},{8,16},{9,17},{10,... | collective-permute-start | bytes 417800 | tf_op jit(solution)/shard_map/ppermute | solution.py:132
  98.3 1.8 %shard_map.157.partial = f32[34,144,128]{2,1,0:T(8,128)S(1)} custom-call(s32[3]{0:T(128)S(1)} %copy-done.13, f32[40,136,128]{2,1,0:T(8,128)S(1)} %get-tuple-element.50.refs_0_, f32[5,136,128]{2,1,0:T(8,128)S(1)} %collective-permute-done.14.refs_1_, f32[5,136,128]{2,1,0:T(8,128)S(1)} %collective-permute-done.15.refs_2_, ...), custom_call_target="tpu_custom_call" | custom-call | flops 8000000 | bytes 8000000 | tf_op jit(solution)/shard_map/pallas_call | solution.py:822
  100.1 1.2 %collective-permute-done.20.refs_1_ = f32[34,8,128]{2,1,0:T(8,128)S(1)} collective-permute-done((f32[34,8,128]{2,1,0:T(8,128)S(1)}, f32[34,8,128]{2,1,0:T(8,128)S(1)}, u32[]{:S(2)}, u32[]{:S(2)}) %collective-permute-start.20) | collective-permute-done | bytes 139296 | tf_op jit(solution)/shard_map/ppermute | solution.py:132
  101.3 8.9 %shard_map.159 = (f32[3,32,32,128]{3,2,1,0:T(8,128)}, f32[3,32,32,128]{3,2,1,0:T(8,128)}) custom-call(s32[3]{0:T(128)S(1)} %copy-done.13, f32[34,144,128]{2,1,0:T(8,128)S(1)} %shard_map.157.partial, f32[42,144,128]{2,1,0:T(8,128)S(1)} %shard_map.154.refs_7_.modulus, f32[42,144,128]{2,1,0:T(8,128)S(1)} %get-tuple-element.56.moved, ...), custom_call_target="tpu_custom_call" | custom-call | tf_op jit(solution)/shard_map/pallas_call | solution.py:822
  (50 shorter events, 3.8 us)
Async XLA Ops:
  0.6 26.7 %copy-start.2 = (bf16[256,256]{1,0:T(8,128)(2,1)S(1)}, bf16[256,256]{1,0:T(8,128)(2,1)}, u32[]{:S(2)}) copy-start(bf16[256,256]{1,0:T(8,128)(2,1)} %constant.39.clone.refs_9_.back_y.refs_11_) | copy-start | bytes 393220
  0.6 26.7 %copy-start.1 = (bf16[136,480]{1,0:T(8,128)(2,1)S(1)}, bf16[136,480]{1,0:T(8,128)(2,1)}, u32[]{:S(2)}) copy-start(bf16[136,480]{1,0:T(8,128)(2,1)} %constant.38.clone.refs_8_.back_x.refs_10_) | copy-start | bytes 391684
  0.7 26.7 %copy-start.3 = (f32[40,8,128]{2,1,0:T(8,128)S(1)}, f32[40,8,128]{2,1,0:T(8,128)}, u32[]{:S(2)}) copy-start(f32[40,8,128]{2,1,0:T(8,128)} %constant.41.clone.refs_11_.refs_13_) | copy-start | bytes 491524
  0.7 26.7 %copy-start.4 = (bf16[160,480]{1,0:T(8,128)(2,1)S(1)}, bf16[160,480]{1,0:T(8,128)(2,1)}, u32[]{:S(2)}) copy-start(bf16[160,480]{1,0:T(8,128)(2,1)} %constant.37.clone.refs_7_.refs_9_) | copy-start | bytes 460804
  0.7 26.7 %copy-start.5 = (bf16[160,480]{1,0:T(8,128)(2,1)S(1)}, bf16[160,480]{1,0:T(8,128)(2,1)}, u32[]{:S(2)}) copy-start(bf16[160,480]{1,0:T(8,128)(2,1)} %constant.36.clone.refs_6_.refs_8_) | copy-start | bytes 460804
  0.7 26.7 %copy-start.6 = (bf16[160,480]{1,0:T(8,128)(2,1)S(1)}, bf16[160,480]{1,0:T(8,128)(2,1)}, u32[]{:S(2)}) copy-start(bf16[160,480]{1,0:T(8,128)(2,1)} %constant.35.clone.refs_5_.refs_7_) | copy-start | bytes 460804
  0.7 26.7 %copy-start.7 = (bf16[160,480]{1,0:T(8,128)(2,1)S(1)}, bf16[160,480]{1,0:T(8,128)(2,1)}, u32[]{:S(2)}) copy-start(bf16[160,480]{1,0:T(8,128)(2,1)} %constant.34.clone.refs_4_.refs_6_) | copy-start | bytes 460804
  0.7 15.2 %copy-start = (f32[3,32,32,128]{3,2,1,0:T(8,128)S(1)}, f32[3,32,32,128]{3,2,1,0:T(8,128)}, u32[]{:S(2)}) copy-start(f32[3,32,32,128]{3,2,1,0:T(8,128)} %load.1) | copy-start | bytes 4718596
  0.7 26.6 %copy-start.8 = (bf16[160,432]{1,0:T(8,128)(2,1)S(1)}, bf16[160,432]{1,0:T(8,128)(2,1)}, u32[]{:S(2)}) copy-start(bf16[160,432]{1,0:T(8,128)(2,1)} %constant.33.clone.refs_3_.refs_5_) | copy-start | bytes 414724
  0.7 26.6 %copy-start.9 = (bf16[256,256]{1,0:T(8,128)(2,1)S(1)}, bf16[256,256]{1,0:T(8,128)(2,1)}, u32[]{:S(2)}) copy-start(bf16[256,256]{1,0:T(8,128)(2,1)} %constant.32.clone.refs_2_.refs_4_) | copy-start | bytes 393220
  0.8 26.6 %copy-start.11 = (f32[160,128]{1,0:T(8,128)S(1)}, f32[160,128]{1,0:T(8,128)}, u32[]{:S(2)}) copy-start(f32[160,128]{1,0:T(8,128)} %constant.40.clone.refs_10_.refs_12_) | copy-start | bytes 245764
  5.2 10.8 %collective-permute-start = (f32[68,8,128]{2,1,0:T(8,128)}, f32[68,8,128]{2,1,0:T(8,128)S(1)}, u32[]{:S(2)}, u32[]{:S(2)}) collective-permute-start(f32[68,8,128]{2,1,0:T(8,128)} %get-tuple-element.31), channel_id=1, source_target_pairs={{0,4},{4,0},{1,5},{5,1},{2,6},{6,2},{3,7},{7,3},{8,12},{12,8},{9,1... | collective-permute-start | bytes 835592 | tf_op jit(solution)/shard_map/ppermute | solution.py:131
  6.5 9.5 %collective-permute-start.1 = (f32[17,32,128]{2,1,0:T(8,128)}, f32[17,32,128]{2,1,0:T(8,128)S(1)}, u32[]{:S(2)}, u32[]{:S(2)}) collective-permute-start(f32[17,32,128]{2,1,0:T(8,128)} %get-tuple-element.32), channel_id=1, source_target_pairs={{0,1},{1,0},{2,3},{3,2},{4,5},{5,4},{6,7},{7,6},{8,9},{9,8},{10,11... | collective-permute-start | bytes 835592 | tf_op jit(solution)/shard_map/ppermute | solution.py:132
  6.7 9.3 %collective-permute-start.2 = (f32[17,32,128]{2,1,0:T(8,128)}, f32[17,32,128]{2,1,0:T(8,128)S(1)}, u32[]{:S(2)}, u32[]{:S(2)}) collective-permute-start(f32[17,32,128]{2,1,0:T(8,128)} %get-tuple-element.33), channel_id=1, source_target_pairs={{0,8},{1,2},{2,1},{3,11},{4,12},{5,6},{6,5},{7,15},{8,0},{9,10},{1... | collective-permute-start | bytes 835592 | tf_op jit(solution)/shard_map/ppermute | solution.py:132
  9.1 5.4 %collective-permute-start.3 = (f32[11,8,128]{2,1,0:T(8,128)}, f32[11,8,128]{2,1,0:T(8,128)S(1)}, u32[]{:S(2)}, u32[]{:S(2)}) collective-permute-start(f32[11,8,128]{2,1,0:T(8,128)} %get-tuple-element.34), channel_id=1, source_target_pairs={{0,5},{1,4},{2,7},{3,6},{4,1},{5,0},{6,3},{7,2},{8,13},{9,12},{10,... | collective-permute-start | bytes 135176 | tf_op jit(solution)/shard_map/ppermute | solution.py:132
  9.1 6.8 %collective-permute-start.4 = (f32[11,8,128]{2,1,0:T(8,128)}, f32[11,8,128]{2,1,0:T(8,128)S(1)}, u32[]{:S(2)}, u32[]{:S(2)}) collective-permute-start(f32[11,8,128]{2,1,0:T(8,128)} %get-tuple-element.35), channel_id=1, source_target_pairs={{0,8},{1,6},{2,5},{3,11},{4,12},{5,2},{6,1},{7,15},{8,0},{9,14},{1... | collective-permute-start | bytes 135176 | tf_op jit(solution)/shard_map/ppermute | solution.py:132
  18.8 5.0 %collective-permute-start.5 = (f32[40,8,128]{2,1,0:T(8,128)S(1)}, f32[40,8,128]{2,1,0:T(8,128)S(1)}, u32[]{:S(2)}, u32[]{:S(2)}) collective-permute-start(f32[40,8,128]{2,1,0:T(8,128)S(1)} %get-tuple-element.37), channel_id=1, source_target_pairs={{0,8},{8,0},{16,24},{24,16},{1,9},{9,1},{17,25},{25,17},{2,10},{10... | collective-permute-start | bytes 491528 | tf_op jit(solution)/shard_map/ppermute | solution.py:131
  20.7 6.6 %collective-permute-start.6 = (f32[40,8,128]{2,1,0:T(8,128)S(1)}, f32[40,8,128]{2,1,0:T(8,128)S(1)}, u32[]{:S(2)}, u32[]{:S(2)}) collective-permute-start(f32[40,8,128]{2,1,0:T(8,128)S(1)} %get-tuple-element.38), channel_id=1, source_target_pairs={{0,0},{8,16},{16,8},{24,24},{1,1},{9,17},{17,9},{25,25},{2,2},{10,... | collective-permute-start | bytes 491528 | tf_op jit(solution)/shard_map/ppermute | solution.py:131
  39.0 18.6 %collective-permute-start.7 = (f32[10,136,128]{2,1,0:T(8,128)S(1)}, f32[10,136,128]{2,1,0:T(8,128)S(1)}, u32[]{:S(2)}, u32[]{:S(2)}) collective-permute-start(f32[10,136,128]{2,1,0:T(8,128)S(1)} %get-tuple-element.42), channel_id=1, source_target_pairs={{0,4},{4,0},{1,5},{5,1},{2,6},{6,2},{3,7},{7,3},{8,12},{12,8},{9,1... | collective-permute-start | bytes 2088968 | tf_op jit(solution)/shard_map/ppermute | solution.py:131
  40.3 16.2 %collective-permute-start.8 = (f32[9,136,128]{2,1,0:T(8,128)S(1)}, f32[9,136,128]{2,1,0:T(8,128)S(1)}, u32[]{:S(2)}, u32[]{:S(2)}) collective-permute-start(f32[9,136,128]{2,1,0:T(8,128)S(1)} %get-tuple-element.43), channel_id=1, source_target_pairs={{0,1},{1,0},{2,3},{3,2},{4,5},{5,4},{6,7},{7,6},{8,9},{9,8},{10,11... | collective-permute-start | bytes 1880072 | tf_op jit(solution)/shard_map/ppermute | solution.py:131
  40.3 16.2 %collective-permute-start.9 = (f32[9,136,128]{2,1,0:T(8,128)S(1)}, f32[9,136,128]{2,1,0:T(8,128)S(1)}, u32[]{:S(2)}, u32[]{:S(2)}) collective-permute-start(f32[9,136,128]{2,1,0:T(8,128)S(1)} %get-tuple-element.44), channel_id=1, source_target_pairs={{0,0},{1,2},{2,1},{3,3},{4,4},{5,6},{6,5},{7,7},{8,8},{9,10},{10,9... | collective-permute-start | bytes 1880072 | tf_op jit(solution)/shard_map/ppermute | solution.py:131
  43.7 11.0 %collective-permute-start.10 = (f32[2,136,128]{2,1,0:T(8,128)S(1)}, f32[2,136,128]{2,1,0:T(8,128)S(1)}, u32[]{:S(2)}, u32[]{:S(2)}) collective-permute-start(f32[2,136,128]{2,1,0:T(8,128)S(1)} %get-tuple-element.45), channel_id=1, source_target_pairs={{0,5},{1,4},{2,7},{3,6},{4,1},{5,0},{6,3},{7,2},{8,13},{9,12},{10,... | collective-permute-start | bytes 417800 | tf_op jit(solution)/shard_map/ppermute | solution.py:132
  43.8 12.8 %collective-permute-start.11 = (f32[2,136,128]{2,1,0:T(8,128)S(1)}, f32[2,136,128]{2,1,0:T(8,128)S(1)}, u32[]{:S(2)}, u32[]{:S(2)}) collective-permute-start(f32[2,136,128]{2,1,0:T(8,128)S(1)} %get-tuple-element.46), channel_id=1, source_target_pairs={{0,0},{1,6},{2,5},{3,3},{4,4},{5,2},{6,1},{7,7},{8,8},{9,14},{10,1... | collective-permute-start | bytes 417800 | tf_op jit(solution)/shard_map/ppermute | solution.py:132
  58.7 5.5 %collective-permute-start.12 = (f32[62,8,128]{2,1,0:T(8,128)S(1)}, f32[62,8,128]{2,1,0:T(8,128)S(1)}, u32[]{:S(2)}, u32[]{:S(2)}) collective-permute-start(f32[62,8,128]{2,1,0:T(8,128)S(1)} %get-tuple-element.48), channel_id=1, source_target_pairs={{0,8},{8,0},{16,24},{24,16},{1,9},{9,1},{17,25},{25,17},{2,10},{10... | collective-permute-start | bytes 761864 | tf_op jit(solution)/shard_map/ppermute | solution.py:131
  58.8 7.6 %collective-permute-start.13 = (f32[62,8,128]{2,1,0:T(8,128)S(1)}, f32[62,8,128]{2,1,0:T(8,128)S(1)}, u32[]{:S(2)}, u32[]{:S(2)}) collective-permute-start(f32[62,8,128]{2,1,0:T(8,128)S(1)} %get-tuple-element.49), channel_id=1, source_target_pairs={{0,0},{8,16},{16,8},{24,24},{1,1},{9,17},{17,9},{25,25},{2,2},{10,... | collective-permute-start | bytes 761864 | tf_op jit(solution)/shard_map/ppermute | solution.py:131
  84.0 11.4 %collective-permute-start.14 = (f32[5,136,128]{2,1,0:T(8,128)S(1)}, f32[5,136,128]{2,1,0:T(8,128)S(1)}, u32[]{:S(2)}, u32[]{:S(2)}) collective-permute-start(f32[5,136,128]{2,1,0:T(8,128)S(1)} %get-tuple-element.51), channel_id=1, source_target_pairs={{0,4},{4,0},{1,5},{5,1},{2,6},{6,2},{3,7},{7,3},{8,12},{12,8},{9,1... | collective-permute-start | bytes 1044488 | tf_op jit(solution)/shard_map/ppermute | solution.py:131
  85.3 10.1 %collective-permute-start.15 = (f32[5,136,128]{2,1,0:T(8,128)S(1)}, f32[5,136,128]{2,1,0:T(8,128)S(1)}, u32[]{:S(2)}, u32[]{:S(2)}) collective-permute-start(f32[5,136,128]{2,1,0:T(8,128)S(1)} %get-tuple-element.52), channel_id=1, source_target_pairs={{0,1},{1,0},{2,3},{3,2},{4,5},{5,4},{6,7},{7,6},{8,9},{9,8},{10,11... | collective-permute-start | bytes 1044488 | tf_op jit(solution)/shard_map/ppermute | solution.py:131
  85.3 10.1 %collective-permute-start.16 = (f32[5,136,128]{2,1,0:T(8,128)S(1)}, f32[5,136,128]{2,1,0:T(8,128)S(1)}, u32[]{:S(2)}, u32[]{:S(2)}) collective-permute-start(f32[5,136,128]{2,1,0:T(8,128)S(1)} %get-tuple-element.53), channel_id=1, source_target_pairs={{0,0},{1,2},{2,1},{3,3},{4,4},{5,6},{6,5},{7,7},{8,8},{9,10},{10,9... | collective-permute-start | bytes 1044488 | tf_op jit(solution)/shard_map/ppermute | solution.py:131
  88.7 4.8 %collective-permute-start.17 = (f32[1,136,128]{2,1,0:T(8,128)S(1)}, f32[1,136,128]{2,1,0:T(8,128)S(1)}, u32[]{:S(2)}, u32[]{:S(2)}) collective-permute-start(f32[1,136,128]{2,1,0:T(8,128)S(1)} %get-tuple-element.54), channel_id=1, source_target_pairs={{0,5},{1,4},{2,7},{3,6},{4,1},{5,0},{6,3},{7,2},{8,13},{9,12},{10,... | collective-permute-start | bytes 208904 | tf_op jit(solution)/shard_map/ppermute | solution.py:132
  88.7 6.6 %collective-permute-start.18 = (f32[1,136,128]{2,1,0:T(8,128)S(1)}, f32[1,136,128]{2,1,0:T(8,128)S(1)}, u32[]{:S(2)}, u32[]{:S(2)}) collective-permute-start(f32[1,136,128]{2,1,0:T(8,128)S(1)} %get-tuple-element.55), channel_id=1, source_target_pairs={{0,0},{1,6},{2,5},{3,3},{4,4},{5,2},{6,1},{7,7},{8,8},{9,14},{10,1... | collective-permute-start | bytes 208904 | tf_op jit(solution)/shard_map/ppermute | solution.py:132
  96.1 3.9 %collective-permute-start.19 = (f32[34,8,128]{2,1,0:T(8,128)S(1)}, f32[34,8,128]{2,1,0:T(8,128)S(1)}, u32[]{:S(2)}, u32[]{:S(2)}) collective-permute-start(f32[34,8,128]{2,1,0:T(8,128)S(1)} %get-tuple-element.58), channel_id=1, source_target_pairs={{0,8},{1,9},{2,10},{3,11},{4,12},{5,13},{6,14},{7,15},{8,0},{9,1},... | collective-permute-start | bytes 417800 | tf_op jit(solution)/shard_map/ppermute | solution.py:132
  96.2 5.1 %collective-permute-start.20 = (f32[34,8,128]{2,1,0:T(8,128)S(1)}, f32[34,8,128]{2,1,0:T(8,128)S(1)}, u32[]{:S(2)}, u32[]{:S(2)}) collective-permute-start(f32[34,8,128]{2,1,0:T(8,128)S(1)} %get-tuple-element.59), channel_id=1, source_target_pairs={{0,4},{1,5},{2,6},{3,7},{4,0},{5,1},{6,2},{7,3},{8,16},{9,17},{10,... | collective-permute-start | bytes 417800 | tf_op jit(solution)/shard_map/ppermute | solution.py:132
  (3 other events, 22.5 us)

commit v7 on v6

--- a/solution.py
+++ b/solution.py
@@ -425,7 +425,7 @@
         lax.fori_loop(0, field.shape[0], one, 0, unroll=2)
 
 
-def widened(pos_ref, counts, modulus, ins_x):
+def widened(pos_ref, counts, modulus, beside, ins_x):
     rows = modulus.shape[1]
     sides = [side(pos_ref, 2, phase, counts[0]) for phase in range(len(ins_x))]
     _, region = spots((PAD, LANES))
@@ -440,12 +440,19 @@
             for target in (0, 1):
                 total = jnp.where(region == target, turn(value, (target - c) * WIDE), total)
             edges.append(total)
-        return jnp.concatenate([edges[0], modulus[z, PAD : rows - PAD, :], edges[1]], axis=0)
+        core = slice(PAD, rows - PAD)
+        if beside is None:
+            return jnp.concatenate([edges[0], modulus[z, core, :], edges[1]], axis=0), None
+        low, high = (pltpu.roll(edge, LANES - 1, 1) for edge in edges)
+        return (
+            jnp.concatenate([edges[0], modulus[z, core, :], edges[1]], axis=0),
+            jnp.concatenate([low, beside[z, core, :], high], axis=0),
+        )
 
     return plane
 
 
-def stiffness(field, modulus, first, last, shift, store):
+def stiffness(field, modulus, first, last, shift, store, unroll):
     rows = field.shape[1]
     _, region = spots((rows, LANES))
     scale = [
@@ -453,21 +460,22 @@
     ]
 
     def one(z, carry):
-        below, m = carry
+        below, m, beside = carry
         v = field[z - shift]
-        next_m = modulus(z + 1)
+        next_m, next_beside = modulus(z + 1)
         above = (m + next_m) * (field[z + 1 - shift] - v)
         gx = (m + pltpu.roll(m, rows - 1, 0)) * (pltpu.roll(v, rows - 1, 0) - v)
-        gy = (m + pltpu.roll(m, LANES - 1, 1)) * (pltpu.roll(v, LANES - 1, 1) - v)
+        beside = pltpu.roll(m, LANES - 1, 1) if beside is None else beside
+        gy = (m + beside) * (pltpu.roll(v, LANES - 1, 1) - v)
         total = SIGMA_SHIFT * m * v + scale[0] * (below - above)
         total = total + scale[1] * (pltpu.roll(gy, 1, 1) - gy)
         total = total + scale[2] * (pltpu.roll(gx, 1, 0) - gx)
         store(z, total)
-        return above, next_m
-
-    m = modulus(first)
-    below = (modulus(first - 1) + m) * (field[first - shift] - field[first - 1 - shift])
-    lax.fori_loop(first, last + 1, one, (below, m), unroll=4)
+        return above, next_m, next_beside
+
+    m, beside = modulus(first)
+    below = (modulus(first - 1)[0] + m) * (field[first - shift] - field[first - 1 - shift])
+    lax.fori_loop(first, last + 1, one, (below, m, beside), unroll=unroll)
 
 
 def groups_of(refs, sizes):
@@ -614,7 +622,9 @@
 
 
 def modulus_kernel(counts, sizes, pos_ref, modulus, *refs):
-    ins_y, ins_z, ins_yz, (modulus_out,), (wide,) = groups_of(refs, sizes[:3] + (1, 1))
+    ins_y, ins_z, ins_yz, (modulus_out, beside_out), (wide,) = groups_of(
+        refs, sizes[:3] + (2, 1)
+    )
     columns = modulus.shape[2]
     rows = columns + 2 * PAD
     count_x, count_y, count_z = counts
@@ -634,7 +644,11 @@
             wide[z, lane + BRICK + thin : lane + BRICK + REACH, :] = high_end
         wide[z, 3 * WIDE :, :] = jnp.zeros((LANES - 3 * WIDE, columns), F32)
         modulus_out[z, :PAD, :] = blank
-        modulus_out[z, PAD : PAD + columns, :] = wide[z].T
+        turned = wide[z].T
+        modulus_out[z, PAD : PAD + columns, :] = turned
+        beside_out[z, :PAD, :] = blank
+        beside_out[z, PAD : PAD + columns, :] = pltpu.roll(turned, LANES - 1, 1)
+        beside_out[z, rows - PAD :, :] = blank
         modulus_out[z, rows - PAD :, :] = blank
 
     for z in range(BRICK):
@@ -785,12 +799,12 @@
         on = inside & (z >= low_z) & (z < high_z)
         renewed[z - 1] = jnp.where(on, before(z - 1) - product, 0.0)
 
-    stiffness(field, widened(pos_ref, counts, modulus, ins_x), 1, WIDE - 2, 0, store)
+    stiffness(field, widened(pos_ref, counts, modulus, None, ins_x), 1, WIDE - 2, 0, store, 4)
     solve(lambda z: renewed[z], mid, solved, consts)
     write_messages(pos_ref, solved, REACH, counts, outs_y, outs_z, outs_yz)
 
 
-def last_kernel(counts, sizes, pos_ref, partial, modulus, moved, left, *refs):
+def last_kernel(counts, sizes, pos_ref, partial, modulus, beside, moved, left, *refs):
     ins_x, ins_modulus, (displacement, residual), (field,) = groups_of(
         refs, (sizes[3], sizes[3], 2, 1)
     )
@@ -810,11 +824,12 @@
 
     stiffness(
         field,
-        widened(pos_ref, counts, modulus, ins_modulus),
+        widened(pos_ref, counts, modulus, beside, ins_modulus),
         REACH,
         REACH + BRICK - 1,
         first,
         store,
+        8,
     )
 
 
@@ -895,10 +910,10 @@
         [(LENGTH, LANES, columns)],
     )
     from_x = exchange_x(out)
-    (modulus,) = call(
+    modulus, beside = call(
         bind(modulus_kernel),
         [pos, modulus_core, *margins],
-        [wide],
+        [wide, wide],
         [(WIDE, LANES, columns)],
         work=8000000,
     )
@@ -945,7 +960,7 @@
     )
     displacement, residual = call(
         bind(last_kernel),
-        [pos, partial, modulus, moved, left, *edges, *first_edges],
+        [pos, partial, modulus, beside, moved, left, *edges, *first_edges],
         [load.shape, load.shape],
         [(near, rows, LANES)],
         limit=32,

time: 111 us -> 109 us (0.982)
  transfers between devices with their start and end apart: 21 -> 21, of which waited for: 10 -> 10; matrix products, arithmetic and copies ran while one was open for 0% -> 0% of each run, Pallas kernels for 5% -> 6%
where the time goes in v7:
time: 109 us
  Pallas kernels  50.9 us (47%)
  starting transfers between devices  32 us (29%)
  waiting for transfers between devices  23.8 us (22%)
    pallas_call x11, Pallas kernels, call(): pl.pallas_call(kernel, out_shape=[jax.ShapeDtypeStruct(shape, F32) for sh...  50.9 us
    ppermute x11, starting transfers between devices, swap(): return lax.ppermute(value, name, list(enumerate(other)))  18.7 us
    ppermute x10, waiting for transfers between devices, swap(): return lax.ppermute(value, names, pairs)  16.9 us
    ppermute x10, starting transfers between devices, swap(): return lax.ppermute(value, names, pairs)  13.2 us
    ppermute x11, waiting for transfers between devices, swap(): return lax.ppermute(value, name, list(enumerate(other)))  6.86 us
  transfers between devices with their start and end apart: 21, of which 10 were waited for; matrix products, arithmetic and copies ran while one was open for 0% of the time, Pallas kernels for 6%

profile of v7, /device:TPU:9, one launch (start us, length us, event | category | flops | bytes accessed | tf_op | source)
XLA Modules:
  0.0 109.0 jit_solution(15927837523916361071)
XLA Ops:
  1.4 3.7 %shard_map.149 = (f32[32,32,128]{2,1,0:T(8,128)}, f32[68,8,128]{2,1,0:T(8,128)}, f32[17,32,128]{2,1,0:T(8,128)}, f32[17,32,128]{2,1,0:T(8,128)}, f32[11,8,128]{2,1,0:T(8,128)}, /*index=5*/f32[11,8,128]{2,1,0:T(8,128)}) custom-call(s32[3]{0:T(128)} %pad_add_fusion.pos_ref, f32[16]{0:T(128)} %table_in.1, f32[3,32,32,128]{3,2,1,0:T(8,128)} %load.1, ...), custom_call_target="tpu_custom_call" | custom-call | tf_op jit(solution)/shard_map/pallas_call | solution.py:837
  5.1 1.3 %collective-permute-start = (f32[68,8,128]{2,1,0:T(8,128)}, f32[68,8,128]{2,1,0:T(8,128)S(1)}, u32[]{:S(2)}, u32[]{:S(2)}) collective-permute-start(f32[68,8,128]{2,1,0:T(8,128)} %get-tuple-element.33), channel_id=1, source_target_pairs={{0,4},{4,0},{1,5},{5,1},{2,6},{6,2},{3,7},{7,3},{8,12},{12,8},{9,1... | collective-permute-start | bytes 835592 | tf_op jit(solution)/shard_map/ppermute | solution.py:131
  6.6 2.4 %collective-permute-start.2 = (f32[17,32,128]{2,1,0:T(8,128)}, f32[17,32,128]{2,1,0:T(8,128)S(1)}, u32[]{:S(2)}, u32[]{:S(2)}) collective-permute-start(f32[17,32,128]{2,1,0:T(8,128)} %get-tuple-element.35), channel_id=1, source_target_pairs={{0,8},{1,2},{2,1},{3,11},{4,12},{5,6},{6,5},{7,15},{8,0},{9,10},{1... | collective-permute-start | bytes 835592 | tf_op jit(solution)/shard_map/ppermute | solution.py:132
  9.1 2.3 %collective-permute-start.4 = (f32[11,8,128]{2,1,0:T(8,128)}, f32[11,8,128]{2,1,0:T(8,128)S(1)}, u32[]{:S(2)}, u32[]{:S(2)}) collective-permute-start(f32[11,8,128]{2,1,0:T(8,128)} %get-tuple-element.37), channel_id=1, source_target_pairs={{0,8},{1,6},{2,5},{3,11},{4,12},{5,2},{6,1},{7,15},{8,0},{9,14},{1... | collective-permute-start | bytes 135176 | tf_op jit(solution)/shard_map/ppermute | solution.py:132
  11.3 3.1 %collective-permute-done.3.refs_3_ = f32[11,8,128]{2,1,0:T(8,128)S(1)} collective-permute-done((f32[11,8,128]{2,1,0:T(8,128)}, f32[11,8,128]{2,1,0:T(8,128)S(1)}, u32[]{:S(2)}, u32[]{:S(2)}) %collective-permute-start.3) | collective-permute-done | bytes 45088 | tf_op jit(solution)/shard_map/ppermute | solution.py:132
  14.5 1.4 %collective-permute-done.4.refs_4_ = f32[11,8,128]{2,1,0:T(8,128)S(1)} collective-permute-done((f32[11,8,128]{2,1,0:T(8,128)}, f32[11,8,128]{2,1,0:T(8,128)S(1)}, u32[]{:S(2)}, u32[]{:S(2)}) %collective-permute-start.4) | collective-permute-done | bytes 45088 | tf_op jit(solution)/shard_map/ppermute | solution.py:132
  16.5 2.1 %shard_map.150 = (f32[40,144,128]{2,1,0:T(8,128)S(1)}, f32[40,8,128]{2,1,0:T(8,128)S(1)}, f32[40,8,128]{2,1,0:T(8,128)S(1)}) custom-call(s32[3]{0:T(128)S(1)} %copy-done.12, f32[3,32,32,128]{3,2,1,0:T(8,128)S(1)} %copy-done, f32[68,8,128]{2,1,0:T(8,128)S(1)} %collective-permute-done.refs_0_, f32[17,32,128]{2,1,0:T(8,128)S(1)} %collective-permute-done.1.refs_1_, ...), custom_call_target="tpu_custom_call" | custom-call | tf_op jit(solution)/shard_map/pallas_call | solution.py:837
  18.6 1.9 %collective-permute-start.5 = (f32[40,8,128]{2,1,0:T(8,128)S(1)}, f32[40,8,128]{2,1,0:T(8,128)S(1)}, u32[]{:S(2)}, u32[]{:S(2)}) collective-permute-start(f32[40,8,128]{2,1,0:T(8,128)S(1)} %get-tuple-element.39), channel_id=1, source_target_pairs={{0,8},{8,0},{16,24},{24,16},{1,9},{9,1},{17,25},{25,17},{2,10},{10... | collective-permute-start | bytes 491528 | tf_op jit(solution)/shard_map/ppermute | solution.py:131
  20.6 3.0 %collective-permute-start.6 = (f32[40,8,128]{2,1,0:T(8,128)S(1)}, f32[40,8,128]{2,1,0:T(8,128)S(1)}, u32[]{:S(2)}, u32[]{:S(2)}) collective-permute-start(f32[40,8,128]{2,1,0:T(8,128)S(1)} %get-tuple-element.40), channel_id=1, source_target_pairs={{0,0},{8,16},{16,8},{24,24},{1,1},{9,17},{17,9},{25,25},{2,2},{10,... | collective-permute-start | bytes 491528 | tf_op jit(solution)/shard_map/ppermute | solution.py:131
  23.6 3.6 %collective-permute-done.6.refs_1_ = f32[40,8,128]{2,1,0:T(8,128)S(1)} collective-permute-done((f32[40,8,128]{2,1,0:T(8,128)S(1)}, f32[40,8,128]{2,1,0:T(8,128)S(1)}, u32[]{:S(2)}, u32[]{:S(2)}) %collective-permute-start.6) | collective-permute-done | bytes 163872 | tf_op jit(solution)/shard_map/ppermute | solution.py:131
  27.3 8.5 %shard_map.151 = (f32[20,136,128]{2,1,0:T(8,128)S(1)}, f32[40,160,128]{2,1,0:T(8,128)S(1)}, f32[9,136,128]{2,1,0:T(8,128)S(1)}, f32[9,136,128]{2,1,0:T(8,128)S(1...) custom-call(s32[3]{0:T(128)S(1)} %copy-done.12, f32[40,144,128]{2,1,0:T(8,128)S(1)} %get-tuple-element.38.residual, ...), custom_call_target="tpu_custom_call" | custom-call | tf_op jit(solution)/shard_map/pallas_call | solution.py:837
  35.8 3.1 %shard_map.152 = (f32[20,136,128]{2,1,0:T(8,128)S(1)}, f32[10,136,128]{2,1,0:T(8,128)S(1)}) custom-call(s32[3]{0:T(128)S(1)} %copy-done.12, f32[20,136,128]{2,1,0:T(8,128)S(1)} %get-tuple-element.41.outer.refs_0_, f32[40,160,128]{2,1,0:T(8,128)S(1)} %get-tuple-element.42.mid, bf16[136,480]{1,0:T(8,128)(2,1)S(1)} %copy-done.1, bf16[256,256]{1,0:T(8,128)(2,1)S(1)} %copy-done.2), custom_call_target="tpu_custom_call" | custom-call | flops 8000000 | bytes 8000000 | tf_op jit(solution)/shard_map/pallas_call | solution.py:837
  38.9 1.3 %collective-permute-start.7 = (f32[10,136,128]{2,1,0:T(8,128)S(1)}, f32[10,136,128]{2,1,0:T(8,128)S(1)}, u32[]{:S(2)}, u32[]{:S(2)}) collective-permute-start(f32[10,136,128]{2,1,0:T(8,128)S(1)} %get-tuple-element.44), channel_id=1, source_target_pairs={{0,4},{4,0},{1,5},{5,1},{2,6},{6,2},{3,7},{7,3},{8,12},{12,8},{9,1... | collective-permute-start | bytes 2088968 | tf_op jit(solution)/shard_map/ppermute | solution.py:131
  40.2 3.4 %collective-permute-start.9 = (f32[9,136,128]{2,1,0:T(8,128)S(1)}, f32[9,136,128]{2,1,0:T(8,128)S(1)}, u32[]{:S(2)}, u32[]{:S(2)}) collective-permute-start(f32[9,136,128]{2,1,0:T(8,128)S(1)} %get-tuple-element.46), channel_id=1, source_target_pairs={{0,0},{1,2},{2,1},{3,3},{4,4},{5,6},{6,5},{7,7},{8,8},{9,10},{10,9... | collective-permute-start | bytes 1880072 | tf_op jit(solution)/shard_map/ppermute | solution.py:131
  43.7 3.0 %collective-permute-start.11 = (f32[2,136,128]{2,1,0:T(8,128)S(1)}, f32[2,136,128]{2,1,0:T(8,128)S(1)}, u32[]{:S(2)}, u32[]{:S(2)}) collective-permute-start(f32[2,136,128]{2,1,0:T(8,128)S(1)} %get-tuple-element.48), channel_id=1, source_target_pairs={{0,0},{1,6},{2,5},{3,3},{4,4},{5,2},{6,1},{7,7},{8,8},{9,14},{10,1... | collective-permute-start | bytes 417800 | tf_op jit(solution)/shard_map/ppermute | solution.py:132
  46.7 2.2 %shard_map.154 = (f32[42,144,128]{2,1,0:T(8,128)S(1)}, f32[42,144,128]{2,1,0:T(8,128)S(1)}) custom-call(s32[3]{0:T(128)S(1)} %copy-done.13, f32[32,32,128]{2,1,0:T(8,128)S(1)} %copy-done.10, f32[68,8,128]{2,1,0:T(8,128)S(1)} %collective-permute-done.refs_0_, f32[17,32,128]{2,1,0:T(8,128)S(1)} %collective-permute-done.1.refs_1_, ...), custom_call_target="tpu_custom_call" | custom-call | flops 8000000 | bytes 8000000 | tf_op jit(solution)/shard_map/pallas_call | solution.py:837
  48.9 5.7 %collective-permute-done.10.refs_5_ = f32[2,136,128]{2,1,0:T(8,128)S(1)} collective-permute-done((f32[2,136,128]{2,1,0:T(8,128)S(1)}, f32[2,136,128]{2,1,0:T(8,128)S(1)}, u32[]{:S(2)}, u32[]{:S(2)}) %collective-permute-start.10) | collective-permute-done | bytes 139296 | tf_op jit(solution)/shard_map/ppermute | solution.py:132
  54.6 1.9 %collective-permute-done.11.refs_6_ = f32[2,136,128]{2,1,0:T(8,128)S(1)} collective-permute-done((f32[2,136,128]{2,1,0:T(8,128)S(1)}, f32[2,136,128]{2,1,0:T(8,128)S(1)}, u32[]{:S(2)}, u32[]{:S(2)}) %collective-permute-start.11) | collective-permute-done | bytes 139296 | tf_op jit(solution)/shard_map/ppermute | solution.py:132
  57.5 1.1 shard_map.155
  58.7 3.0 %collective-permute-start.13 = (f32[62,8,128]{2,1,0:T(8,128)S(1)}, f32[62,8,128]{2,1,0:T(8,128)S(1)}, u32[]{:S(2)}, u32[]{:S(2)}) collective-permute-start(f32[62,8,128]{2,1,0:T(8,128)S(1)} %get-tuple-element.52), channel_id=1, source_target_pairs={{0,0},{8,16},{16,8},{24,24},{1,1},{9,17},{17,9},{25,25},{2,2},{10,... | collective-permute-start | bytes 761864 | tf_op jit(solution)/shard_map/ppermute | solution.py:131
  61.7 2.3 %shard_map.153.partial = f32[42,144,128]{2,1,0:T(8,128)S(1)} custom-call(s32[3]{0:T(128)S(1)} %copy-done.13, f32[20,136,128]{2,1,0:T(8,128)S(1)} %get-tuple-element.41.outer.refs_0_, f32[20,136,128]{2,1,0:T(8,128)S(1)} %get-tuple-element.43.refs_1_, f32[10,136,128]{2,1,0:T(8,128)S(1)} %collective-permute-done.7.refs_2_, ...), custom_call_target="tpu_custom_call" | custom-call | flops 8000000 | bytes 8000000 | tf_op jit(solution)/shard_map/pallas_call | solution.py:837
  64.1 2.2 %collective-permute-done.13.refs_3_ = f32[62,8,128]{2,1,0:T(8,128)S(1)} collective-permute-done((f32[62,8,128]{2,1,0:T(8,128)S(1)}, f32[62,8,128]{2,1,0:T(8,128)S(1)}, u32[]{:S(2)}, u32[]{:S(2)}) %collective-permute-start.13) | collective-permute-done | bytes 253984 | tf_op jit(solution)/shard_map/ppermute | solution.py:131
  66.3 17.6 %shard_map.156 = (f32[40,136,128]{2,1,0:T(8,128)S(1)}, f32[42,144,128]{2,1,0:T(8,128)S(1)}, f32[40,144,128]{2,1,0:T(8,128)S(1)}, f32[5,136,128]{2,1,0:T(8,128)S(...) custom-call(s32[3]{0:T(128)S(1)} %copy-done.13, ...), custom_call_target="tpu_custom_call" | custom-call | tf_op jit(solution)/shard_map/pallas_call | solution.py:837
  83.9 1.3 %collective-permute-start.14 = (f32[5,136,128]{2,1,0:T(8,128)S(1)}, f32[5,136,128]{2,1,0:T(8,128)S(1)}, u32[]{:S(2)}, u32[]{:S(2)}) collective-permute-start(f32[5,136,128]{2,1,0:T(8,128)S(1)} %get-tuple-element.54), channel_id=1, source_target_pairs={{0,4},{4,0},{1,5},{5,1},{2,6},{6,2},{3,7},{7,3},{8,12},{12,8},{9,1... | collective-permute-start | bytes 1044488 | tf_op jit(solution)/shard_map/ppermute | solution.py:131
  85.2 3.4 %collective-permute-start.16 = (f32[5,136,128]{2,1,0:T(8,128)S(1)}, f32[5,136,128]{2,1,0:T(8,128)S(1)}, u32[]{:S(2)}, u32[]{:S(2)}) collective-permute-start(f32[5,136,128]{2,1,0:T(8,128)S(1)} %get-tuple-element.56), channel_id=1, source_target_pairs={{0,0},{1,2},{2,1},{3,3},{4,4},{5,6},{6,5},{7,7},{8,8},{9,10},{10,9... | collective-permute-start | bytes 1044488 | tf_op jit(solution)/shard_map/ppermute | solution.py:131
  88.7 3.0 %collective-permute-start.18 = (f32[1,136,128]{2,1,0:T(8,128)S(1)}, f32[1,136,128]{2,1,0:T(8,128)S(1)}, u32[]{:S(2)}, u32[]{:S(2)}) collective-permute-start(f32[1,136,128]{2,1,0:T(8,128)S(1)} %get-tuple-element.58), channel_id=1, source_target_pairs={{0,0},{1,6},{2,5},{3,3},{4,4},{5,2},{6,1},{7,7},{8,8},{9,14},{10,1... | collective-permute-start | bytes 208904 | tf_op jit(solution)/shard_map/ppermute | solution.py:132
  91.7 1.7 %collective-permute-done.17.refs_4_ = f32[1,136,128]{2,1,0:T(8,128)S(1)} collective-permute-done((f32[1,136,128]{2,1,0:T(8,128)S(1)}, f32[1,136,128]{2,1,0:T(8,128)S(1)}, u32[]{:S(2)}, u32[]{:S(2)}) %collective-permute-start.17) | collective-permute-done | bytes 69664 | tf_op jit(solution)/shard_map/ppermute | solution.py:132
  93.4 1.9 %collective-permute-done.18.refs_5_ = f32[1,136,128]{2,1,0:T(8,128)S(1)} collective-permute-done((f32[1,136,128]{2,1,0:T(8,128)S(1)}, f32[1,136,128]{2,1,0:T(8,128)S(1)}, u32[]{:S(2)}, u32[]{:S(2)}) %collective-permute-start.18) | collective-permute-done | bytes 69664 | tf_op jit(solution)/shard_map/ppermute | solution.py:132
  96.1 2.1 %collective-permute-start.20 = (f32[34,8,128]{2,1,0:T(8,128)S(1)}, f32[34,8,128]{2,1,0:T(8,128)S(1)}, u32[]{:S(2)}, u32[]{:S(2)}) collective-permute-start(f32[34,8,128]{2,1,0:T(8,128)S(1)} %get-tuple-element.63), channel_id=1, source_target_pairs={{0,4},{1,5},{2,6},{3,7},{4,0},{5,1},{6,2},{7,3},{8,16},{9,17},{10,... | collective-permute-start | bytes 417800 | tf_op jit(solution)/shard_map/ppermute | solution.py:132
  98.2 1.8 %shard_map.157.partial = f32[34,144,128]{2,1,0:T(8,128)S(1)} custom-call(s32[3]{0:T(128)S(1)} %copy-done.13, f32[40,136,128]{2,1,0:T(8,128)S(1)} %get-tuple-element.53.refs_0_, f32[5,136,128]{2,1,0:T(8,128)S(1)} %collective-permute-done.14.refs_1_, f32[5,136,128]{2,1,0:T(8,128)S(1)} %collective-permute-done.15.refs_2_, ...), custom_call_target="tpu_custom_call" | custom-call | flops 8000000 | bytes 8000000 | tf_op jit(solution)/shard_map/pallas_call | solution.py:837
  100.0 1.2 %collective-permute-done.20.refs_1_ = f32[34,8,128]{2,1,0:T(8,128)S(1)} collective-permute-done((f32[34,8,128]{2,1,0:T(8,128)S(1)}, f32[34,8,128]{2,1,0:T(8,128)S(1)}, u32[]{:S(2)}, u32[]{:S(2)}) %collective-permute-start.20) | collective-permute-done | bytes 139296 | tf_op jit(solution)/shard_map/ppermute | solution.py:132
  101.3 7.7 %shard_map.159 = (f32[3,32,32,128]{3,2,1,0:T(8,128)}, f32[3,32,32,128]{3,2,1,0:T(8,128)}) custom-call(s32[3]{0:T(128)S(1)} %copy-done.13, f32[34,144,128]{2,1,0:T(8,128)S(1)} %shard_map.157.partial, f32[42,144,128]{2,1,0:T(8,128)S(1)} %get-tuple-element.50.refs_7_.modulus, f32[42,144,128]{2,1,0:T(8,128)S(1)} %get-tuple-element.59.beside, ...), custom_call_target="tpu_custom_call" | custom-call | tf_op jit(solution)/shard_map/pallas_call | solution.py:837
  (50 shorter events, 3.6 us)
Async XLA Ops:
  0.6 26.6 %copy-start.2 = (bf16[256,256]{1,0:T(8,128)(2,1)S(1)}, bf16[256,256]{1,0:T(8,128)(2,1)}, u32[]{:S(2)}) copy-start(bf16[256,256]{1,0:T(8,128)(2,1)} %constant.39.clone.refs_9_.back_y.refs_11_) | copy-start | bytes 393220
  0.6 26.6 %copy-start.1 = (bf16[136,480]{1,0:T(8,128)(2,1)S(1)}, bf16[136,480]{1,0:T(8,128)(2,1)}, u32[]{:S(2)}) copy-start(bf16[136,480]{1,0:T(8,128)(2,1)} %constant.38.clone.refs_8_.back_x.refs_10_) | copy-start | bytes 391684
  0.7 26.5 %copy-start.3 = (f32[40,8,128]{2,1,0:T(8,128)S(1)}, f32[40,8,128]{2,1,0:T(8,128)}, u32[]{:S(2)}) copy-start(f32[40,8,128]{2,1,0:T(8,128)} %constant.41.clone.refs_11_.refs_13_) | copy-start | bytes 491524
  0.7 26.5 %copy-start.4 = (bf16[160,480]{1,0:T(8,128)(2,1)S(1)}, bf16[160,480]{1,0:T(8,128)(2,1)}, u32[]{:S(2)}) copy-start(bf16[160,480]{1,0:T(8,128)(2,1)} %constant.37.clone.refs_7_.refs_9_) | copy-start | bytes 460804
  0.7 26.5 %copy-start.5 = (bf16[160,480]{1,0:T(8,128)(2,1)S(1)}, bf16[160,480]{1,0:T(8,128)(2,1)}, u32[]{:S(2)}) copy-start(bf16[160,480]{1,0:T(8,128)(2,1)} %constant.36.clone.refs_6_.refs_8_) | copy-start | bytes 460804
  0.7 26.5 %copy-start.6 = (bf16[160,480]{1,0:T(8,128)(2,1)S(1)}, bf16[160,480]{1,0:T(8,128)(2,1)}, u32[]{:S(2)}) copy-start(bf16[160,480]{1,0:T(8,128)(2,1)} %constant.35.clone.refs_5_.refs_7_) | copy-start | bytes 460804
  0.7 26.5 %copy-start.7 = (bf16[160,480]{1,0:T(8,128)(2,1)S(1)}, bf16[160,480]{1,0:T(8,128)(2,1)}, u32[]{:S(2)}) copy-start(bf16[160,480]{1,0:T(8,128)(2,1)} %constant.34.clone.refs_4_.refs_6_) | copy-start | bytes 460804
  0.7 15.2 %copy-start = (f32[3,32,32,128]{3,2,1,0:T(8,128)S(1)}, f32[3,32,32,128]{3,2,1,0:T(8,128)}, u32[]{:S(2)}) copy-start(f32[3,32,32,128]{3,2,1,0:T(8,128)} %load.1) | copy-start | bytes 4718596
  0.7 26.5 %copy-start.8 = (bf16[160,432]{1,0:T(8,128)(2,1)S(1)}, bf16[160,432]{1,0:T(8,128)(2,1)}, u32[]{:S(2)}) copy-start(bf16[160,432]{1,0:T(8,128)(2,1)} %constant.33.clone.refs_3_.refs_5_) | copy-start | bytes 414724
  0.7 26.5 %copy-start.9 = (bf16[256,256]{1,0:T(8,128)(2,1)S(1)}, bf16[256,256]{1,0:T(8,128)(2,1)}, u32[]{:S(2)}) copy-start(bf16[256,256]{1,0:T(8,128)(2,1)} %constant.32.clone.refs_2_.refs_4_) | copy-start | bytes 393220
  0.8 26.5 %copy-start.11 = (f32[160,128]{1,0:T(8,128)S(1)}, f32[160,128]{1,0:T(8,128)}, u32[]{:S(2)}) copy-start(f32[160,128]{1,0:T(8,128)} %constant.40.clone.refs_10_.refs_12_) | copy-start | bytes 245764
  5.1 10.8 %collective-permute-start = (f32[68,8,128]{2,1,0:T(8,128)}, f32[68,8,128]{2,1,0:T(8,128)S(1)}, u32[]{:S(2)}, u32[]{:S(2)}) collective-permute-start(f32[68,8,128]{2,1,0:T(8,128)} %get-tuple-element.33), channel_id=1, source_target_pairs={{0,4},{4,0},{1,5},{5,1},{2,6},{6,2},{3,7},{7,3},{8,12},{12,8},{9,1... | collective-permute-start | bytes 835592 | tf_op jit(solution)/shard_map/ppermute | solution.py:131
  6.4 9.5 %collective-permute-start.1 = (f32[17,32,128]{2,1,0:T(8,128)}, f32[17,32,128]{2,1,0:T(8,128)S(1)}, u32[]{:S(2)}, u32[]{:S(2)}) collective-permute-start(f32[17,32,128]{2,1,0:T(8,128)} %get-tuple-element.34), channel_id=1, source_target_pairs={{0,1},{1,0},{2,3},{3,2},{4,5},{5,4},{6,7},{7,6},{8,9},{9,8},{10,11... | collective-permute-start | bytes 835592 | tf_op jit(solution)/shard_map/ppermute | solution.py:132
  6.6 9.3 %collective-permute-start.2 = (f32[17,32,128]{2,1,0:T(8,128)}, f32[17,32,128]{2,1,0:T(8,128)S(1)}, u32[]{:S(2)}, u32[]{:S(2)}) collective-permute-start(f32[17,32,128]{2,1,0:T(8,128)} %get-tuple-element.35), channel_id=1, source_target_pairs={{0,8},{1,2},{2,1},{3,11},{4,12},{5,6},{6,5},{7,15},{8,0},{9,10},{1... | collective-permute-start | bytes 835592 | tf_op jit(solution)/shard_map/ppermute | solution.py:132
  9.0 5.4 %collective-permute-start.3 = (f32[11,8,128]{2,1,0:T(8,128)}, f32[11,8,128]{2,1,0:T(8,128)S(1)}, u32[]{:S(2)}, u32[]{:S(2)}) collective-permute-start(f32[11,8,128]{2,1,0:T(8,128)} %get-tuple-element.36), channel_id=1, source_target_pairs={{0,5},{1,4},{2,7},{3,6},{4,1},{5,0},{6,3},{7,2},{8,13},{9,12},{10,... | collective-permute-start | bytes 135176 | tf_op jit(solution)/shard_map/ppermute | solution.py:132
  9.1 6.8 %collective-permute-start.4 = (f32[11,8,128]{2,1,0:T(8,128)}, f32[11,8,128]{2,1,0:T(8,128)S(1)}, u32[]{:S(2)}, u32[]{:S(2)}) collective-permute-start(f32[11,8,128]{2,1,0:T(8,128)} %get-tuple-element.37), channel_id=1, source_target_pairs={{0,8},{1,6},{2,5},{3,11},{4,12},{5,2},{6,1},{7,15},{8,0},{9,14},{1... | collective-permute-start | bytes 135176 | tf_op jit(solution)/shard_map/ppermute | solution.py:132
  18.6 5.0 %collective-permute-start.5 = (f32[40,8,128]{2,1,0:T(8,128)S(1)}, f32[40,8,128]{2,1,0:T(8,128)S(1)}, u32[]{:S(2)}, u32[]{:S(2)}) collective-permute-start(f32[40,8,128]{2,1,0:T(8,128)S(1)} %get-tuple-element.39), channel_id=1, source_target_pairs={{0,8},{8,0},{16,24},{24,16},{1,9},{9,1},{17,25},{25,17},{2,10},{10... | collective-permute-start | bytes 491528 | tf_op jit(solution)/shard_map/ppermute | solution.py:131
  20.6 6.6 %collective-permute-start.6 = (f32[40,8,128]{2,1,0:T(8,128)S(1)}, f32[40,8,128]{2,1,0:T(8,128)S(1)}, u32[]{:S(2)}, u32[]{:S(2)}) collective-permute-start(f32[40,8,128]{2,1,0:T(8,128)S(1)} %get-tuple-element.40), channel_id=1, source_target_pairs={{0,0},{8,16},{16,8},{24,24},{1,1},{9,17},{17,9},{25,25},{2,2},{10,... | collective-permute-start | bytes 491528 | tf_op jit(solution)/shard_map/ppermute | solution.py:131
  38.9 18.6 %collective-permute-start.7 = (f32[10,136,128]{2,1,0:T(8,128)S(1)}, f32[10,136,128]{2,1,0:T(8,128)S(1)}, u32[]{:S(2)}, u32[]{:S(2)}) collective-permute-start(f32[10,136,128]{2,1,0:T(8,128)S(1)} %get-tuple-element.44), channel_id=1, source_target_pairs={{0,4},{4,0},{1,5},{5,1},{2,6},{6,2},{3,7},{7,3},{8,12},{12,8},{9,1... | collective-permute-start | bytes 2088968 | tf_op jit(solution)/shard_map/ppermute | solution.py:131
  40.2 16.3 %collective-permute-start.8 = (f32[9,136,128]{2,1,0:T(8,128)S(1)}, f32[9,136,128]{2,1,0:T(8,128)S(1)}, u32[]{:S(2)}, u32[]{:S(2)}) collective-permute-start(f32[9,136,128]{2,1,0:T(8,128)S(1)} %get-tuple-element.45), channel_id=1, source_target_pairs={{0,1},{1,0},{2,3},{3,2},{4,5},{5,4},{6,7},{7,6},{8,9},{9,8},{10,11... | collective-permute-start | bytes 1880072 | tf_op jit(solution)/shard_map/ppermute | solution.py:131
  40.2 16.3 %collective-permute-start.9 = (f32[9,136,128]{2,1,0:T(8,128)S(1)}, f32[9,136,128]{2,1,0:T(8,128)S(1)}, u32[]{:S(2)}, u32[]{:S(2)}) collective-permute-start(f32[9,136,128]{2,1,0:T(8,128)S(1)} %get-tuple-element.46), channel_id=1, source_target_pairs={{0,0},{1,2},{2,1},{3,3},{4,4},{5,6},{6,5},{7,7},{8,8},{9,10},{10,9... | collective-permute-start | bytes 1880072 | tf_op jit(solution)/shard_map/ppermute | solution.py:131
  43.6 11.0 %collective-permute-start.10 = (f32[2,136,128]{2,1,0:T(8,128)S(1)}, f32[2,136,128]{2,1,0:T(8,128)S(1)}, u32[]{:S(2)}, u32[]{:S(2)}) collective-permute-start(f32[2,136,128]{2,1,0:T(8,128)S(1)} %get-tuple-element.47), channel_id=1, source_target_pairs={{0,5},{1,4},{2,7},{3,6},{4,1},{5,0},{6,3},{7,2},{8,13},{9,12},{10,... | collective-permute-start | bytes 417800 | tf_op jit(solution)/shard_map/ppermute | solution.py:132
  43.7 12.8 %collective-permute-start.11 = (f32[2,136,128]{2,1,0:T(8,128)S(1)}, f32[2,136,128]{2,1,0:T(8,128)S(1)}, u32[]{:S(2)}, u32[]{:S(2)}) collective-permute-start(f32[2,136,128]{2,1,0:T(8,128)S(1)} %get-tuple-element.48), channel_id=1, source_target_pairs={{0,0},{1,6},{2,5},{3,3},{4,4},{5,2},{6,1},{7,7},{8,8},{9,14},{10,1... | collective-permute-start | bytes 417800 | tf_op jit(solution)/shard_map/ppermute | solution.py:132
  58.6 5.5 %collective-permute-start.12 = (f32[62,8,128]{2,1,0:T(8,128)S(1)}, f32[62,8,128]{2,1,0:T(8,128)S(1)}, u32[]{:S(2)}, u32[]{:S(2)}) collective-permute-start(f32[62,8,128]{2,1,0:T(8,128)S(1)} %get-tuple-element.51), channel_id=1, source_target_pairs={{0,8},{8,0},{16,24},{24,16},{1,9},{9,1},{17,25},{25,17},{2,10},{10... | collective-permute-start | bytes 761864 | tf_op jit(solution)/shard_map/ppermute | solution.py:131
  58.7 7.6 %collective-permute-start.13 = (f32[62,8,128]{2,1,0:T(8,128)S(1)}, f32[62,8,128]{2,1,0:T(8,128)S(1)}, u32[]{:S(2)}, u32[]{:S(2)}) collective-permute-start(f32[62,8,128]{2,1,0:T(8,128)S(1)} %get-tuple-element.52), channel_id=1, source_target_pairs={{0,0},{8,16},{16,8},{24,24},{1,1},{9,17},{17,9},{25,25},{2,2},{10,... | collective-permute-start | bytes 761864 | tf_op jit(solution)/shard_map/ppermute | solution.py:131
  83.9 11.4 %collective-permute-start.14 = (f32[5,136,128]{2,1,0:T(8,128)S(1)}, f32[5,136,128]{2,1,0:T(8,128)S(1)}, u32[]{:S(2)}, u32[]{:S(2)}) collective-permute-start(f32[5,136,128]{2,1,0:T(8,128)S(1)} %get-tuple-element.54), channel_id=1, source_target_pairs={{0,4},{4,0},{1,5},{5,1},{2,6},{6,2},{3,7},{7,3},{8,12},{12,8},{9,1... | collective-permute-start | bytes 1044488 | tf_op jit(solution)/shard_map/ppermute | solution.py:131
  85.2 10.1 %collective-permute-start.15 = (f32[5,136,128]{2,1,0:T(8,128)S(1)}, f32[5,136,128]{2,1,0:T(8,128)S(1)}, u32[]{:S(2)}, u32[]{:S(2)}) collective-permute-start(f32[5,136,128]{2,1,0:T(8,128)S(1)} %get-tuple-element.55), channel_id=1, source_target_pairs={{0,1},{1,0},{2,3},{3,2},{4,5},{5,4},{6,7},{7,6},{8,9},{9,8},{10,11... | collective-permute-start | bytes 1044488 | tf_op jit(solution)/shard_map/ppermute | solution.py:131
  85.2 10.1 %collective-permute-start.16 = (f32[5,136,128]{2,1,0:T(8,128)S(1)}, f32[5,136,128]{2,1,0:T(8,128)S(1)}, u32[]{:S(2)}, u32[]{:S(2)}) collective-permute-start(f32[5,136,128]{2,1,0:T(8,128)S(1)} %get-tuple-element.56), channel_id=1, source_target_pairs={{0,0},{1,2},{2,1},{3,3},{4,4},{5,6},{6,5},{7,7},{8,8},{9,10},{10,9... | collective-permute-start | bytes 1044488 | tf_op jit(solution)/shard_map/ppermute | solution.py:131
  88.6 4.8 %collective-permute-start.17 = (f32[1,136,128]{2,1,0:T(8,128)S(1)}, f32[1,136,128]{2,1,0:T(8,128)S(1)}, u32[]{:S(2)}, u32[]{:S(2)}) collective-permute-start(f32[1,136,128]{2,1,0:T(8,128)S(1)} %get-tuple-element.57), channel_id=1, source_target_pairs={{0,5},{1,4},{2,7},{3,6},{4,1},{5,0},{6,3},{7,2},{8,13},{9,12},{10,... | collective-permute-start | bytes 208904 | tf_op jit(solution)/shard_map/ppermute | solution.py:132
  88.7 6.6 %collective-permute-start.18 = (f32[1,136,128]{2,1,0:T(8,128)S(1)}, f32[1,136,128]{2,1,0:T(8,128)S(1)}, u32[]{:S(2)}, u32[]{:S(2)}) collective-permute-start(f32[1,136,128]{2,1,0:T(8,128)S(1)} %get-tuple-element.58), channel_id=1, source_target_pairs={{0,0},{1,6},{2,5},{3,3},{4,4},{5,2},{6,1},{7,7},{8,8},{9,14},{10,1... | collective-permute-start | bytes 208904 | tf_op jit(solution)/shard_map/ppermute | solution.py:132
  96.1 4.0 %collective-permute-start.19 = (f32[34,8,128]{2,1,0:T(8,128)S(1)}, f32[34,8,128]{2,1,0:T(8,128)S(1)}, u32[]{:S(2)}, u32[]{:S(2)}) collective-permute-start(f32[34,8,128]{2,1,0:T(8,128)S(1)} %get-tuple-element.62), channel_id=1, source_target_pairs={{0,8},{1,9},{2,10},{3,11},{4,12},{5,13},{6,14},{7,15},{8,0},{9,1},... | collective-permute-start | bytes 417800 | tf_op jit(solution)/shard_map/ppermute | solution.py:132
  96.1 5.1 %collective-permute-start.20 = (f32[34,8,128]{2,1,0:T(8,128)S(1)}, f32[34,8,128]{2,1,0:T(8,128)S(1)}, u32[]{:S(2)}, u32[]{:S(2)}) collective-permute-start(f32[34,8,128]{2,1,0:T(8,128)S(1)} %get-tuple-element.63), channel_id=1, source_target_pairs={{0,4},{1,5},{2,6},{3,7},{4,0},{5,1},{6,2},{7,3},{8,16},{9,17},{10,... | collective-permute-start | bytes 417800 | tf_op jit(solution)/shard_map/ppermute | solution.py:132
  (3 other events, 22.5 us)

commit v8 on v7

--- a/solution.py
+++ b/solution.py
@@ -422,7 +422,8 @@
         for z in range(field.shape[0]):
             one(z, 0)
     else:
-        lax.fori_loop(0, field.shape[0], one, 0, unroll=2)
+        for z in range(field.shape[0]):
+            one(z, 0)
 
 
 def widened(pos_ref, counts, modulus, beside, ins_x):
@@ -596,7 +597,7 @@
             finish(2 * t + h + thin)
         return 0
 
-    lax.fori_loop(0, pairs, pair, 0, unroll=2)
+    lax.fori_loop(0, pairs, pair, 0, unroll=4)
     for i in range(thin):
         row = i % 2 * thin
         for c in range(3):
@@ -948,7 +949,7 @@
         [spectral],
         limit=32,
     )
-    margins = exchange_yz(out)
+    margins = exchange_yz(out, "gx")
     edges = exchange_x(
         call(
             bind(edge_kernel, REACH), [pos, solved, *margins], [(near, 8, LANES)] * sizes[3]

time: 109 us -> 108 us (level)
  starting transfers between devices: 32 us -> 28.9 us
  waiting for transfers between devices: 23.8 us -> 25.5 us
    ppermute x11 -> x9, starting transfers between devices: 18.7 us -> 15.3 us  [swap(): return lax.ppermute(value, name, list(enumerate(other)))]
    ppermute x10 -> x12, waiting for transfers between devices: 16.9 us -> 18.6 us  [swap(): return lax.ppermute(value, names, pairs)]
    ppermute x10 -> x12, starting transfers between devices: 13.2 us -> 13.6 us  [swap(): return lax.ppermute(value, names, pairs)]
    ppermute x11 -> x9, waiting for transfers between devices: 6.86 us -> 6.87 us  [swap(): return lax.ppermute(value, name, list(enumerate(other)))]
  transfers between devices with their start and end apart: 21 -> 21, of which waited for: 10 -> 9; matrix products, arithmetic and copies ran while one was open for 0% -> 0% of each run, Pallas kernels for 6% -> 6%
where the time goes in v8:
time: 108 us; the launch traced here: 107 us
  Pallas kernels  50.4 us (47%)
  starting transfers between devices  28.9 us (27%)
  waiting for transfers between devices  25.5 us (24%)
    pallas_call x11, Pallas kernels, call(): pl.pallas_call(kernel, out_shape=[jax.ShapeDtypeStruct(shape, F32) for sh...  50.4 us
    ppermute x12, waiting for transfers between devices, swap(): return lax.ppermute(value, names, pairs)  18.6 us
    ppermute x9, starting transfers between devices, swap(): return lax.ppermute(value, name, list(enumerate(other)))  15.3 us
    ppermute x12, starting transfers between devices, swap(): return lax.ppermute(value, names, pairs)  13.6 us
    ppermute x9, waiting for transfers between devices, swap(): return lax.ppermute(value, name, list(enumerate(other)))  6.87 us
  transfers between devices with their start and end apart: 21, of which 9 were waited for; matrix products, arithmetic and copies ran while one was open for 0% of the time, Pallas kernels for 6%

profile of v8, /device:TPU:9, one launch (start us, length us, event | category | flops | bytes accessed | tf_op | source)
XLA Modules:
  0.0 107.0 jit_solution(13995926358021788948)
XLA Ops:
  1.4 3.7 %shard_map.149 = (f32[32,32,128]{2,1,0:T(8,128)}, f32[68,8,128]{2,1,0:T(8,128)}, f32[17,32,128]{2,1,0:T(8,128)}, f32[17,32,128]{2,1,0:T(8,128)}, f32[11,8,128]{2,1,0:T(8,128)}, /*index=5*/f32[11,8,128]{2,1,0:T(8,128)}) custom-call(s32[3]{0:T(128)} %pad_add_fusion.pos_ref, f32[16]{0:T(128)} %table_in.1, f32[3,32,32,128]{3,2,1,0:T(8,128)} %load.1, ...), custom_call_target="tpu_custom_call" | custom-call | tf_op jit(solution)/shard_map/pallas_call | solution.py:838
  5.1 1.3 %collective-permute-start = (f32[68,8,128]{2,1,0:T(8,128)}, f32[68,8,128]{2,1,0:T(8,128)S(1)}, u32[]{:S(2)}, u32[]{:S(2)}) collective-permute-start(f32[68,8,128]{2,1,0:T(8,128)} %get-tuple-element.33), channel_id=1, source_target_pairs={{0,4},{4,0},{1,5},{5,1},{2,6},{6,2},{3,7},{7,3},{8,12},{12,8},{9,1... | collective-permute-start | bytes 835592 | tf_op jit(solution)/shard_map/ppermute | solution.py:131
  6.6 2.4 %collective-permute-start.2 = (f32[17,32,128]{2,1,0:T(8,128)}, f32[17,32,128]{2,1,0:T(8,128)S(1)}, u32[]{:S(2)}, u32[]{:S(2)}) collective-permute-start(f32[17,32,128]{2,1,0:T(8,128)} %get-tuple-element.35), channel_id=1, source_target_pairs={{0,8},{1,2},{2,1},{3,11},{4,12},{5,6},{6,5},{7,15},{8,0},{9,10},{1... | collective-permute-start | bytes 835592 | tf_op jit(solution)/shard_map/ppermute | solution.py:132
  9.1 2.3 %collective-permute-start.4 = (f32[11,8,128]{2,1,0:T(8,128)}, f32[11,8,128]{2,1,0:T(8,128)S(1)}, u32[]{:S(2)}, u32[]{:S(2)}) collective-permute-start(f32[11,8,128]{2,1,0:T(8,128)} %get-tuple-element.37), channel_id=1, source_target_pairs={{0,8},{1,6},{2,5},{3,11},{4,12},{5,2},{6,1},{7,15},{8,0},{9,14},{1... | collective-permute-start | bytes 135176 | tf_op jit(solution)/shard_map/ppermute | solution.py:132
  11.3 3.1 %collective-permute-done.3.refs_3_ = f32[11,8,128]{2,1,0:T(8,128)S(1)} collective-permute-done((f32[11,8,128]{2,1,0:T(8,128)}, f32[11,8,128]{2,1,0:T(8,128)S(1)}, u32[]{:S(2)}, u32[]{:S(2)}) %collective-permute-start.3) | collective-permute-done | bytes 45088 | tf_op jit(solution)/shard_map/ppermute | solution.py:132
  14.5 1.4 %collective-permute-done.4.refs_4_ = f32[11,8,128]{2,1,0:T(8,128)S(1)} collective-permute-done((f32[11,8,128]{2,1,0:T(8,128)}, f32[11,8,128]{2,1,0:T(8,128)S(1)}, u32[]{:S(2)}, u32[]{:S(2)}) %collective-permute-start.4) | collective-permute-done | bytes 45088 | tf_op jit(solution)/shard_map/ppermute | solution.py:132
  16.5 1.8 %shard_map.150 = (f32[40,144,128]{2,1,0:T(8,128)S(1)}, f32[40,8,128]{2,1,0:T(8,128)S(1)}, f32[40,8,128]{2,1,0:T(8,128)S(1)}) custom-call(s32[3]{0:T(128)S(1)} %copy-done.12, f32[3,32,32,128]{3,2,1,0:T(8,128)S(1)} %copy-done, f32[68,8,128]{2,1,0:T(8,128)S(1)} %collective-permute-done.refs_0_, f32[17,32,128]{2,1,0:T(8,128)S(1)} %collective-permute-done.1.refs_1_, ...), custom_call_target="tpu_custom_call" | custom-call | tf_op jit(solution)/shard_map/pallas_call | solution.py:838
  18.3 1.9 %collective-permute-start.5 = (f32[40,8,128]{2,1,0:T(8,128)S(1)}, f32[40,8,128]{2,1,0:T(8,128)S(1)}, u32[]{:S(2)}, u32[]{:S(2)}) collective-permute-start(f32[40,8,128]{2,1,0:T(8,128)S(1)} %get-tuple-element.39), channel_id=1, source_target_pairs={{0,8},{8,0},{16,24},{24,16},{1,9},{9,1},{17,25},{25,17},{2,10},{10... | collective-permute-start | bytes 491528 | tf_op jit(solution)/shard_map/ppermute | solution.py:131
  20.3 3.0 %collective-permute-start.6 = (f32[40,8,128]{2,1,0:T(8,128)S(1)}, f32[40,8,128]{2,1,0:T(8,128)S(1)}, u32[]{:S(2)}, u32[]{:S(2)}) collective-permute-start(f32[40,8,128]{2,1,0:T(8,128)S(1)} %get-tuple-element.40), channel_id=1, source_target_pairs={{0,0},{8,16},{16,8},{24,24},{1,1},{9,17},{17,9},{25,25},{2,2},{10,... | collective-permute-start | bytes 491528 | tf_op jit(solution)/shard_map/ppermute | solution.py:131
  23.3 3.6 %collective-permute-done.6.refs_1_ = f32[40,8,128]{2,1,0:T(8,128)S(1)} collective-permute-done((f32[40,8,128]{2,1,0:T(8,128)S(1)}, f32[40,8,128]{2,1,0:T(8,128)S(1)}, u32[]{:S(2)}, u32[]{:S(2)}) %collective-permute-start.6) | collective-permute-done | bytes 163872 | tf_op jit(solution)/shard_map/ppermute | solution.py:131
  27.0 8.5 %shard_map.151 = (f32[20,136,128]{2,1,0:T(8,128)S(1)}, f32[40,160,128]{2,1,0:T(8,128)S(1)}, f32[9,136,128]{2,1,0:T(8,128)S(1)}, f32[9,136,128]{2,1,0:T(8,128)S(1...) custom-call(s32[3]{0:T(128)S(1)} %copy-done.12, f32[40,144,128]{2,1,0:T(8,128)S(1)} %get-tuple-element.38.residual, ...), custom_call_target="tpu_custom_call" | custom-call | tf_op jit(solution)/shard_map/pallas_call | solution.py:838
  35.5 3.1 %shard_map.152 = (f32[20,136,128]{2,1,0:T(8,128)S(1)}, f32[10,136,128]{2,1,0:T(8,128)S(1)}) custom-call(s32[3]{0:T(128)S(1)} %copy-done.12, f32[20,136,128]{2,1,0:T(8,128)S(1)} %get-tuple-element.41.outer.refs_0_, f32[40,160,128]{2,1,0:T(8,128)S(1)} %get-tuple-element.42.mid, bf16[136,480]{1,0:T(8,128)(2,1)S(1)} %copy-done.1, bf16[256,256]{1,0:T(8,128)(2,1)S(1)} %copy-done.2), custom_call_target="tpu_custom_call" | custom-call | flops 8000000 | bytes 8000000 | tf_op jit(solution)/shard_map/pallas_call | solution.py:838
  38.6 1.3 %collective-permute-start.7 = (f32[10,136,128]{2,1,0:T(8,128)S(1)}, f32[10,136,128]{2,1,0:T(8,128)S(1)}, u32[]{:S(2)}, u32[]{:S(2)}) collective-permute-start(f32[10,136,128]{2,1,0:T(8,128)S(1)} %get-tuple-element.44), channel_id=1, source_target_pairs={{0,4},{4,0},{1,5},{5,1},{2,6},{6,2},{3,7},{7,3},{8,12},{12,8},{9,1... | collective-permute-start | bytes 2088968 | tf_op jit(solution)/shard_map/ppermute | solution.py:131
  39.9 3.4 %collective-permute-start.9 = (f32[9,136,128]{2,1,0:T(8,128)S(1)}, f32[9,136,128]{2,1,0:T(8,128)S(1)}, u32[]{:S(2)}, u32[]{:S(2)}) collective-permute-start(f32[9,136,128]{2,1,0:T(8,128)S(1)} %get-tuple-element.46), channel_id=1, source_target_pairs={{0,0},{1,2},{2,1},{3,3},{4,4},{5,6},{6,5},{7,7},{8,8},{9,10},{10,9... | collective-permute-start | bytes 1880072 | tf_op jit(solution)/shard_map/ppermute | solution.py:131
  43.4 3.0 %collective-permute-start.11 = (f32[2,136,128]{2,1,0:T(8,128)S(1)}, f32[2,136,128]{2,1,0:T(8,128)S(1)}, u32[]{:S(2)}, u32[]{:S(2)}) collective-permute-start(f32[2,136,128]{2,1,0:T(8,128)S(1)} %get-tuple-element.48), channel_id=1, source_target_pairs={{0,0},{1,6},{2,5},{3,3},{4,4},{5,2},{6,1},{7,7},{8,8},{9,14},{10,1... | collective-permute-start | bytes 417800 | tf_op jit(solution)/shard_map/ppermute | solution.py:132
  46.4 2.2 %shard_map.154 = (f32[42,144,128]{2,1,0:T(8,128)S(1)}, f32[42,144,128]{2,1,0:T(8,128)S(1)}) custom-call(s32[3]{0:T(128)S(1)} %copy-done.13, f32[32,32,128]{2,1,0:T(8,128)S(1)} %copy-done.10, f32[68,8,128]{2,1,0:T(8,128)S(1)} %collective-permute-done.refs_0_, f32[17,32,128]{2,1,0:T(8,128)S(1)} %collective-permute-done.1.refs_1_, ...), custom_call_target="tpu_custom_call" | custom-call | flops 8000000 | bytes 8000000 | tf_op jit(solution)/shard_map/pallas_call | solution.py:838
  48.6 5.7 %collective-permute-done.10.refs_5_ = f32[2,136,128]{2,1,0:T(8,128)S(1)} collective-permute-done((f32[2,136,128]{2,1,0:T(8,128)S(1)}, f32[2,136,128]{2,1,0:T(8,128)S(1)}, u32[]{:S(2)}, u32[]{:S(2)}) %collective-permute-start.10) | collective-permute-done | bytes 139296 | tf_op jit(solution)/shard_map/ppermute | solution.py:132
  54.3 1.8 %collective-permute-done.11.refs_6_ = f32[2,136,128]{2,1,0:T(8,128)S(1)} collective-permute-done((f32[2,136,128]{2,1,0:T(8,128)S(1)}, f32[2,136,128]{2,1,0:T(8,128)S(1)}, u32[]{:S(2)}, u32[]{:S(2)}) %collective-permute-start.11) | collective-permute-done | bytes 139296 | tf_op jit(solution)/shard_map/ppermute | solution.py:132
  56.1 1.1 collective-permute-done.7.refs_2_
  57.2 1.1 %shard_map.155 = (f32[62,8,128]{2,1,0:T(8,128)S(1)}, f32[62,8,128]{2,1,0:T(8,128)S(1)}) custom-call(s32[3]{0:T(128)S(1)} %copy-done.13, f32[20,136,128]{2,1,0:T(8,128)S(1)} %get-tuple-element.41.outer.refs_0_, f32[20,136,128]{2,1,0:T(8,128)S(1)} %get-tuple-element.43.refs_1_, f32[10,136,128]{2,1,0:T(8,128)S(1)} %collective-permute-done.7.refs_2_, ...), custom_call_target="tpu_custom_call" | custom-call | tf_op jit(solution)/shard_map/pallas_call | solution.py:838
  58.4 3.0 %collective-permute-start.13 = (f32[62,8,128]{2,1,0:T(8,128)S(1)}, f32[62,8,128]{2,1,0:T(8,128)S(1)}, u32[]{:S(2)}, u32[]{:S(2)}) collective-permute-start(f32[62,8,128]{2,1,0:T(8,128)S(1)} %get-tuple-element.52), channel_id=1, source_target_pairs={{0,0},{8,16},{16,8},{24,24},{1,1},{9,17},{17,9},{25,25},{2,2},{10,... | collective-permute-start | bytes 761864 | tf_op jit(solution)/shard_map/ppermute | solution.py:131
  61.4 2.3 %shard_map.153.partial = f32[42,144,128]{2,1,0:T(8,128)S(1)} custom-call(s32[3]{0:T(128)S(1)} %copy-done.13, f32[20,136,128]{2,1,0:T(8,128)S(1)} %get-tuple-element.41.outer.refs_0_, f32[20,136,128]{2,1,0:T(8,128)S(1)} %get-tuple-element.43.refs_1_, f32[10,136,128]{2,1,0:T(8,128)S(1)} %collective-permute-done.7.refs_2_, ...), custom_call_target="tpu_custom_call" | custom-call | flops 8000000 | bytes 8000000 | tf_op jit(solution)/shard_map/pallas_call | solution.py:838
  63.8 2.2 %collective-permute-done.13.refs_3_ = f32[62,8,128]{2,1,0:T(8,128)S(1)} collective-permute-done((f32[62,8,128]{2,1,0:T(8,128)S(1)}, f32[62,8,128]{2,1,0:T(8,128)S(1)}, u32[]{:S(2)}, u32[]{:S(2)}) %collective-permute-start.13) | collective-permute-done | bytes 253984 | tf_op jit(solution)/shard_map/ppermute | solution.py:131
  66.0 17.6 %shard_map.156 = (f32[40,136,128]{2,1,0:T(8,128)S(1)}, f32[42,144,128]{2,1,0:T(8,128)S(1)}, f32[40,144,128]{2,1,0:T(8,128)S(1)}, f32[5,136,128]{2,1,0:T(8,128)S(...) custom-call(s32[3]{0:T(128)S(1)} %copy-done.13, ...), custom_call_target="tpu_custom_call" | custom-call | tf_op jit(solution)/shard_map/pallas_call | solution.py:838
  83.6 1.3 %collective-permute-start.14 = (f32[5,136,128]{2,1,0:T(8,128)S(1)}, f32[5,136,128]{2,1,0:T(8,128)S(1)}, u32[]{:S(2)}, u32[]{:S(2)}) collective-permute-start(f32[5,136,128]{2,1,0:T(8,128)S(1)} %get-tuple-element.54), channel_id=1, source_target_pairs={{0,4},{4,0},{1,5},{5,1},{2,6},{6,2},{3,7},{7,3},{8,12},{12,8},{9,1... | collective-permute-start | bytes 1044488 | tf_op jit(solution)/shard_map/ppermute | solution.py:131
  84.9 1.5 %collective-permute-start.16 = (f32[5,136,128]{2,1,0:T(8,128)S(1)}, f32[5,136,128]{2,1,0:T(8,128)S(1)}, u32[]{:S(2)}, u32[]{:S(2)}) collective-permute-start(f32[5,136,128]{2,1,0:T(8,128)S(1)} %get-tuple-element.56), channel_id=1, source_target_pairs={{0,8},{1,2},{2,1},{3,11},{4,12},{5,6},{6,5},{7,15},{8,0},{9,10},{1... | collective-permute-start | bytes 1044488 | tf_op jit(solution)/shard_map/ppermute | solution.py:132
  86.4 2.4 %collective-permute-start.18 = (f32[1,136,128]{2,1,0:T(8,128)S(1)}, f32[1,136,128]{2,1,0:T(8,128)S(1)}, u32[]{:S(2)}, u32[]{:S(2)}) collective-permute-start(f32[1,136,128]{2,1,0:T(8,128)S(1)} %get-tuple-element.58), channel_id=1, source_target_pairs={{0,8},{1,6},{2,5},{3,11},{4,12},{5,2},{6,1},{7,15},{8,0},{9,14},{1... | collective-permute-start | bytes 208904 | tf_op jit(solution)/shard_map/ppermute | solution.py:132
  88.8 5.1 %collective-permute-done.17.refs_4_ = f32[1,136,128]{2,1,0:T(8,128)S(1)} collective-permute-done((f32[1,136,128]{2,1,0:T(8,128)S(1)}, f32[1,136,128]{2,1,0:T(8,128)S(1)}, u32[]{:S(2)}, u32[]{:S(2)}) %collective-permute-start.17) | collective-permute-done | bytes 69664 | tf_op jit(solution)/shard_map/ppermute | solution.py:132
  94.7 1.7 %collective-permute-start.20 = (f32[34,8,128]{2,1,0:T(8,128)S(1)}, f32[34,8,128]{2,1,0:T(8,128)S(1)}, u32[]{:S(2)}, u32[]{:S(2)}) collective-permute-start(f32[34,8,128]{2,1,0:T(8,128)S(1)} %get-tuple-element.63), channel_id=1, source_target_pairs={{0,4},{1,5},{2,6},{3,7},{4,0},{5,1},{6,2},{7,3},{8,16},{9,17},{10,... | collective-permute-start | bytes 417800 | tf_op jit(solution)/shard_map/ppermute | solution.py:132
  96.4 1.8 %shard_map.157.partial = f32[34,144,128]{2,1,0:T(8,128)S(1)} custom-call(s32[3]{0:T(128)S(1)} %copy-done.13, f32[40,136,128]{2,1,0:T(8,128)S(1)} %get-tuple-element.53.refs_0_, f32[5,136,128]{2,1,0:T(8,128)S(1)} %collective-permute-done.14.refs_1_, f32[5,136,128]{2,1,0:T(8,128)S(1)} %collective-permute-done.15.refs_2_, ...), custom_call_target="tpu_custom_call" | custom-call | flops 8000000 | bytes 8000000 | tf_op jit(solution)/shard_map/pallas_call | solution.py:838
  98.2 1.4 %collective-permute-done.20.refs_1_ = f32[34,8,128]{2,1,0:T(8,128)S(1)} collective-permute-done((f32[34,8,128]{2,1,0:T(8,128)S(1)}, f32[34,8,128]{2,1,0:T(8,128)S(1)}, u32[]{:S(2)}, u32[]{:S(2)}) %collective-permute-start.20) | collective-permute-done | bytes 139296 | tf_op jit(solution)/shard_map/ppermute | solution.py:132
  99.6 7.5 %shard_map.159 = (f32[3,32,32,128]{3,2,1,0:T(8,128)}, f32[3,32,32,128]{3,2,1,0:T(8,128)}) custom-call(s32[3]{0:T(128)S(1)} %copy-done.13, f32[34,144,128]{2,1,0:T(8,128)S(1)} %shard_map.157.partial, f32[42,144,128]{2,1,0:T(8,128)S(1)} %get-tuple-element.50.refs_7_.modulus, f32[42,144,128]{2,1,0:T(8,128)S(1)} %get-tuple-element.59.beside, ...), custom_call_target="tpu_custom_call" | custom-call | tf_op jit(solution)/shard_map/pallas_call | solution.py:838
  (50 shorter events, 2.5 us)
Async XLA Ops:
  0.6 26.3 %copy-start.2 = (bf16[256,256]{1,0:T(8,128)(2,1)S(1)}, bf16[256,256]{1,0:T(8,128)(2,1)}, u32[]{:S(2)}) copy-start(bf16[256,256]{1,0:T(8,128)(2,1)} %constant.39.clone.refs_9_.back_y.refs_11_) | copy-start | bytes 393220
  0.6 26.3 %copy-start.1 = (bf16[136,480]{1,0:T(8,128)(2,1)S(1)}, bf16[136,480]{1,0:T(8,128)(2,1)}, u32[]{:S(2)}) copy-start(bf16[136,480]{1,0:T(8,128)(2,1)} %constant.38.clone.refs_8_.back_x.refs_10_) | copy-start | bytes 391684
  0.7 26.2 %copy-start.3 = (f32[40,8,128]{2,1,0:T(8,128)S(1)}, f32[40,8,128]{2,1,0:T(8,128)}, u32[]{:S(2)}) copy-start(f32[40,8,128]{2,1,0:T(8,128)} %constant.41.clone.refs_11_.refs_13_) | copy-start | bytes 491524
  0.7 26.2 %copy-start.4 = (bf16[160,480]{1,0:T(8,128)(2,1)S(1)}, bf16[160,480]{1,0:T(8,128)(2,1)}, u32[]{:S(2)}) copy-start(bf16[160,480]{1,0:T(8,128)(2,1)} %constant.37.clone.refs_7_.refs_9_) | copy-start | bytes 460804
  0.7 26.2 %copy-start.5 = (bf16[160,480]{1,0:T(8,128)(2,1)S(1)}, bf16[160,480]{1,0:T(8,128)(2,1)}, u32[]{:S(2)}) copy-start(bf16[160,480]{1,0:T(8,128)(2,1)} %constant.36.clone.refs_6_.refs_8_) | copy-start | bytes 460804
  0.7 26.2 %copy-start.6 = (bf16[160,480]{1,0:T(8,128)(2,1)S(1)}, bf16[160,480]{1,0:T(8,128)(2,1)}, u32[]{:S(2)}) copy-start(bf16[160,480]{1,0:T(8,128)(2,1)} %constant.35.clone.refs_5_.refs_7_) | copy-start | bytes 460804
  0.7 26.2 %copy-start.7 = (bf16[160,480]{1,0:T(8,128)(2,1)S(1)}, bf16[160,480]{1,0:T(8,128)(2,1)}, u32[]{:S(2)}) copy-start(bf16[160,480]{1,0:T(8,128)(2,1)} %constant.34.clone.refs_4_.refs_6_) | copy-start | bytes 460804
  0.7 15.2 %copy-start = (f32[3,32,32,128]{3,2,1,0:T(8,128)S(1)}, f32[3,32,32,128]{3,2,1,0:T(8,128)}, u32[]{:S(2)}) copy-start(f32[3,32,32,128]{3,2,1,0:T(8,128)} %load.1) | copy-start | bytes 4718596
  0.7 26.2 %copy-start.8 = (bf16[160,432]{1,0:T(8,128)(2,1)S(1)}, bf16[160,432]{1,0:T(8,128)(2,1)}, u32[]{:S(2)}) copy-start(bf16[160,432]{1,0:T(8,128)(2,1)} %constant.33.clone.refs_3_.refs_5_) | copy-start | bytes 414724
  0.7 26.2 %copy-start.9 = (bf16[256,256]{1,0:T(8,128)(2,1)S(1)}, bf16[256,256]{1,0:T(8,128)(2,1)}, u32[]{:S(2)}) copy-start(bf16[256,256]{1,0:T(8,128)(2,1)} %constant.32.clone.refs_2_.refs_4_) | copy-start | bytes 393220
  0.8 26.2 %copy-start.11 = (f32[160,128]{1,0:T(8,128)S(1)}, f32[160,128]{1,0:T(8,128)}, u32[]{:S(2)}) copy-start(f32[160,128]{1,0:T(8,128)} %constant.40.clone.refs_10_.refs_12_) | copy-start | bytes 245764
  5.1 10.8 %collective-permute-start = (f32[68,8,128]{2,1,0:T(8,128)}, f32[68,8,128]{2,1,0:T(8,128)S(1)}, u32[]{:S(2)}, u32[]{:S(2)}) collective-permute-start(f32[68,8,128]{2,1,0:T(8,128)} %get-tuple-element.33), channel_id=1, source_target_pairs={{0,4},{4,0},{1,5},{5,1},{2,6},{6,2},{3,7},{7,3},{8,12},{12,8},{9,1... | collective-permute-start | bytes 835592 | tf_op jit(solution)/shard_map/ppermute | solution.py:131
  6.4 9.5 %collective-permute-start.1 = (f32[17,32,128]{2,1,0:T(8,128)}, f32[17,32,128]{2,1,0:T(8,128)S(1)}, u32[]{:S(2)}, u32[]{:S(2)}) collective-permute-start(f32[17,32,128]{2,1,0:T(8,128)} %get-tuple-element.34), channel_id=1, source_target_pairs={{0,1},{1,0},{2,3},{3,2},{4,5},{5,4},{6,7},{7,6},{8,9},{9,8},{10,11... | collective-permute-start | bytes 835592 | tf_op jit(solution)/shard_map/ppermute | solution.py:132
  6.6 9.3 %collective-permute-start.2 = (f32[17,32,128]{2,1,0:T(8,128)}, f32[17,32,128]{2,1,0:T(8,128)S(1)}, u32[]{:S(2)}, u32[]{:S(2)}) collective-permute-start(f32[17,32,128]{2,1,0:T(8,128)} %get-tuple-element.35), channel_id=1, source_target_pairs={{0,8},{1,2},{2,1},{3,11},{4,12},{5,6},{6,5},{7,15},{8,0},{9,10},{1... | collective-permute-start | bytes 835592 | tf_op jit(solution)/shard_map/ppermute | solution.py:132
  9.0 5.4 %collective-permute-start.3 = (f32[11,8,128]{2,1,0:T(8,128)}, f32[11,8,128]{2,1,0:T(8,128)S(1)}, u32[]{:S(2)}, u32[]{:S(2)}) collective-permute-start(f32[11,8,128]{2,1,0:T(8,128)} %get-tuple-element.36), channel_id=1, source_target_pairs={{0,5},{1,4},{2,7},{3,6},{4,1},{5,0},{6,3},{7,2},{8,13},{9,12},{10,... | collective-permute-start | bytes 135176 | tf_op jit(solution)/shard_map/ppermute | solution.py:132
  9.1 6.8 %collective-permute-start.4 = (f32[11,8,128]{2,1,0:T(8,128)}, f32[11,8,128]{2,1,0:T(8,128)S(1)}, u32[]{:S(2)}, u32[]{:S(2)}) collective-permute-start(f32[11,8,128]{2,1,0:T(8,128)} %get-tuple-element.37), channel_id=1, source_target_pairs={{0,8},{1,6},{2,5},{3,11},{4,12},{5,2},{6,1},{7,15},{8,0},{9,14},{1... | collective-permute-start | bytes 135176 | tf_op jit(solution)/shard_map/ppermute | solution.py:132
  18.3 5.0 %collective-permute-start.5 = (f32[40,8,128]{2,1,0:T(8,128)S(1)}, f32[40,8,128]{2,1,0:T(8,128)S(1)}, u32[]{:S(2)}, u32[]{:S(2)}) collective-permute-start(f32[40,8,128]{2,1,0:T(8,128)S(1)} %get-tuple-element.39), channel_id=1, source_target_pairs={{0,8},{8,0},{16,24},{24,16},{1,9},{9,1},{17,25},{25,17},{2,10},{10... | collective-permute-start | bytes 491528 | tf_op jit(solution)/shard_map/ppermute | solution.py:131
  20.3 6.6 %collective-permute-start.6 = (f32[40,8,128]{2,1,0:T(8,128)S(1)}, f32[40,8,128]{2,1,0:T(8,128)S(1)}, u32[]{:S(2)}, u32[]{:S(2)}) collective-permute-start(f32[40,8,128]{2,1,0:T(8,128)S(1)} %get-tuple-element.40), channel_id=1, source_target_pairs={{0,0},{8,16},{16,8},{24,24},{1,1},{9,17},{17,9},{25,25},{2,2},{10,... | collective-permute-start | bytes 491528 | tf_op jit(solution)/shard_map/ppermute | solution.py:131
  38.6 18.6 %collective-permute-start.7 = (f32[10,136,128]{2,1,0:T(8,128)S(1)}, f32[10,136,128]{2,1,0:T(8,128)S(1)}, u32[]{:S(2)}, u32[]{:S(2)}) collective-permute-start(f32[10,136,128]{2,1,0:T(8,128)S(1)} %get-tuple-element.44), channel_id=1, source_target_pairs={{0,4},{4,0},{1,5},{5,1},{2,6},{6,2},{3,7},{7,3},{8,12},{12,8},{9,1... | collective-permute-start | bytes 2088968 | tf_op jit(solution)/shard_map/ppermute | solution.py:131
  39.9 16.3 %collective-permute-start.8 = (f32[9,136,128]{2,1,0:T(8,128)S(1)}, f32[9,136,128]{2,1,0:T(8,128)S(1)}, u32[]{:S(2)}, u32[]{:S(2)}) collective-permute-start(f32[9,136,128]{2,1,0:T(8,128)S(1)} %get-tuple-element.45), channel_id=1, source_target_pairs={{0,1},{1,0},{2,3},{3,2},{4,5},{5,4},{6,7},{7,6},{8,9},{9,8},{10,11... | collective-permute-start | bytes 1880072 | tf_op jit(solution)/shard_map/ppermute | solution.py:131
  39.9 16.3 %collective-permute-start.9 = (f32[9,136,128]{2,1,0:T(8,128)S(1)}, f32[9,136,128]{2,1,0:T(8,128)S(1)}, u32[]{:S(2)}, u32[]{:S(2)}) collective-permute-start(f32[9,136,128]{2,1,0:T(8,128)S(1)} %get-tuple-element.46), channel_id=1, source_target_pairs={{0,0},{1,2},{2,1},{3,3},{4,4},{5,6},{6,5},{7,7},{8,8},{9,10},{10,9... | collective-permute-start | bytes 1880072 | tf_op jit(solution)/shard_map/ppermute | solution.py:131
  43.3 11.0 %collective-permute-start.10 = (f32[2,136,128]{2,1,0:T(8,128)S(1)}, f32[2,136,128]{2,1,0:T(8,128)S(1)}, u32[]{:S(2)}, u32[]{:S(2)}) collective-permute-start(f32[2,136,128]{2,1,0:T(8,128)S(1)} %get-tuple-element.47), channel_id=1, source_target_pairs={{0,5},{1,4},{2,7},{3,6},{4,1},{5,0},{6,3},{7,2},{8,13},{9,12},{10,... | collective-permute-start | bytes 417800 | tf_op jit(solution)/shard_map/ppermute | solution.py:132
  43.4 12.8 %collective-permute-start.11 = (f32[2,136,128]{2,1,0:T(8,128)S(1)}, f32[2,136,128]{2,1,0:T(8,128)S(1)}, u32[]{:S(2)}, u32[]{:S(2)}) collective-permute-start(f32[2,136,128]{2,1,0:T(8,128)S(1)} %get-tuple-element.48), channel_id=1, source_target_pairs={{0,0},{1,6},{2,5},{3,3},{4,4},{5,2},{6,1},{7,7},{8,8},{9,14},{10,1... | collective-permute-start | bytes 417800 | tf_op jit(solution)/shard_map/ppermute | solution.py:132
  58.3 5.5 %collective-permute-start.12 = (f32[62,8,128]{2,1,0:T(8,128)S(1)}, f32[62,8,128]{2,1,0:T(8,128)S(1)}, u32[]{:S(2)}, u32[]{:S(2)}) collective-permute-start(f32[62,8,128]{2,1,0:T(8,128)S(1)} %get-tuple-element.51), channel_id=1, source_target_pairs={{0,8},{8,0},{16,24},{24,16},{1,9},{9,1},{17,25},{25,17},{2,10},{10... | collective-permute-start | bytes 761864 | tf_op jit(solution)/shard_map/ppermute | solution.py:131
  58.4 7.6 %collective-permute-start.13 = (f32[62,8,128]{2,1,0:T(8,128)S(1)}, f32[62,8,128]{2,1,0:T(8,128)S(1)}, u32[]{:S(2)}, u32[]{:S(2)}) collective-permute-start(f32[62,8,128]{2,1,0:T(8,128)S(1)} %get-tuple-element.52), channel_id=1, source_target_pairs={{0,0},{8,16},{16,8},{24,24},{1,1},{9,17},{17,9},{25,25},{2,2},{10,... | collective-permute-start | bytes 761864 | tf_op jit(solution)/shard_map/ppermute | solution.py:131
  83.6 10.2 %collective-permute-start.14 = (f32[5,136,128]{2,1,0:T(8,128)S(1)}, f32[5,136,128]{2,1,0:T(8,128)S(1)}, u32[]{:S(2)}, u32[]{:S(2)}) collective-permute-start(f32[5,136,128]{2,1,0:T(8,128)S(1)} %get-tuple-element.54), channel_id=1, source_target_pairs={{0,4},{4,0},{1,5},{5,1},{2,6},{6,2},{3,7},{7,3},{8,12},{12,8},{9,1... | collective-permute-start | bytes 1044488 | tf_op jit(solution)/shard_map/ppermute | solution.py:131
  84.9 8.9 %collective-permute-start.15 = (f32[5,136,128]{2,1,0:T(8,128)S(1)}, f32[5,136,128]{2,1,0:T(8,128)S(1)}, u32[]{:S(2)}, u32[]{:S(2)}) collective-permute-start(f32[5,136,128]{2,1,0:T(8,128)S(1)} %get-tuple-element.55), channel_id=1, source_target_pairs={{0,1},{1,0},{2,3},{3,2},{4,5},{5,4},{6,7},{7,6},{8,9},{9,8},{10,11... | collective-permute-start | bytes 1044488 | tf_op jit(solution)/shard_map/ppermute | solution.py:132
  84.9 8.9 %collective-permute-start.16 = (f32[5,136,128]{2,1,0:T(8,128)S(1)}, f32[5,136,128]{2,1,0:T(8,128)S(1)}, u32[]{:S(2)}, u32[]{:S(2)}) collective-permute-start(f32[5,136,128]{2,1,0:T(8,128)S(1)} %get-tuple-element.56), channel_id=1, source_target_pairs={{0,8},{1,2},{2,1},{3,11},{4,12},{5,6},{6,5},{7,15},{8,0},{9,10},{1... | collective-permute-start | bytes 1044488 | tf_op jit(solution)/shard_map/ppermute | solution.py:132
  86.4 7.4 %collective-permute-start.17 = (f32[1,136,128]{2,1,0:T(8,128)S(1)}, f32[1,136,128]{2,1,0:T(8,128)S(1)}, u32[]{:S(2)}, u32[]{:S(2)}) collective-permute-start(f32[1,136,128]{2,1,0:T(8,128)S(1)} %get-tuple-element.57), channel_id=1, source_target_pairs={{0,5},{1,4},{2,7},{3,6},{4,1},{5,0},{6,3},{7,2},{8,13},{9,12},{10,... | collective-permute-start | bytes 208904 | tf_op jit(solution)/shard_map/ppermute | solution.py:132
  86.4 7.4 %collective-permute-start.18 = (f32[1,136,128]{2,1,0:T(8,128)S(1)}, f32[1,136,128]{2,1,0:T(8,128)S(1)}, u32[]{:S(2)}, u32[]{:S(2)}) collective-permute-start(f32[1,136,128]{2,1,0:T(8,128)S(1)} %get-tuple-element.58), channel_id=1, source_target_pairs={{0,8},{1,6},{2,5},{3,11},{4,12},{5,2},{6,1},{7,15},{8,0},{9,14},{1... | collective-permute-start | bytes 208904 | tf_op jit(solution)/shard_map/ppermute | solution.py:132
  94.6 3.5 %collective-permute-start.19 = (f32[34,8,128]{2,1,0:T(8,128)S(1)}, f32[34,8,128]{2,1,0:T(8,128)S(1)}, u32[]{:S(2)}, u32[]{:S(2)}) collective-permute-start(f32[34,8,128]{2,1,0:T(8,128)S(1)} %get-tuple-element.62), channel_id=1, source_target_pairs={{0,8},{1,9},{2,10},{3,11},{4,12},{5,13},{6,14},{7,15},{8,0},{9,1},... | collective-permute-start | bytes 417800 | tf_op jit(solution)/shard_map/ppermute | solution.py:132
  94.7 4.8 %collective-permute-start.20 = (f32[34,8,128]{2,1,0:T(8,128)S(1)}, f32[34,8,128]{2,1,0:T(8,128)S(1)}, u32[]{:S(2)}, u32[]{:S(2)}) collective-permute-start(f32[34,8,128]{2,1,0:T(8,128)S(1)} %get-tuple-element.63), channel_id=1, source_target_pairs={{0,4},{1,5},{2,6},{3,7},{4,0},{5,1},{6,2},{7,3},{8,16},{9,17},{10,... | collective-permute-start | bytes 417800 | tf_op jit(solution)/shard_map/ppermute | solution.py:132
  (3 other events, 22.5 us)

commit v9 on v8

--- a/solution.py
+++ b/solution.py
@@ -937,7 +937,8 @@
             [pos, *solved, *margins, modulus],
             [(THIRD + WIDE // 3, 8, LANES)] * sizes[3],
             [(WIDE, 16, LANES)],
-        )
+        ),
+        "gy",
     )
     (partial,) = call(
         bind(fold_kernel, FOLD), [pos, *solved, *margins], [wide], work=8000000

time: 108 us -> 110 us (1.019)
  waiting for transfers between devices: 25.5 us -> 26.7 us
    ppermute x12 -> x14, starting transfers between devices: 13.6 us -> 17.6 us  [swap(): return lax.ppermute(value, names, pairs)]
    ppermute x12 -> x14, waiting for transfers between devices: 18.6 us -> 22.1 us  [swap(): return lax.ppermute(value, names, pairs)]
    ppermute x9 -> x7, starting transfers between devices: 15.3 us -> 12.2 us  [swap(): return lax.ppermute(value, name, list(enumerate(other)))]
    ppermute x9 -> x7, waiting for transfers between devices: 6.87 us -> 4.65 us  [swap(): return lax.ppermute(value, name, list(enumerate(other)))]
where the time goes in v9:
time: 110 us; the launch traced here: 109 us
  Pallas kernels  50.4 us (46%)
  starting transfers between devices  29.8 us (27%)
  waiting for transfers between devices  26.7 us (24%)
    pallas_call x11, Pallas kernels, call(): pl.pallas_call(kernel, out_shape=[jax.ShapeDtypeStruct(shape, F32) for sh...  50.4 us
    ppermute x14, waiting for transfers between devices, swap(): return lax.ppermute(value, names, pairs)  22.1 us
    ppermute x14, starting transfers between devices, swap(): return lax.ppermute(value, names, pairs)  17.6 us
    ppermute x7, starting transfers between devices, swap(): return lax.ppermute(value, name, list(enumerate(other)))  12.2 us
    ppermute x7, waiting for transfers between devices, swap(): return lax.ppermute(value, name, list(enumerate(other)))  4.65 us
  transfers between devices with their start and end apart: 21, of which 9 were waited for; matrix products, arithmetic and copies ran while one was open for 0% of the time, Pallas kernels for 6%

profile of v9, /device:TPU:9, one launch (start us, length us, event | category | flops | bytes accessed | tf_op | source)
XLA Modules:
  0.0 109.2 jit_solution(17002142988812587129)
XLA Ops:
  1.4 3.7 %shard_map.149 = (f32[32,32,128]{2,1,0:T(8,128)}, f32[68,8,128]{2,1,0:T(8,128)}, f32[17,32,128]{2,1,0:T(8,128)}, f32[17,32,128]{2,1,0:T(8,128)}, f32[11,8,128]{2,1,0:T(8,128)}, /*index=5*/f32[11,8,128]{2,1,0:T(8,128)}) custom-call(s32[3]{0:T(128)} %pad_add_fusion.pos_ref, f32[16]{0:T(128)} %table_in.1, f32[3,32,32,128]{3,2,1,0:T(8,128)} %load.1, ...), custom_call_target="tpu_custom_call" | custom-call | tf_op jit(solution)/shard_map/pallas_call | solution.py:838
  5.1 1.3 %collective-permute-start = (f32[68,8,128]{2,1,0:T(8,128)}, f32[68,8,128]{2,1,0:T(8,128)S(1)}, u32[]{:S(2)}, u32[]{:S(2)}) collective-permute-start(f32[68,8,128]{2,1,0:T(8,128)} %get-tuple-element.33), channel_id=1, source_target_pairs={{0,4},{4,0},{1,5},{5,1},{2,6},{6,2},{3,7},{7,3},{8,12},{12,8},{9,1... | collective-permute-start | bytes 835592 | tf_op jit(solution)/shard_map/ppermute | solution.py:131
  6.6 2.4 %collective-permute-start.2 = (f32[17,32,128]{2,1,0:T(8,128)}, f32[17,32,128]{2,1,0:T(8,128)S(1)}, u32[]{:S(2)}, u32[]{:S(2)}) collective-permute-start(f32[17,32,128]{2,1,0:T(8,128)} %get-tuple-element.35), channel_id=1, source_target_pairs={{0,8},{1,2},{2,1},{3,11},{4,12},{5,6},{6,5},{7,15},{8,0},{9,10},{1... | collective-permute-start | bytes 835592 | tf_op jit(solution)/shard_map/ppermute | solution.py:132
  9.1 2.3 %collective-permute-start.4 = (f32[11,8,128]{2,1,0:T(8,128)}, f32[11,8,128]{2,1,0:T(8,128)S(1)}, u32[]{:S(2)}, u32[]{:S(2)}) collective-permute-start(f32[11,8,128]{2,1,0:T(8,128)} %get-tuple-element.37), channel_id=1, source_target_pairs={{0,8},{1,6},{2,5},{3,11},{4,12},{5,2},{6,1},{7,15},{8,0},{9,14},{1... | collective-permute-start | bytes 135176 | tf_op jit(solution)/shard_map/ppermute | solution.py:132
  11.3 3.1 %collective-permute-done.3.refs_3_ = f32[11,8,128]{2,1,0:T(8,128)S(1)} collective-permute-done((f32[11,8,128]{2,1,0:T(8,128)}, f32[11,8,128]{2,1,0:T(8,128)S(1)}, u32[]{:S(2)}, u32[]{:S(2)}) %collective-permute-start.3) | collective-permute-done | bytes 45088 | tf_op jit(solution)/shard_map/ppermute | solution.py:132
  14.5 1.4 %collective-permute-done.4.refs_4_ = f32[11,8,128]{2,1,0:T(8,128)S(1)} collective-permute-done((f32[11,8,128]{2,1,0:T(8,128)}, f32[11,8,128]{2,1,0:T(8,128)S(1)}, u32[]{:S(2)}, u32[]{:S(2)}) %collective-permute-start.4) | collective-permute-done | bytes 45088 | tf_op jit(solution)/shard_map/ppermute | solution.py:132
  16.5 1.8 %shard_map.150 = (f32[40,144,128]{2,1,0:T(8,128)S(1)}, f32[40,8,128]{2,1,0:T(8,128)S(1)}, f32[40,8,128]{2,1,0:T(8,128)S(1)}) custom-call(s32[3]{0:T(128)S(1)} %copy-done.12, f32[3,32,32,128]{3,2,1,0:T(8,128)S(1)} %copy-done, f32[68,8,128]{2,1,0:T(8,128)S(1)} %collective-permute-done.refs_0_, f32[17,32,128]{2,1,0:T(8,128)S(1)} %collective-permute-done.1.refs_1_, ...), custom_call_target="tpu_custom_call" | custom-call | tf_op jit(solution)/shard_map/pallas_call | solution.py:838
  18.3 1.9 %collective-permute-start.5 = (f32[40,8,128]{2,1,0:T(8,128)S(1)}, f32[40,8,128]{2,1,0:T(8,128)S(1)}, u32[]{:S(2)}, u32[]{:S(2)}) collective-permute-start(f32[40,8,128]{2,1,0:T(8,128)S(1)} %get-tuple-element.39), channel_id=1, source_target_pairs={{0,8},{8,0},{16,24},{24,16},{1,9},{9,1},{17,25},{25,17},{2,10},{10... | collective-permute-start | bytes 491528 | tf_op jit(solution)/shard_map/ppermute | solution.py:131
  20.3 3.0 %collective-permute-start.6 = (f32[40,8,128]{2,1,0:T(8,128)S(1)}, f32[40,8,128]{2,1,0:T(8,128)S(1)}, u32[]{:S(2)}, u32[]{:S(2)}) collective-permute-start(f32[40,8,128]{2,1,0:T(8,128)S(1)} %get-tuple-element.40), channel_id=1, source_target_pairs={{0,0},{8,16},{16,8},{24,24},{1,1},{9,17},{17,9},{25,25},{2,2},{10,... | collective-permute-start | bytes 491528 | tf_op jit(solution)/shard_map/ppermute | solution.py:131
  23.3 3.6 %collective-permute-done.6.refs_1_ = f32[40,8,128]{2,1,0:T(8,128)S(1)} collective-permute-done((f32[40,8,128]{2,1,0:T(8,128)S(1)}, f32[40,8,128]{2,1,0:T(8,128)S(1)}, u32[]{:S(2)}, u32[]{:S(2)}) %collective-permute-start.6) | collective-permute-done | bytes 163872 | tf_op jit(solution)/shard_map/ppermute | solution.py:131
  27.0 8.5 %shard_map.151 = (f32[20,136,128]{2,1,0:T(8,128)S(1)}, f32[40,160,128]{2,1,0:T(8,128)S(1)}, f32[9,136,128]{2,1,0:T(8,128)S(1)}, f32[9,136,128]{2,1,0:T(8,128)S(1...) custom-call(s32[3]{0:T(128)S(1)} %copy-done.12, f32[40,144,128]{2,1,0:T(8,128)S(1)} %get-tuple-element.38.residual, ...), custom_call_target="tpu_custom_call" | custom-call | tf_op jit(solution)/shard_map/pallas_call | solution.py:838
  35.5 3.1 %shard_map.152 = (f32[20,136,128]{2,1,0:T(8,128)S(1)}, f32[10,136,128]{2,1,0:T(8,128)S(1)}) custom-call(s32[3]{0:T(128)S(1)} %copy-done.12, f32[20,136,128]{2,1,0:T(8,128)S(1)} %get-tuple-element.41.outer.refs_0_, f32[40,160,128]{2,1,0:T(8,128)S(1)} %get-tuple-element.42.mid, bf16[136,480]{1,0:T(8,128)(2,1)S(1)} %copy-done.1, bf16[256,256]{1,0:T(8,128)(2,1)S(1)} %copy-done.2), custom_call_target="tpu_custom_call" | custom-call | flops 8000000 | bytes 8000000 | tf_op jit(solution)/shard_map/pallas_call | solution.py:838
  38.6 1.3 %collective-permute-start.7 = (f32[10,136,128]{2,1,0:T(8,128)S(1)}, f32[10,136,128]{2,1,0:T(8,128)S(1)}, u32[]{:S(2)}, u32[]{:S(2)}) collective-permute-start(f32[10,136,128]{2,1,0:T(8,128)S(1)} %get-tuple-element.44), channel_id=1, source_target_pairs={{0,4},{4,0},{1,5},{5,1},{2,6},{6,2},{3,7},{7,3},{8,12},{12,8},{9,1... | collective-permute-start | bytes 2088968 | tf_op jit(solution)/shard_map/ppermute | solution.py:131
  39.9 3.4 %collective-permute-start.9 = (f32[9,136,128]{2,1,0:T(8,128)S(1)}, f32[9,136,128]{2,1,0:T(8,128)S(1)}, u32[]{:S(2)}, u32[]{:S(2)}) collective-permute-start(f32[9,136,128]{2,1,0:T(8,128)S(1)} %get-tuple-element.46), channel_id=1, source_target_pairs={{0,0},{1,2},{2,1},{3,3},{4,4},{5,6},{6,5},{7,7},{8,8},{9,10},{10,9... | collective-permute-start | bytes 1880072 | tf_op jit(solution)/shard_map/ppermute | solution.py:131
  43.4 3.2 %collective-permute-start.11 = (f32[2,136,128]{2,1,0:T(8,128)S(1)}, f32[2,136,128]{2,1,0:T(8,128)S(1)}, u32[]{:S(2)}, u32[]{:S(2)}) collective-permute-start(f32[2,136,128]{2,1,0:T(8,128)S(1)} %get-tuple-element.48), channel_id=1, source_target_pairs={{0,0},{1,6},{2,5},{3,3},{4,4},{5,2},{6,1},{7,7},{8,8},{9,14},{10,1... | collective-permute-start | bytes 417800 | tf_op jit(solution)/shard_map/ppermute | solution.py:132
  46.6 2.2 %shard_map.154 = (f32[42,144,128]{2,1,0:T(8,128)S(1)}, f32[42,144,128]{2,1,0:T(8,128)S(1)}) custom-call(s32[3]{0:T(128)S(1)} %copy-done.13, f32[32,32,128]{2,1,0:T(8,128)S(1)} %copy-done.10, f32[68,8,128]{2,1,0:T(8,128)S(1)} %collective-permute-done.refs_0_, f32[17,32,128]{2,1,0:T(8,128)S(1)} %collective-permute-done.1.refs_1_, ...), custom_call_target="tpu_custom_call" | custom-call | flops 8000000 | bytes 8000000 | tf_op jit(solution)/shard_map/pallas_call | solution.py:838
  48.8 5.5 %collective-permute-done.10.refs_5_ = f32[2,136,128]{2,1,0:T(8,128)S(1)} collective-permute-done((f32[2,136,128]{2,1,0:T(8,128)S(1)}, f32[2,136,128]{2,1,0:T(8,128)S(1)}, u32[]{:S(2)}, u32[]{:S(2)}) %collective-permute-start.10) | collective-permute-done | bytes 139296 | tf_op jit(solution)/shard_map/ppermute | solution.py:132
  54.3 1.8 %collective-permute-done.11.refs_6_ = f32[2,136,128]{2,1,0:T(8,128)S(1)} collective-permute-done((f32[2,136,128]{2,1,0:T(8,128)S(1)}, f32[2,136,128]{2,1,0:T(8,128)S(1)}, u32[]{:S(2)}, u32[]{:S(2)}) %collective-permute-start.11) | collective-permute-done | bytes 139296 | tf_op jit(solution)/shard_map/ppermute | solution.py:132
  56.1 1.1 collective-permute-done.7.refs_2_
  57.2 1.1 shard_map.155
  59.4 2.3 %shard_map.153.partial = f32[42,144,128]{2,1,0:T(8,128)S(1)} custom-call(s32[3]{0:T(128)S(1)} %copy-done.13, f32[20,136,128]{2,1,0:T(8,128)S(1)} %get-tuple-element.41.outer.refs_0_, f32[20,136,128]{2,1,0:T(8,128)S(1)} %get-tuple-element.43.refs_1_, f32[10,136,128]{2,1,0:T(8,128)S(1)} %collective-permute-done.7.refs_2_, ...), custom_call_target="tpu_custom_call" | custom-call | flops 8000000 | bytes 8000000 | tf_op jit(solution)/shard_map/pallas_call | solution.py:838
  61.7 2.7 %collective-permute-done.13.refs_3_ = f32[62,8,128]{2,1,0:T(8,128)S(1)} collective-permute-done((f32[62,8,128]{2,1,0:T(8,128)S(1)}, f32[62,8,128]{2,1,0:T(8,128)S(1)}, u32[]{:S(2)}, u32[]{:S(2)}) %collective-permute-start.13) | collective-permute-done | bytes 253984 | tf_op jit(solution)/shard_map/ppermute | solution.py:132
  64.4 17.6 %shard_map.156 = (f32[40,136,128]{2,1,0:T(8,128)S(1)}, f32[42,144,128]{2,1,0:T(8,128)S(1)}, f32[40,144,128]{2,1,0:T(8,128)S(1)}, f32[5,136,128]{2,1,0:T(8,128)S(...) custom-call(s32[3]{0:T(128)S(1)} %copy-done.13, ...), custom_call_target="tpu_custom_call" | custom-call | tf_op jit(solution)/shard_map/pallas_call | solution.py:838
  82.1 1.3 %collective-permute-start.14 = (f32[5,136,128]{2,1,0:T(8,128)S(1)}, f32[5,136,128]{2,1,0:T(8,128)S(1)}, u32[]{:S(2)}, u32[]{:S(2)}) collective-permute-start(f32[5,136,128]{2,1,0:T(8,128)S(1)} %get-tuple-element.54), channel_id=1, source_target_pairs={{0,4},{4,0},{1,5},{5,1},{2,6},{6,2},{3,7},{7,3},{8,12},{12,8},{9,1... | collective-permute-start | bytes 1044488 | tf_op jit(solution)/shard_map/ppermute | solution.py:131
  83.4 1.5 %collective-permute-start.16 = (f32[5,136,128]{2,1,0:T(8,128)S(1)}, f32[5,136,128]{2,1,0:T(8,128)S(1)}, u32[]{:S(2)}, u32[]{:S(2)}) collective-permute-start(f32[5,136,128]{2,1,0:T(8,128)S(1)} %get-tuple-element.56), channel_id=1, source_target_pairs={{0,8},{1,2},{2,1},{3,11},{4,12},{5,6},{6,5},{7,15},{8,0},{9,10},{1... | collective-permute-start | bytes 1044488 | tf_op jit(solution)/shard_map/ppermute | solution.py:132
  84.9 1.2 %collective-permute-start.17 = (f32[1,136,128]{2,1,0:T(8,128)S(1)}, f32[1,136,128]{2,1,0:T(8,128)S(1)}, u32[]{:S(2)}, u32[]{:S(2)}) collective-permute-start(f32[1,136,128]{2,1,0:T(8,128)S(1)} %get-tuple-element.57), channel_id=1, source_target_pairs={{0,5},{1,4},{2,7},{3,6},{4,1},{5,0},{6,3},{7,2},{8,13},{9,12},{10,... | collective-permute-start | bytes 208904 | tf_op jit(solution)/shard_map/ppermute | solution.py:132
  86.1 2.4 %collective-permute-start.18 = (f32[1,136,128]{2,1,0:T(8,128)S(1)}, f32[1,136,128]{2,1,0:T(8,128)S(1)}, u32[]{:S(2)}, u32[]{:S(2)}) collective-permute-start(f32[1,136,128]{2,1,0:T(8,128)S(1)} %get-tuple-element.58), channel_id=1, source_target_pairs={{0,8},{1,6},{2,5},{3,11},{4,12},{5,2},{6,1},{7,15},{8,0},{9,14},{1... | collective-permute-start | bytes 208904 | tf_op jit(solution)/shard_map/ppermute | solution.py:132
  88.5 4.8 %collective-permute-done.17.refs_4_ = f32[1,136,128]{2,1,0:T(8,128)S(1)} collective-permute-done((f32[1,136,128]{2,1,0:T(8,128)S(1)}, f32[1,136,128]{2,1,0:T(8,128)S(1)}, u32[]{:S(2)}, u32[]{:S(2)}) %collective-permute-start.17) | collective-permute-done | bytes 69664 | tf_op jit(solution)/shard_map/ppermute | solution.py:132
  94.1 2.9 %collective-permute-start.19 = (f32[34,8,128]{2,1,0:T(8,128)S(1)}, f32[34,8,128]{2,1,0:T(8,128)S(1)}, u32[]{:S(2)}, u32[]{:S(2)}) collective-permute-start(f32[34,8,128]{2,1,0:T(8,128)S(1)} %get-tuple-element.62), channel_id=1, source_target_pairs={{0,8},{1,9},{2,10},{3,11},{4,12},{5,13},{6,14},{7,15},{8,0},{9,1},... | collective-permute-start | bytes 417800 | tf_op jit(solution)/shard_map/ppermute | solution.py:132
  97.3 1.8 %shard_map.157.partial = f32[34,144,128]{2,1,0:T(8,128)S(1)} custom-call(s32[3]{0:T(128)S(1)} %copy-done.13, f32[40,136,128]{2,1,0:T(8,128)S(1)} %get-tuple-element.53.refs_0_, f32[5,136,128]{2,1,0:T(8,128)S(1)} %collective-permute-done.14.refs_1_, f32[5,136,128]{2,1,0:T(8,128)S(1)} %collective-permute-done.15.refs_2_, ...), custom_call_target="tpu_custom_call" | custom-call | flops 8000000 | bytes 8000000 | tf_op jit(solution)/shard_map/pallas_call | solution.py:838
  99.1 2.6 %collective-permute-done.20.refs_1_ = f32[34,8,128]{2,1,0:T(8,128)S(1)} collective-permute-done((f32[34,8,128]{2,1,0:T(8,128)S(1)}, f32[34,8,128]{2,1,0:T(8,128)S(1)}, u32[]{:S(2)}, u32[]{:S(2)}) %collective-permute-start.20) | collective-permute-done | bytes 139296 | tf_op jit(solution)/shard_map/ppermute | solution.py:132
  101.7 7.5 %shard_map.159 = (f32[3,32,32,128]{3,2,1,0:T(8,128)}, f32[3,32,32,128]{3,2,1,0:T(8,128)}) custom-call(s32[3]{0:T(128)S(1)} %copy-done.13, f32[34,144,128]{2,1,0:T(8,128)S(1)} %shard_map.157.partial, f32[42,144,128]{2,1,0:T(8,128)S(1)} %get-tuple-element.50.refs_7_.modulus, f32[42,144,128]{2,1,0:T(8,128)S(1)} %get-tuple-element.59.beside, ...), custom_call_target="tpu_custom_call" | custom-call | tf_op jit(solution)/shard_map/pallas_call | solution.py:838
  (50 shorter events, 3.8 us)
Async XLA Ops:
  0.6 26.3 %copy-start.2 = (bf16[256,256]{1,0:T(8,128)(2,1)S(1)}, bf16[256,256]{1,0:T(8,128)(2,1)}, u32[]{:S(2)}) copy-start(bf16[256,256]{1,0:T(8,128)(2,1)} %constant.39.clone.refs_9_.back_y.refs_11_) | copy-start | bytes 393220
  0.6 26.3 %copy-start.1 = (bf16[136,480]{1,0:T(8,128)(2,1)S(1)}, bf16[136,480]{1,0:T(8,128)(2,1)}, u32[]{:S(2)}) copy-start(bf16[136,480]{1,0:T(8,128)(2,1)} %constant.38.clone.refs_8_.back_x.refs_10_) | copy-start | bytes 391684
  0.7 26.2 %copy-start.3 = (f32[40,8,128]{2,1,0:T(8,128)S(1)}, f32[40,8,128]{2,1,0:T(8,128)}, u32[]{:S(2)}) copy-start(f32[40,8,128]{2,1,0:T(8,128)} %constant.41.clone.refs_11_.refs_13_) | copy-start | bytes 491524
  0.7 26.2 %copy-start.4 = (bf16[160,480]{1,0:T(8,128)(2,1)S(1)}, bf16[160,480]{1,0:T(8,128)(2,1)}, u32[]{:S(2)}) copy-start(bf16[160,480]{1,0:T(8,128)(2,1)} %constant.37.clone.refs_7_.refs_9_) | copy-start | bytes 460804
  0.7 26.2 %copy-start.5 = (bf16[160,480]{1,0:T(8,128)(2,1)S(1)}, bf16[160,480]{1,0:T(8,128)(2,1)}, u32[]{:S(2)}) copy-start(bf16[160,480]{1,0:T(8,128)(2,1)} %constant.36.clone.refs_6_.refs_8_) | copy-start | bytes 460804
  0.7 26.2 %copy-start.6 = (bf16[160,480]{1,0:T(8,128)(2,1)S(1)}, bf16[160,480]{1,0:T(8,128)(2,1)}, u32[]{:S(2)}) copy-start(bf16[160,480]{1,0:T(8,128)(2,1)} %constant.35.clone.refs_5_.refs_7_) | copy-start | bytes 460804
  0.7 26.2 %copy-start.7 = (bf16[160,480]{1,0:T(8,128)(2,1)S(1)}, bf16[160,480]{1,0:T(8,128)(2,1)}, u32[]{:S(2)}) copy-start(bf16[160,480]{1,0:T(8,128)(2,1)} %constant.34.clone.refs_4_.refs_6_) | copy-start | bytes 460804
  0.7 15.2 %copy-start = (f32[3,32,32,128]{3,2,1,0:T(8,128)S(1)}, f32[3,32,32,128]{3,2,1,0:T(8,128)}, u32[]{:S(2)}) copy-start(f32[3,32,32,128]{3,2,1,0:T(8,128)} %load.1) | copy-start | bytes 4718596
  0.7 26.2 %copy-start.8 = (bf16[160,432]{1,0:T(8,128)(2,1)S(1)}, bf16[160,432]{1,0:T(8,128)(2,1)}, u32[]{:S(2)}) copy-start(bf16[160,432]{1,0:T(8,128)(2,1)} %constant.33.clone.refs_3_.refs_5_) | copy-start | bytes 414724
  0.7 26.2 %copy-start.9 = (bf16[256,256]{1,0:T(8,128)(2,1)S(1)}, bf16[256,256]{1,0:T(8,128)(2,1)}, u32[]{:S(2)}) copy-start(bf16[256,256]{1,0:T(8,128)(2,1)} %constant.32.clone.refs_2_.refs_4_) | copy-start | bytes 393220
  0.8 26.2 %copy-start.11 = (f32[160,128]{1,0:T(8,128)S(1)}, f32[160,128]{1,0:T(8,128)}, u32[]{:S(2)}) copy-start(f32[160,128]{1,0:T(8,128)} %constant.40.clone.refs_10_.refs_12_) | copy-start | bytes 245764
  5.1 10.8 %collective-permute-start = (f32[68,8,128]{2,1,0:T(8,128)}, f32[68,8,128]{2,1,0:T(8,128)S(1)}, u32[]{:S(2)}, u32[]{:S(2)}) collective-permute-start(f32[68,8,128]{2,1,0:T(8,128)} %get-tuple-element.33), channel_id=1, source_target_pairs={{0,4},{4,0},{1,5},{5,1},{2,6},{6,2},{3,7},{7,3},{8,12},{12,8},{9,1... | collective-permute-start | bytes 835592 | tf_op jit(solution)/shard_map/ppermute | solution.py:131
  6.4 9.5 %collective-permute-start.1 = (f32[17,32,128]{2,1,0:T(8,128)}, f32[17,32,128]{2,1,0:T(8,128)S(1)}, u32[]{:S(2)}, u32[]{:S(2)}) collective-permute-start(f32[17,32,128]{2,1,0:T(8,128)} %get-tuple-element.34), channel_id=1, source_target_pairs={{0,1},{1,0},{2,3},{3,2},{4,5},{5,4},{6,7},{7,6},{8,9},{9,8},{10,11... | collective-permute-start | bytes 835592 | tf_op jit(solution)/shard_map/ppermute | solution.py:132
  6.6 9.3 %collective-permute-start.2 = (f32[17,32,128]{2,1,0:T(8,128)}, f32[17,32,128]{2,1,0:T(8,128)S(1)}, u32[]{:S(2)}, u32[]{:S(2)}) collective-permute-start(f32[17,32,128]{2,1,0:T(8,128)} %get-tuple-element.35), channel_id=1, source_target_pairs={{0,8},{1,2},{2,1},{3,11},{4,12},{5,6},{6,5},{7,15},{8,0},{9,10},{1... | collective-permute-start | bytes 835592 | tf_op jit(solution)/shard_map/ppermute | solution.py:132
  9.0 5.4 %collective-permute-start.3 = (f32[11,8,128]{2,1,0:T(8,128)}, f32[11,8,128]{2,1,0:T(8,128)S(1)}, u32[]{:S(2)}, u32[]{:S(2)}) collective-permute-start(f32[11,8,128]{2,1,0:T(8,128)} %get-tuple-element.36), channel_id=1, source_target_pairs={{0,5},{1,4},{2,7},{3,6},{4,1},{5,0},{6,3},{7,2},{8,13},{9,12},{10,... | collective-permute-start | bytes 135176 | tf_op jit(solution)/shard_map/ppermute | solution.py:132
  9.1 6.8 %collective-permute-start.4 = (f32[11,8,128]{2,1,0:T(8,128)}, f32[11,8,128]{2,1,0:T(8,128)S(1)}, u32[]{:S(2)}, u32[]{:S(2)}) collective-permute-start(f32[11,8,128]{2,1,0:T(8,128)} %get-tuple-element.37), channel_id=1, source_target_pairs={{0,8},{1,6},{2,5},{3,11},{4,12},{5,2},{6,1},{7,15},{8,0},{9,14},{1... | collective-permute-start | bytes 135176 | tf_op jit(solution)/shard_map/ppermute | solution.py:132
  18.3 5.0 %collective-permute-start.5 = (f32[40,8,128]{2,1,0:T(8,128)S(1)}, f32[40,8,128]{2,1,0:T(8,128)S(1)}, u32[]{:S(2)}, u32[]{:S(2)}) collective-permute-start(f32[40,8,128]{2,1,0:T(8,128)S(1)} %get-tuple-element.39), channel_id=1, source_target_pairs={{0,8},{8,0},{16,24},{24,16},{1,9},{9,1},{17,25},{25,17},{2,10},{10... | collective-permute-start | bytes 491528 | tf_op jit(solution)/shard_map/ppermute | solution.py:131
  20.3 6.6 %collective-permute-start.6 = (f32[40,8,128]{2,1,0:T(8,128)S(1)}, f32[40,8,128]{2,1,0:T(8,128)S(1)}, u32[]{:S(2)}, u32[]{:S(2)}) collective-permute-start(f32[40,8,128]{2,1,0:T(8,128)S(1)} %get-tuple-element.40), channel_id=1, source_target_pairs={{0,0},{8,16},{16,8},{24,24},{1,1},{9,17},{17,9},{25,25},{2,2},{10,... | collective-permute-start | bytes 491528 | tf_op jit(solution)/shard_map/ppermute | solution.py:131
  38.6 18.6 %collective-permute-start.7 = (f32[10,136,128]{2,1,0:T(8,128)S(1)}, f32[10,136,128]{2,1,0:T(8,128)S(1)}, u32[]{:S(2)}, u32[]{:S(2)}) collective-permute-start(f32[10,136,128]{2,1,0:T(8,128)S(1)} %get-tuple-element.44), channel_id=1, source_target_pairs={{0,4},{4,0},{1,5},{5,1},{2,6},{6,2},{3,7},{7,3},{8,12},{12,8},{9,1... | collective-permute-start | bytes 2088968 | tf_op jit(solution)/shard_map/ppermute | solution.py:131
  39.9 16.3 %collective-permute-start.8 = (f32[9,136,128]{2,1,0:T(8,128)S(1)}, f32[9,136,128]{2,1,0:T(8,128)S(1)}, u32[]{:S(2)}, u32[]{:S(2)}) collective-permute-start(f32[9,136,128]{2,1,0:T(8,128)S(1)} %get-tuple-element.45), channel_id=1, source_target_pairs={{0,1},{1,0},{2,3},{3,2},{4,5},{5,4},{6,7},{7,6},{8,9},{9,8},{10,11... | collective-permute-start | bytes 1880072 | tf_op jit(solution)/shard_map/ppermute | solution.py:131
  39.9 16.3 %collective-permute-start.9 = (f32[9,136,128]{2,1,0:T(8,128)S(1)}, f32[9,136,128]{2,1,0:T(8,128)S(1)}, u32[]{:S(2)}, u32[]{:S(2)}) collective-permute-start(f32[9,136,128]{2,1,0:T(8,128)S(1)} %get-tuple-element.46), channel_id=1, source_target_pairs={{0,0},{1,2},{2,1},{3,3},{4,4},{5,6},{6,5},{7,7},{8,8},{9,10},{10,9... | collective-permute-start | bytes 1880072 | tf_op jit(solution)/shard_map/ppermute | solution.py:131
  43.3 11.0 %collective-permute-start.10 = (f32[2,136,128]{2,1,0:T(8,128)S(1)}, f32[2,136,128]{2,1,0:T(8,128)S(1)}, u32[]{:S(2)}, u32[]{:S(2)}) collective-permute-start(f32[2,136,128]{2,1,0:T(8,128)S(1)} %get-tuple-element.47), channel_id=1, source_target_pairs={{0,5},{1,4},{2,7},{3,6},{4,1},{5,0},{6,3},{7,2},{8,13},{9,12},{10,... | collective-permute-start | bytes 417800 | tf_op jit(solution)/shard_map/ppermute | solution.py:132
  43.4 12.8 %collective-permute-start.11 = (f32[2,136,128]{2,1,0:T(8,128)S(1)}, f32[2,136,128]{2,1,0:T(8,128)S(1)}, u32[]{:S(2)}, u32[]{:S(2)}) collective-permute-start(f32[2,136,128]{2,1,0:T(8,128)S(1)} %get-tuple-element.48), channel_id=1, source_target_pairs={{0,0},{1,6},{2,5},{3,3},{4,4},{5,2},{6,1},{7,7},{8,8},{9,14},{10,1... | collective-permute-start | bytes 417800 | tf_op jit(solution)/shard_map/ppermute | solution.py:132
  58.3 3.4 %collective-permute-start.12 = (f32[62,8,128]{2,1,0:T(8,128)S(1)}, f32[62,8,128]{2,1,0:T(8,128)S(1)}, u32[]{:S(2)}, u32[]{:S(2)}) collective-permute-start(f32[62,8,128]{2,1,0:T(8,128)S(1)} %get-tuple-element.51), channel_id=1, source_target_pairs={{0,8},{1,9},{2,10},{3,11},{4,12},{5,13},{6,14},{7,15},{8,0},{9,1},... | collective-permute-start | bytes 761864 | tf_op jit(solution)/shard_map/ppermute | solution.py:132
  58.4 6.1 %collective-permute-start.13 = (f32[62,8,128]{2,1,0:T(8,128)S(1)}, f32[62,8,128]{2,1,0:T(8,128)S(1)}, u32[]{:S(2)}, u32[]{:S(2)}) collective-permute-start(f32[62,8,128]{2,1,0:T(8,128)S(1)} %get-tuple-element.52), channel_id=1, source_target_pairs={{0,4},{1,5},{2,6},{3,7},{4,0},{5,1},{6,2},{7,3},{8,16},{9,17},{10,... | collective-permute-start | bytes 761864 | tf_op jit(solution)/shard_map/ppermute | solution.py:132
  82.1 11.2 %collective-permute-start.14 = (f32[5,136,128]{2,1,0:T(8,128)S(1)}, f32[5,136,128]{2,1,0:T(8,128)S(1)}, u32[]{:S(2)}, u32[]{:S(2)}) collective-permute-start(f32[5,136,128]{2,1,0:T(8,128)S(1)} %get-tuple-element.54), channel_id=1, source_target_pairs={{0,4},{4,0},{1,5},{5,1},{2,6},{6,2},{3,7},{7,3},{8,12},{12,8},{9,1... | collective-permute-start | bytes 1044488 | tf_op jit(solution)/shard_map/ppermute | solution.py:131
  83.4 9.9 %collective-permute-start.15 = (f32[5,136,128]{2,1,0:T(8,128)S(1)}, f32[5,136,128]{2,1,0:T(8,128)S(1)}, u32[]{:S(2)}, u32[]{:S(2)}) collective-permute-start(f32[5,136,128]{2,1,0:T(8,128)S(1)} %get-tuple-element.55), channel_id=1, source_target_pairs={{0,1},{1,0},{2,3},{3,2},{4,5},{5,4},{6,7},{7,6},{8,9},{9,8},{10,11... | collective-permute-start | bytes 1044488 | tf_op jit(solution)/shard_map/ppermute | solution.py:132
  83.4 9.9 %collective-permute-start.16 = (f32[5,136,128]{2,1,0:T(8,128)S(1)}, f32[5,136,128]{2,1,0:T(8,128)S(1)}, u32[]{:S(2)}, u32[]{:S(2)}) collective-permute-start(f32[5,136,128]{2,1,0:T(8,128)S(1)} %get-tuple-element.56), channel_id=1, source_target_pairs={{0,8},{1,2},{2,1},{3,11},{4,12},{5,6},{6,5},{7,15},{8,0},{9,10},{1... | collective-permute-start | bytes 1044488 | tf_op jit(solution)/shard_map/ppermute | solution.py:132
  84.9 8.4 %collective-permute-start.17 = (f32[1,136,128]{2,1,0:T(8,128)S(1)}, f32[1,136,128]{2,1,0:T(8,128)S(1)}, u32[]{:S(2)}, u32[]{:S(2)}) collective-permute-start(f32[1,136,128]{2,1,0:T(8,128)S(1)} %get-tuple-element.57), channel_id=1, source_target_pairs={{0,5},{1,4},{2,7},{3,6},{4,1},{5,0},{6,3},{7,2},{8,13},{9,12},{10,... | collective-permute-start | bytes 208904 | tf_op jit(solution)/shard_map/ppermute | solution.py:132
  86.1 7.3 %collective-permute-start.18 = (f32[1,136,128]{2,1,0:T(8,128)S(1)}, f32[1,136,128]{2,1,0:T(8,128)S(1)}, u32[]{:S(2)}, u32[]{:S(2)}) collective-permute-start(f32[1,136,128]{2,1,0:T(8,128)S(1)} %get-tuple-element.58), channel_id=1, source_target_pairs={{0,8},{1,6},{2,5},{3,11},{4,12},{5,2},{6,1},{7,15},{8,0},{9,14},{1... | collective-permute-start | bytes 208904 | tf_op jit(solution)/shard_map/ppermute | solution.py:132
  94.1 5.0 %collective-permute-start.19 = (f32[34,8,128]{2,1,0:T(8,128)S(1)}, f32[34,8,128]{2,1,0:T(8,128)S(1)}, u32[]{:S(2)}, u32[]{:S(2)}) collective-permute-start(f32[34,8,128]{2,1,0:T(8,128)S(1)} %get-tuple-element.62), channel_id=1, source_target_pairs={{0,8},{1,9},{2,10},{3,11},{4,12},{5,13},{6,14},{7,15},{8,0},{9,1},... | collective-permute-start | bytes 417800 | tf_op jit(solution)/shard_map/ppermute | solution.py:132
  97.0 4.7 %collective-permute-start.20 = (f32[34,8,128]{2,1,0:T(8,128)S(1)}, f32[34,8,128]{2,1,0:T(8,128)S(1)}, u32[]{:S(2)}, u32[]{:S(2)}) collective-permute-start(f32[34,8,128]{2,1,0:T(8,128)S(1)} %get-tuple-element.63), channel_id=1, source_target_pairs={{0,4},{1,5},{2,6},{3,7},{4,0},{5,1},{6,2},{7,3},{8,16},{9,17},{10,... | collective-permute-start | bytes 417800 | tf_op jit(solution)/shard_map/ppermute | solution.py:132
  (3 other events, 22.9 us)
